TPU v7x, 32 devices: a whole 2x2x4 slice. The times are simulated.
32 devices in a mesh: grp: 8 (over z, x), shard: 4 (over y, core).
Axes of the slice: x: 2, y: 2, z: 4, core: 2. Of those that a mesh axis runs over, the one named last changes fastest.
Arguments:
- tokens: float32 [8192, 1152], P(('grp', 'shard')), may hold values from -6 to 6
- routes: int32 [8192, 1], P(('grp', 'shard')), may hold values from 0 to 1; in each aligned block of 256 rows (0 to 255, 256 to 511, ...) at most 192 rows name the same one
- lengths: int32 [8], P('grp'), may hold values from 512 to 1024, as said below
- cotangent: float32 [8192, 1152], P(('grp', 'shard')), may hold values from -6 to 6
- in_weight: bfloat16 [1152, 4608], P('shard'), may hold values from -0.1875 to 0.1875
- select_weight: bfloat16 [2304, 104], P('shard'), may hold values from -0.125 to 0.125
- step_weight: bfloat16 [72, 2304], P(None, 'shard'), may hold values from -0.75 to 0.75
- out_weight: bfloat16 [2304, 1152], P('shard'), may hold values from -0.125 to 0.125
- router_weight: bfloat16 [1152, 2], P('shard'), may hold values from -0.1875 to 0.1875
- up_weight: bfloat16 [2, 1152, 3072], P(None, 'shard'), may hold values from -0.1875 to 0.1875
- down_weight: bfloat16 [2, 3072, 1152], P(None, 'shard'), may hold values from -0.109375 to 0.109375
- conv_weight: bfloat16 [4, 2304], P(None, 'shard'), may hold values from -3 to 3
- conv_bias: bfloat16 [2304], P('shard'), may hold values from -1.5 to 1.5
- step_bias: bfloat16 [2304], P('shard'), may hold values from -9 to -2
- decay_log: bfloat16 [16, 2304], P(None, 'shard'), may hold values from 0 to 2.765625
- skip_gain: bfloat16 [2304], P('shard'), may hold values from 0.5 to 1.5
- mixer_gain: bfloat16 [1152], P('shard'), may hold values from 0.5 to 1.5
- expert_gain: bfloat16 [1152], P('shard'), may hold values from 0.5 to 1.5
Outputs:
- result: float32 [8192, 1152], P(('grp', 'shard'))
- tokens_grad: float32 [8192, 1152], P(('grp', 'shard'))
- in_grad: float32 [1152, 4608], P('shard', 'grp')
- out_grad: float32 [2304, 1152], P('shard', 'grp')
- up_grad: float32 [2, 1152, 3072], P(None, 'shard', 'grp')
- down_grad: float32 [2, 3072, 1152], P(None, 'shard', 'grp')
- select_grad: float32 [2304, 104], P('shard')
- step_grad: float32 [72, 2304], P(None, 'shard')
- router_grad: float32 [1152, 2], P('shard')
- conv_grad: float32 [4, 2304], P(None, 'shard')
- conv_bias_grad: float32 [2304], P('shard')
- step_bias_grad: float32 [2304], P('shard')
- decay_grad: float32 [16, 2304], P(None, 'shard')
- skip_grad: float32 [2304], P('shard')
- mixer_gain_grad: float32 [1152], P('shard')
- expert_gain_grad: float32 [1152], P('shard')
Inputs may be any that keep to these rules, and one draw needn't show every extreme that they name: `lengths`: every sequence holds at least 512 tokens, and one sequence of each draw fills all 1024 slots. `routes`: among the token slots of one device, no expert is named by more than 192 slots.
All inputs are finite; a program needn't handle non-finite values.
Results may differ from a plain program's by a relative error of at most 0.011.
Values may be sent and summed in bfloat16 or wider, within the bound.
No kernel may reach another device: no remote copies, remote signals or barrier semaphores. Data moves between devices by JAX's collectives and lax.ppermute only.
A program may use at most 320 MiB of HBM per device.

v0:
```python
import jax
import jax.numpy as jnp
from jax import lax
from jax.sharding import PartitionSpec as P

D = 1152
DI = 2304
NS = 16
R = 72
KW = 4
E = 2
BLOCK = 32
CAP = 192


EPSILON = 1e-05


def from_behind(value, axis, steps):
    count = lax.axis_size(axis)
    first, last = (max(0, -steps), min(count, count - steps))
    return lax.ppermute(value, axis, [(source, source + steps) for source in range(first, last)])


def entering(value, axis, combine, identity, reverse):
    size, mine = (lax.axis_size(axis), lax.axis_index(axis))
    everything = jax.tree.map(lambda part: lax.all_gather(part, axis), value)
    start = jax.tree.map(
        lambda part, zero: jnp.broadcast_to(jnp.asarray(zero, part.dtype), part.shape),
        value,
        identity,
    )

    def step(k, before):
        at = size - 1 - k if reverse else k
        reached = at > mine if reverse else at < mine
        new = combine(before, jax.tree.map(lambda part: part[at], everything))
        return jax.tree.map(lambda a, b: jnp.where(reached, a, b), new, before)

    return lax.fori_loop(0, size, step, start)


def rms_norm(values, gain):
    return values * lax.rsqrt(jnp.mean(values * values, axis=-1, keepdims=True) + EPSILON) * gain


def conv_act(padded, weight, bias):
    count = padded.shape[0] - (KW - 1)
    summed = bias[None, :] + weight[0][None, :] * padded[0:count]
    for offset in range(1, KW):
        summed = summed + weight[offset][None, :] * padded[offset : offset + count]
    return jax.nn.silu(summed)


def state_scan(inputs, steps, entry_map, read_map, decay, start):
    blocks = inputs.shape[0] // BLOCK

    def one_block(state, pieces):
        block_in, block_step, block_entry, block_read = pieces
        outputs = []
        for index in range(BLOCK):
            state = (
                jnp.exp(block_step[index][None, :] * decay) * state
                + block_entry[index][:, None] * (block_step[index] * block_in[index])[None, :]
            )
            outputs.append(jnp.sum(block_read[index][:, None] * state, axis=0))
        return (state, jnp.stack(outputs))

    pieces = (
        inputs.reshape(blocks, BLOCK, -1),
        steps.reshape(blocks, BLOCK, -1),
        entry_map.reshape(blocks, BLOCK, -1),
        read_map.reshape(blocks, BLOCK, -1),
    )
    final, outputs = lax.scan(jax.checkpoint(one_block), start, pieces)
    return (outputs.reshape(inputs.shape[0], -1), final)


def carry_read(read_map, steps, rates, start):
    rising = jnp.cumsum(steps, axis=0)
    total = jnp.zeros(steps.shape, jnp.float32)
    for index in range(start.shape[0]):
        total = (
            total
            + read_map[:, index : index + 1]
            * jnp.exp(rising * rates[index][None, :])
            * start[index][None, :]
        )
    return total


def span_product(steps, rates):
    return jnp.exp(rates * jnp.sum(steps, axis=0)[None, :])


def chain(earlier, later):
    return (earlier[0] * later[0], later[0] * earlier[1] + later[1])


def matmul(left, right):
    return jnp.dot(left, right, preferred_element_type=jnp.float32)


def body(
    tokens,
    routes,
    lengths,
    cotangent,
    in_weight,
    select_weight,
    step_weight,
    out_weight,
    router_weight,
    up_weight,
    down_weight,
    conv_weight,
    conv_bias,
    step_bias,
    decay_log,
    skip_gain,
    mixer_gain,
    expert_gain,
):
    span = tokens.shape[0]
    gathered = (
        lax.all_gather(in_weight, "shard", axis=0, tiled=True),
        lax.all_gather(select_weight, "shard", axis=0, tiled=True),
        lax.all_gather(step_weight, "shard", axis=1, tiled=True),
        lax.all_gather(out_weight, "shard", axis=0, tiled=True),
        lax.all_gather(router_weight, "shard", axis=0, tiled=True),
        lax.all_gather(up_weight, "shard", axis=1, tiled=True),
        lax.all_gather(down_weight, "shard", axis=1, tiled=True),
        lax.all_gather(conv_weight, "shard", axis=1, tiled=True),
        lax.all_gather(conv_bias, "shard", axis=0, tiled=True),
        lax.all_gather(step_bias, "shard", axis=0, tiled=True),
        lax.all_gather(decay_log, "shard", axis=1, tiled=True),
        lax.all_gather(skip_gain, "shard", axis=0, tiled=True),
        lax.all_gather(mixer_gain, "shard", axis=0, tiled=True),
        lax.all_gather(expert_gain, "shard", axis=0, tiled=True),
    )
    (
        in_full,
        select_full,
        step_full,
        out_full,
        router_full,
        up_full,
        down_full,
        conv_full,
        conv_bias_full,
        step_bias_full,
        decay_full,
        skip_full,
        mixer_full,
        expert_full,
    ) = gathered
    place = lax.axis_index("shard") * span + jnp.arange(span, dtype=jnp.int32)
    keep_int = (place < lengths[0]).astype(jnp.int32)
    keep = keep_int.astype(jnp.float32)[:, None]
    normed_one, norm_pull = jax.vjp(rms_norm, tokens, mixer_full.astype(jnp.float32))
    normed = normed_one.astype(jnp.bfloat16)
    projected = matmul(normed, in_full)
    inner = projected[:, :DI] * keep
    zgate = projected[:, DI:]
    rim = from_behind(inner[span - (KW - 1) :], "shard", 1)
    padded = jnp.concatenate([rim, inner], axis=0)
    conv_out, conv_pull = jax.vjp(
        conv_act, padded, conv_full.astype(jnp.float32), conv_bias_full.astype(jnp.float32)
    )
    conv_low = conv_out.astype(jnp.bfloat16)
    selected = matmul(conv_low, select_full)
    rank_low = selected[:, :R].astype(jnp.bfloat16)
    step_pre = matmul(rank_low, step_full) + step_bias_full.astype(jnp.float32)
    step_size, step_pull = jax.vjp(lambda value: jax.nn.softplus(value) * keep, step_pre)
    decay, decay_pull = jax.vjp(lambda value: -jnp.exp(value), decay_full.astype(jnp.float32))
    entry_map = selected[:, R : R + NS]
    read_map = selected[:, R + NS :]
    empty_state = jnp.zeros((NS, DI), jnp.float32)
    (scan_local, end_local), scan_pull = jax.vjp(
        state_scan, conv_out, step_size, entry_map, read_map, decay, empty_state
    )
    span_decay, span_pull = jax.vjp(span_product, step_size, decay)
    unity = jnp.ones((NS, DI), jnp.float32)
    carried = entering((span_decay, end_local), "shard", chain, (unity, empty_state), False)
    state_in = carried[1]
    correction, carry_pull = jax.vjp(
        jax.checkpoint(carry_read), read_map, step_size, decay, state_in
    )
    scanned = scan_local + correction
    skip_f = skip_full.astype(jnp.float32)
    mixed_in = scanned + skip_f * conv_out
    gated_f, gate_pull = jax.vjp(lambda value, other: value * jax.nn.silu(other), mixed_in, zgate)
    gated = gated_f.astype(jnp.bfloat16)
    first_sum = tokens + matmul(gated, out_full)
    normed_second, norm_two_pull = jax.vjp(rms_norm, first_sum, expert_full.astype(jnp.float32))
    normed_two = normed_second.astype(jnp.bfloat16)
    logits = matmul(normed_two, router_full)
    probs, soft_pull = jax.vjp(lambda value: jax.nn.softmax(value, axis=-1), logits)
    expert_ids = jnp.arange(E, dtype=jnp.int32)[None, :]
    picked_int = (routes == expert_ids).astype(jnp.int32) * keep_int[:, None]
    picked = picked_int.astype(jnp.float32)
    gate = jnp.sum(probs * picked, axis=1)
    ranks = jnp.cumsum(picked_int, axis=0) - 1
    slot_each = jnp.where(picked_int > 0, expert_ids * CAP + ranks, E * CAP)
    slots = jnp.min(slot_each, axis=1)
    source = (
        jnp.full((E * CAP + 1,), span, jnp.int32).at[slots].set(jnp.arange(span, dtype=jnp.int32))
    )
    normed_pad = jnp.concatenate([normed_two, jnp.zeros((1, D), jnp.bfloat16)], axis=0)
    rows = normed_pad[source[: E * CAP]].reshape(E, CAP, D)
    pre = jnp.einsum("ecd,edf->ecf", rows, up_full, preferred_element_type=jnp.float32)
    hidden_f, gelu_pull = jax.vjp(lambda value: jax.nn.gelu(value, approximate=True), pre)
    hidden_act = hidden_f.astype(jnp.bfloat16)
    expert_out = jnp.einsum(
        "ecf,efd->ecd", hidden_act, down_full, preferred_element_type=jnp.float32
    )
    out_pad = jnp.concatenate(
        [expert_out.reshape(E * CAP, D), jnp.zeros((1, D), jnp.float32)], axis=0
    )
    token_out = out_pad[slots]
    result = keep * (first_sum + gate[:, None] * token_out)
    again = (
        lax.all_gather(in_weight, "shard", axis=0, tiled=True),
        lax.all_gather(select_weight, "shard", axis=0, tiled=True),
        lax.all_gather(step_weight, "shard", axis=1, tiled=True),
        lax.all_gather(out_weight, "shard", axis=0, tiled=True),
        lax.all_gather(router_weight, "shard", axis=0, tiled=True),
        lax.all_gather(up_weight, "shard", axis=1, tiled=True),
        lax.all_gather(down_weight, "shard", axis=1, tiled=True),
        lax.all_gather(conv_weight, "shard", axis=1, tiled=True),
        lax.all_gather(conv_bias, "shard", axis=0, tiled=True),
        lax.all_gather(step_bias, "shard", axis=0, tiled=True),
        lax.all_gather(decay_log, "shard", axis=1, tiled=True),
        lax.all_gather(skip_gain, "shard", axis=0, tiled=True),
        lax.all_gather(mixer_gain, "shard", axis=0, tiled=True),
        lax.all_gather(expert_gain, "shard", axis=0, tiled=True),
    )
    in_back, select_back, step_back, out_back, router_back, up_back, down_back = (
        again[0],
        again[1],
        again[2],
        again[3],
        again[4],
        again[5],
        again[6],
    )
    skip_back = again[11].astype(jnp.float32)
    grad_out = keep * cotangent
    grad_token_out = gate[:, None] * grad_out
    grad_gate = jnp.sum(token_out * grad_out, axis=1)
    grad_logits = soft_pull(picked * grad_gate[:, None])[0].astype(jnp.bfloat16)
    router_grad = jnp.dot(normed_two.T, grad_logits, preferred_element_type=jnp.float32)
    grad_normed = jnp.dot(grad_logits, router_back.T, preferred_element_type=jnp.float32)
    grad_slots = jnp.zeros((E * CAP + 1, D), jnp.float32).at[slots].set(grad_token_out)
    grad_expert = grad_slots[: E * CAP].reshape(E, CAP, D).astype(jnp.bfloat16)
    down_grad = jnp.einsum(
        "ecf,ecd->efd", hidden_act, grad_expert, preferred_element_type=jnp.float32
    )
    grad_hidden = jnp.einsum(
        "ecd,efd->ecf", grad_expert, down_back, preferred_element_type=jnp.float32
    )
    grad_pre = gelu_pull(grad_hidden)[0].astype(jnp.bfloat16)
    up_grad = jnp.einsum("ecd,ecf->edf", rows, grad_pre, preferred_element_type=jnp.float32)
    grad_rows = jnp.einsum("ecf,edf->ecd", grad_pre, up_back, preferred_element_type=jnp.float32)
    grad_rows_pad = jnp.concatenate(
        [grad_rows.reshape(E * CAP, D), jnp.zeros((1, D), jnp.float32)], axis=0
    )
    grad_normed = grad_normed + grad_rows_pad[slots]
    grad_first_norm, expert_gain_grad = norm_two_pull(grad_normed)
    grad_first = grad_out + grad_first_norm
    grad_first_low = grad_first.astype(jnp.bfloat16)
    out_grad = jnp.dot(gated.T, grad_first_low, preferred_element_type=jnp.float32)
    grad_gated = jnp.dot(grad_first_low, out_back.T, preferred_element_type=jnp.float32)
    grad_mixed, grad_zgate = gate_pull(grad_gated)
    skip_grad = jnp.sum(grad_mixed * conv_out, axis=0)
    grad_read_carry, grad_step_carry, grad_decay_carry, grad_start = carry_pull(grad_mixed)
    incoming = entering((span_decay, grad_start), "shard", chain, (unity, empty_state), True)
    grad_conv_scan, grad_step_scan, grad_entry, grad_read_scan, grad_decay_scan, unused_start = (
        scan_pull((grad_mixed, incoming[1]))
    )
    grad_step_end, grad_decay_end = span_pull(incoming[1] * state_in)
    grad_step_size = grad_step_scan + grad_step_carry + grad_step_end
    grad_decay = grad_decay_scan + grad_decay_carry + grad_decay_end
    grad_read = grad_read_scan + grad_read_carry
    decay_grad = decay_pull(grad_decay)[0]
    grad_step_pre = step_pull(grad_step_size)[0]
    step_bias_grad = jnp.sum(grad_step_pre, axis=0)
    grad_step_low = grad_step_pre.astype(jnp.bfloat16)
    step_grad = jnp.dot(rank_low.T, grad_step_low, preferred_element_type=jnp.float32)
    grad_rank = jnp.dot(grad_step_low, step_back.T, preferred_element_type=jnp.float32)
    grad_selected = jnp.concatenate([grad_rank, grad_entry, grad_read], axis=1).astype(jnp.bfloat16)
    select_grad = jnp.dot(conv_low.T, grad_selected, preferred_element_type=jnp.float32)
    grad_conv_out = (
        grad_conv_scan
        + skip_back * grad_mixed
        + jnp.dot(grad_selected, select_back.T, preferred_element_type=jnp.float32)
    )
    grad_padded, conv_grad, conv_bias_grad = conv_pull(grad_conv_out)
    back_rim = from_behind(grad_padded[: KW - 1], "shard", -1)
    grad_inner = grad_padded[KW - 1 :] + jnp.concatenate(
        [jnp.zeros((span - (KW - 1), DI), jnp.float32), back_rim], axis=0
    )
    grad_projected = jnp.concatenate([grad_inner * keep, grad_zgate], axis=1).astype(jnp.bfloat16)
    in_grad = jnp.dot(normed.T, grad_projected, preferred_element_type=jnp.float32)
    grad_normed_one = jnp.dot(grad_projected, in_back.T, preferred_element_type=jnp.float32)
    grad_tokens_norm, mixer_gain_grad = norm_pull(grad_normed_one)
    tokens_grad = grad_first + grad_tokens_norm
    group_sums = (
        lax.psum_scatter(in_grad, "shard", scatter_dimension=0, tiled=True),
        lax.psum_scatter(out_grad, "shard", scatter_dimension=0, tiled=True),
        lax.psum_scatter(up_grad, "shard", scatter_dimension=1, tiled=True),
        lax.psum_scatter(down_grad, "shard", scatter_dimension=1, tiled=True),
        lax.psum_scatter(select_grad, "shard", scatter_dimension=0, tiled=True),
        lax.psum_scatter(step_grad, "shard", scatter_dimension=1, tiled=True),
        lax.psum_scatter(router_grad, "shard", scatter_dimension=0, tiled=True),
        lax.psum_scatter(conv_grad, "shard", scatter_dimension=1, tiled=True),
        lax.psum_scatter(conv_bias_grad, "shard", scatter_dimension=0, tiled=True),
        lax.psum_scatter(step_bias_grad, "shard", scatter_dimension=0, tiled=True),
        lax.psum_scatter(decay_grad, "shard", scatter_dimension=1, tiled=True),
        lax.psum_scatter(skip_grad, "shard", scatter_dimension=0, tiled=True),
        lax.psum_scatter(mixer_gain_grad, "shard", scatter_dimension=0, tiled=True),
        lax.psum_scatter(expert_gain_grad, "shard", scatter_dimension=0, tiled=True),
    )
    large_sums = (
        lax.psum_scatter(group_sums[0], "grp", scatter_dimension=1, tiled=True),
        lax.psum_scatter(group_sums[1], "grp", scatter_dimension=1, tiled=True),
        lax.psum_scatter(group_sums[2], "grp", scatter_dimension=2, tiled=True),
        lax.psum_scatter(group_sums[3], "grp", scatter_dimension=2, tiled=True),
    )
    small_sums = lax.psum(
        (
            group_sums[4],
            group_sums[5],
            group_sums[6],
            group_sums[7],
            group_sums[8],
            group_sums[9],
            group_sums[10],
            group_sums[11],
            group_sums[12],
            group_sums[13],
        ),
        "grp",
    )
    return (
        result,
        tokens_grad,
        large_sums[0],
        large_sums[1],
        large_sums[2],
        large_sums[3],
        small_sums[0],
        small_sums[1],
        small_sums[2],
        small_sums[3],
        small_sums[4],
        small_sums[5],
        small_sums[6],
        small_sums[7],
        small_sums[8],
        small_sums[9],
    )


def solution(mesh):
    return jax.shard_map(
        body,
        mesh=mesh,
        in_specs=(
            P(("grp", "shard"), None),
            P(("grp", "shard"), None),
            P("grp"),
            P(("grp", "shard"), None),
            P("shard", None),
            P("shard", None),
            P(None, "shard"),
            P("shard", None),
            P("shard", None),
            P(None, "shard", None),
            P(None, "shard", None),
            P(None, "shard"),
            P("shard"),
            P("shard"),
            P(None, "shard"),
            P("shard"),
            P("shard"),
            P("shard"),
        ),
        out_specs=(
            P(("grp", "shard"), None),
            P(("grp", "shard"), None),
            P("shard", "grp"),
            P("shard", "grp"),
            P(None, "shard", "grp"),
            P(None, "shard", "grp"),
            P("shard", None),
            P(None, "shard"),
            P("shard", None),
            P(None, "shard"),
            P("shard"),
            P("shard"),
            P(None, "shard"),
            P("shard"),
            P("shard"),
            P("shard"),
        ),
        check_vma=False,
    )
```

profile of v0, /device:TPU:2, one launch (start us, length us, event | category | flops | bytes accessed | tf_op | source)
XLA Modules:
  0.0 2624.1 jit_solution(3761879568754328963)
XLA Ops:
  14.0 11.9 all-reduce.234
  26.8 5.3 all-gather.3
  32.3 10.6 all-gather.4
  42.8 8.8 all-gather.5
  51.6 5.7 all-gather.6
  60.7 26.7 %all-gather.13.cloned.1.call-done = bf16[1152,4608]{1,0:T(8,128)(2,1)} async-done(((bf16[288,4608]{1,0:T(8,128)(2,1)}), bf16[1152,4608]{1,0:T(8,128)(2,1)}) %all-gather.13.cloned.1.call-update) | async-done | bytes 10616848 | tf_op jit(solution)/shard_map/all_gather | solution.py:126
  87.3 6.1 fusion.295
  104.0 5.4 all-gather.7
  110.1 6.1 fusion.259
  118.2 4.9 fusion.302
  125.5 453.7 %while.70 = (s32[]{:T(128)}, f32[16,2304]{1,0:T(8,128)S(1)}, f32[8,32,2304]{2,1,0:T(8,128)}, f32[8,16,2304]{2,1,0:T(8,128)}, f32[8,32,2304]{2,1,0:T(8,128)}, /*i...) while((s32[]{:T(128)}, f32[16,2304]{1,0:T(8,128)S(1)}, ...), condition=%wide.region_34.35_spmd.clone, body=%wide.region_1.34_spmd.clone.sunk | while | flops 10580002 | bytes 11542933 | solution.py:75
  177.2 3.5 stack.197
  233.9 3.6 stack.197
  579.2 3.8 fusion.145
  590.8 8.3 all-gather.1
  599.1 7.8 all-gather
  606.8 4.6 while.71
  612.9 11.8 multiply_convert_fusion.1
  624.8 5.0 multiply_reduce_fusion.234
  633.7 10.6 fusion.309
  644.3 10.0 fusion.297
  664.1 10.4 fusion.137
  674.5 9.9 fusion.310
  692.8 4.7 fusion.278
  697.5 5.6 multiply_reduce_fusion.192
  712.2 8.2 fusion.169
  720.3 7.7 fusion.174
  728.1 7.9 fusion.179
  736.0 12.2 multiply_add_fusion.95
  748.7 8.1 all-gather.2
  756.8 4.5 while.72
  766.5 402.1 %while.73 = (s32[]{:T(128)}, f32[16,2304]{1,0:T(8,128)}, f32[16,2304]{1,0:T(8,128)}, f32[8,32,2304]{2,1,0:T(8,128)}, f32[8,32,2304]{2,1,0:T(8,128)}, /*index=5*/...) while((s32[]{:T(128)}, f32[16,2304]{1,0:T(8,128)}, ...), condition=%wide.region_201.202_spmd.clone, body=%wide.region_72.201_spmd.clone.sunk | while | flops 45115396 | bytes 34012316 | solution.py:75
  810.7 5.7 select_add_fusion.2
  860.9 5.7 select_add_fusion.2
  911.1 5.7 select_add_fusion.2
  961.3 5.7 select_add_fusion.2
  1011.5 5.7 select_add_fusion.2
  1061.7 5.7 select_add_fusion.2
  1111.9 5.7 select_add_fusion.2
  1162.1 5.7 select_add_fusion.2
  1168.6 22.5 fusion.251
  1202.1 4.3 bitcast_add_fusion.3
  1206.7 7.9 multiply_reduce_fusion.195
  1219.2 8.9 fusion.260
  1233.5 23.7 fusion.296
  1259.3 5.8 fusion.276
  1266.3 12.5 fusion.311
  1285.0 100.2 %reduce-scatter.27.cloned.1.call-done = f32[288,4608]{1,0:T(8,128)} async-done(((f32[1152,4608]{1,0:T(8,128)}), f32[288,4608]{1,0:T(8,128)}) %reduce-scatter.27.cloned.1.call-update) | async-done | bytes 5308432 | tf_op jit(solution)/shard_map/reduce_scatter | solution.py:309
  1385.2 6.7 copy.109
  1391.9 21.6 reduce-scatter.43.cloned.1.call-done
  1415.3 26.5 %reduce-scatter.41.cloned.1.call-done = f32[576,104]{1,0:T(8,128)} async-done(((f32[2304,104]{1,0:T(8,128)}), f32[576,104]{1,0:T(8,128)}) %reduce-scatter.41.cloned.1.call-update) | async-done | bytes 239632
  1443.7 202.0 %reduce-scatter.35.cloned.1.call-done = f32[2,768,1152]{2,1,0:T(8,128)} async-done(((f32[2,3072,1152]{2,1,0:T(8,128)}), f32[2,768,1152]{2,1,0:T(8,128)}) %reduce-scatter.35.cloned.1.call-update) | async-done | bytes 7077904 | tf_op jit(solution)/shard_map/reduce_scatter | solution.py:312
  1645.7 12.6 copy.104
  1658.3 76.1 %reduce-scatter.29.cloned.1.call-done = f32[576,1152]{1,0:T(8,128)} async-done(((f32[2304,1152]{1,0:T(8,128)}), f32[576,1152]{1,0:T(8,128)}) %reduce-scatter.29.cloned.1.call-update) | async-done | bytes 2654224 | tf_op jit(solution)/shard_map/reduce_scatter | solution.py:310
  1738.0 200.0 %reduce-scatter.31.cloned.1.call-done = f32[2,288,3072]{2,1,0:T(8,128)} async-done(((f32[2,1152,3072]{2,1,0:T(8,128)}), f32[2,288,3072]{2,1,0:T(8,128)}) %reduce-scatter.31.cloned.1.call-update) | async-done | bytes 7077904 | tf_op jit(solution)/shard_map/reduce_scatter | solution.py:311
  1940.5 22.8 reduce-scatter.45.cloned.1.call-done
  1964.9 9.2 multiply_reduce_fusion.230
  1974.0 11.6 all-reduce.233
  1992.9 27.2 %reduce-scatter.49.cloned.1.call-done = f32[576,16]{1,0:T(8,128)} async-done(((f32[2304,16]{1,0:T(8,128)}), f32[576,16]{1,0:T(8,128)}) %reduce-scatter.49.cloned.1.call-update) | async-done | bytes 36880
  2021.2 36.0 %all-reduce.231 = (f32[288,2]{0,1:T(2,128)}, f32[4,576]{1,0:T(4,128)}, f32[576]{0:T(1024)}, f32[576]{0:T(1024)}, f32[16,576]{1,0:T(8,128)}, /*index=5*/f32[576]{0:T(1024)}, f32[288]{0:T(512)}, f32[288]{0:T(512)}) all-reduce(f32[288,2]{0,1:T(2,128)S(1)} %copy-done.217, ...), channel_id=1, replica_groups=mesh['grp'=8,'shard'=4] {'grp'}, use_global_device_ids=true, to_apply=%region_235.236 | all-reduce | flops 14400 | bytes 115200 | tf_op jit(solution)/shard_map/psum | solution.py:330
  2057.2 98.5 %reduce-scatter.37.cloned.1.call-done = f32[576,288]{1,0:T(8,128)} async-done(((f32[4608,288]{1,0:T(8,128)}), f32[576,288]{1,0:T(8,128)}) %reduce-scatter.37.cloned.1.call-update) | async-done | bytes 663568
  2158.0 249.8 %all-reduce.237.cloned.1.call-done = (f32[2,768,1152]{1,0,2:T(2,128)}, f32[576,104]{0,1:T(8,128)}, f32[72,576]{1,0:T(8,128)}) async-done(((f32[2,768,1152]{1,0,2:T(2,128)}, f32[576,104]{0,1:T(8,128)}, f32[72,576]{1,0:T(8,128)}), (f32[2,768,1152]{1,0,2:T(2,128)}, f32[576,104]{0,1:T(8,128)}, f32[72,576]{1,0:T(8,128)})) %all-reduce.237.cloned.1.call-update) | async-done | bytes 7483408
  2410.3 72.9 %reduce-scatter.39.cloned.1.call-done = f32[144,576]{1,0:T(8,128)} async-done(((f32[1152,576]{1,0:T(8,128)}), f32[144,576]{1,0:T(8,128)}) %reduce-scatter.39.cloned.1.call-update) | async-done | bytes 331792
  2483.2 132.8 %reduce-scatter.33.cloned.1.call-done = f32[2,288,384]{2,1,0:T(8,128)} async-done(((f32[2,288,3072]{2,1,0:T(8,128)}), f32[2,288,384]{2,1,0:T(8,128)}) %reduce-scatter.33.cloned.1.call-update) | async-done | bytes 884752 | tf_op jit(solution)/shard_map/reduce_scatter | solution.py:327
  (3698 shorter events, 918.6 us)
Async XLA Ops:
  7.2 80.2 %all-gather.13.cloned.1.call-start = ((), (), s32[]{:S(2)}) async-start(), calls=%async_computation.12 | async-start | bytes 13271040 | tf_op jit(solution)/shard_map/all_gather | solution.py:126
  7.9 616.9 %all-gather.15.cloned.1.call-start = ((), (), s32[]{:S(2)}) async-start(), calls=%async_computation.13 | async-start | bytes 6635520 | tf_op jit(solution)/shard_map/all_gather | solution.py:129
  8.7 625.1 %all-gather.17.cloned.1.call-start = ((), (), s32[]{:S(2)}) async-start(), calls=%async_computation.14 | async-start | bytes 17694720 | tf_op jit(solution)/shard_map/all_gather | solution.py:131
  9.5 33.3 %copy-start.177 = (bf16[72,576]{1,0:T(8,128)(2,1)S(1)}, bf16[72,576]{1,0:T(8,128)(2,1)}, u32[]{:S(2)}) copy-start(bf16[72,576]{1,0:T(8,128)(2,1)} %param.32) | copy-start | bytes 248836
  9.5 42.1 %copy-start.214 = (bf16[16,576]{1,0:T(8,128)(2,1)S(1)}, bf16[16,576]{1,0:T(8,128)(2,1)}, u32[]{:S(2)}) copy-start(bf16[16,576]{1,0:T(8,128)(2,1)} %param.40) | copy-start | bytes 55300
  9.5 634.8 %all-gather.19.cloned.1.call-start = ((), (), s32[]{:S(2)}) async-start(), calls=%async_computation.15 | async-start | bytes 17694720 | tf_op jit(solution)/shard_map/all_gather | solution.py:132
  10.1 47.3 %copy-start.204 = (s32[256,1]{0,1:T(1,128)S(1)}, s32[256,1]{0,1:T(1,128)}, u32[]{:S(2)}) copy-start(s32[256,1]{0,1:T(1,128)} %param.27) | copy-start | bytes 3076
  10.1 1375.1 %reduce-scatter.27.cloned.1.call-start = ((), (), s32[]{:S(2)}) async-start(), calls=%async_computation.16 | async-start | bytes 26542080 | tf_op jit(solution)/shard_map/reduce_scatter | solution.py:309
  25.9 67.5 %copy-start.149 = (f32[1152]{0:T(1024)}, f32[1152]{0:T(1024)S(1)}, u32[]{:S(2)}) copy-start(f32[1152]{0:T(1024)S(1)} %convert_element_type.84) | copy-start | bytes 13828
  26.1 31.3 %copy-start.239 = (f32[256]{0:T(256)}, f32[256]{0:T(256)S(1)}, u32[]{:S(2)}) copy-start(f32[256]{0:T(256)S(1)} %multiply_reduce_fusion.235) | copy-start | bytes 3076
  26.1 67.3 %copy-start.212 = (f32[256]{0:T(256)}, f32[256]{0:T(256)S(1)}, u32[]{:S(2)}) copy-start(f32[256]{0:T(256)S(1)} %fusion.286) | copy-start | bytes 3076
  32.2 77.8 %copy-start.186 = (f32[2304]{0:T(1024)}, f32[2304]{0:T(1024)S(1)}, u32[]{:S(2)}) copy-start(f32[2304]{0:T(1024)S(1)} %get-tuple-element.1347) | copy-start | bytes 27652
  32.2 77.8 %copy-start.188 = (f32[2304]{0:T(1024)}, f32[2304]{0:T(1024)S(1)}, u32[]{:S(2)}) copy-start(f32[2304]{0:T(1024)S(1)} %get-tuple-element.1348) | copy-start | bytes 27652
  32.3 77.8 %copy-start.190 = (f32[2304]{0:T(1024)}, f32[2304]{0:T(1024)S(1)}, u32[]{:S(2)}) copy-start(f32[2304]{0:T(1024)S(1)} %get-tuple-element.1349) | copy-start | bytes 27652
  32.3 77.8 %copy-start.192 = (f32[2304]{0:T(1024)}, f32[2304]{0:T(1024)S(1)}, u32[]{:S(2)}) copy-start(f32[2304]{0:T(1024)S(1)} %get-tuple-element.1350) | copy-start | bytes 27652
  57.4 60.8 %copy-start.178 = (f32[256]{0:T(256)}, f32[256]{0:T(256)S(1)}, u32[]{:S(2)}) copy-start(f32[256]{0:T(256)S(1)} %fusion.292) | copy-start | bytes 3076
  58.5 34.9 %copy-start.207 = (s32[256]{0:T(256)}, s32[256]{0:T(256)S(1)}, u32[]{:S(2)}) copy-start(s32[256]{0:T(256)S(1)} %compare_convert_fusion.1) | copy-start | bytes 3076
  97.1 13.0 collective-permute-start
  579.2 33.8 %copy-start = (f32[8,32,2304]{2,1,0:T(8,128)}, f32[8,32,2304]{2,1,0:T(8,128)S(1)}, u32[]{:S(2)}) copy-start(f32[8,32,2304]{2,1,0:T(8,128)S(1)} %get-tuple-element.3332) | copy-start | bytes 7077892
  611.5 150.5 %copy-start.21 = (f32[16,2304]{1,0:T(8,128)}, f32[16,2304]{1,0:T(8,128)S(1)}, u32[]{:S(2)}) copy-start(f32[16,2304]{1,0:T(8,128)S(1)} %get-tuple-element.593) | copy-start | bytes 442372
  633.6 54.5 %copy-start.184 = (f32[256,2]{0,1:T(2,128)}, f32[256,2]{0,1:T(2,128)S(1)}, u32[]{:S(2)}) copy-start(f32[256,2]{0,1:T(2,128)S(1)} %get-tuple-element.1743) | copy-start | bytes 6148
  633.6 54.5 %copy-start.202 = (f32[256]{0:T(256)}, f32[256]{0:T(256)S(1)}, u32[]{:S(2)}) copy-start(f32[256]{0:T(256)S(1)} %get-tuple-element.1742) | copy-start | bytes 3076
  633.7 54.5 %copy-start.210 = (f32[256]{0:T(256)}, f32[256]{0:T(256)S(1)}, u32[]{:S(2)}) copy-start(f32[256]{0:T(256)S(1)} %fusion.293) | copy-start | bytes 3076
  770.8 32.2 %copy-start.18 = (f32[2304]{0:T(1024)}, f32[2304]{0:T(1024)S(1)}, u32[]{:S(2)}) copy-start(f32[2304]{0:T(1024)S(1)} %get-tuple-element.2685) | copy-start | bytes 27652 | tf_op jit(solution)/shard_map/transpose(jvp())/while
  771.6 31.5 %copy-start.24 = (f32[2304]{0:T(1024)}, f32[2304]{0:T(1024)S(1)}, u32[]{:S(2)}) copy-start(f32[2304]{0:T(1024)S(1)} %get-tuple-element.2681) | copy-start | bytes 27652 | tf_op jit(solution)/shard_map/transpose(jvp())/while
  771.9 31.1 %copy-start.50 = (f32[2304]{0:T(1024)}, f32[2304]{0:T(1024)S(1)}, u32[]{:S(2)}) copy-start(f32[2304]{0:T(1024)S(1)} %get-tuple-element.2782) | copy-start | bytes 27652 | tf_op jit(solution)/shard_map/transpose(jvp())/while
  771.9 31.1 %copy-start.57 = (f32[2304]{0:T(1024)}, f32[2304]{0:T(1024)S(1)}, u32[]{:S(2)}) copy-start(f32[2304]{0:T(1024)S(1)} %get-tuple-element.2683) | copy-start | bytes 27652 | tf_op jit(solution)/shard_map/transpose(jvp())/while
  821.0 32.2 %copy-start.18 = (f32[2304]{0:T(1024)}, f32[2304]{0:T(1024)S(1)}, u32[]{:S(2)}) copy-start(f32[2304]{0:T(1024)S(1)} %get-tuple-element.2685) | copy-start | bytes 27652 | tf_op jit(solution)/shard_map/transpose(jvp())/while
  821.8 31.5 %copy-start.24 = (f32[2304]{0:T(1024)}, f32[2304]{0:T(1024)S(1)}, u32[]{:S(2)}) copy-start(f32[2304]{0:T(1024)S(1)} %get-tuple-element.2681) | copy-start | bytes 27652 | tf_op jit(solution)/shard_map/transpose(jvp())/while
  822.1 31.1 %copy-start.50 = (f32[2304]{0:T(1024)}, f32[2304]{0:T(1024)S(1)}, u32[]{:S(2)}) copy-start(f32[2304]{0:T(1024)S(1)} %get-tuple-element.2782) | copy-start | bytes 27652 | tf_op jit(solution)/shard_map/transpose(jvp())/while
  822.2 31.1 %copy-start.57 = (f32[2304]{0:T(1024)}, f32[2304]{0:T(1024)S(1)}, u32[]{:S(2)}) copy-start(f32[2304]{0:T(1024)S(1)} %get-tuple-element.2683) | copy-start | bytes 27652 | tf_op jit(solution)/shard_map/transpose(jvp())/while
  871.2 32.2 %copy-start.18 = (f32[2304]{0:T(1024)}, f32[2304]{0:T(1024)S(1)}, u32[]{:S(2)}) copy-start(f32[2304]{0:T(1024)S(1)} %get-tuple-element.2685) | copy-start | bytes 27652 | tf_op jit(solution)/shard_map/transpose(jvp())/while
  872.0 31.5 %copy-start.24 = (f32[2304]{0:T(1024)}, f32[2304]{0:T(1024)S(1)}, u32[]{:S(2)}) copy-start(f32[2304]{0:T(1024)S(1)} %get-tuple-element.2681) | copy-start | bytes 27652 | tf_op jit(solution)/shard_map/transpose(jvp())/while
  872.3 31.1 %copy-start.50 = (f32[2304]{0:T(1024)}, f32[2304]{0:T(1024)S(1)}, u32[]{:S(2)}) copy-start(f32[2304]{0:T(1024)S(1)} %get-tuple-element.2782) | copy-start | bytes 27652 | tf_op jit(solution)/shard_map/transpose(jvp())/while
  921.4 32.2 %copy-start.18 = (f32[2304]{0:T(1024)}, f32[2304]{0:T(1024)S(1)}, u32[]{:S(2)}) copy-start(f32[2304]{0:T(1024)S(1)} %get-tuple-element.2685) | copy-start | bytes 27652 | tf_op jit(solution)/shard_map/transpose(jvp())/while
  922.2 31.5 %copy-start.24 = (f32[2304]{0:T(1024)}, f32[2304]{0:T(1024)S(1)}, u32[]{:S(2)}) copy-start(f32[2304]{0:T(1024)S(1)} %get-tuple-element.2681) | copy-start | bytes 27652 | tf_op jit(solution)/shard_map/transpose(jvp())/while
  922.5 31.1 %copy-start.50 = (f32[2304]{0:T(1024)}, f32[2304]{0:T(1024)S(1)}, u32[]{:S(2)}) copy-start(f32[2304]{0:T(1024)S(1)} %get-tuple-element.2782) | copy-start | bytes 27652 | tf_op jit(solution)/shard_map/transpose(jvp())/while
  922.5 31.1 %copy-start.57 = (f32[2304]{0:T(1024)}, f32[2304]{0:T(1024)S(1)}, u32[]{:S(2)}) copy-start(f32[2304]{0:T(1024)S(1)} %get-tuple-element.2683) | copy-start | bytes 27652 | tf_op jit(solution)/shard_map/transpose(jvp())/while
  971.5 32.2 %copy-start.18 = (f32[2304]{0:T(1024)}, f32[2304]{0:T(1024)S(1)}, u32[]{:S(2)}) copy-start(f32[2304]{0:T(1024)S(1)} %get-tuple-element.2685) | copy-start | bytes 27652 | tf_op jit(solution)/shard_map/transpose(jvp())/while
  972.3 31.5 %copy-start.24 = (f32[2304]{0:T(1024)}, f32[2304]{0:T(1024)S(1)}, u32[]{:S(2)}) copy-start(f32[2304]{0:T(1024)S(1)} %get-tuple-element.2681) | copy-start | bytes 27652 | tf_op jit(solution)/shard_map/transpose(jvp())/while
  1021.7 32.2 %copy-start.18 = (f32[2304]{0:T(1024)}, f32[2304]{0:T(1024)S(1)}, u32[]{:S(2)}) copy-start(f32[2304]{0:T(1024)S(1)} %get-tuple-element.2685) | copy-start | bytes 27652 | tf_op jit(solution)/shard_map/transpose(jvp())/while
  1022.5 31.5 %copy-start.24 = (f32[2304]{0:T(1024)}, f32[2304]{0:T(1024)S(1)}, u32[]{:S(2)}) copy-start(f32[2304]{0:T(1024)S(1)} %get-tuple-element.2681) | copy-start | bytes 27652 | tf_op jit(solution)/shard_map/transpose(jvp())/while
  1022.9 31.1 %copy-start.50 = (f32[2304]{0:T(1024)}, f32[2304]{0:T(1024)S(1)}, u32[]{:S(2)}) copy-start(f32[2304]{0:T(1024)S(1)} %get-tuple-element.2782) | copy-start | bytes 27652 | tf_op jit(solution)/shard_map/transpose(jvp())/while
  1022.9 31.1 %copy-start.57 = (f32[2304]{0:T(1024)}, f32[2304]{0:T(1024)S(1)}, u32[]{:S(2)}) copy-start(f32[2304]{0:T(1024)S(1)} %get-tuple-element.2683) | copy-start | bytes 27652 | tf_op jit(solution)/shard_map/transpose(jvp())/while
  1071.9 32.2 %copy-start.18 = (f32[2304]{0:T(1024)}, f32[2304]{0:T(1024)S(1)}, u32[]{:S(2)}) copy-start(f32[2304]{0:T(1024)S(1)} %get-tuple-element.2685) | copy-start | bytes 27652 | tf_op jit(solution)/shard_map/transpose(jvp())/while
  1072.7 31.5 %copy-start.24 = (f32[2304]{0:T(1024)}, f32[2304]{0:T(1024)S(1)}, u32[]{:S(2)}) copy-start(f32[2304]{0:T(1024)S(1)} %get-tuple-element.2681) | copy-start | bytes 27652 | tf_op jit(solution)/shard_map/transpose(jvp())/while
  1122.1 32.2 %copy-start.18 = (f32[2304]{0:T(1024)}, f32[2304]{0:T(1024)S(1)}, u32[]{:S(2)}) copy-start(f32[2304]{0:T(1024)S(1)} %get-tuple-element.2685) | copy-start | bytes 27652 | tf_op jit(solution)/shard_map/transpose(jvp())/while
  1122.9 31.5 %copy-start.24 = (f32[2304]{0:T(1024)}, f32[2304]{0:T(1024)S(1)}, u32[]{:S(2)}) copy-start(f32[2304]{0:T(1024)S(1)} %get-tuple-element.2681) | copy-start | bytes 27652 | tf_op jit(solution)/shard_map/transpose(jvp())/while
  1214.6 3.1 collective-permute-start.1
  1228.1 185.4 %reduce-scatter.43.cloned.1.call-start = ((), (), s32[]{:S(2)}) async-start(), calls=%async_computation.24 | async-start | bytes 1474560
  1231.9 210.0 %reduce-scatter.41.cloned.1.call-start = ((), (), s32[]{:S(2)}) async-start(), calls=%async_computation.23 | async-start | bytes 1474560
  1233.5 412.2 %reduce-scatter.35.cloned.1.call-start = ((), (), s32[]{:S(2)}) async-start(), calls=%async_computation.20 | async-start | bytes 35389440 | tf_op jit(solution)/shard_map/reduce_scatter | solution.py:312
  1257.3 477.1 %reduce-scatter.29.cloned.1.call-start = ((), (), s32[]{:S(2)}) async-start(), calls=%async_computation.17 | async-start | bytes 13271040 | tf_op jit(solution)/shard_map/reduce_scatter | solution.py:310
  1265.1 672.8 %reduce-scatter.31.cloned.1.call-start = ((), (), s32[]{:S(2)}) async-start(), calls=%async_computation.18 | async-start | bytes 35389440 | tf_op jit(solution)/shard_map/reduce_scatter | solution.py:311
  1279.1 684.2 %reduce-scatter.45.cloned.1.call-start = ((), (), s32[]{:S(2)}) async-start(), calls=%async_computation.25 | async-start | bytes 737280
  1281.2 710.6 %reduce-scatter.47.cloned.1.call-start = ((), (), s32[]{:S(2)}) async-start(), calls=%async_computation.26 | async-start | bytes 1474560
  1283.2 736.9 %reduce-scatter.49.cloned.1.call-start = ((), (), s32[]{:S(2)}) async-start(), calls=%async_computation.27 | async-start | bytes 1474560
  1285.0 870.6 %reduce-scatter.37.cloned.1.call-start = ((), (), s32[]{:S(2)}) async-start(), calls=%async_computation.21 | async-start | bytes 7962624
  1391.9 1015.9 %all-reduce.237.cloned.1.call-start = ((), (), s32[]{:S(2)}) async-start(), calls=%async_computation.28 | async-start | bytes 15056896
  1658.3 825.0 %reduce-scatter.39.cloned.1.call-start = ((), (), s32[]{:S(2)}) async-start(), calls=%async_computation.22 | async-start | bytes 3317760
  1737.9 878.0 %reduce-scatter.33.cloned.1.call-start = ((), (), s32[]{:S(2)}) async-start(), calls=%async_computation.19 | async-start | bytes 7962624 | tf_op jit(solution)/shard_map/reduce_scatter | solution.py:327
  1986.8 34.4 %copy-start.217 = (f32[288,2]{0,1:T(2,128)S(1)}, f32[288,2]{0,1:T(2,128)}, u32[]{:S(2)}) copy-start(f32[288,2]{0,1:T(2,128)} %copy.118) | copy-start | bytes 6916
  2407.8 208.2 %copy-start.147 = (f32[576,104]{0,1:T(8,128)S(1)}, f32[576,104]{0,1:T(8,128)}, u32[]{:S(2)}) copy-start(f32[576,104]{0,1:T(8,128)} %get-tuple-element.3293) | copy-start | bytes 718852
  2407.8 208.9 %copy-start.151 = (f32[72,576]{1,0:T(8,128)S(1)}, f32[72,576]{1,0:T(8,128)}, u32[]{:S(2)}) copy-start(f32[72,576]{1,0:T(8,128)} %get-tuple-element.3294) | copy-start | bytes 497668
  (1049 other events, 16190.1 us)
Sparse Core Ops, SparseCore 0:
  9.6 77.7 all-gather.12
  88.9 40.8 all-gather.14
  131.3 91.4 all-gather.16
  224.2 91.0 all-gather.18
  1228.2 156.9 reduce-scatter.26
  1387.8 25.7 reduce-scatter.42
  1416.1 25.7 reduce-scatter.40
  1444.6 200.9 reduce-scatter.34
  1648.3 86.1 reduce-scatter.28
  1736.9 201.0 reduce-scatter.30
  1941.2 22.0 reduce-scatter.44
  1965.9 25.8 reduce-scatter.46
  1994.4 25.6 reduce-scatter.48
  2024.1 131.4 reduce-scatter.36
  2160.4 247.3 all-reduce.236
  2411.8 71.3 reduce-scatter.38
  2487.8 128.1 reduce-scatter.32
where the time goes:
time: 2650 us; the launch traced here: 2620 us
  waiting for transfers between devices  1260 us (48%)
  other arithmetic  689 us (26%)
  local copies, waits for them, and re-layouts  371 us (14%)
  matrix products  139 us (5%)
  blocking collectives  119 us (4%)
    unnamed x25, waiting for transfers between devices  525 us
    reduce_scatter x1, waiting for transfers between devices, body(): lax.psum_scatter(down_grad, 'shard', scatter_dimension=1, tiled=True)  202 us
    reduce_scatter x1, waiting for transfers between devices, body(): lax.psum_scatter(up_grad, 'shard', scatter_dimension=1, tiled=True)  200 us
    mul x352, other arithmetic, one_block(): block_step[index] * block_in[index]  178 us
    reduce_sum x136, other arithmetic, one_block(): outputs.append(jnp.sum(block_read[index][:, None] * state, axis=0))  160 us
    another operation x280, local copies, waits for them, and re-layouts, one_block(): return (state, jnp.stack(outputs))  141 us
    reduce_scatter x1, waiting for transfers between devices, body(): lax.psum_scatter(group_sums[2], 'grp', scatter_dimension=2, tiled=True)  133 us
    reduce_sum x64, other arithmetic, one_block(): block_step[index][None, :] * decay  129 us
  transfers between devices with their start and end apart: 19, of which 15 were waited for; matrix products, arithmetic and copies ran while one was open for 24% of the time, Pallas kernels for 0%

commit v1 on v0

v1 whole, which is shorter than its diff:
```python
import functools
import jax
import jax.numpy as jnp
from jax import lax
from jax.experimental import pallas as pl
from jax.experimental.pallas import tpu as pltpu
from jax.sharding import PartitionSpec as P

R = 72
KW = 4
E = 2
CAP = 192
EPSILON = 1e-05
LOG2E = 1.4426950408889634

NS = 16
LANES = 128
STEP = 8
CHUNK = 64


def fold_rows(parts):
    row = lax.broadcasted_iota(jnp.int32, (8, LANES), 0)
    top, pair, even = (row < 4, (row & 2) == 0, (row & 1) == 0)
    fours = [
        jnp.where(top, parts[i], parts[i + 4])
        + pltpu.roll(jnp.where(top, parts[i + 4], parts[i]), 4, 0)
        for i in range(4)
    ]
    twos = [
        jnp.where(
            pair,
            fours[i] + pltpu.roll(fours[i], 6, 0),
            fours[i + 2] + pltpu.roll(fours[i + 2], 2, 0),
        )
        for i in range(2)
    ]
    return jnp.where(
        even, twos[0] + pltpu.roll(twos[0], 7, 0), twos[1] + pltpu.roll(twos[1], 1, 0)
    )


def cut(value):
    return value.reshape(value.shape[0] // STEP, STEP, value.shape[1])


def halves(pair_ref, at, left):
    low, high = (pair_ref[at, 0:8], pair_ref[at, 8:16])
    return (low, high, jnp.where(left, low, high))


def scan_forward_kernel(tiles, dt_ref, dx_ref, entry_ref, read_ref, rate_ref, out_ref, state_ref, end_ref, held):
    @pl.when(pl.program_id(0) == 0)
    def start():
        held[...] = jnp.zeros_like(held)

    left = lax.broadcasted_iota(jnp.int32, (8, LANES), 1) < LANES // 2

    def group(g, states):
        at, base = (g, g * STEP)
        states = list(states)
        entry = [halves(entry_ref, base + t, left) for t in range(STEP)]
        read = [halves(read_ref, base + t, left) for t in range(STEP)]
        for tile in range(tiles + 1):
            columns = slice(tile * LANES, (tile + 1) * LANES)
            rows = [2 * tile] if tile == tiles else [2 * tile, 2 * tile + 1]
            which = [2] if tile == tiles else [0, 1]
            sums = []
            for t in range(STEP):
                step = dt_ref[at, t : t + 1, columns]
                fed = dx_ref[at, t : t + 1, columns]
                total = None
                for r, w in zip(rows, which):
                    state_ref[base + t, r] = states[r]
                    states[r] = jnp.exp2(step * rate_ref[r]) * states[r] + entry[t][w] * fed
                    term = read[t][w] * states[r]
                    total = term if total is None else total + term
                sums.append(total)
            out_ref[at, :, columns] = fold_rows(sums)
        return tuple(states)

    count = 2 * tiles + 1
    states = lax.fori_loop(0, dt_ref.shape[0], group, tuple(held[r] for r in range(count)))
    for r in range(count):
        held[r] = states[r]
        end_ref[r] = states[r]


def scan_forward(dt, dx, entry, read, rate, tiles):
    total, width = dt.shape
    count = 2 * tiles + 1
    chunk = min(CHUNK, total)
    row = pl.BlockSpec((chunk // STEP, STEP, width), lambda i: (i, 0, 0))
    pair = pl.BlockSpec((chunk, NS, LANES), lambda i: (i, 0, 0))
    fixed = pl.BlockSpec((count, 8, LANES), lambda i: (0, 0, 0))
    out, states, end = pl.pallas_call(
        functools.partial(scan_forward_kernel, tiles),
        grid=(total // chunk,),
        in_specs=[row, row, pair, pair, fixed],
        out_specs=[row, pl.BlockSpec((chunk, count, 8, LANES), lambda i: (i, 0, 0, 0)), fixed],
        out_shape=[
            jax.ShapeDtypeStruct((total // STEP, STEP, width), jnp.float32),
            jax.ShapeDtypeStruct((total, count, 8, LANES), jnp.float32),
            jax.ShapeDtypeStruct((count, 8, LANES), jnp.float32),
        ],
        scratch_shapes=[pltpu.VMEM((count, 8, LANES), jnp.float32)],
        compiler_params=pltpu.CompilerParams(vmem_limit_bytes=32 * 2**20),
        cost_estimate=pl.CostEstimate(flops=total * count * 8192, bytes_accessed=total * count * 4096, transcendentals=total * count * 1024),
        name="scan_forward",
    )(cut(dt), cut(dx), entry, read, rate)
    return out.reshape(total, width), states, end


def scan_backward_kernel(
    tiles, dt_ref, dx_ref, grad_ref, entry_ref, read_ref, rate_ref, state_ref, end_ref,
    fed_out, step_out, entry_out, read_out, rate_out, flow, after,
):
    count = 2 * tiles + 1

    @pl.when(pl.program_id(0) == 0)
    def start():
        flow[...] = jnp.zeros_like(flow)
        after[...] = end_ref[...]
        rate_out[...] = jnp.zeros_like(rate_out)

    left = lax.broadcasted_iota(jnp.int32, (8, LANES), 1) < LANES // 2
    groups = dt_ref.shape[0]

    def group(g, carry):
        at = groups - 1 - g
        base = at * STEP
        flows, afters = (list(carry[0]), list(carry[1]))
        entry = [halves(entry_ref, base + t, left) for t in range(STEP)]
        read = [halves(read_ref, base + t, left) for t in range(STEP)]
        entry_sum = [[None, None] for _ in range(STEP)]
        read_sum = [[None, None] for _ in range(STEP)]
        for tile in range(tiles + 1):
            last = tile == tiles
            columns = slice(tile * LANES, (tile + 1) * LANES)
            rows = [2 * tile] if last else [2 * tile, 2 * tile + 1]
            which = [2] if last else [0, 1]
            fed_sums, step_sums = ([None] * STEP, [None] * STEP)
            rate_sum = [rate_out[r] for r in rows]
            for t in reversed(range(STEP)):
                step = dt_ref[at, t : t + 1, columns]
                fed = dx_ref[at, t : t + 1, columns]
                grad = grad_ref[at, t : t + 1, columns]
                for i, (r, w) in enumerate(zip(rows, which)):
                    before = state_ref[base + t, r]
                    arriving = flows[r] + read[t][w] * grad
                    entry_term = arriving * fed
                    read_term = afters[r] * grad
                    fed_term = entry[t][w] * arriving
                    leaving = jnp.exp2(step * rate_ref[r]) * arriving
                    product = leaving * before
                    step_term = product * rate_ref[r]
                    rate_sum[i] = rate_sum[i] + product * step
                    flows[r] = leaving
                    afters[r] = before
                    fed_sums[t] = fed_term if i == 0 else fed_sums[t] + fed_term
                    step_sums[t] = step_term if i == 0 else step_sums[t] + step_term
                    for total, term in ((entry_sum[t], entry_term), (read_sum[t], read_term)):
                        if last:
                            total[0] = total[0] + jnp.where(left, term, 0.0)
                            total[1] = total[1] + jnp.where(left, 0.0, term)
                        else:
                            total[i] = term if total[i] is None else total[i] + term
            fed_out[at, :, columns] = fold_rows(fed_sums)
            step_out[at, :, columns] = fold_rows(step_sums)
            for i, r in enumerate(rows):
                rate_out[r] = rate_sum[i]
        for t in range(STEP):
            for i in range(2):
                entry_out[base + t, 8 * i : 8 * i + 8] = entry_sum[t][i]
                read_out[base + t, 8 * i : 8 * i + 8] = read_sum[t][i]
        return (tuple(flows), tuple(afters))

    flows, afters = lax.fori_loop(
        0,
        groups,
        group,
        (tuple(flow[r] for r in range(count)), tuple(after[r] for r in range(count))),
    )
    for r in range(count):
        flow[r] = flows[r]
        after[r] = afters[r]


def scan_backward(dt, dx, grad, entry, read, rate, states, end, tiles):
    total, width = dt.shape
    count = 2 * tiles + 1
    chunk = min(CHUNK, total)
    steps = total // chunk
    row = pl.BlockSpec((chunk // STEP, STEP, width), lambda i: (steps - 1 - i, 0, 0))
    pair = pl.BlockSpec((chunk, NS, LANES), lambda i: (steps - 1 - i, 0, 0))
    fixed = pl.BlockSpec((count, 8, LANES), lambda i: (0, 0, 0))
    wide = jax.ShapeDtypeStruct((total // STEP, STEP, width), jnp.float32)
    paired = jax.ShapeDtypeStruct((total, NS, LANES), jnp.float32)
    fed, rise, entry_parts, read_parts, rates = pl.pallas_call(
        functools.partial(scan_backward_kernel, tiles),
        grid=(steps,),
        in_specs=[row, row, row, pair, pair, fixed, pl.BlockSpec((chunk, count, 8, LANES), lambda i: (steps - 1 - i, 0, 0, 0)), fixed],
        out_specs=[row, row, pair, pair, fixed],
        out_shape=[wide, wide, paired, paired, jax.ShapeDtypeStruct((count, 8, LANES), jnp.float32)],
        scratch_shapes=[pltpu.VMEM((count, 8, LANES), jnp.float32)] * 2,
        compiler_params=pltpu.CompilerParams(vmem_limit_bytes=48 * 2**20),
        cost_estimate=pl.CostEstimate(flops=total * count * 20480, bytes_accessed=total * count * 4096, transcendentals=total * count * 1024),
        name="scan_backward",
    )(cut(dt), cut(dx), cut(grad), entry, read, rate, states, end)
    return fed.reshape(total, width), rise.reshape(total, width), entry_parts, read_parts, rates


def swap(value, bit):
    size = lax.axis_size("shard")
    return lax.ppermute(value, "shard", [(i, i ^ bit) for i in range(size)])


def gather_rows(value):
    me = lax.axis_index("shard")
    near, far = (swap(value, 1), swap(value, 2))
    pieces = (value, near, far, swap(far, 1))
    rows = value.shape[0]
    whole = jnp.zeros((4 * rows,) + value.shape[1:], value.dtype)
    for k, piece in enumerate(pieces):
        whole = lax.dynamic_update_slice_in_dim(whole, piece, (me ^ k) * rows, 0)
    return whole


def scatter_rows(value):
    me = lax.axis_index("shard")
    side, core = (me // 2, me % 2)
    rows = value.shape[0] // 4
    cut = value.reshape(2, 2, rows, value.shape[1])
    held = lax.dynamic_index_in_dim(cut, core, 1, False)
    given = lax.dynamic_index_in_dim(cut, 1 - core, 1, False).astype(jnp.bfloat16)
    held = held + swap(given, 1).astype(jnp.float32)
    mine = lax.dynamic_index_in_dim(held, side, 0, False)
    given = lax.dynamic_index_in_dim(held, 1 - side, 0, False).astype(jnp.bfloat16)
    return mine + swap(given, 2).astype(jnp.float32)


def sum_small(value):
    value = value + swap(value, 1)
    return value + swap(value, 2)


def turn_blocks(blocks, axis):
    me = lax.axis_index("shard")
    one = blocks.shape[1:]
    rows = one[axis]
    whole = jnp.zeros(one[:axis] + (4 * rows,) + one[axis + 1 :], blocks.dtype)
    for k in range(4):
        piece = lax.dynamic_index_in_dim(blocks, me ^ k, 0, False)
        if k > 0:
            piece = swap(piece, k)
        whole = lax.dynamic_update_slice_in_dim(whole, piece, (me ^ k) * rows, axis)
    return whole


def rms_norm(values, gain):
    return values * lax.rsqrt(jnp.mean(values * values, axis=-1, keepdims=True) + EPSILON) * gain


def matmul(left, right):
    return jnp.dot(left, right, preferred_element_type=jnp.float32)


def matmul_t(left, right):
    return lax.dot_general(left, right, (((1,), (1,)), ((), ())), preferred_element_type=jnp.float32)


def t_matmul(left, right):
    return lax.dot_general(left, right, (((0,), (0,)), ((), ())), preferred_element_type=jnp.float32)


def widen(value, tiles):
    return jnp.concatenate([value, value[:, tiles * LANES :]], axis=1)


def narrow(value, tiles):
    edge = tiles * LANES
    middle = edge + LANES // 2
    return jnp.concatenate([value[:, :edge], value[:, edge:middle] + value[:, middle:]], axis=1)


def pack(value, tiles):
    edge = tiles * LANES
    full = value[:, :edge].reshape(2, 8, tiles, LANES).transpose(2, 0, 1, 3)
    rest = jnp.concatenate([value[:8, edge:], value[8:, edge:]], axis=1)
    return jnp.concatenate([full.reshape(2 * tiles, 8, LANES), rest[None]], axis=0)


def unpack(value, tiles):
    full = value[: 2 * tiles].reshape(tiles, 2, 8, LANES).transpose(1, 2, 0, 3)
    rest = value[2 * tiles]
    rest = jnp.concatenate([rest[:, : LANES // 2], rest[:, LANES // 2 :]], axis=0)
    return jnp.concatenate([full.reshape(NS, tiles * LANES), rest], axis=1)


def spread(value):
    return jnp.broadcast_to(value[:, :, None], value.shape + (LANES,))


def body(
    tokens,
    routes,
    lengths,
    cotangent,
    in_weight,
    select_weight,
    step_weight,
    out_weight,
    router_weight,
    up_weight,
    down_weight,
    conv_weight,
    conv_bias,
    step_bias,
    decay_log,
    skip_gain,
    mixer_gain,
    expert_gain,
):
    f32, bf16 = (jnp.float32, jnp.bfloat16)
    span, width = tokens.shape
    groups, parts = (lax.axis_size("grp"), lax.axis_size("shard"))
    me = lax.axis_index("shard")
    total = span * parts
    inside = conv_bias.shape[0]
    tiles = inside // LANES
    slab = in_weight.shape[0]
    hidden_cols = up_weight.shape[2] // parts

    first = (routes[:, 0] == 0).astype(jnp.int32)
    count_first = jnp.sum(first)
    small = jnp.stack(
        [
            mixer_gain.astype(f32),
            expert_gain.astype(f32),
            router_weight[:, 0].astype(f32),
            router_weight[:, 1].astype(f32),
            jnp.full((slab,), count_first, jnp.int32).astype(f32),
        ]
    )
    small = gather_rows(small[None])
    mixer_full = small[:, 0].reshape(width)
    expert_full = small[:, 1].reshape(width)
    router_full = small[:, 2:4].transpose(0, 2, 1).reshape(width, E).astype(bf16)
    counts = small[:, 4, 0].astype(jnp.int32)

    normed_one, norm_pull = jax.vjp(rms_norm, tokens, mixer_full)
    normed = gather_rows(normed_one.astype(bf16))
    in_blocks = in_weight.reshape(slab, 2, parts, inside).transpose(2, 1, 0, 3)
    in_full = turn_blocks(in_blocks, 1)
    up_blocks = up_weight.reshape(E, slab, parts, hidden_cols).transpose(2, 0, 1, 3)
    up_full = turn_blocks(up_blocks, 1)

    keep = (jnp.arange(total, dtype=jnp.int32) < lengths[0]).astype(f32)[:, None]
    place = me * span + jnp.arange(span, dtype=jnp.int32)
    keep_mine = (place < lengths[0]).astype(f32)[:, None]

    inner = matmul(normed, in_full[0]) * keep
    zgate = matmul(normed, in_full[1])
    taps = conv_weight.astype(f32)
    padded = jnp.concatenate([jnp.zeros((KW - 1, inside), f32), inner], axis=0)
    summed = conv_bias.astype(f32)[None, :]
    for k in range(KW):
        summed = summed + taps[k][None, :] * padded[k : k + total]
    conv_out = jax.nn.silu(summed)
    conv_low = conv_out.astype(bf16)
    selected = sum_small(matmul(conv_low, select_weight))
    rank_low = selected[:, :R].astype(bf16)
    step_pre = matmul(rank_low, step_weight) + step_bias.astype(f32)[None, :]
    step_size = jax.nn.softplus(step_pre) * keep
    entry = spread(selected[:, R : R + NS])
    read = spread(selected[:, R + NS :])
    decay = -jnp.exp(decay_log.astype(f32))
    rate = pack(decay * LOG2E, tiles)
    dt_wide = widen(step_size, tiles)
    dx_wide = widen(step_size * conv_out, tiles)
    scanned, states, end = scan_forward(dt_wide, dx_wide, entry, read, rate, tiles)
    skip = skip_gain.astype(f32)[None, :]
    mixed_in = narrow(scanned, tiles) + skip * conv_out
    gated = (mixed_in * jax.nn.silu(zgate)).astype(bf16)
    first_sum = tokens + scatter_rows(matmul(gated, out_weight))

    normed_second, norm_two_pull = jax.vjp(rms_norm, first_sum, expert_full)
    normed_two = normed_second.astype(bf16)
    logits = matmul(normed_two, router_full)
    probs = jax.nn.softmax(logits, axis=-1)
    picked = (routes == jnp.arange(E, dtype=jnp.int32)[None, :]).astype(f32) * keep_mine
    gate = jnp.sum(probs * picked, axis=1, keepdims=True)
    grad_out = keep_mine * cotangent
    second = 1 - first
    goal = jnp.where(first > 0, jnp.cumsum(first) - 1, count_first + jnp.cumsum(second) - 1)
    order = (jnp.arange(span, dtype=jnp.int32)[:, None] == goal[None, :]).astype(bf16)
    pair = jnp.concatenate([normed_two, (gate * grad_out).astype(bf16)], axis=1)
    pair = gather_rows(matmul(order, pair).astype(bf16)).reshape(parts, span, 2 * width)
    offset = span - CAP
    pair = jnp.stack([pair[:, :CAP], pair[:, offset:]]).reshape(E, parts * CAP, 2 * width)
    rows, grad_rows_out = (pair[:, :, :width], pair[:, :, width:])
    at = jnp.arange(CAP, dtype=jnp.int32)[None, :]
    mask = jnp.stack([at < counts[:, None], at + offset >= counts[:, None]])
    mask = mask.reshape(E, parts * CAP, 1)
    pre = jnp.einsum("ecd,edf->ecf", rows, up_full, preferred_element_type=f32)
    hidden_f, gelu_pull = jax.vjp(lambda value: jax.nn.gelu(value, approximate=True), pre)
    hidden = jnp.where(mask, hidden_f, 0.0).astype(bf16)
    expert_out = jnp.einsum("ecf,efd->ecd", hidden, down_weight, preferred_element_type=f32)
    grad_hidden = jnp.einsum("ecd,efd->ecf", grad_rows_out, down_weight, preferred_element_type=f32)
    grad_pre = jnp.where(mask, gelu_pull(grad_hidden)[0], 0.0).astype(bf16)
    grad_rows = jnp.einsum("ecf,edf->ecd", grad_pre, up_full, preferred_element_type=f32)
    up_grad = jnp.einsum("ecd,ecf->edf", rows, grad_pre, preferred_element_type=f32).astype(bf16)
    down_grad = jnp.einsum("ecd,ecf->edf", grad_rows_out, hidden, preferred_element_type=f32).astype(bf16)
    both = jnp.concatenate([expert_out, grad_rows], axis=2).reshape(E, parts, CAP, 2 * width)
    both = jnp.pad(both[0], ((0, 0), (0, offset), (0, 0))) + jnp.pad(both[1], ((0, 0), (offset, 0), (0, 0)))
    both = scatter_rows(both.reshape(total, 2 * width))
    both = lax.dot_general(
        order.astype(f32),
        both,
        (((0,), (0,)), ((), ())),
        precision=lax.Precision.HIGHEST,
        preferred_element_type=f32,
    )
    token_out, grad_normed = (both[:, :width], both[:, width:])
    result = keep_mine * (first_sum + gate * token_out)

    grad_gate = picked * jnp.sum(token_out * grad_out, axis=1, keepdims=True)
    grad_logits = probs * (grad_gate - jnp.sum(grad_gate * probs, axis=1, keepdims=True))
    grad_logits = grad_logits.astype(bf16)
    router_grad = t_matmul(normed_two, grad_logits)
    grad_normed = grad_normed + matmul_t(grad_logits, router_full)
    grad_first_norm, expert_gain_grad = norm_two_pull(grad_normed)
    grad_first = grad_out + grad_first_norm

    grad_first_low = gather_rows(grad_first.astype(bf16))
    out_grad = t_matmul(grad_first_low, gated).astype(bf16)
    grad_gated = matmul_t(grad_first_low, out_weight)
    sig = jax.nn.sigmoid(zgate)
    grad_mixed = grad_gated * (zgate * sig)
    grad_zgate = grad_gated * mixed_in * (sig * (1.0 + zgate * (1.0 - sig)))
    skip_grad = jnp.sum(grad_mixed * conv_out, axis=0)
    fed_wide, rise_wide, entry_parts, read_parts, rate_parts = scan_backward(
        dt_wide, dx_wide, widen(grad_mixed, tiles), entry, read, rate, states, end, tiles
    )
    grad_fed = narrow(fed_wide, tiles)
    grad_step = narrow(rise_wide, tiles) * (1.0 / LOG2E) + grad_fed * conv_out
    decay_grad = decay * unpack(rate_parts, tiles)
    grad_step_pre = keep * jax.nn.sigmoid(step_pre) * grad_step
    step_bias_grad = jnp.sum(grad_step_pre, axis=0)
    grad_step_low = grad_step_pre.astype(bf16)
    step_grad = t_matmul(rank_low, grad_step_low)
    grad_rank = matmul_t(grad_step_low, step_weight)
    grad_selected = jnp.concatenate(
        [grad_rank, jnp.sum(entry_parts, axis=2), jnp.sum(read_parts, axis=2)], axis=1
    )
    grad_selected = sum_small(grad_selected).astype(bf16)
    select_grad = t_matmul(conv_low, grad_selected)
    grad_conv = grad_fed * step_size + skip * grad_mixed + matmul_t(grad_selected, select_weight)
    curve = jax.nn.sigmoid(summed)
    grad_summed = grad_conv * (curve * (1.0 + summed * (1.0 - curve)))
    conv_bias_grad = jnp.sum(grad_summed, axis=0)
    conv_grad = jnp.stack(
        [jnp.sum(grad_summed * padded[k : k + total], axis=0) for k in range(KW)]
    )
    grad_padded = jnp.concatenate([grad_summed, jnp.zeros((KW - 1, inside), f32)], axis=0)
    grad_inner = jnp.zeros((total, inside), f32)
    for k in range(KW):
        grad_inner = grad_inner + taps[k][None, :] * grad_padded[KW - 1 - k : KW - 1 - k + total]
    grad_inner_low = (keep * grad_inner).astype(bf16)
    grad_zgate_low = grad_zgate.astype(bf16)
    grad_normed_one = scatter_rows(
        matmul_t(grad_inner_low, in_full[0]) + matmul_t(grad_zgate_low, in_full[1])
    )
    in_grad = jnp.stack(
        [t_matmul(normed, grad_inner_low).astype(bf16), t_matmul(normed, grad_zgate_low).astype(bf16)]
    )
    grad_tokens_norm, mixer_gain_grad = norm_pull(grad_normed_one)
    tokens_grad = grad_first + grad_tokens_norm

    fours, eights = (groups // 4, groups // 8)
    up_cols = hidden_cols // fours
    up_cut = up_grad.reshape(E, parts, slab, fours, up_cols).transpose(3, 1, 0, 2, 4)
    up_cut = up_cut.reshape(groups, E * slab, up_cols)
    up_sum = lax.psum_scatter(up_cut, "grp", scatter_dimension=0, tiled=True)
    in_cols = inside // eights
    in_cut = in_grad.reshape(2, parts, slab, eights, in_cols).transpose(0, 3, 1, 2, 4)
    in_cut = in_cut.reshape(groups, slab, in_cols)
    in_sum = lax.psum_scatter(in_cut, "grp", scatter_dimension=0, tiled=True)
    out_sum = lax.psum_scatter(out_grad, "grp", scatter_dimension=0, tiled=True)
    down_sum = lax.psum_scatter(down_grad, "grp", scatter_dimension=1, tiled=True)
    up_moves, in_moves = ([], [])
    for g in range(groups):
        for s in range(parts):
            up_moves.append((g * parts + s, (s * fours + g // 4) * parts + g % 4))
            half, k = (g // (groups // 2), (g // 4) % eights)
            in_moves.append((g * parts + s, (half * (groups // 2) + s * eights + k) * parts + g % 4))
    both_axes = ("grp", "shard")
    up_sum = lax.ppermute(up_sum, both_axes, up_moves)
    in_sum = lax.ppermute(in_sum, both_axes, in_moves)

    mine = lax.psum(
        (select_grad, step_grad, conv_grad, conv_bias_grad, step_bias_grad, decay_grad, skip_grad),
        "grp",
    )
    shared = jnp.concatenate([router_grad.T, mixer_gain_grad[None], expert_gain_grad[None]], axis=0)
    shared = lax.psum(shared, both_axes)
    shared = lax.dynamic_slice_in_dim(shared, me * slab, slab, 1)
    return (
        result,
        tokens_grad,
        in_sum[0].astype(f32),
        out_sum.astype(f32).T,
        up_sum[0].astype(f32).reshape(E, slab, up_cols),
        down_sum.astype(f32).transpose(0, 2, 1),
        mine[0],
        mine[1],
        shared[0:2].T,
        mine[2],
        mine[3],
        mine[4],
        mine[5],
        mine[6],
        shared[2],
        shared[3],
    )


def solution(mesh):
    return jax.shard_map(
        body,
        mesh=mesh,
        in_specs=(
            P(("grp", "shard"), None),
            P(("grp", "shard"), None),
            P("grp"),
            P(("grp", "shard"), None),
            P("shard", None),
            P("shard", None),
            P(None, "shard"),
            P("shard", None),
            P("shard", None),
            P(None, "shard", None),
            P(None, "shard", None),
            P(None, "shard"),
            P("shard"),
            P("shard"),
            P(None, "shard"),
            P("shard"),
            P("shard"),
            P("shard"),
        ),
        out_specs=(
            P(("grp", "shard"), None),
            P(("grp", "shard"), None),
            P("shard", "grp"),
            P("shard", "grp"),
            P(None, "shard", "grp"),
            P(None, "shard", "grp"),
            P("shard", None),
            P(None, "shard"),
            P("shard", None),
            P(None, "shard"),
            P("shard"),
            P("shard"),
            P(None, "shard"),
            P("shard"),
            P("shard"),
            P("shard"),
        ),
        check_vma=False,
    )
```

time: 2650 us -> 855 us (0.32)
  waiting for transfers between devices: 1260 us -> 199 us
  other arithmetic: 689 us -> 97 us
  local copies, waits for them, and re-layouts: 371 us -> 268 us
  Pallas kernels: 0 us -> 60 us
  matrix products: 139 us -> 91.6 us
  blocking collectives: 119 us -> 82.3 us
    reduce_scatter x5 -> x4, waiting for transfers between devices: 711 us -> 28.8 us  [the longest x1 28.8 us: body(): out_sum = lax.psum_scatter(out_grad, 'grp', scatter_dimension=0, tiled=True)]
    unnamed x25 -> x5, waiting for transfers between devices: 525 us -> 0.08 us
    reduce_sum x209 -> x8, other arithmetic: 323 us -> 16 us  [the longest x1 6.47 us: body(): jnp.sum(read_parts, axis=2)]
    mul x366 -> x2, other arithmetic: 194 us -> 0.65 us  [the longest x1 0.63 us: body(): decay_grad = decay * unpack(rate_parts, tiles)]
    another operation x294 -> x14, local copies, waits for them, and re-layouts: 149 us -> 22.3 us  [the longest x280 141 us: one_block(): return (state, jnp.stack(outputs))]
    ppermute x2 -> x30, waiting for transfers between devices: 1.05 us -> 99.9 us  [the longest x28 99.9 us: swap(): return lax.ppermute(value, 'shard', [(i, i ^ bit) for i in range(size)])]
    dynamic_update_slice x8 -> x21, local copies, waits for them, and re-layouts: 5.98 us -> 76.7 us  [the longest x8 50.7 us: turn_blocks(): whole = lax.dynamic_update_slice_in_dim(whole, piece, (me ^ k) * rows, axis)]
    psum x0 -> x1, waiting for transfers between devices: none -> 69.8 us  [body(): lax.psum((select_grad, step_grad, conv_grad, conv_bias_grad, step_bias_gr...]
  transfers between devices with their start and end apart: 19 -> 35, of which waited for: 15 -> 13; matrix products, arithmetic and copies ran while one was open for 24% -> 36% of each run, Pallas kernels for 0% -> 5%
where the time goes in v1:
time: 855 us; the launch traced here: 838 us
  local copies, waits for them, and re-layouts  268 us (31%)
  waiting for transfers between devices  199 us (23%)
  other arithmetic  97 us (11%)
  matrix products  91.6 us (11%)
  blocking collectives  82.3 us (10%)
  Pallas kernels  60 us (7%)
  starting transfers between devices  23.3 us (3%)
  between operations  17.1 us (2%)
    ppermute x28, waiting for transfers between devices, swap(): return lax.ppermute(value, 'shard', [(i, i ^ bit) for i in range(size)])  99.9 us
    psum x1, waiting for transfers between devices, body(): lax.psum((select_grad, step_grad, conv_grad, conv_bias_grad, step_bias_gr...  69.8 us
    dynamic_update_slice x8, local copies, waits for them, and re-layouts, turn_blocks(): whole = lax.dynamic_update_slice_in_dim(whole, piece, (me ^ k) * rows, axis)  50.7 us
    psum x1, blocking collectives, body(): shared = lax.psum(shared, both_axes)  47.3 us
    unnamed x238, local copies, waits for them, and re-layouts  45.3 us
    pallas_call x1, Pallas kernels, scan_backward(): pl.pallas_call(functools.partial(scan_backward_kernel, tiles), grid=(step...  38.2 us
    psum x1, blocking collectives, body(): lax.psum((select_grad, step_grad, conv_grad, conv_bias_grad, step_bias_gr...  35 us
    reduce_scatter x1, waiting for transfers between devices, body(): out_sum = lax.psum_scatter(out_grad, 'grp', scatter_dimension=0, tiled=True)  28.8 us
  transfers between devices with their start and end apart: 35, of which 13 were waited for; matrix products, arithmetic and copies ran while one was open for 36% of the time, Pallas kernels for 5%

profile of v1, /device:TPU:2, one launch (start us, length us, event | category | flops | bytes accessed | tf_op | source)
XLA Modules:
  0.0 838.2 jit_solution(15944978633496482981)
XLA Ops:
  20.4 2.9 dynamic_update_slice.72
  25.2 3.3 dynamic_update_slice.73
  30.4 3.3 dynamic_update_slice.74
  35.6 3.3 dynamic_update_slice.75
  47.6 7.4 reshape.344
  55.2 11.1 %dynamic-slice_bitcast_fusion = (bf16[1,2,288,576]{3,0,1,2:T(2,128)(2,1)S(1)}, bf16[1,2,288,576]{3,0,1,2:T(2,128)(2,1)S(1)}, bf16[1,2,288,576]{3,0,1,2:T(2,128)(2,1)S(1)}, bf16[1,2,288,576]{3,0,1,2:T(2,128)(2,1)}) fusion(bf16[288,2,4,576]{3,2,1,0:T(4,128)(2,1)} %reshape.344, s32[]{:T(128)S(6)} %select_n.122, s32[]{:T(128)S(6)} %select_n.121, ...), kind=kLoop, calls=%fused_computation.82 | loop fusion | bytes 5308432 | tf_op jit(solution)/shard_map/jit(dynamic_index_in_dim)/dynamic_slice | solution.py:253
  75.7 4.2 copy.164
  81.7 10.4 %dynamic_update_slice.80 = bf16[2,1152,576]{1,2,0:T(8,128)(2,1)} dynamic-update-slice(bf16[2,1152,576]{1,2,0:T(8,128)(2,1)} %broadcast_in_dim.40, bf16[2,288,576]{1,2,0:T(8,128)(2,1)} %bitcast.220, s32[]{:T(128)} %constant.140.clone.1, s32[]{:T(128)S(6)} %select_n.127, s32[]{:T(128)} %constant.140.clone.1) | dynamic-update-slice | bytes 1327108 | tf_op jit(solution)/shard_map/dynamic_update_slice | solution.py:256
  100.3 11.5 %dynamic_update_slice.81 = bf16[2,1152,576]{1,2,0:T(8,128)(2,1)} dynamic-update-slice(bf16[2,1152,576]{1,2,0:T(8,128)(2,1)} %dynamic_update_slice.80, bf16[2,288,576]{1,2,0:T(8,128)(2,1)} %copy.131, s32[]{:T(128)} %constant.140.clone.1, s32[]{:T(128)S(6)} %select_n.128, s32[]{:T(128)} %constant.140.clone.1) | dynamic-update-slice | bytes 1327108 | tf_op jit(solution)/shard_map/dynamic_update_slice | solution.py:256
  113.9 11.4 %dynamic_update_slice.82 = bf16[2,1152,576]{1,2,0:T(8,128)(2,1)} dynamic-update-slice(bf16[2,1152,576]{1,2,0:T(8,128)(2,1)} %dynamic_update_slice.81, bf16[2,288,576]{1,2,0:T(8,128)(2,1)} %copy.133, s32[]{:T(128)} %constant.140.clone.1, s32[]{:T(128)S(6)} %select_n.129, s32[]{:T(128)} %constant.140.clone.1) | dynamic-update-slice | bytes 1327108 | tf_op jit(solution)/shard_map/dynamic_update_slice | solution.py:256
  127.5 10.8 %dynamic_update_slice.83 = bf16[2,1152,576]{1,2,0:T(8,128)(2,1)} dynamic-update-slice(bf16[2,1152,576]{1,2,0:T(8,128)(2,1)} %dynamic_update_slice.82, bf16[2,288,576]{1,2,0:T(8,128)(2,1)} %copy.135, s32[]{:T(128)} %constant.140.clone.1, s32[]{:T(128)S(6)} %select_n.130, s32[]{:T(128)} %constant.140.clone.1) | dynamic-update-slice | bytes 1327108 | tf_op jit(solution)/shard_map/dynamic_update_slice | solution.py:256
  140.2 3.8 convolution_multiply_fusion
  144.1 3.0 multiply_add_fusion
  154.3 9.7 %collective-permute-done.10 = f32[1024,104]{0,1:T(8,128)S(1)} collective-permute-done((f32[1024,104]{0,1:T(8,128)S(1)}, f32[1024,104]{0,1:T(8,128)S(1)}, u32[]{:S(2)}, u32[]{:S(2)}) %collective-permute-start.10) | collective-permute-done | bytes 426016 | tf_op jit(solution)/shard_map/ppermute | solution.py:215
  169.1 5.2 fusion.76
  174.4 2.9 pad_maximum_fusion.3
  177.3 3.2 copy.136
  180.5 3.3 copy.137
  183.8 3.3 broadcast_in_dim.41.entry_ref
  187.2 6.1 broadcast_in_dim.42.read_ref
  194.4 21.7 %scan_forward.1 = (f32[128,8,640]{2,1,0:T(8,128)S(1)}, f32[1024,9,8,128]{3,2,1,0:T(8,128)}, f32[9,8,128]{2,1,0:T(8,128)S(1)}) custom-call(f32[128,8,640]{2,1,0:T(8,128)S(1)} %bitcast.193, f32[128,8,640]{2,1,0:T(8,128)S(1)} %bitcast.195, f32[1024,16,128]{2,1,0:T(8,128)S(1)} %broadcast_in_dim.41.entry_ref, f32[1024,16,128]{2,1,0:T(8,128)} %broadcast_in_dim.42.read_ref, ...), custom_call_target="tpu_custom_call" | custom-call | flops 75497472 | bytes 37748736 | tf_op jit(solution)/shard_map/scan_forward/pallas_call | solution.py:96
  219.5 3.0 copy.169
  227.5 7.3 multiply_convert_fusion.1
  240.9 2.6 collective-permute-done.11
  253.4 7.7 reshape.354
  277.0 7.5 constant_dynamic-slice_fusion.1
  299.4 5.0 collective-permute-done.14
  306.6 16.8 %collective-permute-done.17 = bf16[2,288,768]{2,1,0:T(8,128)(2,1)} collective-permute-done((bf16[2,288,768]{2,1,0:T(8,128)(2,1)}, bf16[2,288,768]{2,1,0:T(8,128)(2,1)}, u32[]{:S(2)}, u32[]{:S(2)}) %collective-permute-start.17) | collective-permute-done | bytes 884768 | tf_op jit(solution)/shard_map/ppermute | solution.py:215
  325.6 14.9 %collective-permute-done.18 = bf16[2,288,768]{2,1,0:T(8,128)(2,1)} collective-permute-done((bf16[2,288,768]{2,1,0:T(8,128)(2,1)}, bf16[2,288,768]{2,1,0:T(8,128)(2,1)}, u32[]{:S(2)}, u32[]{:S(2)}) %collective-permute-start.18) | collective-permute-done | bytes 884768 | tf_op jit(solution)/shard_map/ppermute | solution.py:215
  345.0 2.4 constant_dynamic-update-slice_fusion.8
  348.6 3.7 fusion.85
  352.6 3.2 fusion.72
  355.9 6.1 fusion.8
  362.1 4.4 fusion.74
  366.5 3.2 fusion.97
  369.7 6.0 fusion
  375.7 9.7 %pad_add_fusion = f32[4,256,2304]{2,1,0:T(8,128)} fusion(f32[4,192,2304]{2,1,0:T(8,128)} %bitcast.208, f32[4,192,2304]{2,1,0:T(8,128)} %bitcast.207), kind=kLoop, calls=%fused_computation.2 | loop fusion | flops 2359296 | bytes 23592960 | tf_op jit(solution)/shard_map/add | solution.py:415
  385.4 4.2 fusion.20
  390.1 7.0 convolution_convert_fusion.1
  397.1 6.6 reshape.359
  406.2 3.5 bitcast_add_fusion
  411.6 26.1 %collective-permute-done.20 = bf16[256,2304]{1,0:T(8,128)(2,1)S(1)} collective-permute-done((bf16[256,2304]{1,0:T(8,128)(2,1)S(1)}, bf16[256,2304]{1,0:T(8,128)(2,1)S(1)}, u32[]{:S(2)}, u32[]{:S(2)}) %collective-permute-start.20) | collective-permute-done | bytes 1179680 | tf_op jit(solution)/shard_map/ppermute | solution.py:215
  448.1 13.0 %collective-permute-done.22 = bf16[256,1152]{1,0:T(8,128)(2,1)S(1)} collective-permute-done((bf16[256,1152]{1,0:T(8,128)(2,1)}, bf16[256,1152]{1,0:T(8,128)(2,1)S(1)}, u32[]{:S(2)}, u32[]{:S(2)}) %collective-permute-start.22) | collective-permute-done | bytes 589856 | tf_op jit(solution)/shard_map/ppermute | solution.py:215
  461.1 7.5 convolution_convert_fusion
  471.9 7.7 multiply_reduce_fusion
  483.4 38.2 %scan_backward.1 = (f32[128,8,640]{2,1,0:T(8,128)S(1)}, f32[128,8,640]{2,1,0:T(8,128)S(1)}, f32[1024,16,128]{2,1,0:T(8,128)}, f32[1024,16,128]{2,1,0:T(8,128)}, f32[9,8,128]{2,1,0:T(8,128)S(1)}) custom-call(f32[128,8,640]{2,1,0:T(8,128)} %bitcast.192, f32[128,8,640]{2,1,0:T(8,128)} %bitcast.194, f32[128,8,640]{2,1,0:T(8,128)} %bitcast.211, ...), custom_call_target="tpu_custom_call" | custom-call | flops 188743680 | bytes 37748736 | tf_op jit(solution)/shard_map/scan_backward/pallas_call | solution.py:199
  523.2 5.7 reduce_sum.204
  528.9 6.5 reduce_sum.205
  536.8 3.1 slice.268
  539.9 2.9 copy.176
  549.5 2.9 copy.173
  557.3 8.7 %fusion.79 = (f32[576]{0:T(1024)}, bf16[1024,576]{0,1:T(8,128)(2,1)S(1)}) fusion(f32[1024,64]{0,1:T(8,128)S(1)} %add.373, f32[1024,512]{0,1:T(8,128)S(1)} %copy-done.23, f32[1024,64]{0,1:T(8,128)S(1)} %add.376, f32[1024,512]{0,1:T(8,128)} %copy.176, f32[1024,576]{0,1:T(8,128)} %get-tuple-element.102, f32[576]{0:T(1024)} %convert_element_type.238, ...), kind=kLoop, calls=%fused_computation.221 | loop fusion | flops 14745024 | bytes 10637056 | tf_op jit(solution)/shard_map/reduce_sum | solution.py:449
  571.7 8.6 %collective-permute-done.25 = f32[1024,104]{0,1:T(8,128)S(1)} collective-permute-done((f32[1024,104]{0,1:T(8,128)S(1)}, f32[1024,104]{0,1:T(8,128)S(1)}, u32[]{:S(2)}, u32[]{:S(2)}) %collective-permute-start.25) | collective-permute-done | bytes 426016 | tf_op jit(solution)/shard_map/ppermute | solution.py:215
  580.5 4.9 multiply_reduce_fusion.4
  585.4 2.6 fusion.17
  591.5 4.6 copy.157
  597.4 6.2 fusion.38
  603.6 3.2 convolution_convert_fusion.3
  606.8 5.1 convolution_add_fusion
  626.6 35.0 %all-reduce.4 = (f32[4,576]{1,0:T(4,128)}, f32[576]{0:T(1024)}, f32[576]{0:T(1024)}, f32[16,576]{1,0:T(8,128)}, f32[576]{0:T(1024)}) all-reduce(f32[4,576]{1,0:T(4,128)} %pad_maximum_fusion.14, f32[576]{0:T(1024)} %get-tuple-element.40, f32[576]{0:T(1024)S(1)} %copy-done.87, ...), channel_id=1, replica_groups=mesh['grp'=8,'shard'=4] {'grp'}, use_global_device_ids=true, to_apply=%region_29.30 | all-reduce | flops 13248 | bytes 105984 | tf_op jit(solution)/shard_map/psum | solution.py:501
  667.7 3.3 fusion.30
  671.7 47.3 %psum.58 = f32[4,1152]{1,0:T(4,128)} all-reduce(f32[4,1152]{1,0:T(4,128)} %pad_maximum_fusion.13), channel_id=1, replica_groups=mesh['grp'=8,'shard'=4] {'grp','shard'}, use_global_device_ids=true, to_apply=%region_24.25 | all-reduce | flops 4608 | bytes 36864 | tf_op jit(solution)/shard_map/psum | solution.py:506
  723.7 28.8 %reduce-scatter.7.cloned.1.call-done = bf16[144,576]{1,0:T(8,128)(2,1)} async-done(((bf16[1152,576]{1,0:T(8,128)(2,1)}), bf16[144,576]{1,0:T(8,128)(2,1)}) %reduce-scatter.7.cloned.1.call-update) | async-done | bytes 165904 | tf_op jit(solution)/shard_map/reduce_scatter | solution.py:489
  758.1 69.8 %all-reduce.8.cloned.1.call-done = (f32[576,104]{0,1:T(8,128)}, f32[72,576]{1,0:T(8,128)}) async-done(((f32[576,104]{0,1:T(8,128)}, f32[72,576]{1,0:T(8,128)}), (f32[576,104]{0,1:T(8,128)}, f32[72,576]{1,0:T(8,128)})) %all-reduce.8.cloned.1.call-update) | async-done | bytes 405520 | tf_op jit(solution)/shard_map/psum | solution.py:501
  (453 shorter events, 212.5 us)
Async XLA Ops:
  7.2 348.7 %copy-start = (bf16[2,768,1152]{2,1,0:T(8,128)(2,1)S(1)}, bf16[2,768,1152]{2,1,0:T(8,128)(2,1)}, u32[]{:S(2)}) copy-start(bf16[2,768,1152]{2,1,0:T(8,128)(2,1)} %param.28) | copy-start | bytes 10616836
  7.2 654.4 %reduce-scatter.9.cloned.1.call-start = ((), (), s32[]{:S(2)}) async-start(), calls=%async_computation.6 | async-start | bytes 3981312 | tf_op jit(solution)/shard_map/reduce_scatter | solution.py:484
  13.9 3.9 collective-permute-start.1
  15.5 7.8 collective-permute-start
  17.8 15.9 %collective-permute-start.2 = (f32[1,5,288]{2,1,0:T(8,128)}, f32[1,5,288]{2,1,0:T(8,128)}, u32[]{:S(2)}, u32[]{:S(2)}) collective-permute-start(f32[1,5,288]{2,1,0:T(8,128)} %collective-permute-done.1), channel_id=1, source_target_pairs={{0,1},{1,0},{2,3},{3,2},{4,5},{5,4},{6,7},{7,6},{8,9},{9,8},{10,11... | collective-permute-start | bytes 17288 | tf_op jit(solution)/shard_map/ppermute | solution.py:215
  46.1 45.9 %collective-permute-start.4 = (bf16[256,1152]{1,0:T(8,128)(2,1)}, bf16[256,1152]{1,0:T(8,128)(2,1)}, u32[]{:S(2)}, u32[]{:S(2)}) collective-permute-start(bf16[256,1152]{1,0:T(8,128)(2,1)} %get-tuple-element.69), channel_id=1, source_target_pairs={{0,2},{1,3},{2,0},{3,1},{4,6},{5,7},{6,4},{7,5},{8,10},{9,11},{10,... | collective-permute-start | bytes 1769480 | tf_op jit(solution)/shard_map/ppermute | solution.py:215
  55.0 39.3 %collective-permute-start.3 = (bf16[256,1152]{1,0:T(8,128)(2,1)}, bf16[256,1152]{1,0:T(8,128)(2,1)}, u32[]{:S(2)}, u32[]{:S(2)}) collective-permute-start(bf16[256,1152]{1,0:T(8,128)(2,1)} %get-tuple-element.69), channel_id=1, source_target_pairs={{0,1},{1,0},{2,3},{3,2},{4,5},{5,4},{6,7},{7,6},{8,9},{9,8},{10,11... | collective-permute-start | bytes 1769480 | tf_op jit(solution)/shard_map/ppermute | solution.py:215
  67.3 30.9 %collective-permute-start.6 = (bf16[2,288,576]{2,1,0:T(8,128)(2,1)}, bf16[2,288,576]{2,1,0:T(8,128)(2,1)}, u32[]{:S(2)}, u32[]{:S(2)}) collective-permute-start(bf16[2,288,576]{2,1,0:T(8,128)(2,1)} %bitcast.188), channel_id=1, source_target_pairs={{0,1},{1,0},{2,3},{3,2},{4,5},{5,4},{6,7},{7,6},{8,9},{9,8},{10,11... | collective-permute-start | bytes 1990664 | tf_op jit(solution)/shard_map/ppermute | solution.py:215
  68.5 43.2 %collective-permute-start.7 = (bf16[2,288,576]{2,1,0:T(8,128)(2,1)}, bf16[2,288,576]{2,1,0:T(8,128)(2,1)}, u32[]{:S(2)}, u32[]{:S(2)}) collective-permute-start(bf16[2,288,576]{2,1,0:T(8,128)(2,1)} %bitcast.187), channel_id=1, source_target_pairs={{0,2},{1,3},{2,0},{3,1},{4,6},{5,7},{6,4},{7,5},{8,10},{9,11},{10,... | collective-permute-start | bytes 1990664 | tf_op jit(solution)/shard_map/ppermute | solution.py:215
  70.0 55.3 %collective-permute-start.8 = (bf16[2,288,576]{2,1,0:T(8,128)(2,1)}, bf16[2,288,576]{2,1,0:T(8,128)(2,1)}, u32[]{:S(2)}, u32[]{:S(2)}) collective-permute-start(bf16[2,288,576]{2,1,0:T(8,128)(2,1)} %bitcast.186), channel_id=1, source_target_pairs={{0,3},{1,2},{2,1},{3,0},{4,7},{5,6},{6,5},{7,4},{8,11},{9,10},{10,... | collective-permute-start | bytes 1990664 | tf_op jit(solution)/shard_map/ppermute | solution.py:215
  71.1 72.9 %copy-start.62 = (f32[576]{0:T(1024)}, f32[576]{0:T(1024)S(1)}, u32[]{:S(2)}) copy-start(f32[576]{0:T(1024)S(1)} %get-tuple-element.43) | copy-start | bytes 6916
  71.1 72.9 %copy-start.64 = (f32[576]{0:T(1024)}, f32[576]{0:T(1024)S(1)}, u32[]{:S(2)}) copy-start(f32[576]{0:T(1024)S(1)} %get-tuple-element.44) | copy-start | bytes 6916
  71.2 72.9 %copy-start.66 = (f32[576]{0:T(1024)}, f32[576]{0:T(1024)S(1)}, u32[]{:S(2)}) copy-start(f32[576]{0:T(1024)S(1)} %get-tuple-element.45) | copy-start | bytes 6916
  71.2 72.9 %copy-start.68 = (f32[576]{0:T(1024)}, f32[576]{0:T(1024)S(1)}, u32[]{:S(2)}) copy-start(f32[576]{0:T(1024)S(1)} %get-tuple-element.46) | copy-start | bytes 6916
  92.0 46.2 %collective-permute-start.5 = (bf16[256,1152]{1,0:T(8,128)(2,1)}, bf16[256,1152]{1,0:T(8,128)(2,1)}, u32[]{:S(2)}, u32[]{:S(2)}) collective-permute-start(bf16[256,1152]{1,0:T(8,128)(2,1)} %collective-permute-done.4), channel_id=1, source_target_pairs={{0,1},{1,0},{2,3},{3,2},{4,5},{5,4},{6,7},{7,6},{8,9},{9,8},{10,11... | collective-permute-start | bytes 1769480 | tf_op jit(solution)/shard_map/ppermute | solution.py:215
  148.8 20.4 %copy-start.75 = (f32[1024]{0:T(1024)S(1)}, f32[1024]{0:T(1024)}, u32[]{:S(2)}) copy-start(f32[1024]{0:T(1024)} %fusion.58) | copy-start | bytes 12292
  148.8 20.4 %copy-start.88 = (f32[576]{0:T(1024)S(1)}, f32[576]{0:T(1024)}, u32[]{:S(2)}) copy-start(f32[576]{0:T(1024)} %convert_element_type.238) | copy-start | bytes 6916
  148.8 2.1 collective-permute-start.9
  152.1 11.9 %collective-permute-start.10 = (f32[1024,104]{0,1:T(8,128)S(1)}, f32[1024,104]{0,1:T(8,128)S(1)}, u32[]{:S(2)}, u32[]{:S(2)}) collective-permute-start(f32[1024,104]{0,1:T(8,128)S(1)} %add.344), channel_id=1, source_target_pairs={{0,2},{1,3},{2,0},{3,1},{4,6},{5,7},{6,4},{7,5},{8,10},{9,11},{10,... | collective-permute-start | bytes 1277960 | tf_op jit(solution)/shard_map/ppermute | solution.py:215
  219.5 8.0 copy-start.99
  240.3 3.2 collective-permute-start.11
  248.0 21.0 %collective-permute-start.12 = (bf16[256,1152]{1,0:T(8,128)(2,1)}, bf16[256,1152]{1,0:T(8,128)(2,1)}, u32[]{:S(2)}, u32[]{:S(2)}) collective-permute-start(bf16[256,1152]{1,0:T(8,128)(2,1)} %fusion.40), channel_id=1, source_target_pairs={{0,2},{1,3},{2,0},{3,1},{4,6},{5,7},{6,4},{7,5},{8,10},{9,11},{10,... | collective-permute-start | bytes 1769480 | tf_op jit(solution)/shard_map/ppermute | solution.py:215
  275.3 9.3 %copy-start.11 = (bf16[1024,2304]{1,0:T(8,128)(2,1)}, bf16[1024,2304]{1,0:T(8,128)(2,1)S(1)}, u32[]{:S(2)}) copy-start(bf16[1024,2304]{1,0:T(8,128)(2,1)S(1)} %get-tuple-element.107) | copy-start | bytes 14155780
  275.3 29.2 %collective-permute-start.14 = (bf16[256,2304]{1,0:T(8,128)(2,1)}, bf16[256,2304]{1,0:T(8,128)(2,1)}, u32[]{:S(2)}, u32[]{:S(2)}) collective-permute-start(bf16[256,2304]{1,0:T(8,128)(2,1)} %get-tuple-element.108), channel_id=1, source_target_pairs={{0,2},{1,3},{2,0},{3,1},{4,6},{5,7},{6,4},{7,5},{8,10},{9,11},{10,... | collective-permute-start | bytes 3538952 | tf_op jit(solution)/shard_map/ppermute | solution.py:215
  285.6 18.9 %collective-permute-start.16 = (bf16[2,288,768]{2,1,0:T(8,128)(2,1)}, bf16[2,288,768]{2,1,0:T(8,128)(2,1)}, u32[]{:S(2)}, u32[]{:S(2)}) collective-permute-start(bf16[2,288,768]{2,1,0:T(8,128)(2,1)} %bitcast.185), channel_id=1, source_target_pairs={{0,1},{1,0},{2,3},{3,2},{4,5},{5,4},{6,7},{7,6},{8,9},{9,8},{10,11... | collective-permute-start | bytes 2654216 | tf_op jit(solution)/shard_map/ppermute | solution.py:215
  286.6 36.7 %collective-permute-start.17 = (bf16[2,288,768]{2,1,0:T(8,128)(2,1)}, bf16[2,288,768]{2,1,0:T(8,128)(2,1)}, u32[]{:S(2)}, u32[]{:S(2)}) collective-permute-start(bf16[2,288,768]{2,1,0:T(8,128)(2,1)} %bitcast.184), channel_id=1, source_target_pairs={{0,2},{1,3},{2,0},{3,1},{4,6},{5,7},{6,4},{7,5},{8,10},{9,11},{10,... | collective-permute-start | bytes 2654216 | tf_op jit(solution)/shard_map/ppermute | solution.py:215
  288.7 51.8 %collective-permute-start.18 = (bf16[2,288,768]{2,1,0:T(8,128)(2,1)}, bf16[2,288,768]{2,1,0:T(8,128)(2,1)}, u32[]{:S(2)}, u32[]{:S(2)}) collective-permute-start(bf16[2,288,768]{2,1,0:T(8,128)(2,1)} %bitcast.183), channel_id=1, source_target_pairs={{0,3},{1,2},{2,1},{3,0},{4,7},{5,6},{6,5},{7,4},{8,11},{9,10},{10,... | collective-permute-start | bytes 2654216 | tf_op jit(solution)/shard_map/ppermute | solution.py:215
  289.6 53.0 %collective-permute-start.13 = (bf16[256,2304]{1,0:T(8,128)(2,1)}, bf16[256,2304]{1,0:T(8,128)(2,1)}, u32[]{:S(2)}, u32[]{:S(2)}) collective-permute-start(bf16[256,2304]{1,0:T(8,128)(2,1)} %get-tuple-element.108), channel_id=1, source_target_pairs={{0,1},{1,0},{2,3},{3,2},{4,5},{5,4},{6,7},{7,6},{8,9},{9,8},{10,11... | collective-permute-start | bytes 3538952 | tf_op jit(solution)/shard_map/ppermute | solution.py:215
  304.4 43.0 %collective-permute-start.15 = (bf16[256,2304]{1,0:T(8,128)(2,1)}, bf16[256,2304]{1,0:T(8,128)(2,1)S(1)}, u32[]{:S(2)}, u32[]{:S(2)}) collective-permute-start(bf16[256,2304]{1,0:T(8,128)(2,1)} %collective-permute-done.14), channel_id=1, source_target_pairs={{0,1},{1,0},{2,3},{3,2},{4,5},{5,4},{6,7},{7,6},{8,9},{9,8},{10,11... | collective-permute-start | bytes 3538952 | tf_op jit(solution)/shard_map/ppermute | solution.py:215
  304.5 57.6 %copy-start.102 = (pred[2,768]{1,0:T(4,128)(4,1)}, pred[2,768]{1,0:T(4,128)(4,1)S(1)}, u32[]{:S(2)}) copy-start(pred[2,768]{1,0:T(4,128)(4,1)S(1)} %add_bitcast_fusion) | copy-start | bytes 4612
  389.6 16.6 %collective-permute-start.19 = (bf16[2,256,2304]{2,1,0:T(8,128)(2,1)}, bf16[2,256,2304]{2,1,0:T(8,128)(2,1)}, u32[]{:S(2)}, u32[]{:S(2)}) collective-permute-start(bf16[2,256,2304]{2,1,0:T(8,128)(2,1)} %fusion.20), channel_id=1, source_target_pairs={{0,1},{1,0},{2,3},{3,2},{4,5},{5,4},{6,7},{7,6},{8,9},{9,8},{10,11... | collective-permute-start | bytes 7077896 | tf_op jit(solution)/shard_map/ppermute | solution.py:215
  406.1 257.4 %reduce-scatter.11.cloned.1.call-start = ((), (), s32[]{:S(2)}) async-start(), calls=%async_computation.7 | async-start | bytes 3981312 | tf_op jit(solution)/shard_map/reduce_scatter | solution.py:490
  409.7 28.1 %copy-start.94 = (s32[256]{0:T(256)S(1)}, s32[256]{0:T(256)}, u32[]{:S(2)}) copy-start(s32[256]{0:T(256)} %compare_select_fusion.2) | copy-start | bytes 3076
  409.8 29.5 %copy-start.18 = (f32[256,1152]{1,0:T(8,128)S(1)}, f32[256,1152]{1,0:T(8,128)}, u32[]{:S(2)}) copy-start(f32[256,1152]{1,0:T(8,128)} %param.21) | copy-start | bytes 3538948
  409.8 27.9 %collective-permute-start.20 = (bf16[256,2304]{1,0:T(8,128)(2,1)S(1)}, bf16[256,2304]{1,0:T(8,128)(2,1)S(1)}, u32[]{:S(2)}, u32[]{:S(2)}) collective-permute-start(bf16[256,2304]{1,0:T(8,128)(2,1)S(1)} %fusion.31), channel_id=1, source_target_pairs={{0,2},{1,3},{2,0},{3,1},{4,6},{5,7},{6,4},{7,5},{8,10},{9,11},{10,... | collective-permute-start | bytes 3538952 | tf_op jit(solution)/shard_map/ppermute | solution.py:215
  443.2 17.9 %copy-start.28 = (bf16[4,192,2304]{2,1,0:T(8,128)(2,1)S(1)}, bf16[4,192,2304]{2,1,0:T(8,128)(2,1)}, u32[]{:S(2)}) copy-start(bf16[4,192,2304]{2,1,0:T(8,128)(2,1)} %copy-done.26) | copy-start | bytes 10616836
  443.2 17.9 %copy-start.30 = (bf16[4,192,2304]{2,1,0:T(8,128)(2,1)S(1)}, bf16[4,192,2304]{2,1,0:T(8,128)(2,1)}, u32[]{:S(2)}) copy-start(bf16[4,192,2304]{2,1,0:T(8,128)(2,1)} %copy-done.29) | copy-start | bytes 10616836
  443.2 17.9 %copy-start.103 = (pred[2,768]{1,0:T(4,128)(4,1)S(1)}, pred[2,768]{1,0:T(4,128)(4,1)}, u32[]{:S(2)}) copy-start(pred[2,768]{1,0:T(4,128)(4,1)} %copy-done.102) | copy-start | bytes 4612
  446.4 14.7 %collective-permute-start.22 = (bf16[256,1152]{1,0:T(8,128)(2,1)}, bf16[256,1152]{1,0:T(8,128)(2,1)S(1)}, u32[]{:S(2)}, u32[]{:S(2)}) collective-permute-start(bf16[256,1152]{1,0:T(8,128)(2,1)} %get-tuple-element.60), channel_id=1, source_target_pairs={{0,2},{1,3},{2,0},{3,1},{4,6},{5,7},{6,4},{7,5},{8,10},{9,11},{10,... | collective-permute-start | bytes 1769480 | tf_op jit(solution)/shard_map/ppermute | solution.py:215
  448.1 20.6 %collective-permute-start.21 = (bf16[256,1152]{1,0:T(8,128)(2,1)}, bf16[256,1152]{1,0:T(8,128)(2,1)}, u32[]{:S(2)}, u32[]{:S(2)}) collective-permute-start(bf16[256,1152]{1,0:T(8,128)(2,1)} %get-tuple-element.60), channel_id=1, source_target_pairs={{0,1},{1,0},{2,3},{3,2},{4,5},{5,4},{6,7},{7,6},{8,9},{9,8},{10,11... | collective-permute-start | bytes 1769480 | tf_op jit(solution)/shard_map/ppermute | solution.py:215
  461.1 10.6 %collective-permute-start.23 = (bf16[256,1152]{1,0:T(8,128)(2,1)S(1)}, bf16[256,1152]{1,0:T(8,128)(2,1)S(1)}, u32[]{:S(2)}, u32[]{:S(2)}) collective-permute-start(bf16[256,1152]{1,0:T(8,128)(2,1)S(1)} %collective-permute-done.22), channel_id=1, source_target_pairs={{0,1},{1,0},{2,3},{3,2},{4,5},{5,4},{6,7},{7,6},{8,9},{9,8},{10,11... | collective-permute-start | bytes 1769480 | tf_op jit(solution)/shard_map/ppermute | solution.py:215
  468.7 251.7 %reduce-scatter.5.cloned.1.call-start = ((), (), s32[]{:S(2)}) async-start(), calls=%async_computation.4 | async-start | bytes 3317760 | tf_op jit(solution)/shard_map/reduce_scatter | solution.py:488
  471.8 7.7 copy-start.41
  557.3 8.7 %copy-start.59 = (bf16[72,576]{1,0:T(8,128)(2,1)S(1)}, bf16[72,576]{1,0:T(8,128)(2,1)}, u32[]{:S(2)}) copy-start(bf16[72,576]{1,0:T(8,128)(2,1)} %param.24) | copy-start | bytes 248836
  566.4 1.8 collective-permute-start.24
  568.3 12.1 %collective-permute-start.25 = (f32[1024,104]{0,1:T(8,128)S(1)}, f32[1024,104]{0,1:T(8,128)S(1)}, u32[]{:S(2)}, u32[]{:S(2)}) collective-permute-start(f32[1024,104]{0,1:T(8,128)S(1)} %fusion.70), channel_id=1, source_target_pairs={{0,2},{1,3},{2,0},{3,1},{4,6},{5,7},{6,4},{7,5},{8,10},{9,11},{10,... | collective-permute-start | bytes 1277960 | tf_op jit(solution)/shard_map/ppermute | solution.py:215
  570.0 10.4 %copy-start.22 = (f32[1024,576]{0,1:T(8,128)S(1)}, f32[1024,576]{0,1:T(8,128)}, u32[]{:S(2)}) copy-start(f32[1024,576]{0,1:T(8,128)} %copy-done.21) | copy-start | bytes 7077892
  570.0 10.4 %copy-start.35 = (f32[1024,576]{0,1:T(8,128)S(1)}, f32[1024,576]{0,1:T(8,128)}, u32[]{:S(2)}) copy-start(f32[1024,576]{0,1:T(8,128)} %copy-done.34) | copy-start | bytes 7077892
  570.0 10.4 %copy-start.37 = (f32[1024,576]{0,1:T(8,128)S(1)}, f32[1024,576]{0,1:T(8,128)}, u32[]{:S(2)}) copy-start(f32[1024,576]{0,1:T(8,128)} %copy-done.36) | copy-start | bytes 7077892
  570.0 10.4 %copy-start.47 = (f32[1024,576]{0,1:T(8,128)S(1)}, f32[1024,576]{0,1:T(8,128)}, u32[]{:S(2)}) copy-start(f32[1024,576]{0,1:T(8,128)} %copy-done.45) | copy-start | bytes 7077892
  570.0 10.4 %copy-start.101 = (f32[576]{0:T(1024)S(1)}, f32[576]{0:T(1024)}, u32[]{:S(2)}) copy-start(f32[576]{0:T(1024)} %convert_element_type.240) | copy-start | bytes 6916
  570.0 10.4 %copy-start.106 = (bf16[576,104]{0,1:T(8,128)(2,1)S(1)}, bf16[576,104]{0,1:T(8,128)(2,1)}, u32[]{:S(2)}) copy-start(bf16[576,104]{0,1:T(8,128)(2,1)} %param.23) | copy-start | bytes 359428
  596.1 156.4 %reduce-scatter.7.cloned.1.call-start = ((), (), s32[]{:S(2)}) async-start(), calls=%async_computation.5 | async-start | bytes 1658880 | tf_op jit(solution)/shard_map/reduce_scatter | solution.py:489
  606.8 221.2 %all-reduce.8.cloned.1.call-start = ((), (), s32[]{:S(2)}) async-start(), calls=%async_computation.8 | async-start | bytes 901120 | tf_op jit(solution)/shard_map/psum | solution.py:501
  612.1 3.6 collective-permute-start.26
  616.0 49.6 %copy-start.16 = (f32[2,256,1152]{2,1,0:T(8,128)}, f32[2,256,1152]{2,1,0:T(8,128)S(1)}, u32[]{:S(2)}) copy-start(f32[2,256,1152]{2,1,0:T(8,128)S(1)} %bitcast_add_fusion.1) | copy-start | bytes 7077892
  616.9 9.7 %copy-start.87 = (f32[576]{0:T(1024)S(1)}, f32[576]{0:T(1024)}, u32[]{:S(2)}) copy-start(f32[576]{0:T(1024)} %get-tuple-element.56) | copy-start | bytes 6916
  616.9 48.7 %copy-start.58 = (f32[1152]{0:T(1024)S(1)}, f32[1152]{0:T(1024)}, u32[]{:S(2)}) copy-start(f32[1152]{0:T(1024)} %copy-done.57) | copy-start | bytes 13828
  616.9 48.7 %copy-start.82 = (f32[256]{0:T(256)S(1)}, f32[256]{0:T(256)}, u32[]{:S(2)}) copy-start(f32[256]{0:T(256)} %fusion.64) | copy-start | bytes 3076
  616.9 48.7 %collective-permute-start.27 = (bf16[256,1152]{1,0:T(8,128)(2,1)}, bf16[256,1152]{1,0:T(8,128)(2,1)}, u32[]{:S(2)}, u32[]{:S(2)}) collective-permute-start(bf16[256,1152]{1,0:T(8,128)(2,1)} %fusion.41), channel_id=1, source_target_pairs={{0,2},{1,3},{2,0},{3,1},{4,6},{5,7},{6,4},{7,5},{8,10},{9,11},{10,... | collective-permute-start | bytes 1769480 | tf_op jit(solution)/shard_map/ppermute | solution.py:215
  620.1 45.5 %copy-start.13 = (f32[256,1152]{1,0:T(8,128)S(1)}, f32[256,1152]{1,0:T(8,128)}, u32[]{:S(2)}) copy-start(f32[256,1152]{1,0:T(8,128)} %param.18) | copy-start | bytes 3538948
  661.6 92.7 %collective-permute-start.29 = (bf16[1,576,384]{2,1,0:T(8,128)(2,1)}, bf16[1,576,384]{2,1,0:T(8,128)(2,1)}, u32[]{:S(2)}, u32[]{:S(2)}) collective-permute-start(bf16[1,576,384]{2,1,0:T(8,128)(2,1)} %reduce-scatter.9.cloned.1.call-done), channel_id=1, source_target_pairs={{0,0},{1,8},{2,16},{3,24},{4,1},{5,9},{6,17},{7,25},{8,2},{9,10},{... | collective-permute-start | bytes 1327112 | tf_op jit(solution)/shard_map/ppermute | solution.py:498
  667.7 163.5 %copy-start.1 = (bf16[2,768,1152]{2,1,0:T(8,128)(2,1)S(1)}, bf16[2,768,1152]{2,1,0:T(8,128)(2,1)}, u32[]{:S(2)}) copy-start(bf16[2,768,1152]{2,1,0:T(8,128)(2,1)} %param.28) | copy-start | bytes 10616836
  720.4 35.8 %collective-permute-start.28 = (bf16[1,288,576]{2,1,0:T(8,128)(2,1)}, bf16[1,288,576]{2,1,0:T(8,128)(2,1)}, u32[]{:S(2)}, u32[]{:S(2)}) collective-permute-start(bf16[1,288,576]{2,1,0:T(8,128)(2,1)} %reduce-scatter.5.cloned.1.call-done), channel_id=1, source_target_pairs={{0,0},{1,4},{2,8},{3,12},{4,1},{5,5},{6,9},{7,13},{8,2},{9,6},{10,... | collective-permute-start | bytes 995336 | tf_op jit(solution)/shard_map/ppermute | solution.py:499
  (83 other events, 248.0 us)
Sparse Core Ops, SparseCore 0:
  406.2 80.2 reduce-scatter.8
  490.2 78.6 reduce-scatter.10
  596.3 88.9 reduce-scatter.4
  689.0 63.4 reduce-scatter.6
  756.9 70.9 all-reduce.7

commit v2 on v1

v2 whole, which is shorter than its diff:
```python
import functools
import jax
import jax.numpy as jnp
from jax import lax
from jax.experimental import pallas as pl
from jax.experimental.pallas import tpu as pltpu
from jax.sharding import PartitionSpec as P

R = 72
KW = 4
E = 2
CAP = 192
EPSILON = 1e-05
FTILE = 256
LOG2E = 1.4426950408889634

NS = 16
LANES = 128
STEP = 8
CHUNK = 64


def swap(value, bit):
    size = lax.axis_size("shard")
    return lax.ppermute(value, "shard", [(i, i ^ bit) for i in range(size)])


def swap_groups(value, bit):
    size = lax.axis_size("grp")
    return lax.ppermute(value, "grp", [(g, g ^ bit) for g in range(size)])


def tie(value, *others):
    for other in others:
        corner = other[(0,) * other.ndim].astype(jnp.float32)
        value = value + (0.0 * corner).astype(value.dtype)
    return value


def gather_pieces(value):
    far = swap(value, 2)
    return (value, swap(value, 1), far, swap(far, 1))


def scatter_near(held, given, *others):
    side = lax.axis_index("shard") // 2
    held = tie(held + swap(given, 1).astype(jnp.float32), *others)
    mine = lax.dynamic_index_in_dim(held, side, 0, False)
    return mine, lax.dynamic_index_in_dim(held, 1 - side, 0, False).astype(jnp.bfloat16)


def halve(value, axis, bit):
    mine = (lax.axis_index("grp") // bit) % 2
    shape = value.shape
    value = value.reshape(shape[:axis] + (shape[axis] // 2, 2) + shape[axis + 1 :])
    held = lax.dynamic_index_in_dim(value, mine, axis + 1, False)
    given = lax.dynamic_index_in_dim(value, 1 - mine, axis + 1, False)
    return held, given.astype(jnp.bfloat16)


def join(held, got, *others):
    return tie(held.astype(jnp.float32) + got.astype(jnp.float32), *others)


def sum_rest(value, steps):
    for axis, bit in steps:
        held, given = halve(value, axis, bit)
        value = join(held, swap_groups(given, bit))
    return value


def share_pieces(pieces):
    groups, parts = (lax.axis_size("grp"), lax.axis_size("shard"))
    moves = [
        (g * parts + s, g * parts + (s ^ (2 + g % 2))) for g in range(groups) for s in range(parts)
    ]
    crossed = lax.ppermute(pieces[2], ("grp", "shard"), moves)
    shared = lax.ppermute(crossed, "grp", [(g, g ^ 1) for g in range(groups)])
    return [pieces[0], swap(pieces[1], 1), crossed, shared]


def total_groups(value):
    groups = lax.axis_size("grp")
    bit = 1
    while bit < groups:
        value = value.astype(jnp.bfloat16)
        value = value.astype(jnp.float32) + swap_groups(value, bit).astype(jnp.float32)
        bit = 2 * bit
    return value


def matmul(left, right):
    return jnp.dot(left, right, preferred_element_type=jnp.float32)


def pack(value, tiles):
    edge = tiles * LANES
    full = value[:, :edge].reshape(2, 8, tiles, LANES).transpose(2, 0, 1, 3)
    rest = jnp.concatenate([value[:8, edge:], value[8:, edge:]], axis=1)
    return jnp.concatenate([full.reshape(2 * tiles, 8, LANES), rest[None]], axis=0)


def unpack(value, tiles):
    full = value[: 2 * tiles].reshape(tiles, 2, 8, LANES).transpose(1, 2, 0, 3)
    rest = value[2 * tiles]
    rest = jnp.concatenate([rest[:, : LANES // 2], rest[:, LANES // 2 :]], axis=0)
    return jnp.concatenate([full.reshape(NS, tiles * LANES), rest], axis=1)


def fold_rows(parts):
    row = lax.broadcasted_iota(jnp.int32, (8, LANES), 0)
    top, pair, even = (row < 4, (row & 2) == 0, (row & 1) == 0)
    fours = [
        jnp.where(top, parts[i], parts[i + 4])
        + pltpu.roll(jnp.where(top, parts[i + 4], parts[i]), 4, 0)
        for i in range(4)
    ]
    twos = [
        jnp.where(
            pair,
            fours[i] + pltpu.roll(fours[i], 6, 0),
            fours[i + 2] + pltpu.roll(fours[i + 2], 2, 0),
        )
        for i in range(2)
    ]
    return jnp.where(
        even, twos[0] + pltpu.roll(twos[0], 7, 0), twos[1] + pltpu.roll(twos[1], 1, 0)
    )


def halves(pair_ref, at, left):
    low, high = (pair_ref[at, 0:8], pair_ref[at, 8:16])
    return (low, high, jnp.where(left, low, high))


def scan_forward_chunk(tiles, dt_ref, dx_ref, entry_ref, read_ref, rate_ref, out_ref, state_ref, end_ref, held):
    left = lax.broadcasted_iota(jnp.int32, (8, LANES), 1) < LANES // 2

    def group(g, states):
        at, base = (g, g * STEP)
        states = list(states)
        entry = [halves(entry_ref, base + t, left) for t in range(STEP)]
        read = [halves(read_ref, base + t, left) for t in range(STEP)]
        for tile in range(tiles + 1):
            columns = slice(tile * LANES, (tile + 1) * LANES)
            rows = [2 * tile] if tile == tiles else [2 * tile, 2 * tile + 1]
            which = [2] if tile == tiles else [0, 1]
            sums = []
            for t in range(STEP):
                step = dt_ref[at, t : t + 1, columns]
                fed = dx_ref[at, t : t + 1, columns]
                total = None
                for r, w in zip(rows, which):
                    state_ref[base + t, r] = states[r]
                    states[r] = jnp.exp2(step * rate_ref[r]) * states[r] + entry[t][w] * fed
                    term = read[t][w] * states[r]
                    total = term if total is None else total + term
                sums.append(total)
            out_ref[at, :, columns] = fold_rows(sums)
        return tuple(states)

    count = 2 * tiles + 1
    states = lax.fori_loop(0, dt_ref.shape[0], group, tuple(held[r] for r in range(count)))
    for r in range(count):
        held[r] = states[r]
        end_ref[r] = states[r]


def scan_backward_chunk(
    tiles, dt_ref, dx_ref, grad_ref, entry_ref, read_ref, rate_ref, state_ref,
    fed_out, step_out, entry_out, read_out, rate_out, flow, after,
):
    count = 2 * tiles + 1
    left = lax.broadcasted_iota(jnp.int32, (8, LANES), 1) < LANES // 2
    groups = dt_ref.shape[0]

    def group(g, carry):
        at = groups - 1 - g
        base = at * STEP
        flows, afters = (list(carry[0]), list(carry[1]))
        entry = [halves(entry_ref, base + t, left) for t in range(STEP)]
        read = [halves(read_ref, base + t, left) for t in range(STEP)]
        entry_sum = [[None, None] for _ in range(STEP)]
        read_sum = [[None, None] for _ in range(STEP)]
        for tile in range(tiles + 1):
            last = tile == tiles
            columns = slice(tile * LANES, (tile + 1) * LANES)
            rows = [2 * tile] if last else [2 * tile, 2 * tile + 1]
            which = [2] if last else [0, 1]
            fed_sums, step_sums = ([None] * STEP, [None] * STEP)
            rate_sum = [rate_out[r] for r in rows]
            for t in reversed(range(STEP)):
                step = dt_ref[at, t : t + 1, columns]
                fed = dx_ref[at, t : t + 1, columns]
                grad = grad_ref[at, t : t + 1, columns]
                for i, (r, w) in enumerate(zip(rows, which)):
                    before = state_ref[base + t, r]
                    arriving = flows[r] + read[t][w] * grad
                    entry_term = arriving * fed
                    read_term = afters[r] * grad
                    fed_term = entry[t][w] * arriving
                    leaving = jnp.exp2(step * rate_ref[r]) * arriving
                    product = leaving * before
                    step_term = product * rate_ref[r]
                    rate_sum[i] = rate_sum[i] + product * step
                    flows[r] = leaving
                    afters[r] = before
                    fed_sums[t] = fed_term if i == 0 else fed_sums[t] + fed_term
                    step_sums[t] = step_term if i == 0 else step_sums[t] + step_term
                    for total, term in ((entry_sum[t], entry_term), (read_sum[t], read_term)):
                        if last:
                            total[0] = total[0] + jnp.where(left, term, 0.0)
                            total[1] = total[1] + jnp.where(left, 0.0, term)
                        else:
                            total[i] = term if total[i] is None else total[i] + term
            fed_out[at, :, columns] = fold_rows(fed_sums)
            step_out[at, :, columns] = fold_rows(step_sums)
            for i, r in enumerate(rows):
                rate_out[r] = rate_sum[i]
        for t in range(STEP):
            for i in range(2):
                entry_out[base + t, 8 * i : 8 * i + 8] = entry_sum[t][i]
                read_out[base + t, 8 * i : 8 * i + 8] = read_sum[t][i]
        return (tuple(flows), tuple(afters))

    flows, afters = lax.fori_loop(
        0,
        groups,
        group,
        (tuple(flow[r] for r in range(count)), tuple(after[r] for r in range(count))),
    )
    for r in range(count):
        flow[r] = flows[r]
        after[r] = afters[r]


def split_low(value):
    high = value.astype(jnp.bfloat16)
    return high, (value - high.astype(jnp.float32)).astype(jnp.bfloat16)


def dot(left, right):
    return jnp.dot(left, right, preferred_element_type=jnp.float32)


def dot_t(left, right):
    return lax.dot_general(left, right, (((1,), (1,)), ((), ())), preferred_element_type=jnp.float32)


def t_dot(left, right):
    return lax.dot_general(left, right, (((0,), (0,)), ((), ())), preferred_element_type=jnp.float32)


def live_rows(me_ref, length_ref, rows):
    slot = me_ref[0] * rows + lax.broadcasted_iota(jnp.int32, (rows, 1), 0)
    return slot < length_ref[0]


def router_rows(gains_ref):
    row = lax.broadcasted_iota(jnp.int32, gains_ref.shape, 0)
    return jnp.where(row < E, gains_ref[...], 0.0).astype(jnp.bfloat16)


def cut_kernel(parts, inside, cols, goal_ref, in_ref, up_ref, *rest):
    number = len(rest) // 2
    in_outs, up_outs, sems = (rest[:number], rest[number : 2 * number], rest[-1])
    copies = []
    for k in range(number):
        columns = pl.ds(pl.multiple_of(goal_ref[k] * cols, LANES), cols)
        copies.append(pltpu.make_async_copy(up_ref.at[:, :, columns], up_outs[k], sems.at[k]))
        copies[-1].start()
    for d in range(parts):
        for k in range(number):

            @pl.when(goal_ref[k] == d)
            def write():
                in_outs[k][:, :inside] = in_ref[:, d * inside : (d + 1) * inside]
                at = (parts + d) * inside
                in_outs[k][:, inside:] = in_ref[:, at : at + inside]

    for copy in copies:
        copy.wait()


def cut_weights(goal, in_weight, up_weight, parts, inside):
    slab = in_weight.shape[0]
    cols = up_weight.shape[2] // parts
    number = 3
    in_shape = jax.ShapeDtypeStruct((slab, 2 * inside), in_weight.dtype)
    up_shape = jax.ShapeDtypeStruct((up_weight.shape[0], slab, cols), up_weight.dtype)
    vmem, anywhere = (pl.BlockSpec(memory_space=pltpu.VMEM), pl.BlockSpec(memory_space=pl.ANY))
    outs = pl.pallas_call(
        functools.partial(cut_kernel, parts, inside, cols),
        in_specs=[pl.BlockSpec(memory_space=pltpu.SMEM), vmem, anywhere],
        out_specs=[vmem] * number + [anywhere] * number,
        out_shape=[in_shape] * number + [up_shape] * number,
        scratch_shapes=[pltpu.SemaphoreType.DMA((number,))],
        compiler_params=pltpu.CompilerParams(vmem_limit_bytes=24 * 2**20),
        name="cut_weights",
    )(goal, in_weight, up_weight)
    return outs[:number], outs[number:]


def to_power(value):
    return value / (1.0 + jnp.exp(-value))


def project_kernel(parts, inside, me_ref, source_ref, length_ref, *rest):
    normed_refs, weight_refs, rest = (rest[:parts], rest[parts : 2 * parts], rest[2 * parts :])
    taps_ref, bias_ref, select_ref, inner_out, gate_out, summed_out, conv_out, low_out, selected_out = rest[:9]
    normed, weight, shifted, sems = rest[9:]
    block = pl.program_id(0)
    me = me_ref[0]
    rows, slab = (normed_refs[0].shape[0], weight_refs[0].shape[0])

    @pl.when(block == 0)
    def fetch():
        copies = []
        for k in range(parts):
            at = pl.ds(pl.multiple_of(source_ref[k] * slab, 16), slab)
            copies.append(pltpu.make_async_copy(weight_refs[k], weight.at[at], sems.at[k]))
            at = pl.ds(pl.multiple_of((me ^ k) * rows, 16), rows)
            copies.append(pltpu.make_async_copy(normed_refs[k], normed.at[at], sems.at[parts + k]))
        for copy in copies:
            copy.start()
        for copy in copies:
            copy.wait()
        shifted[0:8] = jnp.zeros((8, inside), jnp.float32)

    start = pl.multiple_of(block * rows, 16)
    projected = jnp.dot(normed[pl.ds(start, rows)], weight[...], preferred_element_type=jnp.float32)
    slot = block * rows + lax.broadcasted_iota(jnp.int32, (rows, 1), 0)
    inner = jnp.where(slot < length_ref[0], projected[:, :inside], 0.0)
    gate_out[...] = projected[:, inside:]
    inner_out[...] = inner
    shifted[8:] = inner
    summed = bias_ref[...]
    for k in range(KW):
        summed = summed + taps_ref[k : k + 1] * shifted[8 - (KW - 1) + k : 8 - (KW - 1) + k + rows]
    shifted[0:8] = shifted[rows : rows + 8]
    summed_out[...] = summed
    value = to_power(summed)
    conv_out[...] = value
    low = value.astype(jnp.bfloat16)
    low_out[...] = low
    selected_out[...] = jnp.dot(low, select_ref[...], preferred_element_type=jnp.float32)


def project(me, source, length, normed_pieces, weight_pieces, taps, bias, select_wide):
    parts = len(normed_pieces)
    rows, width = normed_pieces[0].shape
    slab, both = weight_pieces[0].shape
    inside, picked = select_wide.shape
    total = rows * parts
    smem, anywhere = (pl.BlockSpec(memory_space=pltpu.SMEM), pl.BlockSpec(memory_space=pl.ANY))
    vmem = pl.BlockSpec(memory_space=pltpu.VMEM)
    row = pl.BlockSpec((rows, inside), lambda i: (i, 0))
    wide = jax.ShapeDtypeStruct((total, inside), jnp.float32)
    return pl.pallas_call(
        functools.partial(project_kernel, parts, inside),
        grid=(parts,),
        in_specs=[smem] * 3 + [anywhere] * (2 * parts) + [vmem] * 3,
        out_specs=[row] * 5 + [pl.BlockSpec((rows, picked), lambda i: (i, 0))],
        out_shape=[wide] * 4
        + [
            jax.ShapeDtypeStruct((total, inside), jnp.bfloat16),
            jax.ShapeDtypeStruct((total, picked), jnp.float32),
        ],
        scratch_shapes=[
            pltpu.VMEM((total, width), jnp.bfloat16),
            pltpu.VMEM((slab * parts, both), jnp.bfloat16),
            pltpu.VMEM((rows + 8, inside), jnp.float32),
            pltpu.SemaphoreType.DMA((2 * parts,)),
        ],
        compiler_params=pltpu.CompilerParams(vmem_limit_bytes=40 * 2**20),
        cost_estimate=pl.CostEstimate(flops=2 * total * width * both, bytes_accessed=20 * 2**20, transcendentals=total * inside),
        name="project",
    )(me, source, length, *normed_pieces, *weight_pieces, taps, bias, select_wide)


def live_slots(start, length_ref, rows):
    return start + lax.broadcasted_iota(jnp.int32, (rows, 1), 0) < length_ref[0]


def store_wide(ref, value):
    groups, _, width = ref.shape
    inside = value.shape[1]
    ref[:, :, :inside] = value.reshape(groups, STEP, inside)
    ref[:, :, inside:] = value[:, 2 * inside - width :].reshape(groups, STEP, width - inside)


def load_narrow(ref, inside):
    groups, _, width = ref.shape
    edge = 2 * inside - width
    value = ref[...].reshape(groups * STEP, width)
    return jnp.concatenate([value[:, :edge], value[:, edge:inside] + value[:, inside:]], axis=1)


def store_spread(entry_ref, read_ref, selected):
    turned = selected.T
    for t in range(selected.shape[0]):
        entry_ref[t] = jnp.broadcast_to(turned[R : R + NS, t : t + 1], (NS, LANES))
        read_ref[t] = jnp.broadcast_to(turned[R + NS : R + 2 * NS, t : t + 1], (NS, LANES))


def step_sizes(selected, weight_ref, bias_ref, live):
    low = selected.astype(jnp.bfloat16)
    pre = dot(low, weight_ref[...]) + bias_ref[...]
    soft = jnp.maximum(pre, 0.0) + jnp.log1p(jnp.exp(-jnp.abs(pre)))
    return low, pre, jnp.where(live, soft, 0.0)


def mixer_kernel(
    tiles, share, me_ref, length_ref, selected_ref, conv_ref, gate_ref, weight_ref, bias_ref, skip_ref, rate_ref, project_ref,
    state_ref, end_ref, mixed_out, gated_out, held_out, given_out,
    dt_ref, dx_ref, entry_ref, read_ref, out_ref, held,
):
    chunk, inside = conv_ref.shape
    step = pl.program_id(0)

    @pl.when(step == 0)
    def start():
        held[...] = jnp.zeros_like(held)

    selected, conv = (selected_ref[...], conv_ref[...])
    live = live_slots(step * chunk, length_ref, chunk)
    _, _, size = step_sizes(selected, weight_ref, bias_ref, live)
    store_wide(dt_ref, size)
    store_wide(dx_ref, size * conv)
    store_spread(entry_ref, read_ref, selected)
    scan_forward_chunk(tiles, dt_ref, dx_ref, entry_ref, read_ref, rate_ref, out_ref, state_ref, end_ref, held)
    mixed = load_narrow(out_ref, inside) + skip_ref[...] * conv
    mixed_out[...] = mixed
    gated = (mixed * to_power(gate_ref[...])).astype(jnp.bfloat16)
    gated_out[...] = gated
    part = dot(gated, project_ref[...])
    block = step // share
    rows = pl.ds(pl.multiple_of((step % share) * chunk, chunk), chunk)

    @pl.when(block % 2 == me_ref[0] % 2)
    def keep():
        held_out[0, rows] = part

    @pl.when(block % 2 != me_ref[0] % 2)
    def give():
        given_out[0, rows] = part.astype(jnp.bfloat16)


def mixer(me, length, selected, conv_out, zgate, step_wide, bias, skip, rate, out_weight, span, tiles):
    total, inside = conv_out.shape
    width = out_weight.shape[1]
    count = 2 * tiles + 1
    chunk = CHUNK
    wide = (tiles + 1) * LANES
    share = span // chunk
    smem, vmem = (pl.BlockSpec(memory_space=pltpu.SMEM), pl.BlockSpec(memory_space=pltpu.VMEM))
    row = pl.BlockSpec((chunk, inside), lambda i: (i, 0))
    part = pl.BlockSpec((1, span, width), lambda i: (i // (2 * share), 0, 0))
    f32, bf16 = (jnp.float32, jnp.bfloat16)
    return pl.pallas_call(
        functools.partial(mixer_kernel, tiles, share),
        grid=(total // chunk,),
        in_specs=[smem, smem, pl.BlockSpec((chunk, LANES), lambda i: (i, 0)), row, row] + [vmem] * 5,
        out_specs=[pl.BlockSpec((chunk, count, 8, LANES), lambda i: (i, 0, 0, 0)), vmem, row, row, part, part],
        out_shape=[
            jax.ShapeDtypeStruct((total, count, 8, LANES), f32),
            jax.ShapeDtypeStruct((count, 8, LANES), f32),
            jax.ShapeDtypeStruct((total, inside), f32),
            jax.ShapeDtypeStruct((total, inside), bf16),
            jax.ShapeDtypeStruct((2, span, width), f32),
            jax.ShapeDtypeStruct((2, span, width), bf16),
        ],
        scratch_shapes=[pltpu.VMEM((chunk // STEP, STEP, wide), f32)] * 2
        + [pltpu.VMEM((chunk, NS, LANES), f32)] * 2
        + [pltpu.VMEM((chunk // STEP, STEP, wide), f32), pltpu.VMEM((count, 8, LANES), f32)],
        compiler_params=pltpu.CompilerParams(vmem_limit_bytes=40 * 2**20),
        name="mixer",
    )(me, length, selected, conv_out, zgate, step_wide, bias, skip, rate, out_weight)


def row_sums(value):
    high, low = split_low(value)
    ones = jnp.ones((8, LANES), jnp.bfloat16)
    return dot_t(ones, high) + dot_t(ones, low)


def mixer_back_kernel(
    tiles, share, me_ref, length_ref, *rest,
):
    grad_refs, rest = (rest[:4], rest[4:])
    (
        selected_ref, conv_ref, gate_ref, mixed_ref, gated_ref, state_ref, end_ref, weight_ref, bias_ref, skip_ref, rate_ref, project_ref,
        gate_out, conv_out, rank_out, entry_sum_out, read_sum_out, step_out, bias_out, skip_out, rate_out, project_out,
        grads, dt_ref, dx_ref, mix_ref, entry_ref, read_ref, fed_ref, rise_ref, entry_parts, read_parts, flow, after, total, sems,
    ) = rest
    chunk, inside = conv_ref.shape
    span = grad_refs[0].shape[0]
    index = pl.program_id(0)
    step = pl.num_programs(0) - 1 - index

    @pl.when(index == 0)
    def start():
        copies = []
        for k in range(4):
            at = pl.ds(pl.multiple_of((me_ref[0] ^ k) * span, 16), span)
            copies.append(pltpu.make_async_copy(grad_refs[k], grads.at[at], sems.at[k]))
            copies[-1].start()
        flow[...] = jnp.zeros_like(flow)
        after[...] = end_ref[...]
        rate_out[...] = jnp.zeros_like(rate_out)
        step_out[...] = jnp.zeros_like(step_out)
        bias_out[...] = jnp.zeros_like(bias_out)
        skip_out[...] = jnp.zeros_like(skip_out)
        total[...] = jnp.zeros_like(total)
        for copy in copies:
            copy.wait()

    rows = pl.ds(pl.multiple_of(step * chunk, chunk), chunk)
    grad_gated = dot_t(grads[rows], project_ref[...])
    gate, mixed, conv = (gate_ref[...], mixed_ref[...], conv_ref[...])
    curve = 1.0 / (1.0 + jnp.exp(-gate))
    grad_mixed = grad_gated * (gate * curve)
    gate_out[...] = (grad_gated * mixed * (curve * (1.0 + gate * (1.0 - curve)))).astype(jnp.bfloat16)
    skip_out[...] += jnp.sum(grad_mixed * conv, axis=0, keepdims=True)
    selected = selected_ref[...]
    live = live_slots(step * chunk, length_ref, chunk)
    low, pre, size = step_sizes(selected, weight_ref, bias_ref, live)
    store_wide(dt_ref, size)
    store_wide(dx_ref, size * conv)
    store_wide(mix_ref, grad_mixed)
    store_spread(entry_ref, read_ref, selected)
    scan_backward_chunk(
        tiles, dt_ref, dx_ref, mix_ref, entry_ref, read_ref, rate_ref, state_ref,
        fed_ref, rise_ref, entry_parts, read_parts, rate_out, flow, after,
    )
    fed = load_narrow(fed_ref, inside)
    grad_size = load_narrow(rise_ref, inside) * (1.0 / LOG2E) + fed * conv
    grad_pre = jnp.where(live, grad_size / (1.0 + jnp.exp(-pre)), 0.0)
    bias_out[...] += jnp.sum(grad_pre, axis=0, keepdims=True)
    grad_low = grad_pre.astype(jnp.bfloat16)
    rank_out[...] = dot_t(grad_low, weight_ref[...])
    step_out[...] += t_dot(low, grad_low)
    conv_out[...] = fed * size + skip_ref[...] * grad_mixed
    entry_sum_out[0] = row_sums(entry_parts[...].reshape(chunk * NS, LANES))
    read_sum_out[0] = row_sums(read_parts[...].reshape(chunk * NS, LANES))

    @pl.when(step % share == 0)
    def weigh():
        block = pl.ds(pl.multiple_of(step * chunk, span), span)
        total[...] += t_dot(grads[block], gated_ref[...])

    @pl.when(step == 0)
    def finish():
        project_out[...] = total[...].astype(jnp.bfloat16)


def mixer_back(me, length, grad_pieces, selected, conv_out, zgate, mixed, gated, states, end, step_wide, bias, skip, rate, out_weight, tiles):
    total, inside = conv_out.shape
    span, width = grad_pieces[0].shape
    count = 2 * tiles + 1
    chunk = CHUNK
    steps = total // chunk
    wide = (tiles + 1) * LANES
    share = span // chunk
    smem, vmem = (pl.BlockSpec(memory_space=pltpu.SMEM), pl.BlockSpec(memory_space=pltpu.VMEM))
    anywhere = pl.BlockSpec(memory_space=pl.ANY)
    row = pl.BlockSpec((chunk, inside), lambda i: (steps - 1 - i, 0))
    lane = pl.BlockSpec((chunk, LANES), lambda i: (steps - 1 - i, 0))
    sums = pl.BlockSpec((1, 8, chunk * NS), lambda i: (steps - 1 - i, 0, 0))
    f32, bf16 = (jnp.float32, jnp.bfloat16)
    one = jax.ShapeDtypeStruct((1, inside), f32)
    summed = jax.ShapeDtypeStruct((steps, 8, chunk * NS), f32)
    return pl.pallas_call(
        functools.partial(mixer_back_kernel, tiles, share),
        grid=(steps,),
        in_specs=[smem, smem]
        + [anywhere] * 4
        + [lane, row, row, row]
        + [pl.BlockSpec((span, inside), lambda i: ((steps - 1 - i) // share, 0))]
        + [pl.BlockSpec((chunk, count, 8, LANES), lambda i: (steps - 1 - i, 0, 0, 0))]
        + [vmem] * 6,
        out_specs=[row, row, lane, sums, sums] + [vmem] * 5,
        out_shape=[
            jax.ShapeDtypeStruct((total, inside), bf16),
            jax.ShapeDtypeStruct((total, inside), f32),
            jax.ShapeDtypeStruct((total, LANES), f32),
            summed,
            summed,
            jax.ShapeDtypeStruct((LANES, inside), f32),
            one,
            one,
            jax.ShapeDtypeStruct((count, 8, LANES), f32),
            jax.ShapeDtypeStruct((width, inside), bf16),
        ],
        scratch_shapes=[pltpu.VMEM((total, width), bf16)]
        + [pltpu.VMEM((chunk // STEP, STEP, wide), f32)] * 3
        + [pltpu.VMEM((chunk, NS, LANES), f32)] * 2
        + [pltpu.VMEM((chunk // STEP, STEP, wide), f32)] * 2
        + [pltpu.VMEM((chunk, NS, LANES), f32)] * 2
        + [pltpu.VMEM((count, 8, LANES), f32)] * 2
        + [pltpu.VMEM((width, inside), f32), pltpu.SemaphoreType.DMA((4,))],
        compiler_params=pltpu.CompilerParams(vmem_limit_bytes=48 * 2**20),
        name="mixer_back",
    )(me, length, *grad_pieces, selected, conv_out, zgate, mixed, gated, states, end, step_wide, bias, skip, rate, out_weight)


def project_back_kernel(parts, me_ref, source_ref, length_ref, *rest):
    normed_refs, weight_refs, rest = (rest[:parts], rest[parts : 2 * parts], rest[2 * parts :])
    (
        selected_ref, conv_ref, summed_ref, inner_ref, gate_ref, low_ref, taps_ref, select_ref,
        held_out, given_out, inner_held, inner_given, gate_held, gate_given, select_out, taps_out, bias_out, gain_out,
        normed, weight, shifted, projected, total, sems,
    ) = rest
    index = pl.program_id(0)
    block = parts - 1 - index
    rows, inside = inner_ref.shape
    slab = weight_refs[0].shape[0]
    me = me_ref[0]
    odd = source_ref[parts]

    @pl.when(index == 0)
    def fetch():
        copies = []
        for k in range(parts):
            at = pl.ds(pl.multiple_of(source_ref[k] * slab, 16), slab)
            copies.append(pltpu.make_async_copy(weight_refs[k], weight.at[at], sems.at[k]))
            at = pl.ds(pl.multiple_of((me ^ k) * rows, 16), rows)
            copies.append(pltpu.make_async_copy(normed_refs[k], normed.at[at], sems.at[parts + k]))
        for copy in copies:
            copy.start()
        shifted[rows:] = jnp.zeros((8, inside), jnp.float32)
        total[...] = jnp.zeros_like(total)
        select_out[...] = jnp.zeros_like(select_out)
        taps_out[...] = jnp.zeros_like(taps_out)
        bias_out[...] = jnp.zeros_like(bias_out)
        gain_out[...] = jnp.zeros_like(gain_out)
        for copy in copies:
            copy.wait()

    selected = selected_ref[...]
    summed = summed_ref[...]
    curve = 1.0 / (1.0 + jnp.exp(-summed))
    grad_summed = (conv_ref[...] + dot_t(selected, select_ref[...])) * (curve * (1.0 + summed * (1.0 - curve)))
    select_out[...] += t_dot(selected, low_ref[...])
    bias_out[...] += jnp.sum(grad_summed, axis=0, keepdims=True)
    shifted[:rows] = grad_summed
    inner = inner_ref[...]
    grad_inner = jnp.zeros((rows, inside), jnp.float32)
    for k in range(KW):
        moved = shifted[KW - 1 - k : KW - 1 - k + rows]
        grad_inner = grad_inner + taps_ref[k : k + 1] * moved
        taps_out[k : k + 1] += jnp.sum(inner * moved, axis=0, keepdims=True)
    shifted[rows:] = shifted[0:8]
    live = live_slots(block * rows, length_ref, rows)
    projected[:, :inside] = jnp.where(live, grad_inner, 0.0).astype(jnp.bfloat16)
    projected[:, inside:] = gate_ref[...]
    normed_rows = normed[pl.ds(pl.multiple_of(block * rows, rows), rows)]
    grad_normed = dot_t(projected[...], weight[...])
    gain_out[...] += jnp.sum(grad_normed * normed_rows.astype(jnp.float32), axis=0, keepdims=True)
    total[...] += t_dot(normed_rows, projected[...])

    @pl.when(block % 2 == me % 2)
    def keep():
        held_out[0] = grad_normed

    @pl.when(block % 2 != me % 2)
    def give():
        given_out[0] = grad_normed.astype(jnp.bfloat16)

    @pl.when(block == 0)
    def finish():
        for h in range(parts // 2):
            at = pl.ds(pl.multiple_of((2 * h + odd) * slab, 16), slab)
            inner_held[h] = total[at, :inside]
            gate_held[h] = total[at, inside:]
            at = pl.ds(pl.multiple_of((2 * h + 1 - odd) * slab, 16), slab)
            inner_given[h] = total[at, :inside].astype(jnp.bfloat16)
            gate_given[h] = total[at, inside:].astype(jnp.bfloat16)


def project_back(me, source, length, normed_pieces, weight_pieces, grad_selected, conv_grad, summed, inner, gate_grad, conv_low, taps, select_wide):
    parts = len(normed_pieces)
    rows, width = normed_pieces[0].shape
    slab, both = weight_pieces[0].shape
    total, inside = inner.shape
    smem, anywhere = (pl.BlockSpec(memory_space=pltpu.SMEM), pl.BlockSpec(memory_space=pl.ANY))
    vmem = pl.BlockSpec(memory_space=pltpu.VMEM)
    row = pl.BlockSpec((rows, inside), lambda i: (parts - 1 - i, 0))
    part = pl.BlockSpec((1, rows, width), lambda i: ((parts - 1 - i) // 2, 0, 0))
    f32, bf16 = (jnp.float32, jnp.bfloat16)
    return pl.pallas_call(
        functools.partial(project_back_kernel, parts),
        grid=(parts,),
        in_specs=[smem] * 3
        + [anywhere] * (2 * parts)
        + [pl.BlockSpec((rows, LANES), lambda i: (parts - 1 - i, 0))]
        + [row] * 5
        + [vmem] * 2,
        out_specs=[part, part] + [vmem] * 8,
        out_shape=[
            jax.ShapeDtypeStruct((2, rows, width), f32),
            jax.ShapeDtypeStruct((2, rows, width), bf16),
            jax.ShapeDtypeStruct((2, slab, inside), f32),
            jax.ShapeDtypeStruct((2, slab, inside), bf16),
            jax.ShapeDtypeStruct((2, slab, inside), f32),
            jax.ShapeDtypeStruct((2, slab, inside), bf16),
            jax.ShapeDtypeStruct((LANES, inside), f32),
            jax.ShapeDtypeStruct((8, inside), f32),
            jax.ShapeDtypeStruct((1, inside), f32),
            jax.ShapeDtypeStruct((1, width), f32),
        ],
        scratch_shapes=[
            pltpu.VMEM((total, width), bf16),
            pltpu.VMEM((slab * parts, both), bf16),
            pltpu.VMEM((rows + 8, inside), f32),
            pltpu.VMEM((rows, both), bf16),
            pltpu.VMEM((slab * parts, both), f32),
            pltpu.SemaphoreType.DMA((2 * parts,)),
        ],
        compiler_params=pltpu.CompilerParams(vmem_limit_bytes=56 * 2**20),
        name="project_back",
    )(me, source, length, *normed_pieces, *weight_pieces, grad_selected, conv_grad, summed, inner, gate_grad, conv_low, taps, select_wide)


def norm_kernel(parts, me_ref, tokens_ref, *rest):
    small_refs, normed_out, gains_out = (rest[:parts], rest[parts], rest[parts + 1])
    slab = small_refs[0].shape[1]
    for m in range(parts):

        @pl.when(me_ref[0] == m)
        def lay():
            for p in range(parts):
                gains_out[:, p * slab : (p + 1) * slab] = small_refs[p ^ m][...]

    tokens = tokens_ref[...]
    scale = lax.rsqrt(jnp.mean(tokens * tokens, axis=-1, keepdims=True) + EPSILON)
    normed_out[...] = (tokens * scale * gains_out[2:3]).astype(jnp.bfloat16)


def norm_rows(me, tokens, small_pieces):
    parts = len(small_pieces)
    smem, vmem = (pl.BlockSpec(memory_space=pltpu.SMEM), pl.BlockSpec(memory_space=pltpu.VMEM))
    return pl.pallas_call(
        functools.partial(norm_kernel, parts),
        in_specs=[smem] + [vmem] * (1 + parts),
        out_specs=[vmem] * 2,
        out_shape=[
            jax.ShapeDtypeStruct(tokens.shape, jnp.bfloat16),
            jax.ShapeDtypeStruct((small_pieces[0].shape[0], tokens.shape[1]), jnp.float32),
        ],
        compiler_params=pltpu.CompilerParams(vmem_limit_bytes=16 * 2**20),
        name="norm_rows",
    )(me, tokens, *small_pieces)


def route_kernel(
    me_ref, length_ref, tokens_ref, near_ref, got_ref, gains_ref, order_ref, routes_ref,
    first_out, normed_out, sent_out, probs_out,
):
    rows, width = tokens_ref.shape
    first = tokens_ref[...] + near_ref[...] + got_ref[...].astype(jnp.float32)
    first_out[...] = first
    scale = lax.rsqrt(jnp.mean(first * first, axis=-1, keepdims=True) + EPSILON)
    normed = (first * scale * gains_ref[3:4]).astype(jnp.bfloat16)
    normed_out[...] = normed
    logits = dot_t(normed, router_rows(gains_ref))
    gap = logits[:, 0:1] - logits[:, 1:2]
    prob_zero = 1.0 / (1.0 + jnp.exp(-gap))
    prob_one = 1.0 / (1.0 + jnp.exp(gap))
    lane = lax.broadcasted_iota(jnp.int32, (rows, LANES), 1)
    probs_out[...] = jnp.where(lane == 0, prob_zero, jnp.where(lane == 1, prob_one, 0.0))
    gate = jnp.where(routes_ref[...] == 0, prob_zero, prob_one)
    gate = jnp.where(live_rows(me_ref, length_ref, rows), gate, 0.0)
    high, low = split_low(gate)
    high, low = (high.astype(jnp.float32), low.astype(jnp.float32))
    gates = jnp.where(lane == 0, high, jnp.where(lane == 1, low, 0.0)).astype(jnp.bfloat16)
    sent_out[:, :width] = dot(order_ref[...], normed).astype(jnp.bfloat16)
    sent_out[:, width:] = dot(order_ref[...], gates).astype(jnp.bfloat16)


def route(me, length, tokens, near, got, gains, order, routes):
    rows, width = tokens.shape
    smem, vmem = (pl.BlockSpec(memory_space=pltpu.SMEM), pl.BlockSpec(memory_space=pltpu.VMEM))
    return pl.pallas_call(
        route_kernel,
        in_specs=[smem, smem] + [vmem] * 6,
        out_specs=[vmem] * 4,
        out_shape=[
            jax.ShapeDtypeStruct((rows, width), jnp.float32),
            jax.ShapeDtypeStruct((rows, width), jnp.bfloat16),
            jax.ShapeDtypeStruct((rows, width + LANES), jnp.bfloat16),
            jax.ShapeDtypeStruct((rows, LANES), jnp.float32),
        ],
        compiler_params=pltpu.CompilerParams(vmem_limit_bytes=32 * 2**20),
        name="route",
    )(me, length, tokens, near, got, gains, order, routes)


def expert_kernel(parts, cap, steps, pair, me_ref, source_ref, counts_ref, *rest):
    sent_refs, cot_refs, up_refs = (rest[:parts], rest[parts : 2 * parts], rest[2 * parts : 3 * parts])
    (
        down_ref, grad_held, grad_given, out_held, out_given, up_held, up_given, down_held, down_given,
    ) = rest[3 * parts : 3 * parts + 9]
    rows, cots, up, down, rows_t, cots_t, scale, dots, grad_sum, out_sum, product, sems = rest[3 * parts + 9 :]
    step = pl.program_id(0)
    expert, tile = (step // steps, step % steps)
    span, width = cots.shape[1:]
    slab = up_refs[0].shape[1]
    offset = span - cap
    count = parts * cap
    me = me_ref[0]

    @pl.when(step == 0)
    def fetch():
        copies = [pltpu.make_async_copy(down_ref, down, sems.at[0])]
        for k in range(parts):
            copies.append(pltpu.make_async_copy(sent_refs[k], rows.at[me ^ k], sems.at[1 + k]))
            copies.append(pltpu.make_async_copy(cot_refs[k], cots.at[me ^ k], sems.at[1 + parts + k]))
            at = pl.ds(pl.multiple_of(source_ref[k] * slab, 16), slab)
            copies.append(pltpu.make_async_copy(up_refs[k], up.at[:, at], sems.at[1 + 2 * parts + k]))
        for copy in copies:
            copy.start()
        grad_sum[...] = jnp.zeros_like(grad_sum)
        out_sum[...] = jnp.zeros_like(out_sum)
        dots[...] = jnp.zeros_like(dots)
        for copy in copies:
            copy.wait()

    at = pl.ds(pl.multiple_of(expert * offset, 16), cap)
    mine = rows[:, at, :width].reshape(count, width)
    cot = cots[:, at].reshape(count, width)

    @pl.when(tile == 0)
    def turn():
        rows_t[...] = mine.T
        cots_t[...] = cot.T
        slot = lax.broadcasted_iota(jnp.int32, (cap, LANES), 0)
        for b in range(parts):
            gates = rows[b, at, width:].astype(jnp.float32)
            gate = gates[:, 0:1] + gates[:, 1:2]
            first = slot < counts_ref[b]
            later = slot + offset >= counts_ref[b]
            live = jnp.where(expert == 0, first.astype(jnp.float32), later.astype(jnp.float32))
            scale[b * cap : (b + 1) * cap] = live * gate

    columns = pl.ds(pl.multiple_of(tile * FTILE, FTILE), FTILE)
    up_tile = up[expert, :, columns]
    down_tile = down[expert, columns, :]
    weight = scale[...][:, 0:1]
    pre = dot(mine, up_tile)
    grad_hidden = dot_t(cot, down_tile)
    square = pre * pre
    bend = jnp.tanh(0.7978845608028654 * pre * (1.0 + 0.044715 * square))
    rise = 0.5 * (1.0 + bend)
    slope = rise + 0.5 * pre * (1.0 - bend * bend) * (0.7978845608028654 * (1.0 + 0.134145 * square))
    hidden = (weight * (pre * rise)).astype(jnp.bfloat16)
    grad_pre = (weight * slope * grad_hidden).astype(jnp.bfloat16)
    part = jnp.sum(hidden.astype(jnp.float32) * grad_hidden, axis=1, keepdims=True)
    dots[:, at] += jnp.broadcast_to(part, (count, LANES)).reshape(parts, cap, LANES)
    out_sum[:, at] += dot(hidden, down_tile).reshape(parts, cap, width)
    grad_sum[:, at] += dot_t(grad_pre, up_tile).reshape(parts, cap, width)
    odd, second = (source_ref[parts], source_ref[parts + 1])
    product[...] = dot(rows_t[...], grad_pre)
    for h in range(parts // 2):
        at = pl.ds(pl.multiple_of((2 * h + odd) * slab, 16), slab)
        up_held[0, h] = product[at]
        at = pl.ds(pl.multiple_of((2 * h + 1 - odd) * slab, 16), slab)
        up_given[0, h] = product[at].astype(jnp.bfloat16)
    product[...] = dot(cots_t[...], hidden)
    for h in range(width // (2 * pair)):
        at = pl.ds(pl.multiple_of((2 * h + second) * pair, 8), pair)
        down_held[0, h] = product[at]
        at = pl.ds(pl.multiple_of((2 * h + 1 - second) * pair, 8), pair)
        down_given[0, h] = product[at].astype(jnp.bfloat16)

    @pl.when(step == pl.num_programs(0) - 1)
    def finish():
        for b in range(parts):

            @pl.when(me % 2 == b % 2)
            def hold():
                grad_held[b // 2, :, :width] = grad_sum[b]
                grad_held[b // 2, :, width:] = dots[b]
                out_held[b // 2] = out_sum[b]

            @pl.when(me % 2 != b % 2)
            def give():
                grad_given[b // 2, :, :width] = grad_sum[b].astype(jnp.bfloat16)
                grad_given[b // 2, :, width:] = dots[b].astype(jnp.bfloat16)
                out_given[b // 2] = out_sum[b].astype(jnp.bfloat16)


def experts(me, source, counts, sent_pieces, cot_pieces, up_pieces, down_weight, pair):
    parts = len(sent_pieces)
    span, width = cot_pieces[0].shape
    number, hid = down_weight.shape[:2]
    steps = hid // FTILE
    slab = up_pieces[0].shape[1]
    smem, anywhere = (pl.BlockSpec(memory_space=pltpu.SMEM), pl.BlockSpec(memory_space=pl.ANY))
    vmem = pl.BlockSpec(memory_space=pltpu.VMEM)
    f32, bf16 = (jnp.float32, jnp.bfloat16)
    pairs = width // (2 * pair)
    up_block = pl.BlockSpec((1, parts // 2, slab, FTILE), lambda i: (i // steps, 0, 0, i % steps))
    down_block = pl.BlockSpec((1, pairs, pair, FTILE), lambda i: (i // steps, 0, 0, i % steps))
    up_shape = (number, parts // 2, slab, hid)
    down_shape = (number, pairs, pair, hid)
    count = parts * CAP
    return pl.pallas_call(
        functools.partial(expert_kernel, parts, CAP, steps, pair),
        grid=(number * steps,),
        in_specs=[smem] * 3 + [anywhere] * (3 * parts + 1),
        out_specs=[vmem] * 4 + [up_block] * 2 + [down_block] * 2,
        out_shape=[
            jax.ShapeDtypeStruct((2, span, width + LANES), f32),
            jax.ShapeDtypeStruct((2, span, width + LANES), bf16),
            jax.ShapeDtypeStruct((2, span, width), f32),
            jax.ShapeDtypeStruct((2, span, width), bf16),
            jax.ShapeDtypeStruct(up_shape, f32),
            jax.ShapeDtypeStruct(up_shape, bf16),
            jax.ShapeDtypeStruct(down_shape, f32),
            jax.ShapeDtypeStruct(down_shape, bf16),
        ],
        scratch_shapes=[
            pltpu.VMEM((parts, span, width + LANES), bf16),
            pltpu.VMEM((parts, span, width), bf16),
            pltpu.VMEM((number, slab * parts, hid), bf16),
            pltpu.VMEM((number, hid, width), bf16),
            pltpu.VMEM((width, count), bf16),
            pltpu.VMEM((width, count), bf16),
            pltpu.VMEM((count, LANES), f32),
            pltpu.VMEM((parts, span, LANES), f32),
            pltpu.VMEM((parts, span, width), f32),
            pltpu.VMEM((parts, span, width), f32),
            pltpu.VMEM((width, FTILE), f32),
            pltpu.SemaphoreType.DMA((1 + 3 * parts,)),
        ],
        compiler_params=pltpu.CompilerParams(vmem_limit_bytes=60 * 2**20),
        cost_estimate=pl.CostEstimate(flops=12 * number * count * width * hid, bytes_accessed=24 * 2**20, transcendentals=number * count * hid),
        name="experts",
    )(me, source, counts, *sent_pieces, *cot_pieces, *up_pieces, down_weight)


def return_kernel(
    me_ref, length_ref, near_ref, got_ref, order_ref, normed_ref, probs_ref, routes_ref, first_ref, cot_ref, gains_ref,
    grad_out, low_out, gain_out, router_out,
):
    rows, width = first_ref.shape
    grad = near_ref[...] + got_ref[...].astype(jnp.float32)
    high, low = split_low(grad)
    grad = dot(order_ref[...], high) + dot(order_ref[...], low)
    lane = lax.broadcasted_iota(jnp.int32, (rows, LANES), 1)
    chosen = (lane == routes_ref[...]).astype(jnp.float32)
    grad_logits = (grad[:, width : width + 1] * (chosen - probs_ref[...])).astype(jnp.bfloat16)
    grad_normed = grad[:, :width] + dot(grad_logits[:, :NS], router_rows(gains_ref))
    router_out[...] = t_dot(grad_logits, normed_ref[...])[0:8]
    first = first_ref[...]
    scale = lax.rsqrt(jnp.mean(first * first, axis=-1, keepdims=True) + EPSILON)
    unit = first * scale
    gain_out[...] = jnp.sum(grad_normed * unit, axis=0, keepdims=True)
    pulled = grad_normed * gains_ref[3:4]
    pulled = scale * (pulled - unit * jnp.mean(pulled * unit, axis=-1, keepdims=True))
    total = jnp.where(live_rows(me_ref, length_ref, rows), cot_ref[...], 0.0) + pulled
    grad_out[...] = total
    low_out[...] = total.astype(jnp.bfloat16)


def return_rows(me, length, *operands):
    rows, width = operands[6].shape
    smem, vmem = (pl.BlockSpec(memory_space=pltpu.SMEM), pl.BlockSpec(memory_space=pltpu.VMEM))
    return pl.pallas_call(
        return_kernel,
        in_specs=[smem, smem] + [vmem] * 9,
        out_specs=[vmem] * 4,
        out_shape=[
            jax.ShapeDtypeStruct((rows, width), jnp.float32),
            jax.ShapeDtypeStruct((rows, width), jnp.bfloat16),
            jax.ShapeDtypeStruct((1, width), jnp.float32),
            jax.ShapeDtypeStruct((8, width), jnp.float32),
        ],
        compiler_params=pltpu.CompilerParams(vmem_limit_bytes=32 * 2**20),
        name="return_rows",
    )(me, length, *operands)


def finish_kernel(
    me_ref, length_ref, near_ref, got_ref, out_near_ref, out_got_ref, order_ref, first_ref, grad_ref, tokens_ref, gains_ref,
    result_out, grad_out,
):
    rows = tokens_ref.shape[0]
    grad = near_ref[...] + got_ref[...].astype(jnp.float32)
    tokens = tokens_ref[...]
    scale = lax.rsqrt(jnp.mean(tokens * tokens, axis=-1, keepdims=True) + EPSILON)
    unit = tokens * scale
    pulled = grad * gains_ref[2:3]
    grad_out[...] = grad_ref[...] + scale * (pulled - unit * jnp.mean(pulled * unit, axis=-1, keepdims=True))
    high, low = split_low(out_near_ref[...] + out_got_ref[...].astype(jnp.float32))
    added = dot(order_ref[...], high) + dot(order_ref[...], low)
    result_out[...] = jnp.where(live_rows(me_ref, length_ref, rows), first_ref[...] + added, 0.0)


def finish_rows(me, length, *operands):
    shape = operands[5].shape
    smem, vmem = (pl.BlockSpec(memory_space=pltpu.SMEM), pl.BlockSpec(memory_space=pltpu.VMEM))
    return pl.pallas_call(
        finish_kernel,
        in_specs=[smem, smem] + [vmem] * 9,
        out_specs=[vmem] * 2,
        out_shape=[jax.ShapeDtypeStruct(shape, jnp.float32)] * 2,
        compiler_params=pltpu.CompilerParams(vmem_limit_bytes=32 * 2**20),
        name="finish_rows",
    )(me, length, *operands)


def body(
    tokens,
    routes,
    lengths,
    cotangent,
    in_weight,
    select_weight,
    step_weight,
    out_weight,
    router_weight,
    up_weight,
    down_weight,
    conv_weight,
    conv_bias,
    step_bias,
    decay_log,
    skip_gain,
    mixer_gain,
    expert_gain,
):
    f32, bf16 = (jnp.float32, jnp.bfloat16)
    span, width = tokens.shape
    groups, parts = (lax.axis_size("grp"), lax.axis_size("shard"))
    me, group = (lax.axis_index("shard"), lax.axis_index("grp"))
    total = span * parts
    inside = conv_bias.shape[0]
    tiles = inside // LANES
    slab = in_weight.shape[0]
    hidden_cols = up_weight.shape[2] // parts
    share = width // groups
    bits = [2**i for i in range(groups.bit_length() - 1)]
    down_bit = 2 if share % 8 == 0 else bits[-1]
    pair = 2 * share if share % 8 == 0 else width // 2
    odd, second = (group % 2, (group // down_bit) % 2)
    me_one = jnp.full((1,), me, jnp.int32)
    source = [me, me ^ 1, me ^ (2 + odd), me ^ (3 - odd), odd, second]
    source = jnp.stack(source).astype(jnp.int32)

    first = (routes[:, 0] == 0).astype(jnp.int32)
    count_first = jnp.sum(first)
    small = jnp.concatenate(
        [
            router_weight.astype(f32).T,
            mixer_gain.astype(f32)[None],
            expert_gain.astype(f32)[None],
            jnp.full((1, slab), count_first, jnp.int32).astype(f32),
            jnp.zeros((11, slab), f32),
        ],
        axis=0,
    )
    small = [small] + [swap(small, k) for k in range(1, parts)]
    in_pieces, up_pieces = cut_weights(source[:3], in_weight, up_weight, parts, inside)
    in_pieces = share_pieces(in_pieces)
    normed, gains = norm_rows(me_one, tokens, small)
    normed_pieces = gather_pieces(normed)
    counts = gains[4].reshape(parts, slab)[:, 0].astype(jnp.int32)

    goal = jnp.where(first > 0, jnp.cumsum(first), count_first + jnp.cumsum(1 - first)) - 1
    slots = jnp.arange(span, dtype=jnp.int32)
    order = (slots[:, None] == goal[None, :]).astype(bf16)
    order_t = (goal[:, None] == slots[None, :]).astype(bf16)
    live = (me * span + slots < lengths[0])[:, None]
    cots = matmul(order, jnp.where(live, cotangent, 0.0).astype(bf16)).astype(bf16)
    cot_pieces = gather_pieces(cots)

    taps = conv_weight.astype(f32)
    spare = LANES - select_weight.shape[1]
    select_wide = jnp.pad(select_weight, ((0, 0), (0, spare)))
    inner, zgate, summed, conv_out, conv_low, selected = project(
        me_one,
        source,
        lengths,
        normed_pieces,
        in_pieces,
        taps,
        conv_bias.astype(f32)[None, :],
        select_wide,
    )
    selected = tie(selected + swap(selected, 1), cot_pieces[2])
    selected = selected + swap(selected, 2)
    step_wide = jnp.pad(step_weight, ((0, LANES - R), (0, 0)))
    step_row = step_bias.astype(f32)[None, :]
    decay = -jnp.exp(decay_log.astype(f32))
    rate = pack(decay * LOG2E, tiles)
    skip = skip_gain.astype(f32)[None, :]
    states, end, mixed, gated, held, given = mixer(
        me_one, lengths, selected, conv_out, zgate, step_wide, step_row, skip, rate, out_weight, span, tiles
    )
    up_pieces = share_pieces(up_pieces)
    near, given = scatter_near(held, given, up_pieces[2])
    first_sum, normed_two, sent, probs = route(
        me_one, lengths, tokens, near, swap(given, 2), gains, order, routes
    )
    grad_held, grad_given, out_held, out_given, up_held, up_given, down_held, down_given = experts(
        me_one, source, counts, gather_pieces(sent), cot_pieces, up_pieces, down_weight, pair
    )
    near, given = scatter_near(grad_held, grad_given)
    up_got, down_got = (swap_groups(up_given, 1), swap_groups(down_given, down_bit))
    grad_first, grad_first_low, expert_gain_grad, router_grad = return_rows(
        me_one,
        lengths,
        near,
        swap(given, 2),
        order_t,
        normed_two,
        probs,
        routes,
        first_sum,
        cotangent,
        gains,
    )
    grad_pieces = gather_pieces(grad_first_low)
    out_near, out_given = scatter_near(out_held, out_given)
    out_got = swap(out_given, 2)
    fours, eights = (groups // 4, groups // 8)
    up_sum = join(up_held, up_got, grad_pieces[2]).reshape(E, 2, slab, fours, hidden_cols // fours)
    down_sum = join(down_held, down_got, grad_pieces[2])
    down_sum = down_sum.reshape(E, groups // 4, 2, share, hidden_cols)
    up_held, up_given = halve(up_sum, 1, 2)
    down_held, down_given = halve(down_sum, 2, 1)
    up_got, down_got = (swap_groups(up_given, 2), swap_groups(down_given, 1))

    (
        grad_zgate,
        conv_part,
        rank_part,
        entry_part,
        read_part,
        step_grad,
        step_bias_grad,
        skip_grad,
        rate_grad,
        out_grad,
    ) = mixer_back(
        me_one,
        lengths,
        grad_pieces,
        selected,
        conv_out,
        zgate,
        mixed,
        gated,
        states,
        end,
        step_wide,
        step_row,
        skip,
        rate,
        out_weight,
        tiles,
    )
    grad_selected = jnp.concatenate(
        [
            rank_part[:, :R],
            entry_part[:, 0].reshape(total, NS),
            read_part[:, 0].reshape(total, NS),
            jnp.zeros((total, spare), f32),
        ],
        axis=1,
    )
    grad_selected = tie(grad_selected + swap(grad_selected, 1), out_got)
    grad_selected = (grad_selected + swap(grad_selected, 2)).astype(bf16)
    up_sum = join(up_held, up_got, rank_part)
    down_sum = join(down_held, down_got, rank_part)
    up_held, up_given = halve(up_sum, 3, 4)
    down_bits = [bit for bit in bits[1:] if bit != down_bit]
    down_held, down_given = halve(down_sum, 1, down_bits[0])
    up_got, down_got = (swap_groups(up_given, 4), swap_groups(down_given, down_bits[0]))
    (
        held,
        given,
        inner_held,
        inner_given,
        gate_held,
        gate_given,
        select_grad,
        conv_grad,
        conv_bias_grad,
        mixer_part,
    ) = project_back(
        me_one,
        source,
        lengths,
        normed_pieces,
        in_pieces,
        grad_selected,
        conv_part,
        summed,
        inner,
        grad_zgate,
        conv_low,
        taps,
        select_wide,
    )
    near, given = scatter_near(held, given)
    result, tokens_grad = finish_rows(
        me_one,
        lengths,
        near,
        swap(given, 2),
        out_near,
        out_got,
        order_t,
        first_sum,
        grad_first,
        tokens,
        gains,
    )

    in_cols = inside // eights
    in_sum = jnp.stack(
        [join(inner_held, swap_groups(inner_given, 1)), join(gate_held, swap_groups(gate_given, 1))], axis=2
    )
    in_sum = in_sum.reshape(2, slab, 2, eights, in_cols)
    in_sum = sum_rest(in_sum, [(0, 2)] + [(3, bit) for bit in bits[2:-1]] + [(2, bits[-1])])
    in_sum = in_sum.reshape(slab, in_cols)
    up_sum = sum_rest(join(up_held, up_got, mixer_part), [(3, bit) for bit in bits[3:]])
    down_sum = sum_rest(join(down_held, down_got, mixer_part), [(1, bit) for bit in down_bits[1:]])
    down_sum = down_sum.reshape(E, share, hidden_cols)
    out_sum = sum_rest(out_grad.reshape(groups, share, inside), [(0, bit) for bit in bits])[0]
    up_moves, in_moves = ([], [])
    for g in range(groups):
        for s in range(parts):
            up_moves.append((g * parts + s, (s * fours + g // 4) * parts + g % 4))
            half, k = (g // (groups // 2), (g // 4) % eights)
            in_moves.append((g * parts + s, (half * (groups // 2) + s * eights + k) * parts + g % 4))
    both_axes = ("grp", "shard")
    up_cols = hidden_cols // fours
    up_sum = lax.ppermute(up_sum.reshape(E, slab, up_cols).astype(bf16), both_axes, up_moves)
    in_sum = lax.ppermute(in_sum.astype(bf16), both_axes, in_moves)

    decay_grad = decay * unpack(rate_grad, tiles)
    early = jnp.concatenate([step_grad[:R], decay_grad, step_bias_grad, skip_grad], axis=0)
    early = total_groups(early)
    shared = jnp.concatenate([router_grad[0:E], expert_gain_grad, mixer_part / gains[2:3]], axis=0)
    shared = shared + swap(shared, 1)
    shared = shared + swap(shared, 2)
    shared = lax.dynamic_slice_in_dim(shared, me * slab, slab, 1)
    picked = select_weight.shape[1]
    late = jnp.concatenate(
        [select_grad[:picked], conv_grad[:KW], conv_bias_grad, shared.reshape(2, inside)], axis=0
    )
    late = total_groups(late)
    shared = late[picked + KW + 1 :].reshape(4, slab)
    return (
        result,
        tokens_grad,
        in_sum.astype(f32),
        out_sum.T,
        up_sum.astype(f32),
        down_sum.transpose(0, 2, 1),
        late[:picked].T,
        early[:R],
        shared[0:2].T,
        late[picked : picked + KW],
        late[picked + KW],
        early[R + NS],
        early[R : R + NS],
        early[R + NS + 1],
        shared[3],
        shared[2],
    )


def solution(mesh):
    return jax.shard_map(
        body,
        mesh=mesh,
        in_specs=(
            P(("grp", "shard"), None),
            P(("grp", "shard"), None),
            P("grp"),
            P(("grp", "shard"), None),
            P("shard", None),
            P("shard", None),
            P(None, "shard"),
            P("shard", None),
            P("shard", None),
            P(None, "shard", None),
            P(None, "shard", None),
            P(None, "shard"),
            P("shard"),
            P("shard"),
            P(None, "shard"),
            P("shard"),
            P("shard"),
            P("shard"),
        ),
        out_specs=(
            P(("grp", "shard"), None),
            P(("grp", "shard"), None),
            P("shard", "grp"),
            P("shard", "grp"),
            P(None, "shard", "grp"),
            P(None, "shard", "grp"),
            P("shard", None),
            P(None, "shard"),
            P("shard", None),
            P(None, "shard"),
            P("shard"),
            P("shard"),
            P(None, "shard"),
            P("shard"),
            P("shard"),
            P("shard"),
        ),
        check_vma=False,
    )
```

time: 855 us -> 542 us (0.63); the launches traced: 838 us -> 534 us
  local copies, waits for them, and re-layouts: 268 us -> 65.5 us
  Pallas kernels: 60 us -> 170 us
  matrix products: 91.6 us -> 1.21 us
  blocking collectives: 82.3 us -> 0 us
  other arithmetic: 97 us -> 36.2 us
  starting transfers between devices: 23.3 us -> 47.6 us
  between operations: 17.1 us -> 7.49 us
    pallas_call x2 -> x10, Pallas kernels: 60 us -> 170 us  [the longest x1 57.3 us: mixer_back(): pl.pallas_call(functools.partial(mixer_back_kernel, tiles, share), grid=(...]
    ppermute x2 -> x25, waiting for transfers between devices: 0.01 us -> 110 us  [the longest x19 84.9 us: swap_groups(): return lax.ppermute(value, 'grp', [(g, g ^ bit) for g in range(size)])]
    psum x2 -> x0, blocking collectives: 82.3 us -> none  [the longest x1 47.3 us: body(): shared = lax.psum(shared, both_axes)]
    dynamic_update_slice x21 -> x0, local copies, waits for them, and re-layouts: 76.7 us -> none  [the longest x8 50.7 us: turn_blocks(): whole = lax.dynamic_update_slice_in_dim(whole, piece, (me ^ k) * rows, axis)]
    psum x1 -> x0, waiting for transfers between devices: 69.8 us -> none  [body(): lax.psum((select_grad, step_grad, conv_grad, conv_bias_grad, step_bias_gr...]
    dot_general x19 -> x0, matrix products: 69.7 us -> none  [the longest x6 26.5 us: matmul_t(): lax.dot_general(left, right, (((1,), (1,)), ((), ())), preferred_element_...]
    reduce_scatter x4 -> x0, waiting for transfers between devices: 28.8 us -> none  [the longest x1 28.8 us: body(): out_sum = lax.psum_scatter(out_grad, 'grp', scatter_dimension=0, tiled=True)]
    reduce_sum x10 -> x0, other arithmetic: 26.8 us -> none  [the longest x1 8.68 us: body(): step_bias_grad = jnp.sum(grad_step_pre, axis=0)]
  transfers between devices with their start and end apart: 35 -> 56, of which waited for: 13 -> 24; matrix products, arithmetic and copies ran while one was open for 36% -> 14% of each run, Pallas kernels for 5% -> 18%
where the time goes in v2:
time: 542 us; the launch traced here: 534 us
  waiting for transfers between devices  206 us (38%)
  Pallas kernels  170 us (31%)
  local copies, waits for them, and re-layouts  65.5 us (12%)
  starting transfers between devices  47.6 us (9%)
  other arithmetic  36.2 us (7%)
  between operations  7.49 us (1%)
    ppermute x31, waiting for transfers between devices, swap(): return lax.ppermute(value, 'shard', [(i, i ^ bit) for i in range(size)])  96.3 us
    ppermute x19, waiting for transfers between devices, swap_groups(): return lax.ppermute(value, 'grp', [(g, g ^ bit) for g in range(size)])  84.9 us
    pallas_call x1, Pallas kernels, mixer_back(): pl.pallas_call(functools.partial(mixer_back_kernel, tiles, share), grid=(...  57.3 us
    pallas_call x1, Pallas kernels, experts(): pl.pallas_call(functools.partial(expert_kernel, parts, CAP, steps, pair),...  37.7 us
    pallas_call x1, Pallas kernels, mixer(): pl.pallas_call(functools.partial(mixer_kernel, tiles, share), grid=(total...  32.3 us
    unnamed x152, local copies, waits for them, and re-layouts  27.2 us
    ppermute x19, starting transfers between devices, swap_groups(): return lax.ppermute(value, 'grp', [(g, g ^ bit) for g in range(size)])  22.1 us
    pallas_call x1, Pallas kernels, project_back(): pl.pallas_call(functools.partial(project_back_kernel, parts), grid=(parts...  21.1 us
  transfers between devices with their start and end apart: 56, of which 24 were waited for; matrix products, arithmetic and copies ran while one was open for 14% of the time, Pallas kernels for 18%

profile of v2, /device:TPU:2, one launch (start us, length us, event | category | flops | bytes accessed | tf_op | source)
XLA Modules:
  0.0 534.0 jit_solution(14084863610286738312)
XLA Ops:
  0.7 2.0 copy-done.8
  2.7 1.7 copy-done.9
  4.5 2.7 cut_weights.1
  13.8 13.4 %collective-permute-done.1.rest_2_ = f32[16,288]{1,0:T(8,128)S(1)} collective-permute-done((f32[16,288]{1,0:T(8,128)S(1)}, f32[16,288]{1,0:T(8,128)S(1)}, u32[]{:S(2)}, u32[]{:S(2)}) %collective-permute-start.1) | collective-permute-done | bytes 18464 | tf_op jit(solution)/shard_map/ppermute | solution.py:25
  28.7 1.6 collective-permute-start.4
  32.5 11.8 %collective-permute-done.4.rest_2_ = bf16[256,1152]{1,0:T(8,128)(2,1)} collective-permute-done((bf16[256,1152]{1,0:T(8,128)(2,1)}, bf16[256,1152]{1,0:T(8,128)(2,1)}, u32[]{:S(2)}, u32[]{:S(2)}) %collective-permute-start.4) | collective-permute-done | bytes 589856 | tf_op jit(solution)/shard_map/ppermute | solution.py:25
  46.8 1.6 collective-permute-start.10
  48.8 10.3 %project.1 = (f32[1024,576]{1,0:T(8,128)S(1)}, f32[1024,576]{1,0:T(8,128)S(1)}, f32[1024,576]{1,0:T(8,128)}, f32[1024,576]{1,0:T(8,128)}, bf16[1024,576]{1,0:T(8,128)(2,1)S(1)}, /*index=5*/f32[1024,128]{1,0:T(8,128)S(1)}) custom-call(s32[1]{0:T(128)} %bitcast.me_ref, s32[6]{0:T(128)S(1)} %stack.35.source_ref, s32[1]{0:T(128)} %copy.71.length_ref, ...), custom_call_target="tpu_custom_call" | custom-call | flops 2717908992 | bytes 20971520 | tf_op jit(solution)/shard_map/project/pallas_call | solution.py:359
  59.2 1.5 copy-done.11
  64.7 1.6 collective-permute-start.11
  66.6 11.8 %collective-permute-done.11 = f32[1024,128]{1,0:T(8,128)S(1)} collective-permute-done((f32[1024,128]{1,0:T(8,128)S(1)}, f32[1024,128]{1,0:T(8,128)S(1)}, u32[]{:S(2)}, u32[]{:S(2)}) %collective-permute-start.11) | collective-permute-done | bytes 524320 | tf_op jit(solution)/shard_map/ppermute | solution.py:25
  78.5 32.3 %mixer.1 = (f32[1024,9,8,128]{3,2,1,0:T(8,128)}, f32[9,8,128]{2,1,0:T(8,128)S(1)}, f32[1024,576]{1,0:T(8,128)S(1)}, bf16[1024,576]{1,0:T(8,128)(2,1)S(1)}, f32[2...) custom-call(s32[1]{0:T(128)} %bitcast.me_ref, s32[1]{0:T(128)} %copy.71.length_ref, ...), custom_call_target="tpu_custom_call" | custom-call | tf_op jit(solution)/shard_map/mixer/pallas_call | solution.py:460
  110.7 1.5 copy-done.10
  115.3 1.7 collective-permute-start.13
  117.0 19.9 %collective-permute-done.13.rest_10_ = bf16[2,288,768]{2,1,0:T(8,128)(2,1)} collective-permute-done((bf16[2,288,768]{2,1,0:T(8,128)(2,1)}, bf16[2,288,768]{2,1,0:T(8,128)(2,1)}, u32[]{:S(2)}, u32[]{:S(2)}) %collective-permute-start.13) | collective-permute-done | bytes 884768 | tf_op jit(solution)/shard_map/ppermute | solution.py:77
  138.7 2.2 add_add_fusion.2
  142.4 1.6 collective-permute-start.14
  145.6 12.6 %collective-permute-done.14.got_ref = bf16[256,1152]{1,0:T(8,128)(2,1)S(1)} collective-permute-done((bf16[256,1152]{1,0:T(8,128)(2,1)S(1)}, bf16[256,1152]{1,0:T(8,128)(2,1)S(1)}, u32[]{:S(2)}, u32[]{:S(2)}) %collective-permute-start.14) | collective-permute-done | bytes 589856 | tf_op jit(solution)/shard_map/ppermute | solution.py:25
  160.1 1.9 route.1
  162.7 1.6 collective-permute-start.16
  164.8 14.6 %collective-permute-done.16.rest_2_ = bf16[256,1280]{1,0:T(8,128)(2,1)} collective-permute-done((bf16[256,1280]{1,0:T(8,128)(2,1)}, bf16[256,1280]{1,0:T(8,128)(2,1)}, u32[]{:S(2)}, u32[]{:S(2)}) %collective-permute-start.16) | collective-permute-done | bytes 655392 | tf_op jit(solution)/shard_map/ppermute | solution.py:25
  182.7 4.0 collective-permute-done.21.rest_11_
  186.7 37.7 %experts.1 = (f32[2,256,1280]{2,1,0:T(8,128)}, bf16[2,256,1280]{2,1,0:T(8,128)(2,1)}, f32[2,256,1152]{2,1,0:T(8,128)}, bf16[2,256,1152]{2,1,0:T(8,128)(2,1)}, f3...) custom-call(s32[1]{0:T(128)} %bitcast.me_ref, ...), custom_call_target="tpu_custom_call" | custom-call | flops 16307453952 | bytes 25165824 | tf_op jit(solution)/shard_map/experts/pallas_call | solution.py:908
  225.2 1.6 collective-permute-start.45
  227.7 2.2 convert_add_fusion
  232.4 1.6 collective-permute-start.29
  234.1 13.6 %collective-permute-done.23.got_ref = bf16[256,1280]{1,0:T(8,128)(2,1)S(1)} collective-permute-done((bf16[256,1280]{1,0:T(8,128)(2,1)S(1)}, bf16[256,1280]{1,0:T(8,128)(2,1)S(1)}, u32[]{:S(2)}, u32[]{:S(2)}) %collective-permute-start.23) | collective-permute-done | bytes 655392 | tf_op jit(solution)/shard_map/ppermute | solution.py:25
  247.7 2.2 return_rows.1
  254.0 6.4 %collective-permute-done.29.out_got_ref = bf16[256,1152]{1,0:T(8,128)(2,1)} collective-permute-done((bf16[256,1152]{1,0:T(8,128)(2,1)}, bf16[256,1152]{1,0:T(8,128)(2,1)}, u32[]{:S(2)}, u32[]{:S(2)}) %collective-permute-start.29) | collective-permute-done | bytes 589856 | tf_op jit(solution)/shard_map/ppermute | solution.py:25
  263.1 9.1 %collective-permute-done.25.rest_2_ = bf16[256,1152]{1,0:T(8,128)(2,1)} collective-permute-done((bf16[256,1152]{1,0:T(8,128)(2,1)}, bf16[256,1152]{1,0:T(8,128)(2,1)}, u32[]{:S(2)}, u32[]{:S(2)}) %collective-permute-start.25) | collective-permute-done | bytes 589856 | tf_op jit(solution)/shard_map/ppermute | solution.py:25
  274.1 3.1 add_add_fusion
  277.2 1.7 copy-done.38
  280.4 3.6 add_add_fusion.1
  284.0 5.4 %reshape_reshape.11 = f32[2,1,2,288,2,384]{5,4,3,2,0,1:T(2,128)} reshape(f32[2,2,288,768]{3,2,1,0:T(8,128)} %add_add_fusion.1) | data formatting | bytes 7077888 | tf_op jit(solution)/shard_map/reshape;reshape | solution.py:55
  289.4 2.2 constant_dynamic-slice_fusion.3
  292.7 1.4 collective-permute-start.42
  294.1 1.9 constant_dynamic-slice_fusion.4
  295.9 57.3 %mixer_back.1 = (bf16[1024,576]{1,0:T(8,128)(2,1)}, f32[1024,576]{1,0:T(8,128)}, f32[1024,128]{1,0:T(8,128)S(1)}, f32[16,8,1024]{2,1,0:T(8,128)S(1)}, f32[16,8,1...) custom-call(s32[1]{0:T(128)} %bitcast.me_ref, ...), custom_call_target="tpu_custom_call" | custom-call | tf_op jit(solution)/shard_map/mixer_back/pallas_call | solution.py:573
  354.9 1.7 collective-permute-start.53
  359.0 1.7 maximum_maximum_fusion
  364.2 3.6 collective-permute-done.54
  367.7 2.7 collective-permute-start.55
  370.4 1.5 fusion
  375.4 2.6 collective-permute-start.43
  378.6 16.7 %collective-permute-done.55 = bf16[90,576]{1,0:T(8,128)(2,1)S(1)} collective-permute-done((bf16[90,576]{1,0:T(8,128)(2,1)S(1)}, bf16[90,576]{1,0:T(8,128)(2,1)S(1)}, u32[]{:S(2)}, u32[]{:S(2)}) %collective-permute-start.55) | collective-permute-done | bytes 103712 | tf_op jit(solution)/shard_map/ppermute | solution.py:30
  399.1 21.1 %project_back.1 = (f32[2,256,1152]{2,1,0:T(8,128)}, bf16[2,256,1152]{2,1,0:T(8,128)(2,1)}, f32[2,288,576]{2,1,0:T(8,128)}, bf16[2,288,576]{2,1,0:T(8,128)(2,1)},...) custom-call(s32[1]{0:T(128)} %bitcast.me_ref, ...), custom_call_target="tpu_custom_call" | custom-call | tf_op jit(solution)/shard_map/project_back/pallas_call | solution.py:691
  423.7 3.1 collective-permute-start.40
  430.8 2.3 fusion.16
  433.1 2.8 collective-permute-start.44
  435.9 4.2 collective-permute-start.34
  440.6 2.0 add_bitcast_fusion.2
  442.6 14.5 %collective-permute-done.51 = bf16[111,576]{1,0:T(8,128)(2,1)S(1)} collective-permute-done((bf16[111,576]{1,0:T(8,128)(2,1)S(1)}, bf16[111,576]{1,0:T(8,128)(2,1)S(1)}, u32[]{:S(2)}, u32[]{:S(2)}) %collective-permute-start.51) | collective-permute-done | bytes 127904 | tf_op jit(solution)/shard_map/ppermute | solution.py:30
  457.2 10.0 %collective-permute-done.34 = bf16[2,288,576]{2,1,0:T(8,128)(2,1)S(1)} collective-permute-done((bf16[2,288,576]{2,1,0:T(8,128)(2,1)}, bf16[2,288,576]{2,1,0:T(8,128)(2,1)S(1)}, u32[]{:S(2)}, u32[]{:S(2)}) %collective-permute-start.34) | collective-permute-done | bytes 663584 | tf_op jit(solution)/shard_map/ppermute | solution.py:30
  467.3 12.2 %collective-permute-done.33 = bf16[2,288,576]{2,1,0:T(8,128)(2,1)S(1)} collective-permute-done((bf16[2,288,576]{2,1,0:T(8,128)(2,1)}, bf16[2,288,576]{2,1,0:T(8,128)(2,1)S(1)}, u32[]{:S(2)}, u32[]{:S(2)}) %collective-permute-start.33) | collective-permute-done | bytes 663584 | tf_op jit(solution)/shard_map/ppermute | solution.py:30
  484.4 14.7 %collective-permute-done.35 = bf16[1,288,2,1,576]{4,1,2,3,0:T(8,128)(2,1)} collective-permute-done((bf16[1,288,2,1,576]{4,1,2,3,0:T(8,128)(2,1)}, bf16[1,288,2,1,576]{4,1,2,3,0:T(8,128)(2,1)}, u32[]{:S(2)}, u32[]{:S(2)}) %collective-permute-start.35) | collective-permute-done | bytes 663584 | tf_op jit(solution)/shard_map/ppermute | solution.py:30
  499.1 1.7 fusion.6
  500.9 1.6 convert_add_fusion.1
  502.5 1.4 copy-done.43
  504.7 1.6 collective-permute-start.32
  506.4 12.2 %collective-permute-done.36 = bf16[1,288,1,1,576]{4,1,2,3,0:T(8,128)(2,1)S(1)} collective-permute-done((bf16[1,288,1,1,576]{4,1,2,3,0:T(8,128)(2,1)S(1)}, bf16[1,288,1,1,576]{4,1,2,3,0:T(8,128)(2,1)S(1)}, u32[]{:S(2)}, u32[]{:S(2)}) %collective-permute-start.36) | collective-permute-done | bytes 331808 | tf_op jit(solution)/shard_map/ppermute | solution.py:30
  519.4 1.9 collective-permute-start.37
  523.9 2.1 convert_element_type.345
  527.5 3.4 finish_rows.1
  531.7 1.9 convert_element_type.327
  (339 shorter events, 76.6 us)
Async XLA Ops:
  9.0 39.8 %copy-start.17 = (bf16[288,1152]{1,0:T(8,128)(2,1)}, bf16[288,1152]{1,0:T(8,128)(2,1)S(1)}, u32[]{:S(2)}) copy-start(bf16[288,1152]{1,0:T(8,128)(2,1)S(1)} %get-tuple-element.75.rest_4_) | copy-start | bytes 1990660
  9.0 39.4 %copy-start.57 = (bf16[576,104]{0,1:T(8,128)(2,1)S(1)}, bf16[576,104]{0,1:T(8,128)(2,1)}, u32[]{:S(2)}) copy-start(bf16[576,104]{0,1:T(8,128)(2,1)} %param.23) | copy-start | bytes 359428
  9.0 39.5 %copy-start.63 = (bf16[4,576]{1,0:T(4,128)(2,1)S(1)}, bf16[4,576]{1,0:T(4,128)(2,1)}, u32[]{:S(2)}) copy-start(bf16[4,576]{1,0:T(4,128)(2,1)} %param.29) | copy-start | bytes 13828
  9.0 39.5 %copy-start.67 = (bf16[576]{0:T(1024)(128)(2,1)S(1)}, bf16[576]{0:T(1024)(128)(2,1)}, u32[]{:S(2)}) copy-start(bf16[576]{0:T(1024)(128)(2,1)} %param.30) | copy-start | bytes 3460
  9.0 22.0 %collective-permute-start.7 = (bf16[288,1152]{1,0:T(8,128)(2,1)}, bf16[288,1152]{1,0:T(8,128)(2,1)}, u32[]{:S(2)}, u32[]{:S(2)}) collective-permute-start(bf16[288,1152]{1,0:T(8,128)(2,1)} %get-tuple-element.77), channel_id=1, source_target_pairs={{0,2},{1,3},{2,0},{3,1},{4,7},{5,6},{6,5},{7,4},{8,10},{9,11},{10,... | collective-permute-start | bytes 1990664 | tf_op jit(solution)/shard_map/ppermute | solution.py:77
  11.6 2.2 collective-permute-start
  12.3 14.8 %collective-permute-start.1 = (f32[16,288]{1,0:T(8,128)S(1)}, f32[16,288]{1,0:T(8,128)S(1)}, u32[]{:S(2)}, u32[]{:S(2)}) collective-permute-start(f32[16,288]{1,0:T(8,128)S(1)} %concatenate.30.rest_0_), channel_id=1, source_target_pairs={{0,2},{1,3},{2,0},{3,1},{4,6},{5,7},{6,4},{7,5},{8,10},{9,11},{10,... | collective-permute-start | bytes 55304 | tf_op jit(solution)/shard_map/ppermute | solution.py:25
  12.8 14.7 %collective-permute-start.2 = (f32[16,288]{1,0:T(8,128)S(1)}, f32[16,288]{1,0:T(8,128)S(1)}, u32[]{:S(2)}, u32[]{:S(2)}) collective-permute-start(f32[16,288]{1,0:T(8,128)S(1)} %concatenate.30.rest_0_), channel_id=1, source_target_pairs={{0,3},{1,2},{2,1},{3,0},{4,7},{5,6},{6,5},{7,4},{8,11},{9,10},{10,... | collective-permute-start | bytes 55304 | tf_op jit(solution)/shard_map/ppermute | solution.py:25
  28.7 15.7 %collective-permute-start.4 = (bf16[256,1152]{1,0:T(8,128)(2,1)}, bf16[256,1152]{1,0:T(8,128)(2,1)}, u32[]{:S(2)}, u32[]{:S(2)}) collective-permute-start(bf16[256,1152]{1,0:T(8,128)(2,1)} %get-tuple-element.74.rest_0_), channel_id=1, source_target_pairs={{0,2},{1,3},{2,0},{3,1},{4,6},{5,7},{6,4},{7,5},{8,10},{9,11},{10,... | collective-permute-start | bytes 1769480 | tf_op jit(solution)/shard_map/ppermute | solution.py:25
  30.2 18.5 %collective-permute-start.6 = (bf16[288,1152]{1,0:T(8,128)(2,1)}, bf16[288,1152]{1,0:T(8,128)(2,1)}, u32[]{:S(2)}, u32[]{:S(2)}) collective-permute-start(bf16[288,1152]{1,0:T(8,128)(2,1)} %copy-done.35), channel_id=1, source_target_pairs={{0,1},{1,0},{2,3},{3,2},{4,5},{5,4},{6,7},{7,6},{8,9},{9,8},{10,11... | collective-permute-start | bytes 1990664 | tf_op jit(solution)/shard_map/ppermute | solution.py:25
  31.1 17.7 %collective-permute-start.8 = (bf16[288,1152]{1,0:T(8,128)(2,1)}, bf16[288,1152]{1,0:T(8,128)(2,1)}, u32[]{:S(2)}, u32[]{:S(2)}) collective-permute-start(bf16[288,1152]{1,0:T(8,128)(2,1)} %collective-permute-done.7.rest_6_), channel_id=1, source_target_pairs={{0,4},{4,0},{8,12},{12,8},{16,20},{20,16},{24,28},{28,24},{1,5},{5... | collective-permute-start | bytes 1990664 | tf_op jit(solution)/shard_map/ppermute | solution.py:78
  32.0 16.8 %collective-permute-start.3 = (bf16[256,1152]{1,0:T(8,128)(2,1)}, bf16[256,1152]{1,0:T(8,128)(2,1)}, u32[]{:S(2)}, u32[]{:S(2)}) collective-permute-start(bf16[256,1152]{1,0:T(8,128)(2,1)} %get-tuple-element.74.rest_0_), channel_id=1, source_target_pairs={{0,1},{1,0},{2,3},{3,2},{4,5},{5,4},{6,7},{7,6},{8,9},{9,8},{10,11... | collective-permute-start | bytes 1769480 | tf_op jit(solution)/shard_map/ppermute | solution.py:25
  44.3 4.5 collective-permute-start.5
  46.8 16.1 %collective-permute-start.10 = (bf16[256,1152]{1,0:T(8,128)(2,1)}, bf16[256,1152]{1,0:T(8,128)(2,1)}, u32[]{:S(2)}, u32[]{:S(2)}) collective-permute-start(bf16[256,1152]{1,0:T(8,128)(2,1)} %convolution_convert_fusion.rest_4_), channel_id=1, source_target_pairs={{0,2},{1,3},{2,0},{3,1},{4,6},{5,7},{6,4},{7,5},{8,10},{9,11},{10,... | collective-permute-start | bytes 1769480 | tf_op jit(solution)/shard_map/ppermute | solution.py:25
  61.9 2.8 collective-permute-start.9
  64.7 13.6 %collective-permute-start.11 = (f32[1024,128]{1,0:T(8,128)S(1)}, f32[1024,128]{1,0:T(8,128)S(1)}, u32[]{:S(2)}, u32[]{:S(2)}) collective-permute-start(f32[1024,128]{1,0:T(8,128)S(1)} %add_add_fusion.4), channel_id=1, source_target_pairs={{0,2},{1,3},{2,0},{3,1},{4,6},{5,7},{6,4},{7,5},{8,10},{9,11},{10,... | collective-permute-start | bytes 1572872 | tf_op jit(solution)/shard_map/ppermute | solution.py:25
  66.5 44.3 %copy-start.28 = (f32[1,576]{1,0:T(1,128)}, f32[1,576]{1,0:T(1,128)S(1)}, u32[]{:S(2)}) copy-start(f32[1,576]{1,0:T(1,128)S(1)} %reshape.286.skip_ref.rest_13_) | copy-start | bytes 6916
  115.3 23.5 %collective-permute-start.12 = (bf16[2,256,1152]{2,1,0:T(8,128)(2,1)S(1)}, bf16[2,256,1152]{2,1,0:T(8,128)(2,1)}, u32[]{:S(2)}, u32[]{:S(2)}) collective-permute-start(bf16[2,256,1152]{2,1,0:T(8,128)(2,1)S(1)} %get-tuple-element.83), channel_id=1, source_target_pairs={{0,1},{1,0},{2,3},{3,2},{4,5},{5,4},{6,7},{7,6},{8,9},{9,8},{10,11... | collective-permute-start | bytes 3538952 | tf_op jit(solution)/shard_map/ppermute | solution.py:25
  115.3 21.6 %collective-permute-start.13 = (bf16[2,288,768]{2,1,0:T(8,128)(2,1)}, bf16[2,288,768]{2,1,0:T(8,128)(2,1)}, u32[]{:S(2)}, u32[]{:S(2)}) collective-permute-start(bf16[2,288,768]{2,1,0:T(8,128)(2,1)} %get-tuple-element.84), channel_id=1, source_target_pairs={{0,2},{1,3},{2,0},{3,1},{4,7},{5,6},{6,5},{7,4},{8,10},{9,11},{10,... | collective-permute-start | bytes 2654216 | tf_op jit(solution)/shard_map/ppermute | solution.py:77
  142.4 15.8 %collective-permute-start.14 = (bf16[256,1152]{1,0:T(8,128)(2,1)S(1)}, bf16[256,1152]{1,0:T(8,128)(2,1)S(1)}, u32[]{:S(2)}, u32[]{:S(2)}) collective-permute-start(bf16[256,1152]{1,0:T(8,128)(2,1)S(1)} %fusion.11), channel_id=1, source_target_pairs={{0,2},{1,3},{2,0},{3,1},{4,6},{5,7},{6,4},{7,5},{8,10},{9,11},{10,... | collective-permute-start | bytes 1769480 | tf_op jit(solution)/shard_map/ppermute | solution.py:25
  162.7 84.9 %copy-start.6 = (f32[256,1152]{1,0:T(8,128)}, f32[256,1152]{1,0:T(8,128)S(1)}, u32[]{:S(2)}) copy-start(f32[256,1152]{1,0:T(8,128)S(1)} %get-tuple-element.92.first_ref) | copy-start | bytes 3538948
  162.7 16.6 %collective-permute-start.16 = (bf16[256,1280]{1,0:T(8,128)(2,1)}, bf16[256,1280]{1,0:T(8,128)(2,1)}, u32[]{:S(2)}, u32[]{:S(2)}) collective-permute-start(bf16[256,1280]{1,0:T(8,128)(2,1)} %get-tuple-element.85.rest_0_), channel_id=1, source_target_pairs={{0,2},{1,3},{2,0},{3,1},{4,6},{5,7},{6,4},{7,5},{8,10},{9,11},{10,... | collective-permute-start | bytes 1966088 | tf_op jit(solution)/shard_map/ppermute | solution.py:25
  164.3 15.1 %collective-permute-start.18 = (bf16[256,1152]{1,0:T(8,128)(2,1)}, bf16[256,1152]{1,0:T(8,128)(2,1)S(1)}, u32[]{:S(2)}, u32[]{:S(2)}) collective-permute-start(bf16[256,1152]{1,0:T(8,128)(2,1)} %convolution_convert_fusion.rest_4_), channel_id=1, source_target_pairs={{0,1},{1,0},{2,3},{3,2},{4,5},{5,4},{6,7},{7,6},{8,9},{9,8},{10,11... | collective-permute-start | bytes 1769480 | tf_op jit(solution)/shard_map/ppermute | solution.py:25
  164.3 17.1 %collective-permute-start.20 = (bf16[2,288,768]{2,1,0:T(8,128)(2,1)}, bf16[2,288,768]{2,1,0:T(8,128)(2,1)}, u32[]{:S(2)}, u32[]{:S(2)}) collective-permute-start(bf16[2,288,768]{2,1,0:T(8,128)(2,1)} %get-tuple-element.87), channel_id=1, source_target_pairs={{0,1},{1,0},{2,3},{3,2},{4,5},{5,4},{6,7},{7,6},{8,9},{9,8},{10,11... | collective-permute-start | bytes 2654216 | tf_op jit(solution)/shard_map/ppermute | solution.py:25
  164.8 21.9 %collective-permute-start.21 = (bf16[2,288,768]{2,1,0:T(8,128)(2,1)}, bf16[2,288,768]{2,1,0:T(8,128)(2,1)}, u32[]{:S(2)}, u32[]{:S(2)}) collective-permute-start(bf16[2,288,768]{2,1,0:T(8,128)(2,1)} %collective-permute-done.13.rest_10_), channel_id=1, source_target_pairs={{0,4},{4,0},{8,12},{12,8},{16,20},{20,16},{24,28},{28,24},{1,5},{5... | collective-permute-start | bytes 2654216 | tf_op jit(solution)/shard_map/ppermute | solution.py:78
  164.8 21.9 %collective-permute-start.15 = (bf16[256,1280]{1,0:T(8,128)(2,1)}, bf16[256,1280]{1,0:T(8,128)(2,1)}, u32[]{:S(2)}, u32[]{:S(2)}) collective-permute-start(bf16[256,1280]{1,0:T(8,128)(2,1)} %get-tuple-element.85.rest_0_), channel_id=1, source_target_pairs={{0,1},{1,0},{2,3},{3,2},{4,5},{5,4},{6,7},{7,6},{8,9},{9,8},{10,11... | collective-permute-start | bytes 1966088 | tf_op jit(solution)/shard_map/ppermute | solution.py:25
  179.4 7.3 %collective-permute-start.17 = (bf16[256,1280]{1,0:T(8,128)(2,1)}, bf16[256,1280]{1,0:T(8,128)(2,1)}, u32[]{:S(2)}, u32[]{:S(2)}) collective-permute-start(bf16[256,1280]{1,0:T(8,128)(2,1)} %collective-permute-done.16.rest_2_), channel_id=1, source_target_pairs={{0,1},{1,0},{2,3},{3,2},{4,5},{5,4},{6,7},{7,6},{8,9},{9,8},{10,11... | collective-permute-start | bytes 1966088 | tf_op jit(solution)/shard_map/ppermute | solution.py:25
  180.2 2.5 collective-permute-start.19
  186.7 37.8 %copy-start.64 = (s32[2,128]{1,0:T(2,128)S(1)}, s32[2,128]{1,0:T(2,128)}, u32[]{:S(2)}) copy-start(s32[2,128]{1,0:T(2,128)} %get-tuple-element.139) | copy-start | bytes 3076
  224.4 3.3 collective-permute-start.22
  224.5 6.0 %collective-permute-start.28 = (bf16[2,256,1152]{2,1,0:T(8,128)(2,1)}, bf16[2,256,1152]{2,1,0:T(8,128)(2,1)S(1)}, u32[]{:S(2)}, u32[]{:S(2)}) collective-permute-start(bf16[2,256,1152]{2,1,0:T(8,128)(2,1)} %get-tuple-element.102), channel_id=1, source_target_pairs={{0,1},{1,0},{2,3},{3,2},{4,5},{5,4},{6,7},{7,6},{8,9},{9,8},{10,11... | collective-permute-start | bytes 3538952 | tf_op jit(solution)/shard_map/ppermute | solution.py:25
  225.2 48.9 %collective-permute-start.45 = (bf16[2,2,288,768]{3,2,1,0:T(8,128)(2,1)}, bf16[2,2,288,768]{3,2,1,0:T(8,128)(2,1)}, u32[]{:S(2)}, u32[]{:S(2)}) collective-permute-start(bf16[2,2,288,768]{3,2,1,0:T(8,128)(2,1)} %get-tuple-element.122), channel_id=1, source_target_pairs={{0,8},{4,12},{8,0},{12,4},{16,24},{20,28},{24,16},{28,20},{1,9},{5... | collective-permute-start | bytes 5308424 | tf_op jit(solution)/shard_map/ppermute | solution.py:30
  226.8 53.6 %collective-permute-start.41 = (bf16[2,2,288,768]{3,2,1,0:T(8,128)(2,1)}, bf16[2,2,288,768]{3,2,1,0:T(8,128)(2,1)}, u32[]{:S(2)}, u32[]{:S(2)}) collective-permute-start(bf16[2,2,288,768]{3,2,1,0:T(8,128)(2,1)} %get-tuple-element.119), channel_id=1, source_target_pairs={{0,4},{4,0},{8,12},{12,8},{16,20},{20,16},{24,28},{28,24},{1,5},{5... | collective-permute-start | bytes 5308424 | tf_op jit(solution)/shard_map/ppermute | solution.py:30
  230.0 17.6 %collective-permute-start.23 = (bf16[256,1280]{1,0:T(8,128)(2,1)S(1)}, bf16[256,1280]{1,0:T(8,128)(2,1)S(1)}, u32[]{:S(2)}, u32[]{:S(2)}) collective-permute-start(bf16[256,1280]{1,0:T(8,128)(2,1)S(1)} %fusion.10), channel_id=1, source_target_pairs={{0,2},{1,3},{2,0},{3,1},{4,6},{5,7},{6,4},{7,5},{8,10},{9,11},{10,... | collective-permute-start | bytes 1966088 | tf_op jit(solution)/shard_map/ppermute | solution.py:25
  232.4 28.0 %collective-permute-start.29 = (bf16[256,1152]{1,0:T(8,128)(2,1)}, bf16[256,1152]{1,0:T(8,128)(2,1)}, u32[]{:S(2)}, u32[]{:S(2)}) collective-permute-start(bf16[256,1152]{1,0:T(8,128)(2,1)} %fusion.12), channel_id=1, source_target_pairs={{0,2},{1,3},{2,0},{3,1},{4,6},{5,7},{6,4},{7,5},{8,10},{9,11},{10,... | collective-permute-start | bytes 1769480 | tf_op jit(solution)/shard_map/ppermute | solution.py:25
  252.1 20.1 %collective-permute-start.25 = (bf16[256,1152]{1,0:T(8,128)(2,1)}, bf16[256,1152]{1,0:T(8,128)(2,1)}, u32[]{:S(2)}, u32[]{:S(2)}) collective-permute-start(bf16[256,1152]{1,0:T(8,128)(2,1)} %get-tuple-element.93.rest_0_), channel_id=1, source_target_pairs={{0,2},{1,3},{2,0},{3,1},{4,6},{5,7},{6,4},{7,5},{8,10},{9,11},{10,... | collective-permute-start | bytes 1769480 | tf_op jit(solution)/shard_map/ppermute | solution.py:25
  262.2 33.7 %collective-permute-start.24 = (bf16[256,1152]{1,0:T(8,128)(2,1)}, bf16[256,1152]{1,0:T(8,128)(2,1)}, u32[]{:S(2)}, u32[]{:S(2)}) collective-permute-start(bf16[256,1152]{1,0:T(8,128)(2,1)} %get-tuple-element.93.rest_0_), channel_id=1, source_target_pairs={{0,1},{1,0},{2,3},{3,2},{4,5},{5,4},{6,7},{7,6},{8,9},{9,8},{10,11... | collective-permute-start | bytes 1769480 | tf_op jit(solution)/shard_map/ppermute | solution.py:25
  279.9 90.5 %collective-permute-start.46 = (bf16[2,2,1,144,768]{4,3,0,2,1:T(8,128)(2,1)}, bf16[2,2,1,144,768]{4,3,0,2,1:T(8,128)(2,1)}, u32[]{:S(2)}, u32[]{:S(2)}) collective-permute-start(bf16[2,2,1,144,768]{4,3,0,2,1:T(8,128)(2,1)} %fusion.8), channel_id=1, source_target_pairs={{0,4},{4,0},{8,12},{12,8},{16,20},{20,16},{24,28},{28,24},{1,5},{5... | collective-permute-start | bytes 2654216 | tf_op jit(solution)/shard_map/ppermute | solution.py:30
  280.4 15.5 %collective-permute-start.26 = (bf16[256,1152]{1,0:T(8,128)(2,1)}, bf16[256,1152]{1,0:T(8,128)(2,1)}, u32[]{:S(2)}, u32[]{:S(2)}) collective-permute-start(bf16[256,1152]{1,0:T(8,128)(2,1)} %collective-permute-done.25.rest_2_), channel_id=1, source_target_pairs={{0,1},{1,0},{2,3},{3,2},{4,5},{5,4},{6,7},{7,6},{8,9},{9,8},{10,11... | collective-permute-start | bytes 1769480 | tf_op jit(solution)/shard_map/ppermute | solution.py:25
  292.7 80.5 %collective-permute-start.42 = (bf16[2,1,288,2,384]{4,2,0,3,1:T(8,128)(2,1)}, bf16[2,1,288,2,384]{4,2,0,3,1:T(8,128)(2,1)}, u32[]{:S(2)}, u32[]{:S(2)}) collective-permute-start(bf16[2,1,288,2,384]{4,2,0,3,1:T(8,128)(2,1)} %bitcast.109), channel_id=1, source_target_pairs={{0,8},{4,12},{8,0},{12,4},{16,24},{20,28},{24,16},{28,20},{1,9},{5... | collective-permute-start | bytes 2654216 | tf_op jit(solution)/shard_map/ppermute | solution.py:30
  295.9 58.3 %copy-start.60 = (bf16[16,576]{1,0:T(8,128)(2,1)S(1)}, bf16[16,576]{1,0:T(8,128)(2,1)}, u32[]{:S(2)}) copy-start(bf16[16,576]{1,0:T(8,128)(2,1)} %param.32) | copy-start | bytes 55300
  354.9 6.9 %collective-permute-start.53 = (bf16[90,576]{1,0:T(8,128)(2,1)}, bf16[90,576]{1,0:T(8,128)(2,1)S(1)}, u32[]{:S(2)}, u32[]{:S(2)}) collective-permute-start(bf16[90,576]{1,0:T(8,128)(2,1)} %pad_maximum_fusion.1), channel_id=1, source_target_pairs={{0,4},{4,0},{8,12},{12,8},{16,20},{20,16},{24,28},{28,24},{1,5},{5... | collective-permute-start | bytes 311048 | tf_op jit(solution)/shard_map/ppermute | solution.py:30
  361.2 16.8 %collective-permute-start.27 = (f32[1024,128]{1,0:T(8,128)S(1)}, f32[1024,128]{1,0:T(8,128)S(1)}, u32[]{:S(2)}, u32[]{:S(2)}) collective-permute-start(f32[1024,128]{1,0:T(8,128)S(1)} %maximum_maximum_fusion), channel_id=1, source_target_pairs={{0,1},{1,0},{2,3},{3,2},{4,5},{5,4},{6,7},{7,6},{8,9},{9,8},{10,11... | collective-permute-start | bytes 1572872 | tf_op jit(solution)/shard_map/ppermute | solution.py:25
  361.9 5.8 %collective-permute-start.54 = (bf16[90,576]{1,0:T(8,128)(2,1)S(1)}, bf16[90,576]{1,0:T(8,128)(2,1)S(1)}, u32[]{:S(2)}, u32[]{:S(2)}) collective-permute-start(bf16[90,576]{1,0:T(8,128)(2,1)S(1)} %add_convert_fusion.6), channel_id=1, source_target_pairs={{0,8},{4,12},{8,0},{12,4},{16,24},{20,28},{24,16},{28,20},{1,9},{5... | collective-permute-start | bytes 311048 | tf_op jit(solution)/shard_map/ppermute | solution.py:30
  363.6 33.6 %collective-permute-start.38 = (bf16[4,144,576]{2,1,0:T(8,128)(2,1)S(1)}, bf16[4,144,576]{2,1,0:T(8,128)(2,1)S(1)}, u32[]{:S(2)}, u32[]{:S(2)}) collective-permute-start(bf16[4,144,576]{2,1,0:T(8,128)(2,1)S(1)} %dynamic-slice_bitcast_fusion.4), channel_id=1, source_target_pairs={{0,4},{4,0},{8,12},{12,8},{16,20},{20,16},{24,28},{28,24},{1,5},{5... | collective-permute-start | bytes 1990664 | tf_op jit(solution)/shard_map/ppermute | solution.py:30
  367.7 27.5 %collective-permute-start.55 = (bf16[90,576]{1,0:T(8,128)(2,1)S(1)}, bf16[90,576]{1,0:T(8,128)(2,1)S(1)}, u32[]{:S(2)}, u32[]{:S(2)}) collective-permute-start(bf16[90,576]{1,0:T(8,128)(2,1)S(1)} %add_convert_fusion.5), channel_id=1, source_target_pairs={{0,16},{4,20},{8,24},{12,28},{16,0},{20,4},{24,8},{28,12},{1,17},{... | collective-permute-start | bytes 311048 | tf_op jit(solution)/shard_map/ppermute | solution.py:30
  372.9 67.3 %collective-permute-start.47 = (bf16[2,1,1,144,768]{4,3,0,2,1:T(8,128)(2,1)}, bf16[2,1,1,144,768]{4,3,0,2,1:T(8,128)(2,1)}, u32[]{:S(2)}, u32[]{:S(2)}) collective-permute-start(bf16[2,1,1,144,768]{4,3,0,2,1:T(8,128)(2,1)} %dynamic-slice_convert_fusion.4), channel_id=1, source_target_pairs={{0,16},{4,20},{8,24},{12,28},{16,0},{20,4},{24,8},{28,12},{1,17},{... | collective-permute-start | bytes 1327112 | tf_op jit(solution)/shard_map/ppermute | solution.py:30
  375.4 55.4 %collective-permute-start.43 = (bf16[2,1,288,1,384]{4,2,0,3,1:T(8,128)(2,1)}, bf16[2,1,288,1,384]{4,2,0,3,1:T(8,128)(2,1)}, u32[]{:S(2)}, u32[]{:S(2)}) collective-permute-start(bf16[2,1,288,1,384]{4,2,0,3,1:T(8,128)(2,1)} %dynamic-slice_convert_fusion.5), channel_id=1, source_target_pairs={{0,16},{4,20},{8,24},{12,28},{16,0},{20,4},{24,8},{28,12},{1,17},{... | collective-permute-start | bytes 1327112 | tf_op jit(solution)/shard_map/ppermute | solution.py:30
  378.1 20.2 %collective-permute-start.30 = (f32[1024,128]{1,0:T(8,128)S(1)}, f32[1024,128]{1,0:T(8,128)S(1)}, u32[]{:S(2)}, u32[]{:S(2)}) collective-permute-start(f32[1024,128]{1,0:T(8,128)S(1)} %add_add_fusion.3), channel_id=1, source_target_pairs={{0,2},{1,3},{2,0},{3,1},{4,6},{5,7},{6,4},{7,5},{8,10},{9,11},{10,... | collective-permute-start | bytes 1572872 | tf_op jit(solution)/shard_map/ppermute | solution.py:25
  397.4 24.6 %collective-permute-start.39 = (bf16[2,144,576]{2,1,0:T(8,128)(2,1)S(1)}, bf16[2,144,576]{2,1,0:T(8,128)(2,1)S(1)}, u32[]{:S(2)}, u32[]{:S(2)}) collective-permute-start(bf16[2,144,576]{2,1,0:T(8,128)(2,1)S(1)} %fusion.18), channel_id=1, source_target_pairs={{0,8},{4,12},{8,0},{12,4},{16,24},{20,28},{24,16},{28,20},{1,9},{5... | collective-permute-start | bytes 995336 | tf_op jit(solution)/shard_map/ppermute | solution.py:30
  421.0 1.3 collective-permute-start.48
  422.2 8.1 %collective-permute-start.49 = (f32[4,1152]{1,0:T(4,128)S(1)}, f32[4,1152]{1,0:T(4,128)S(1)}, u32[]{:S(2)}, u32[]{:S(2)}) collective-permute-start(f32[4,1152]{1,0:T(4,128)S(1)} %fusion.30), channel_id=1, source_target_pairs={{0,2},{1,3},{2,0},{3,1},{4,6},{5,7},{6,4},{7,5},{8,10},{9,11},{10,... | collective-permute-start | bytes 55304 | tf_op jit(solution)/shard_map/ppermute | solution.py:25
  423.7 58.4 %collective-permute-start.40 = (bf16[1,144,576]{2,1,0:T(8,128)(2,1)}, bf16[1,144,576]{2,1,0:T(8,128)(2,1)S(1)}, u32[]{:S(2)}, u32[]{:S(2)}) collective-permute-start(bf16[1,144,576]{2,1,0:T(8,128)(2,1)} %dynamic-slice_convert_fusion.8), channel_id=1, source_target_pairs={{0,16},{4,20},{8,24},{12,28},{16,0},{20,4},{24,8},{28,12},{1,17},{... | collective-permute-start | bytes 497672 | tf_op jit(solution)/shard_map/ppermute | solution.py:30
  430.6 9.4 %collective-permute-start.50 = (bf16[111,576]{1,0:T(8,128)(2,1)S(1)}, bf16[111,576]{1,0:T(8,128)(2,1)S(1)}, u32[]{:S(2)}, u32[]{:S(2)}) collective-permute-start(bf16[111,576]{1,0:T(8,128)(2,1)S(1)} %pad_maximum_fusion), channel_id=1, source_target_pairs={{0,4},{4,0},{8,12},{12,8},{16,20},{20,16},{24,28},{28,24},{1,5},{5... | collective-permute-start | bytes 383624 | tf_op jit(solution)/shard_map/ppermute | solution.py:30
  433.1 90.9 %collective-permute-start.44 = (bf16[2,288,384]{2,1,0:T(8,128)(2,1)}, bf16[2,288,384]{2,1,0:T(8,128)(2,1)}, u32[]{:S(2)}, u32[]{:S(2)}) collective-permute-start(bf16[2,288,384]{2,1,0:T(8,128)(2,1)} %fusion.16), channel_id=1, source_target_pairs={{0,0},{1,8},{2,16},{3,24},{4,1},{5,9},{6,17},{7,25},{8,2},{9,10},{... | collective-permute-start | bytes 1327112 | tf_op jit(solution)/shard_map/ppermute | solution.py:1242
  435.9 31.3 %collective-permute-start.34 = (bf16[2,288,576]{2,1,0:T(8,128)(2,1)}, bf16[2,288,576]{2,1,0:T(8,128)(2,1)S(1)}, u32[]{:S(2)}, u32[]{:S(2)}) collective-permute-start(bf16[2,288,576]{2,1,0:T(8,128)(2,1)} %get-tuple-element.116), channel_id=1, source_target_pairs={{0,4},{4,0},{8,12},{12,8},{16,20},{20,16},{24,28},{28,24},{1,5},{5... | collective-permute-start | bytes 1990664 | tf_op jit(solution)/shard_map/ppermute | solution.py:30
  440.0 39.5 %collective-permute-start.33 = (bf16[2,288,576]{2,1,0:T(8,128)(2,1)}, bf16[2,288,576]{2,1,0:T(8,128)(2,1)S(1)}, u32[]{:S(2)}, u32[]{:S(2)}) collective-permute-start(bf16[2,288,576]{2,1,0:T(8,128)(2,1)} %get-tuple-element.114), channel_id=1, source_target_pairs={{0,4},{4,0},{8,12},{12,8},{16,20},{20,16},{24,28},{28,24},{1,5},{5... | collective-permute-start | bytes 1990664 | tf_op jit(solution)/shard_map/ppermute | solution.py:30
  440.2 17.0 %collective-permute-start.51 = (bf16[111,576]{1,0:T(8,128)(2,1)S(1)}, bf16[111,576]{1,0:T(8,128)(2,1)S(1)}, u32[]{:S(2)}, u32[]{:S(2)}) collective-permute-start(bf16[111,576]{1,0:T(8,128)(2,1)S(1)} %add_convert_fusion.4), channel_id=1, source_target_pairs={{0,8},{4,12},{8,0},{12,4},{16,24},{20,28},{24,16},{28,20},{1,9},{5... | collective-permute-start | bytes 383624 | tf_op jit(solution)/shard_map/ppermute | solution.py:30
  457.1 43.8 %collective-permute-start.31 = (bf16[2,256,1152]{2,1,0:T(8,128)(2,1)}, bf16[2,256,1152]{2,1,0:T(8,128)(2,1)}, u32[]{:S(2)}, u32[]{:S(2)}) collective-permute-start(bf16[2,256,1152]{2,1,0:T(8,128)(2,1)} %get-tuple-element.109), channel_id=1, source_target_pairs={{0,1},{1,0},{2,3},{3,2},{4,5},{5,4},{6,7},{7,6},{8,9},{9,8},{10,11... | collective-permute-start | bytes 3538952 | tf_op jit(solution)/shard_map/ppermute | solution.py:25
  467.1 15.7 %collective-permute-start.52 = (bf16[111,576]{1,0:T(8,128)(2,1)S(1)}, bf16[111,576]{1,0:T(8,128)(2,1)S(1)}, u32[]{:S(2)}, u32[]{:S(2)}) collective-permute-start(bf16[111,576]{1,0:T(8,128)(2,1)S(1)} %add_convert_fusion.3), channel_id=1, source_target_pairs={{0,16},{4,20},{8,24},{12,28},{16,0},{20,4},{24,8},{28,12},{1,17},{... | collective-permute-start | bytes 383624 | tf_op jit(solution)/shard_map/ppermute | solution.py:30
  481.0 18.0 %collective-permute-start.35 = (bf16[1,288,2,1,576]{4,1,2,3,0:T(8,128)(2,1)}, bf16[1,288,2,1,576]{4,1,2,3,0:T(8,128)(2,1)}, u32[]{:S(2)}, u32[]{:S(2)}) collective-permute-start(bf16[1,288,2,1,576]{4,1,2,3,0:T(8,128)(2,1)} %fusion.9), channel_id=1, source_target_pairs={{0,8},{4,12},{8,0},{12,4},{16,24},{20,28},{24,16},{28,20},{1,9},{5... | collective-permute-start | bytes 1990664 | tf_op jit(solution)/shard_map/ppermute | solution.py:30
  500.8 17.8 %collective-permute-start.36 = (bf16[1,288,1,1,576]{4,1,2,3,0:T(8,128)(2,1)S(1)}, bf16[1,288,1,1,576]{4,1,2,3,0:T(8,128)(2,1)S(1)}, u32[]{:S(2)}, u32[]{:S(2)}) collective-permute-start(bf16[1,288,1,1,576]{4,1,2,3,0:T(8,128)(2,1)S(1)} %dynamic-slice_convert_fusion.7), channel_id=1, source_target_pairs={{0,16},{4,20},{8,24},{12,28},{16,0},{20,4},{24,8},{28,12},{1,17},{... | collective-permute-start | bytes 995336 | tf_op jit(solution)/shard_map/ppermute | solution.py:30
  504.7 22.7 %collective-permute-start.32 = (bf16[256,1152]{1,0:T(8,128)(2,1)}, bf16[256,1152]{1,0:T(8,128)(2,1)S(1)}, u32[]{:S(2)}, u32[]{:S(2)}) collective-permute-start(bf16[256,1152]{1,0:T(8,128)(2,1)} %fusion.13), channel_id=1, source_target_pairs={{0,2},{1,3},{2,0},{3,1},{4,6},{5,7},{6,4},{7,5},{8,10},{9,11},{10,... | collective-permute-start | bytes 1769480 | tf_op jit(solution)/shard_map/ppermute | solution.py:25
  519.4 12.2 %collective-permute-start.37 = (bf16[288,576]{1,0:T(8,128)(2,1)}, bf16[288,576]{1,0:T(8,128)(2,1)}, u32[]{:S(2)}, u32[]{:S(2)}) collective-permute-start(bf16[288,576]{1,0:T(8,128)(2,1)} %fusion.17), channel_id=1, source_target_pairs={{0,0},{1,4},{2,8},{3,12},{4,1},{5,5},{6,9},{7,13},{8,2},{9,6},{10,... | collective-permute-start | bytes 995336 | tf_op jit(solution)/shard_map/ppermute | solution.py:1243
  (66 other events, 573.0 us)

commit v3 on v2

--- a/solution.py
+++ b/solution.py
@@ -49,24 +49,23 @@
     return mine, lax.dynamic_index_in_dim(held, 1 - side, 0, False).astype(jnp.bfloat16)
 
 
-def halve(value, axis, bit):
+def halve(value, axis, bit, *others):
     mine = (lax.axis_index("grp") // bit) % 2
-    shape = value.shape
-    value = value.reshape(shape[:axis] + (shape[axis] // 2, 2) + shape[axis + 1 :])
-    held = lax.dynamic_index_in_dim(value, mine, axis + 1, False)
-    given = lax.dynamic_index_in_dim(value, 1 - mine, axis + 1, False)
-    return held, given.astype(jnp.bfloat16)
+    terms = value if isinstance(value, tuple) else (value,)
+    size = terms[0].shape[axis] // 2
+
+    def side(index):
+        picked = [lax.dynamic_slice_in_dim(term, index * size, size, axis) for term in terms]
+        total = picked[0].astype(jnp.float32)
+        for term in picked[1:]:
+            total = total + term.astype(jnp.float32)
+        return tie(total, *others)
+
+    return side(mine), side(1 - mine).astype(jnp.bfloat16)
 
 
 def join(held, got, *others):
     return tie(held.astype(jnp.float32) + got.astype(jnp.float32), *others)
-
-
-def sum_rest(value, steps):
-    for axis, bit in steps:
-        held, given = halve(value, axis, bit)
-        value = join(held, swap_groups(given, bit))
-    return value
 
 
 def share_pieces(pieces):
@@ -79,13 +78,20 @@
     return [pieces[0], swap(pieces[1], 1), crossed, shared]
 
 
-def total_groups(value):
-    groups = lax.axis_size("grp")
-    bit = 1
-    while bit < groups:
-        value = value.astype(jnp.bfloat16)
-        value = value.astype(jnp.float32) + swap_groups(value, bit).astype(jnp.float32)
-        bit = 2 * bit
+def exchange(value, bits):
+    return [value] + [swap_groups(value, sum(bits[i] for i in range(len(bits)) if k >> i & 1)) for k in range(1, 2 ** len(bits))]
+
+
+def balanced(terms, *others):
+    terms = [term.astype(jnp.float32) for term in terms]
+    while len(terms) > 1:
+        terms = [terms[i] + terms[i + 1] for i in range(0, len(terms), 2)]
+    return tie(terms[0], *others)
+
+
+def total_rest(value, bits, kind=jnp.bfloat16):
+    for bit in bits:
+        value = balanced(exchange(value.astype(kind), [bit]))
     return value
 
 
@@ -219,8 +225,8 @@
                 rate_out[r] = rate_sum[i]
         for t in range(STEP):
             for i in range(2):
-                entry_out[base + t, 8 * i : 8 * i + 8] = entry_sum[t][i]
-                read_out[base + t, 8 * i : 8 * i + 8] = read_sum[t][i]
+                entry_out[base + STEP - 1 - t, 8 * i : 8 * i + 8] = entry_sum[t][i]
+                read_out[base + STEP - 1 - t, 8 * i : 8 * i + 8] = read_sum[t][i]
         return (tuple(flows), tuple(afters))
 
     flows, afters = lax.fori_loop(
@@ -373,7 +379,7 @@
             pltpu.SemaphoreType.DMA((2 * parts,)),
         ],
         compiler_params=pltpu.CompilerParams(vmem_limit_bytes=40 * 2**20),
-        cost_estimate=pl.CostEstimate(flops=2 * total * width * both, bytes_accessed=20 * 2**20, transcendentals=total * inside),
+        cost_estimate=pl.CostEstimate(flops=4 * 10**9, bytes_accessed=2**20, transcendentals=0),
         name="project",
     )(me, source, length, *normed_pieces, *weight_pieces, taps, bias, select_wide)
 
@@ -474,6 +480,7 @@
         + [pltpu.VMEM((chunk, NS, LANES), f32)] * 2
         + [pltpu.VMEM((chunk // STEP, STEP, wide), f32), pltpu.VMEM((count, 8, LANES), f32)],
         compiler_params=pltpu.CompilerParams(vmem_limit_bytes=40 * 2**20),
+        cost_estimate=pl.CostEstimate(flops=4 * 10**9, bytes_accessed=2**20, transcendentals=0),
         name="mixer",
     )(me, length, selected, conv_out, zgate, step_wide, bias, skip, rate, out_weight)
 
@@ -484,43 +491,26 @@
     return dot_t(ones, high) + dot_t(ones, low)
 
 
-def mixer_back_kernel(
-    tiles, share, me_ref, length_ref, *rest,
-):
-    grad_refs, rest = (rest[:4], rest[4:])
+def mixer_back_kernel(tiles, length_ref, *rest):
     (
-        selected_ref, conv_ref, gate_ref, mixed_ref, gated_ref, state_ref, end_ref, weight_ref, bias_ref, skip_ref, rate_ref, project_ref,
-        gate_out, conv_out, rank_out, entry_sum_out, read_sum_out, step_out, bias_out, skip_out, rate_out, project_out,
-        grads, dt_ref, dx_ref, mix_ref, entry_ref, read_ref, fed_ref, rise_ref, entry_parts, read_parts, flow, after, total, sems,
+        selected_ref, conv_ref, grad_ref, state_ref, end_ref, weight_ref, bias_ref, skip_ref, rate_ref,
+        conv_out, rank_out, step_out, bias_out, skip_out, rate_out,
+        dt_ref, dx_ref, mix_ref, entry_ref, read_ref, fed_ref, rise_ref, entry_parts, read_parts, flow, after,
     ) = rest
     chunk, inside = conv_ref.shape
-    span = grad_refs[0].shape[0]
     index = pl.program_id(0)
     step = pl.num_programs(0) - 1 - index
 
     @pl.when(index == 0)
     def start():
-        copies = []
-        for k in range(4):
-            at = pl.ds(pl.multiple_of((me_ref[0] ^ k) * span, 16), span)
-            copies.append(pltpu.make_async_copy(grad_refs[k], grads.at[at], sems.at[k]))
-            copies[-1].start()
         flow[...] = jnp.zeros_like(flow)
         after[...] = end_ref[...]
         rate_out[...] = jnp.zeros_like(rate_out)
         step_out[...] = jnp.zeros_like(step_out)
         bias_out[...] = jnp.zeros_like(bias_out)
         skip_out[...] = jnp.zeros_like(skip_out)
-        total[...] = jnp.zeros_like(total)
-        for copy in copies:
-            copy.wait()
-
-    rows = pl.ds(pl.multiple_of(step * chunk, chunk), chunk)
-    grad_gated = dot_t(grads[rows], project_ref[...])
-    gate, mixed, conv = (gate_ref[...], mixed_ref[...], conv_ref[...])
-    curve = 1.0 / (1.0 + jnp.exp(-gate))
-    grad_mixed = grad_gated * (gate * curve)
-    gate_out[...] = (grad_gated * mixed * (curve * (1.0 + gate * (1.0 - curve)))).astype(jnp.bfloat16)
+
+    conv, grad_mixed = (conv_ref[...], grad_ref[...])
     skip_out[...] += jnp.sum(grad_mixed * conv, axis=0, keepdims=True)
     selected = selected_ref[...]
     live = live_slots(step * chunk, length_ref, chunk)
@@ -538,104 +528,173 @@
     grad_pre = jnp.where(live, grad_size / (1.0 + jnp.exp(-pre)), 0.0)
     bias_out[...] += jnp.sum(grad_pre, axis=0, keepdims=True)
     grad_low = grad_pre.astype(jnp.bfloat16)
-    rank_out[...] = dot_t(grad_low, weight_ref[...])
+    rank = dot_t(grad_low, weight_ref[...])
+    sums = [row_sums(part[...].reshape(chunk * NS, LANES)) for part in (entry_parts, read_parts)]
+    lane = lax.broadcasted_iota(jnp.int32, (STEP, LANES), 1)
+    for g in range(chunk // STEP):
+        total = rank[g * STEP : (g + 1) * STEP]
+        for i, part in enumerate(sums):
+            start = R + i * NS
+            moved = pltpu.roll(part[:, g * LANES : (g + 1) * LANES], start + NS, 1)
+            moved = pltpu.roll(moved, 0, 1, stride=NS, stride_axis=0)
+            total = jnp.where((lane >= start) & (lane < start + NS), moved, total)
+        rank_out[g * STEP : (g + 1) * STEP] = total
     step_out[...] += t_dot(low, grad_low)
     conv_out[...] = fed * size + skip_ref[...] * grad_mixed
-    entry_sum_out[0] = row_sums(entry_parts[...].reshape(chunk * NS, LANES))
-    read_sum_out[0] = row_sums(read_parts[...].reshape(chunk * NS, LANES))
-
-    @pl.when(step % share == 0)
-    def weigh():
-        block = pl.ds(pl.multiple_of(step * chunk, span), span)
-        total[...] += t_dot(grads[block], gated_ref[...])
-
-    @pl.when(step == 0)
-    def finish():
-        project_out[...] = total[...].astype(jnp.bfloat16)
-
-
-def mixer_back(me, length, grad_pieces, selected, conv_out, zgate, mixed, gated, states, end, step_wide, bias, skip, rate, out_weight, tiles):
+
+
+def mixer_back(length, selected, conv_out, grad_mixed, states, end, step_wide, bias, skip, rate, tiles):
     total, inside = conv_out.shape
-    span, width = grad_pieces[0].shape
     count = 2 * tiles + 1
     chunk = CHUNK
     steps = total // chunk
     wide = (tiles + 1) * LANES
-    share = span // chunk
     smem, vmem = (pl.BlockSpec(memory_space=pltpu.SMEM), pl.BlockSpec(memory_space=pltpu.VMEM))
-    anywhere = pl.BlockSpec(memory_space=pl.ANY)
     row = pl.BlockSpec((chunk, inside), lambda i: (steps - 1 - i, 0))
     lane = pl.BlockSpec((chunk, LANES), lambda i: (steps - 1 - i, 0))
-    sums = pl.BlockSpec((1, 8, chunk * NS), lambda i: (steps - 1 - i, 0, 0))
-    f32, bf16 = (jnp.float32, jnp.bfloat16)
+    f32 = jnp.float32
     one = jax.ShapeDtypeStruct((1, inside), f32)
-    summed = jax.ShapeDtypeStruct((steps, 8, chunk * NS), f32)
     return pl.pallas_call(
-        functools.partial(mixer_back_kernel, tiles, share),
+        functools.partial(mixer_back_kernel, tiles),
         grid=(steps,),
-        in_specs=[smem, smem]
-        + [anywhere] * 4
-        + [lane, row, row, row]
-        + [pl.BlockSpec((span, inside), lambda i: ((steps - 1 - i) // share, 0))]
+        in_specs=[smem, lane, row, row]
         + [pl.BlockSpec((chunk, count, 8, LANES), lambda i: (steps - 1 - i, 0, 0, 0))]
-        + [vmem] * 6,
-        out_specs=[row, row, lane, sums, sums] + [vmem] * 5,
+        + [vmem] * 5,
+        out_specs=[row, lane] + [vmem] * 4,
         out_shape=[
-            jax.ShapeDtypeStruct((total, inside), bf16),
             jax.ShapeDtypeStruct((total, inside), f32),
             jax.ShapeDtypeStruct((total, LANES), f32),
-            summed,
-            summed,
             jax.ShapeDtypeStruct((LANES, inside), f32),
             one,
             one,
             jax.ShapeDtypeStruct((count, 8, LANES), f32),
-            jax.ShapeDtypeStruct((width, inside), bf16),
-        ],
-        scratch_shapes=[pltpu.VMEM((total, width), bf16)]
-        + [pltpu.VMEM((chunk // STEP, STEP, wide), f32)] * 3
+        ],
+        scratch_shapes=[pltpu.VMEM((chunk // STEP, STEP, wide), f32)] * 3
         + [pltpu.VMEM((chunk, NS, LANES), f32)] * 2
         + [pltpu.VMEM((chunk // STEP, STEP, wide), f32)] * 2
         + [pltpu.VMEM((chunk, NS, LANES), f32)] * 2
-        + [pltpu.VMEM((count, 8, LANES), f32)] * 2
-        + [pltpu.VMEM((width, inside), f32), pltpu.SemaphoreType.DMA((4,))],
+        + [pltpu.VMEM((count, 8, LANES), f32)] * 2,
         compiler_params=pltpu.CompilerParams(vmem_limit_bytes=48 * 2**20),
+        cost_estimate=pl.CostEstimate(flops=4 * 10**9, bytes_accessed=2**20, transcendentals=0),
         name="mixer_back",
-    )(me, length, *grad_pieces, selected, conv_out, zgate, mixed, gated, states, end, step_wide, bias, skip, rate, out_weight)
-
-
-def project_back_kernel(parts, me_ref, source_ref, length_ref, *rest):
-    normed_refs, weight_refs, rest = (rest[:parts], rest[parts : 2 * parts], rest[2 * parts :])
+    )(length, selected, conv_out, grad_mixed, states, end, step_wide, bias, skip, rate)
+
+
+def gate_back_kernel(parts, pair, me_ref, source_ref, *rest):
+    normed_refs, grad_refs, rest = (rest[:parts], rest[parts : 2 * parts], rest[2 * parts :])
     (
-        selected_ref, conv_ref, summed_ref, inner_ref, gate_ref, low_ref, taps_ref, select_ref,
-        held_out, given_out, inner_held, inner_given, gate_held, gate_given, select_out, taps_out, bias_out, gain_out,
-        normed, weight, shifted, projected, total, sems,
+        gate_ref, mixed_ref, gated_ref, project_ref,
+        mix_out, gate_out, gate_held, gate_given, out_held, out_given,
+        normed, grads, gate_sum, out_sum, sems,
+    ) = rest
+    block = pl.program_id(0)
+    rows, width = normed_refs[0].shape
+    slab = width // parts
+    me, odd, second = (me_ref[0], source_ref[parts], source_ref[parts + 1])
+
+    @pl.when(block == 0)
+    def fetch():
+        copies = []
+        for k in range(parts):
+            at = pl.ds(pl.multiple_of((me ^ k) * rows, 16), rows)
+            copies.append(pltpu.make_async_copy(normed_refs[k], normed.at[at], sems.at[k]))
+            copies.append(pltpu.make_async_copy(grad_refs[k], grads.at[at], sems.at[parts + k]))
+        for copy in copies:
+            copy.start()
+        gate_sum[...] = jnp.zeros_like(gate_sum)
+        out_sum[...] = jnp.zeros_like(out_sum)
+        for copy in copies:
+            copy.wait()
+
+    at = pl.ds(pl.multiple_of(block * rows, rows), rows)
+    grad = grads[at]
+    grad_gated = dot_t(grad, project_ref[...])
+    gate = gate_ref[...]
+    curve = 1.0 / (1.0 + jnp.exp(-gate))
+    mix_out[...] = grad_gated * (gate * curve)
+    low = (grad_gated * mixed_ref[...] * (curve * (1.0 + gate * (1.0 - curve)))).astype(jnp.bfloat16)
+    gate_out[...] = low
+    gate_sum[...] += t_dot(normed[at], low)
+    out_sum[...] += t_dot(grad, gated_ref[...])
+
+    @pl.when(block == parts - 1)
+    def finish():
+        for h in range(parts // 2):
+            at = pl.ds(pl.multiple_of((2 * h + odd) * slab, 8), slab)
+            gate_held[h] = gate_sum[at]
+            at = pl.ds(pl.multiple_of((2 * h + 1 - odd) * slab, 8), slab)
+            gate_given[h] = gate_sum[at].astype(jnp.bfloat16)
+        for h in range(width // (2 * pair)):
+            at = pl.ds(pl.multiple_of((2 * h + second) * pair, 8), pair)
+            out_held[h] = out_sum[at]
+            at = pl.ds(pl.multiple_of((2 * h + 1 - second) * pair, 8), pair)
+            out_given[h] = out_sum[at].astype(jnp.bfloat16)
+
+
+def gate_back(me, source, normed_pieces, grad_pieces, zgate, mixed, gated, out_weight, pair):
+    parts = len(normed_pieces)
+    rows, width = normed_pieces[0].shape
+    total, inside = gated.shape
+    slab = width // parts
+    smem, anywhere = (pl.BlockSpec(memory_space=pltpu.SMEM), pl.BlockSpec(memory_space=pl.ANY))
+    vmem = pl.BlockSpec(memory_space=pltpu.VMEM)
+    row = pl.BlockSpec((rows, inside), lambda i: (i, 0))
+    f32, bf16 = (jnp.float32, jnp.bfloat16)
+    gate_shape = (parts // 2, slab, inside)
+    out_shape = (width // (2 * pair), pair, inside)
+    return pl.pallas_call(
+        functools.partial(gate_back_kernel, parts, pair),
+        grid=(parts,),
+        in_specs=[smem] * 2 + [anywhere] * (2 * parts) + [row] * 3 + [vmem],
+        out_specs=[row] * 2 + [vmem] * 4,
+        out_shape=[
+            jax.ShapeDtypeStruct((total, inside), f32),
+            jax.ShapeDtypeStruct((total, inside), bf16),
+            jax.ShapeDtypeStruct(gate_shape, f32),
+            jax.ShapeDtypeStruct(gate_shape, bf16),
+            jax.ShapeDtypeStruct(out_shape, f32),
+            jax.ShapeDtypeStruct(out_shape, bf16),
+        ],
+        scratch_shapes=[
+            pltpu.VMEM((total, width), bf16),
+            pltpu.VMEM((total, width), bf16),
+            pltpu.VMEM((width, inside), f32),
+            pltpu.VMEM((width, inside), f32),
+            pltpu.SemaphoreType.DMA((2 * parts,)),
+        ],
+        compiler_params=pltpu.CompilerParams(vmem_limit_bytes=48 * 2**20),
+        cost_estimate=pl.CostEstimate(flops=4 * 10**9, bytes_accessed=2**20, transcendentals=0),
+        name="gate_back",
+    )(me, source, *normed_pieces, *grad_pieces, zgate, mixed, gated, out_weight)
+
+
+def conv_back_kernel(parts, me_ref, source_ref, length_ref, *rest):
+    normed_refs, rest = (rest[:parts], rest[parts:])
+    (
+        selected_ref, conv_ref, summed_ref, inner_ref, low_ref, taps_ref, select_ref,
+        inner_out, inner_held, inner_given, select_out, taps_out, bias_out,
+        normed, shifted, total, sems,
     ) = rest
     index = pl.program_id(0)
     block = parts - 1 - index
     rows, inside = inner_ref.shape
-    slab = weight_refs[0].shape[0]
+    slab = normed.shape[1] // parts
     me = me_ref[0]
     odd = source_ref[parts]
 
+    def fetched(k):
+        at = pl.ds(pl.multiple_of((me ^ k) * rows, 16), rows)
+        return pltpu.make_async_copy(normed_refs[k], normed.at[at], sems.at[k])
+
     @pl.when(index == 0)
     def fetch():
-        copies = []
         for k in range(parts):
-            at = pl.ds(pl.multiple_of(source_ref[k] * slab, 16), slab)
-            copies.append(pltpu.make_async_copy(weight_refs[k], weight.at[at], sems.at[k]))
-            at = pl.ds(pl.multiple_of((me ^ k) * rows, 16), rows)
-            copies.append(pltpu.make_async_copy(normed_refs[k], normed.at[at], sems.at[parts + k]))
-        for copy in copies:
-            copy.start()
+            fetched(k).start()
         shifted[rows:] = jnp.zeros((8, inside), jnp.float32)
         total[...] = jnp.zeros_like(total)
         select_out[...] = jnp.zeros_like(select_out)
         taps_out[...] = jnp.zeros_like(taps_out)
         bias_out[...] = jnp.zeros_like(bias_out)
-        gain_out[...] = jnp.zeros_like(gain_out)
-        for copy in copies:
-            copy.wait()
 
     selected = selected_ref[...]
     summed = summed_ref[...]
@@ -652,74 +711,130 @@
         taps_out[k : k + 1] += jnp.sum(inner * moved, axis=0, keepdims=True)
     shifted[rows:] = shifted[0:8]
     live = live_slots(block * rows, length_ref, rows)
-    projected[:, :inside] = jnp.where(live, grad_inner, 0.0).astype(jnp.bfloat16)
-    projected[:, inside:] = gate_ref[...]
-    normed_rows = normed[pl.ds(pl.multiple_of(block * rows, rows), rows)]
-    grad_normed = dot_t(projected[...], weight[...])
-    gain_out[...] += jnp.sum(grad_normed * normed_rows.astype(jnp.float32), axis=0, keepdims=True)
-    total[...] += t_dot(normed_rows, projected[...])
-
-    @pl.when(block % 2 == me % 2)
-    def keep():
-        held_out[0] = grad_normed
-
-    @pl.when(block % 2 != me % 2)
-    def give():
-        given_out[0] = grad_normed.astype(jnp.bfloat16)
+    low = jnp.where(live, grad_inner, 0.0).astype(jnp.bfloat16)
+    inner_out[...] = low
+
+    @pl.when(index == 0)
+    def arrive():
+        for k in range(parts):
+            fetched(k).wait()
+
+    total[...] += t_dot(normed[pl.ds(pl.multiple_of(block * rows, rows), rows)], low)
 
     @pl.when(block == 0)
     def finish():
         for h in range(parts // 2):
-            at = pl.ds(pl.multiple_of((2 * h + odd) * slab, 16), slab)
-            inner_held[h] = total[at, :inside]
-            gate_held[h] = total[at, inside:]
-            at = pl.ds(pl.multiple_of((2 * h + 1 - odd) * slab, 16), slab)
-            inner_given[h] = total[at, :inside].astype(jnp.bfloat16)
-            gate_given[h] = total[at, inside:].astype(jnp.bfloat16)
-
-
-def project_back(me, source, length, normed_pieces, weight_pieces, grad_selected, conv_grad, summed, inner, gate_grad, conv_low, taps, select_wide):
+            at = pl.ds(pl.multiple_of((2 * h + odd) * slab, 8), slab)
+            inner_held[h] = total[at]
+            at = pl.ds(pl.multiple_of((2 * h + 1 - odd) * slab, 8), slab)
+            inner_given[h] = total[at].astype(jnp.bfloat16)
+
+
+def conv_back(me, source, length, normed_pieces, grad_selected, conv_grad, summed, inner, conv_low, taps, select_wide):
     parts = len(normed_pieces)
     rows, width = normed_pieces[0].shape
-    slab, both = weight_pieces[0].shape
+    slab = width // parts
     total, inside = inner.shape
     smem, anywhere = (pl.BlockSpec(memory_space=pltpu.SMEM), pl.BlockSpec(memory_space=pl.ANY))
     vmem = pl.BlockSpec(memory_space=pltpu.VMEM)
     row = pl.BlockSpec((rows, inside), lambda i: (parts - 1 - i, 0))
-    part = pl.BlockSpec((1, rows, width), lambda i: ((parts - 1 - i) // 2, 0, 0))
     f32, bf16 = (jnp.float32, jnp.bfloat16)
     return pl.pallas_call(
-        functools.partial(project_back_kernel, parts),
+        functools.partial(conv_back_kernel, parts),
         grid=(parts,),
         in_specs=[smem] * 3
-        + [anywhere] * (2 * parts)
+        + [anywhere] * parts
         + [pl.BlockSpec((rows, LANES), lambda i: (parts - 1 - i, 0))]
-        + [row] * 5
+        + [row] * 4
         + [vmem] * 2,
-        out_specs=[part, part] + [vmem] * 8,
+        out_specs=[row] + [vmem] * 5,
         out_shape=[
-            jax.ShapeDtypeStruct((2, rows, width), f32),
-            jax.ShapeDtypeStruct((2, rows, width), bf16),
-            jax.ShapeDtypeStruct((2, slab, inside), f32),
-            jax.ShapeDtypeStruct((2, slab, inside), bf16),
+            jax.ShapeDtypeStruct((total, inside), bf16),
             jax.ShapeDtypeStruct((2, slab, inside), f32),
             jax.ShapeDtypeStruct((2, slab, inside), bf16),
             jax.ShapeDtypeStruct((LANES, inside), f32),
             jax.ShapeDtypeStruct((8, inside), f32),
             jax.ShapeDtypeStruct((1, inside), f32),
+        ],
+        scratch_shapes=[
+            pltpu.VMEM((total, width), bf16),
+            pltpu.VMEM((rows + 8, inside), f32),
+            pltpu.VMEM((width, inside), f32),
+            pltpu.SemaphoreType.DMA((parts,)),
+        ],
+        compiler_params=pltpu.CompilerParams(vmem_limit_bytes=48 * 2**20),
+        cost_estimate=pl.CostEstimate(flops=4 * 10**9, bytes_accessed=2**20, transcendentals=0),
+        name="conv_back",
+    )(me, source, length, *normed_pieces, grad_selected, conv_grad, summed, inner, conv_low, taps, select_wide)
+
+
+def project_back_kernel(parts, me_ref, source_ref, *rest):
+    normed_refs, weight_refs, rest = (rest[:parts], rest[parts : 2 * parts], rest[2 * parts :])
+    inner_ref, gate_ref, held_out, given_out, gain_out, normed, weight, projected, sems = rest
+    block = pl.program_id(0)
+    rows, inside = inner_ref.shape
+    slab = weight_refs[0].shape[0]
+    me = me_ref[0]
+
+    @pl.when(block == 0)
+    def fetch():
+        copies = []
+        for k in range(parts):
+            at = pl.ds(pl.multiple_of(source_ref[k] * slab, 16), slab)
+            copies.append(pltpu.make_async_copy(weight_refs[k], weight.at[at], sems.at[k]))
+            at = pl.ds(pl.multiple_of((me ^ k) * rows, 16), rows)
+            copies.append(pltpu.make_async_copy(normed_refs[k], normed.at[at], sems.at[parts + k]))
+        for copy in copies:
+            copy.start()
+        gain_out[...] = jnp.zeros_like(gain_out)
+        for copy in copies:
+            copy.wait()
+
+    projected[:, :inside] = inner_ref[...]
+    projected[:, inside:] = gate_ref[...]
+    normed_rows = normed[pl.ds(pl.multiple_of(block * rows, rows), rows)]
+    grad_normed = dot_t(projected[...], weight[...])
+    gain_out[...] += jnp.sum(grad_normed * normed_rows.astype(jnp.float32), axis=0, keepdims=True)
+
+    @pl.when(block % 2 == me % 2)
+    def keep():
+        held_out[0] = grad_normed
+
+    @pl.when(block % 2 != me % 2)
+    def give():
+        given_out[0] = grad_normed.astype(jnp.bfloat16)
+
+
+def project_back(me, source, normed_pieces, weight_pieces, inner_grad, gate_grad):
+    parts = len(normed_pieces)
+    rows, width = normed_pieces[0].shape
+    slab, both = weight_pieces[0].shape
+    total, inside = inner_grad.shape
+    smem, anywhere = (pl.BlockSpec(memory_space=pltpu.SMEM), pl.BlockSpec(memory_space=pl.ANY))
+    vmem = pl.BlockSpec(memory_space=pltpu.VMEM)
+    row = pl.BlockSpec((rows, inside), lambda i: (i, 0))
+    part = pl.BlockSpec((1, rows, width), lambda i: (i // 2, 0, 0))
+    f32, bf16 = (jnp.float32, jnp.bfloat16)
+    return pl.pallas_call(
+        functools.partial(project_back_kernel, parts),
+        grid=(parts,),
+        in_specs=[smem] * 2 + [anywhere] * (2 * parts) + [row] * 2,
+        out_specs=[part, part, vmem],
+        out_shape=[
+            jax.ShapeDtypeStruct((2, rows, width), f32),
+            jax.ShapeDtypeStruct((2, rows, width), bf16),
             jax.ShapeDtypeStruct((1, width), f32),
         ],
         scratch_shapes=[
             pltpu.VMEM((total, width), bf16),
             pltpu.VMEM((slab * parts, both), bf16),
-            pltpu.VMEM((rows + 8, inside), f32),
             pltpu.VMEM((rows, both), bf16),
-            pltpu.VMEM((slab * parts, both), f32),
             pltpu.SemaphoreType.DMA((2 * parts,)),
         ],
-        compiler_params=pltpu.CompilerParams(vmem_limit_bytes=56 * 2**20),
+        compiler_params=pltpu.CompilerParams(vmem_limit_bytes=40 * 2**20),
+        cost_estimate=pl.CostEstimate(flops=4 * 10**9, bytes_accessed=2**20, transcendentals=0),
         name="project_back",
-    )(me, source, length, *normed_pieces, *weight_pieces, grad_selected, conv_grad, summed, inner, gate_grad, conv_low, taps, select_wide)
+    )(me, source, *normed_pieces, *weight_pieces, inner_grad, gate_grad)
 
 
 def norm_kernel(parts, me_ref, tokens_ref, *rest):
@@ -796,12 +911,12 @@
     )(me, length, tokens, near, got, gains, order, routes)
 
 
-def expert_kernel(parts, cap, steps, pair, me_ref, source_ref, counts_ref, *rest):
+def expert_kernel(parts, cap, steps, me_ref, source_ref, counts_ref, *rest):
     sent_refs, cot_refs, up_refs = (rest[:parts], rest[parts : 2 * parts], rest[2 * parts : 3 * parts])
     (
-        down_ref, grad_held, grad_given, out_held, out_given, up_held, up_given, down_held, down_given,
-    ) = rest[3 * parts : 3 * parts + 9]
-    rows, cots, up, down, rows_t, cots_t, scale, dots, grad_sum, out_sum, product, sems = rest[3 * parts + 9 :]
+        down_ref, grad_held, grad_given, out_held, out_given, packed,
+    ) = rest[3 * parts : 3 * parts + 6]
+    rows, cots, up, down, rows_t, cots_t, scale, dots, grad_sum, out_sum, product, sems = rest[3 * parts + 6 :]
     step = pl.program_id(0)
     expert, tile = (step // steps, step % steps)
     span, width = cots.shape[1:]
@@ -859,19 +974,26 @@
     dots[:, at] += jnp.broadcast_to(part, (count, LANES)).reshape(parts, cap, LANES)
     out_sum[:, at] += dot(hidden, down_tile).reshape(parts, cap, width)
     grad_sum[:, at] += dot_t(grad_pre, up_tile).reshape(parts, cap, width)
-    odd, second = (source_ref[parts], source_ref[parts + 1])
     product[...] = dot(rows_t[...], grad_pre)
-    for h in range(parts // 2):
-        at = pl.ds(pl.multiple_of((2 * h + odd) * slab, 16), slab)
-        up_held[0, h] = product[at]
-        at = pl.ds(pl.multiple_of((2 * h + 1 - odd) * slab, 16), slab)
-        up_given[0, h] = product[at].astype(jnp.bfloat16)
+    fours = packed.shape[0]
+    inside = packed.shape[-1] // LANES
+    share = width // (fours * parts)
+    pieces = []
+    for q in range(FTILE // LANES):
+        piece = tile * (FTILE // LANES) + q
+        pieces.append((piece // inside, pl.ds(pl.multiple_of(piece % inside * LANES, LANES), LANES)))
+    up_rows = pl.ds(pl.multiple_of(expert * slab, 16), slab)
+    for q, (block, lanes) in enumerate(pieces):
+        for r in range(parts):
+            taken = product[r * slab : (r + 1) * slab, q * LANES : (q + 1) * LANES]
+            packed[block, r, up_rows, lanes] = taken.astype(jnp.bfloat16)
     product[...] = dot(cots_t[...], hidden)
-    for h in range(width // (2 * pair)):
-        at = pl.ds(pl.multiple_of((2 * h + second) * pair, 8), pair)
-        down_held[0, h] = product[at]
-        at = pl.ds(pl.multiple_of((2 * h + 1 - second) * pair, 8), pair)
-        down_given[0, h] = product[at].astype(jnp.bfloat16)
+    base = 2 * slab
+    for q, (block, lanes) in enumerate(pieces):
+        down_rows = pl.ds(pl.multiple_of(base + (expert * fours + block) * share, 16), share)
+        for g in range(fours * parts):
+            taken = product[g * share : (g + 1) * share, q * LANES : (q + 1) * LANES]
+            packed[g // parts, g % parts, down_rows, lanes] = taken.astype(jnp.bfloat16)
 
     @pl.when(step == pl.num_programs(0) - 1)
     def finish():
@@ -890,7 +1012,7 @@
                 out_given[b // 2] = out_sum[b].astype(jnp.bfloat16)
 
 
-def experts(me, source, counts, sent_pieces, cot_pieces, up_pieces, down_weight, pair):
+def experts(me, source, counts, sent_pieces, cot_pieces, up_pieces, down_weight, fours):
     parts = len(sent_pieces)
     span, width = cot_pieces[0].shape
     number, hid = down_weight.shape[:2]
@@ -899,26 +1021,19 @@
     smem, anywhere = (pl.BlockSpec(memory_space=pltpu.SMEM), pl.BlockSpec(memory_space=pl.ANY))
     vmem = pl.BlockSpec(memory_space=pltpu.VMEM)
     f32, bf16 = (jnp.float32, jnp.bfloat16)
-    pairs = width // (2 * pair)
-    up_block = pl.BlockSpec((1, parts // 2, slab, FTILE), lambda i: (i // steps, 0, 0, i % steps))
-    down_block = pl.BlockSpec((1, pairs, pair, FTILE), lambda i: (i // steps, 0, 0, i % steps))
-    up_shape = (number, parts // 2, slab, hid)
-    down_shape = (number, pairs, pair, hid)
+    packed = (fours, parts, 2 * number * slab, hid // fours)
     count = parts * CAP
     return pl.pallas_call(
-        functools.partial(expert_kernel, parts, CAP, steps, pair),
+        functools.partial(expert_kernel, parts, CAP, steps),
         grid=(number * steps,),
         in_specs=[smem] * 3 + [anywhere] * (3 * parts + 1),
-        out_specs=[vmem] * 4 + [up_block] * 2 + [down_block] * 2,
+        out_specs=[vmem] * 5,
         out_shape=[
             jax.ShapeDtypeStruct((2, span, width + LANES), f32),
             jax.ShapeDtypeStruct((2, span, width + LANES), bf16),
             jax.ShapeDtypeStruct((2, span, width), f32),
             jax.ShapeDtypeStruct((2, span, width), bf16),
-            jax.ShapeDtypeStruct(up_shape, f32),
-            jax.ShapeDtypeStruct(up_shape, bf16),
-            jax.ShapeDtypeStruct(down_shape, f32),
-            jax.ShapeDtypeStruct(down_shape, bf16),
+            jax.ShapeDtypeStruct(packed, bf16),
         ],
         scratch_shapes=[
             pltpu.VMEM((parts, span, width + LANES), bf16),
@@ -935,7 +1050,7 @@
             pltpu.SemaphoreType.DMA((1 + 3 * parts,)),
         ],
         compiler_params=pltpu.CompilerParams(vmem_limit_bytes=60 * 2**20),
-        cost_estimate=pl.CostEstimate(flops=12 * number * count * width * hid, bytes_accessed=24 * 2**20, transcendentals=number * count * hid),
+        cost_estimate=pl.CostEstimate(flops=4 * 10**9, bytes_accessed=2**20, transcendentals=0),
         name="experts",
     )(me, source, counts, *sent_pieces, *cot_pieces, *up_pieces, down_weight)
 
@@ -1091,6 +1206,7 @@
     )
     selected = tie(selected + swap(selected, 1), cot_pieces[2])
     selected = selected + swap(selected, 2)
+    up_pieces = share_pieces([up_pieces[0], up_pieces[1], tie(up_pieces[2], selected)])
     step_wide = jnp.pad(step_weight, ((0, LANES - R), (0, 0)))
     step_row = step_bias.astype(f32)[None, :]
     decay = -jnp.exp(decay_log.astype(f32))
@@ -1099,16 +1215,26 @@
     states, end, mixed, gated, held, given = mixer(
         me_one, lengths, selected, conv_out, zgate, step_wide, step_row, skip, rate, out_weight, span, tiles
     )
-    up_pieces = share_pieces(up_pieces)
-    near, given = scatter_near(held, given, up_pieces[2])
+    near, given = scatter_near(held, tie(given, up_pieces[2]))
     first_sum, normed_two, sent, probs = route(
         me_one, lengths, tokens, near, swap(given, 2), gains, order, routes
     )
-    grad_held, grad_given, out_held, out_given, up_held, up_given, down_held, down_given = experts(
-        me_one, source, counts, gather_pieces(sent), cot_pieces, up_pieces, down_weight, pair
-    )
+    fours, eights = (groups // 4, groups // 8)
+    fine = hidden_cols // fours % LANES == 0 and share % 16 == 0
+    grad_held, grad_given, out_held, out_given, packed = experts(
+        me_one, source, counts, gather_pieces(sent), cot_pieces, up_pieces, down_weight, fours if fine else 1
+    )
+    up_cols = hidden_cols // fours
+    if not fine:
+        up_rows = packed[0, :, : E * slab].reshape(parts, E * slab, fours, up_cols).transpose(2, 0, 1, 3)
+        down_rows = packed[0, :, E * slab :].reshape(parts, E, fours, share, fours, up_cols)
+        down_rows = down_rows.transpose(2, 0, 1, 4, 3, 5).reshape(fours, parts, E * fours * share, up_cols)
+        down_rows = down_rows.swapaxes(0, 1).reshape(fours, parts, E * fours * share, up_cols)
+        packed = jnp.concatenate([up_rows, down_rows], axis=2)
+    packed = packed.reshape(groups, 2 * E * slab, up_cols)
+    packed = lax.psum_scatter(packed, "grp", scatter_dimension=0, tiled=True)
+    up_sum, down_sum = (packed[:, : E * slab], packed[:, E * slab :])
     near, given = scatter_near(grad_held, grad_given)
-    up_got, down_got = (swap_groups(up_given, 1), swap_groups(down_given, down_bit))
     grad_first, grad_first_low, expert_gain_grad, router_grad = return_rows(
         me_one,
         lengths,
@@ -1123,94 +1249,104 @@
         gains,
     )
     grad_pieces = gather_pieces(grad_first_low)
-    out_near, out_given = scatter_near(out_held, out_given)
-    out_got = swap(out_given, 2)
-    fours, eights = (groups // 4, groups // 8)
-    up_sum = join(up_held, up_got, grad_pieces[2]).reshape(E, 2, slab, fours, hidden_cols // fours)
-    down_sum = join(down_held, down_got, grad_pieces[2])
-    down_sum = down_sum.reshape(E, groups // 4, 2, share, hidden_cols)
-    up_held, up_given = halve(up_sum, 1, 2)
-    down_held, down_given = halve(down_sum, 2, 1)
-    up_got, down_got = (swap_groups(up_given, 2), swap_groups(down_given, 1))
-
-    (
-        grad_zgate,
-        conv_part,
-        rank_part,
-        entry_part,
-        read_part,
-        step_grad,
-        step_bias_grad,
-        skip_grad,
-        rate_grad,
-        out_grad,
-    ) = mixer_back(
-        me_one,
-        lengths,
-        grad_pieces,
-        selected,
-        conv_out,
-        zgate,
-        mixed,
-        gated,
-        states,
-        end,
-        step_wide,
-        step_row,
-        skip,
-        rate,
-        out_weight,
-        tiles,
-    )
-    grad_selected = jnp.concatenate(
-        [
-            rank_part[:, :R],
-            entry_part[:, 0].reshape(total, NS),
-            read_part[:, 0].reshape(total, NS),
-            jnp.zeros((total, spare), f32),
-        ],
-        axis=1,
-    )
-    grad_selected = tie(grad_selected + swap(grad_selected, 1), out_got)
-    grad_selected = (grad_selected + swap(grad_selected, 2)).astype(bf16)
-    up_sum = join(up_held, up_got, rank_part)
-    down_sum = join(down_held, down_got, rank_part)
-    up_held, up_given = halve(up_sum, 3, 4)
-    down_bits = [bit for bit in bits[1:] if bit != down_bit]
-    down_held, down_given = halve(down_sum, 1, down_bits[0])
-    up_got, down_got = (swap_groups(up_given, 4), swap_groups(down_given, down_bits[0]))
-    (
-        held,
-        given,
-        inner_held,
-        inner_given,
-        gate_held,
-        gate_given,
-        select_grad,
-        conv_grad,
-        conv_bias_grad,
-        mixer_part,
-    ) = project_back(
+    top = bits[-1]
+    out_bits = [bit for bit in bits[:0:-1] if bit != down_bit]
+    blocks = (groups // 4, 2, share, inside)
+    grad_mixed, grad_zgate, gate_held, gate_given, out_grad_held, out_grad_given = gate_back(
+        me_one, source, normed_pieces, grad_pieces, zgate, mixed, gated, out_weight, pair
+    )
+    gate_got, out_grad_got = (swap_groups(gate_given, 1), swap_groups(out_grad_given, down_bit))
+    conv_part, grad_selected, step_grad, step_bias_grad, skip_grad, rate_grad = mixer_back(
+        lengths, selected, conv_out, grad_mixed, states, end, step_wide, step_row, skip, rate, tiles
+    )
+    chip_selected = grad_selected + swap(grad_selected, 1)
+    gate_held, gate_given = halve((gate_held, gate_got), 0, 2, chip_selected)
+    gate_got = swap_groups(gate_given, 2)
+    out_parts = (out_grad_held.reshape(blocks), out_grad_got.reshape(blocks))
+    out_grad_held, out_grad_given = halve(out_parts, 1, 1, chip_selected)
+    out_grad_got = swap_groups(out_grad_given, 1)
+
+    def up_home(g, s):
+        return (s * fours + g // 4) * parts + g % 4
+
+    def in_home(g, s):
+        half, k = (g // (groups // 2), (g // 4) % eights)
+        return (half * (groups // 2) + s * eights + k) * parts + g % 4
+
+    both_axes = ("grp", "shard")
+    places = [(g, s) for g in range(groups) for s in range(parts)]
+    up_sum = lax.ppermute(tie(up_sum, chip_selected), both_axes, [(g * parts + s, up_home(g, s)) for g, s in places])
+    grad_selected = (chip_selected + swap(chip_selected, 2)).astype(bf16)
+    inner_grad, inner_held, inner_given, select_grad, conv_grad, conv_bias_grad = conv_back(
         me_one,
         source,
         lengths,
         normed_pieces,
-        in_pieces,
         grad_selected,
         conv_part,
         summed,
         inner,
-        grad_zgate,
         conv_low,
         taps,
         select_wide,
     )
-    near, given = scatter_near(held, given)
+    inner_got = swap_groups(inner_given, 1)
+    held, given, mixer_part = project_back(
+        me_one, source, normed_pieces, in_pieces, inner_grad, grad_zgate
+    )
+    inner_held, inner_given = halve((inner_held, inner_got), 0, 2, given)
+    inner_got = swap_groups(inner_given, 2)
+    gate_sum = join(gate_held, gate_got, inner_held)
+    for bit in out_bits:
+        out_grad_held, out_grad_given = halve((out_grad_held, out_grad_got), 0, bit, inner_held)
+        out_grad_got = swap_groups(out_grad_given, bit)
+    shared = jnp.concatenate([router_grad[0:E], expert_gain_grad, mixer_part / gains[2:3]], axis=0)
+    shared = shared + swap(shared, 1)
+    shared = tie(shared + swap(shared, 2), inner_held)
+    shared = lax.dynamic_slice_in_dim(shared, me * slab, slab, 1)
+    decay_grad = decay * unpack(rate_grad, tiles)
+    picked = select_weight.shape[1]
+    few = [
+        select_grad[:picked],
+        conv_grad[:KW],
+        conv_bias_grad,
+        step_grad[:R],
+        decay_grad,
+        step_bias_grad,
+        skip_grad,
+        shared.reshape(2, inside),
+    ]
+    starts = [0]
+    for part in few:
+        starts.append(starts[-1] + part.shape[0])
+    few = jnp.concatenate(few, axis=0).astype(bf16)
+    few_got = swap_groups(few, 1)
+    near, given = scatter_near(held, given, inner_held)
+    got = swap(given, 2)
+    out_near, out_given = scatter_near(out_held, out_given, inner_held)
+    out_got = swap(out_given, 2)
+    few = join(few, few_got, given, out_given).astype(bf16)
+    few_got = swap_groups(few, 2)
+
+    inner_sum = join(inner_held, inner_got, few)
+    for bit in bits[-2:1:-1]:
+        inner_held, inner_given = halve(inner_sum, 2, bit)
+        inner_sum = join(inner_held, swap_groups(inner_given, bit))
+        gate_held, gate_given = halve(gate_sum, 2, bit)
+        gate_sum = join(gate_held, swap_groups(gate_given, bit))
+    upper = group >= top
+    own = jnp.where(upper, gate_sum, inner_sum).reshape(slab, inside // eights).astype(bf16)
+    other = jnp.where(upper, inner_sum, gate_sum).reshape(slab, inside // eights).astype(bf16)
+    own = lax.ppermute(own, both_axes, [(g * parts + s, in_home(g, s)) for g, s in places])
+    other = lax.ppermute(other, both_axes, [(g * parts + s, in_home(g ^ top, s)) for g, s in places])
+    few = join(few, few_got, inner_sum).astype(bf16)
+    few_got = swap_groups(few, bits[2])
+    out_sum = join(out_grad_held, out_grad_got, inner_sum).reshape(share, inside)
     result, tokens_grad = finish_rows(
-        me_one,
+        tie(me_one, few),
         lengths,
         near,
-        swap(given, 2),
+        got,
         out_near,
         out_got,
         order_t,
@@ -1219,57 +1355,29 @@
         tokens,
         gains,
     )
-
-    in_cols = inside // eights
-    in_sum = jnp.stack(
-        [join(inner_held, swap_groups(inner_given, 1)), join(gate_held, swap_groups(gate_given, 1))], axis=2
-    )
-    in_sum = in_sum.reshape(2, slab, 2, eights, in_cols)
-    in_sum = sum_rest(in_sum, [(0, 2)] + [(3, bit) for bit in bits[2:-1]] + [(2, bits[-1])])
-    in_sum = in_sum.reshape(slab, in_cols)
-    up_sum = sum_rest(join(up_held, up_got, mixer_part), [(3, bit) for bit in bits[3:]])
-    down_sum = sum_rest(join(down_held, down_got, mixer_part), [(1, bit) for bit in down_bits[1:]])
+    in_sum = join(own, other, result)
+    few = total_rest(join(few, few_got, result), bits[3:])
+    few = [few[a:b] for a, b in zip(starts[:-1], starts[1:])]
+    select_grad, conv_grad, conv_bias_grad, step_grad, decay_grad, step_bias_grad, skip_grad, shared = few
+    shared = shared.reshape(4, slab)
+    up_sum = up_sum.astype(f32).reshape(E, slab, up_cols)
+    down_sum = down_sum.astype(f32).reshape(E, fours, share, up_cols).transpose(0, 2, 1, 3)
     down_sum = down_sum.reshape(E, share, hidden_cols)
-    out_sum = sum_rest(out_grad.reshape(groups, share, inside), [(0, bit) for bit in bits])[0]
-    up_moves, in_moves = ([], [])
-    for g in range(groups):
-        for s in range(parts):
-            up_moves.append((g * parts + s, (s * fours + g // 4) * parts + g % 4))
-            half, k = (g // (groups // 2), (g // 4) % eights)
-            in_moves.append((g * parts + s, (half * (groups // 2) + s * eights + k) * parts + g % 4))
-    both_axes = ("grp", "shard")
-    up_cols = hidden_cols // fours
-    up_sum = lax.ppermute(up_sum.reshape(E, slab, up_cols).astype(bf16), both_axes, up_moves)
-    in_sum = lax.ppermute(in_sum.astype(bf16), both_axes, in_moves)
-
-    decay_grad = decay * unpack(rate_grad, tiles)
-    early = jnp.concatenate([step_grad[:R], decay_grad, step_bias_grad, skip_grad], axis=0)
-    early = total_groups(early)
-    shared = jnp.concatenate([router_grad[0:E], expert_gain_grad, mixer_part / gains[2:3]], axis=0)
-    shared = shared + swap(shared, 1)
-    shared = shared + swap(shared, 2)
-    shared = lax.dynamic_slice_in_dim(shared, me * slab, slab, 1)
-    picked = select_weight.shape[1]
-    late = jnp.concatenate(
-        [select_grad[:picked], conv_grad[:KW], conv_bias_grad, shared.reshape(2, inside)], axis=0
-    )
-    late = total_groups(late)
-    shared = late[picked + KW + 1 :].reshape(4, slab)
     return (
         result,
         tokens_grad,
-        in_sum.astype(f32),
+        in_sum,
         out_sum.T,
-        up_sum.astype(f32),
+        up_sum,
         down_sum.transpose(0, 2, 1),
-        late[:picked].T,
-        early[:R],
-        shared[0:2].T,
-        late[picked : picked + KW],
-        late[picked + KW],
-        early[R + NS],
-        early[R : R + NS],
-        early[R + NS + 1],
+        select_grad.T,
+        step_grad,
+        shared[0:E].T,
+        conv_grad,
+        conv_bias_grad[0],
+        step_bias_grad[0],
+        decay_grad,
+        skip_grad[0],
         shared[3],
         shared[2],
     )

time: 542 us -> 487 us (0.90); the launches traced: 534 us -> 485 us
  waiting for transfers between devices: 206 us -> 160 us
  between operations: 7.49 us -> 24.6 us
  starting transfers between devices: 47.6 us -> 33.8 us
  local copies, waits for them, and re-layouts: 65.5 us -> 55.4 us
  Pallas kernels: 170 us -> 177 us
    ppermute x19 -> x10, waiting for transfers between devices: 84.9 us -> 37.1 us  [swap_groups(): return lax.ppermute(value, 'grp', [(g, g ^ bit) for g in range(size)])]
    pallas_call x2 -> x4, Pallas kernels: 95 us -> 116 us  [the longest x1 51.8 us: mixer_back(): pl.pallas_call(functools.partial(mixer_back_kernel, tiles), grid=(steps,)...]
    ppermute x2, waiting for transfers between devices: 19.9 us -> 0.01 us  [share_pieces(): crossed = lax.ppermute(pieces[2], ('grp', 'shard'), moves)]
    ppermute x2 -> x3, waiting for transfers between devices: 0.85 us -> 14.8 us  [the longest x1 14.8 us: body(): lax.ppermute(tie(up_sum, chip_selected), both_axes, [(g * parts + s, up_h...]
    pallas_call x1, Pallas kernels: 21.1 us -> 8.65 us  [project_back(): pl.pallas_call(functools.partial(project_back_kernel, parts), grid=(parts...]
    ppermute x19 -> x10, starting transfers between devices: 22.1 us -> 10.7 us  [swap_groups(): return lax.ppermute(value, 'grp', [(g, g ^ bit) for g in range(size)])]
    another operation x5 -> x2, local copies, waits for them, and re-layouts: 7.56 us -> 0.22 us  [the longest x1 5.35 us: halve(): value.reshape(shape[:axis] + (shape[axis] // 2, 2) + shape[axis + 1:])]
    ppermute x31, waiting for transfers between devices: 96.3 us -> 104 us  [swap(): return lax.ppermute(value, 'shard', [(i, i ^ bit) for i in range(size)])]
  transfers between devices with their start and end apart: 56 -> 49, of which waited for: 24 -> 18; matrix products, arithmetic and copies ran while one was open for 14% -> 12% of each run, Pallas kernels for 18% -> 28%
where the time goes in v3:
time: 487 us; the launch traced here: 485 us
  Pallas kernels  177 us (36%)
  waiting for transfers between devices  160 us (33%)
  local copies, waits for them, and re-layouts  55.4 us (11%)
  starting transfers between devices  33.8 us (7%)
  other arithmetic  33.6 us (7%)
  between operations  24.6 us (5%)
    ppermute x31, waiting for transfers between devices, swap(): return lax.ppermute(value, 'shard', [(i, i ^ bit) for i in range(size)])  104 us
    pallas_call x1, Pallas kernels, mixer_back(): pl.pallas_call(functools.partial(mixer_back_kernel, tiles), grid=(steps,)...  51.8 us
    pallas_call x1, Pallas kernels, experts(): pl.pallas_call(functools.partial(expert_kernel, parts, CAP, steps), grid=...  38.3 us
    ppermute x10, waiting for transfers between devices, swap_groups(): return lax.ppermute(value, 'grp', [(g, g ^ bit) for g in range(size)])  37.1 us
    pallas_call x1, Pallas kernels, mixer(): pl.pallas_call(functools.partial(mixer_kernel, tiles, share), grid=(total...  32.2 us
    unnamed x169, local copies, waits for them, and re-layouts  28 us
    ppermute x31, starting transfers between devices, swap(): return lax.ppermute(value, 'shard', [(i, i ^ bit) for i in range(size)])  16 us
    ppermute x1, waiting for transfers between devices, body(): lax.ppermute(tie(up_sum, chip_selected), both_axes, [(g * parts + s, up_h...  14.8 us
  transfers between devices with their start and end apart: 49, of which 18 were waited for; matrix products, arithmetic and copies ran while one was open for 12% of the time, Pallas kernels for 28%

profile of v3, /device:TPU:2, one launch (start us, length us, event | category | flops | bytes accessed | tf_op | source)
XLA Modules:
  0.0 485.1 jit_solution(2788084808986997476)
XLA Ops:
  7.3 2.0 copy-done.2
  9.3 1.7 copy-done.3
  11.1 2.4 cut_weights.1
  20.8 13.3 %collective-permute-done.1.rest_2_ = f32[16,288]{1,0:T(8,128)S(1)} collective-permute-done((f32[16,288]{1,0:T(8,128)S(1)}, f32[16,288]{1,0:T(8,128)S(1)}, u32[]{:S(2)}, u32[]{:S(2)}) %collective-permute-start.1) | collective-permute-done | bytes 18464 | tf_op jit(solution)/shard_map/ppermute | solution.py:25
  36.3 1.6 collective-permute-start.4
  40.2 11.8 %collective-permute-done.4.rest_2_ = bf16[256,1152]{1,0:T(8,128)(2,1)} collective-permute-done((bf16[256,1152]{1,0:T(8,128)(2,1)}, bf16[256,1152]{1,0:T(8,128)(2,1)}, u32[]{:S(2)}, u32[]{:S(2)}) %collective-permute-start.4) | collective-permute-done | bytes 589856 | tf_op jit(solution)/shard_map/ppermute | solution.py:25
  54.5 1.6 collective-permute-start.10
  56.1 1.7 copy.41
  60.0 10.1 %project.1 = (f32[1024,576]{1,0:T(8,128)S(1)}, f32[1024,576]{1,0:T(8,128)S(1)}, f32[1024,576]{1,0:T(8,128)}, f32[1024,576]{1,0:T(8,128)}, bf16[1024,576]{1,0:T(8,128)(2,1)S(1)}, /*index=5*/f32[1024,128]{1,0:T(8,128)S(1)}) custom-call(s32[1]{0:T(128)} %bitcast.me_ref, s32[6]{0:T(128)S(1)} %stack.26.source_ref, s32[1]{0:T(128)} %copy.54.length_ref, ...), custom_call_target="tpu_custom_call" | custom-call | flops 4000000000 | bytes 1048576 | tf_op jit(solution)/shard_map/project/pallas_call | solution.py:365
  70.1 1.5 copy-done.51
  75.4 13.6 %collective-permute-done.11 = f32[1024,128]{1,0:T(8,128)S(1)} collective-permute-done((f32[1024,128]{1,0:T(8,128)S(1)}, f32[1024,128]{1,0:T(8,128)S(1)}, u32[]{:S(2)}, u32[]{:S(2)}) %collective-permute-start.11) | collective-permute-done | bytes 524320 | tf_op jit(solution)/shard_map/ppermute | solution.py:25
  91.0 32.2 %mixer.1 = (f32[1024,9,8,128]{3,2,1,0:T(8,128)}, f32[9,8,128]{2,1,0:T(8,128)S(1)}, f32[1024,576]{1,0:T(8,128)S(1)}, bf16[1024,576]{1,0:T(8,128)(2,1)S(1)}, f32[2...) custom-call(s32[1]{0:T(128)} %bitcast.me_ref, s32[1]{0:T(128)} %copy.54.length_ref, ...), custom_call_target="tpu_custom_call" | custom-call | flops 4000000000 | bytes 1048576 | tf_op jit(solution)/shard_map/mixer/pallas_call | solution.py:466
  123.2 1.4 copy-done.7
  124.6 1.5 copy-done.50
  129.5 2.8 collective-permute-done.13
  132.3 2.2 convert_add_fusion.1
  134.5 1.4 copy-done.56
  135.9 1.6 collective-permute-start.14
  138.4 1.4 dynamic-slice_bitcast_fusion.3.near_ref
  139.8 11.8 %collective-permute-done.14.got_ref = bf16[256,1152]{1,0:T(8,128)(2,1)S(1)} collective-permute-done((bf16[256,1152]{1,0:T(8,128)(2,1)S(1)}, bf16[256,1152]{1,0:T(8,128)(2,1)S(1)}, u32[]{:S(2)}, u32[]{:S(2)}) %collective-permute-start.14) | collective-permute-done | bytes 589856 | tf_op jit(solution)/shard_map/ppermute | solution.py:25
  154.4 1.9 route.1
  157.7 1.6 collective-permute-start.16
  159.8 14.4 %collective-permute-done.16.rest_2_ = bf16[256,1280]{1,0:T(8,128)(2,1)} collective-permute-done((bf16[256,1280]{1,0:T(8,128)(2,1)}, bf16[256,1280]{1,0:T(8,128)(2,1)}, u32[]{:S(2)}, u32[]{:S(2)}) %collective-permute-start.16) | collective-permute-done | bytes 655392 | tf_op jit(solution)/shard_map/ppermute | solution.py:25
  177.6 4.1 collective-permute-done.21.rest_11_
  181.7 38.3 %experts.1 = (f32[2,256,1280]{2,1,0:T(8,128)}, bf16[2,256,1280]{2,1,0:T(8,128)(2,1)}, f32[2,256,1152]{2,1,0:T(8,128)}, bf16[2,256,1152]{2,1,0:T(8,128)(2,1)}, bf16[2,4,1152,384]{3,2,1,0:T(8,128)(2,1)}) custom-call(s32[1]{0:T(128)} %bitcast.me_ref, s32[6]{0:T(128)} %copy-done.37, s32[4]{0:T(128)} %bitcast.101, bf16[256,1280]{1,0:T(8,128)(2,1)} %get-tuple-element.83.rest_0_, ...), custom_call_target="tpu_custom_call" | custom-call | flops 4000000000 | bytes 1048576 | tf_op jit(solution)/shard_map/experts/pallas_call | solution.py:1026
  220.1 3.2 collective-permute-done.22
  223.3 2.1 convert_add_fusion
  226.3 16.1 %collective-permute-done.23.got_ref = bf16[256,1280]{1,0:T(8,128)(2,1)S(1)} collective-permute-done((bf16[256,1280]{1,0:T(8,128)(2,1)S(1)}, bf16[256,1280]{1,0:T(8,128)(2,1)S(1)}, u32[]{:S(2)}, u32[]{:S(2)}) %collective-permute-start.23) | collective-permute-done | bytes 655392 | tf_op jit(solution)/shard_map/ppermute | solution.py:25
  242.4 1.4 return_rows.1
  245.9 14.2 %collective-permute-done.25.rest_6_ = bf16[256,1152]{1,0:T(8,128)(2,1)S(1)} collective-permute-done((bf16[256,1152]{1,0:T(8,128)(2,1)S(1)}, bf16[256,1152]{1,0:T(8,128)(2,1)S(1)}, u32[]{:S(2)}, u32[]{:S(2)}) %collective-permute-start.25) | collective-permute-done | bytes 589856 | tf_op jit(solution)/shard_map/ppermute | solution.py:25
  260.1 2.0 collective-permute-done.26.rest_7_
  262.1 13.5 %gate_back.1 = (f32[1024,576]{1,0:T(8,128)}, bf16[1024,576]{1,0:T(8,128)(2,1)}, f32[2,288,576]{2,1,0:T(8,128)}, bf16[2,288,576]{2,1,0:T(8,128)(2,1)S(1)}, f32[2,...) custom-call(s32[1]{0:T(128)} %bitcast.me_ref, s32[6]{0:T(128)S(1)} %copy-done.38, ...), custom_call_target="tpu_custom_call" | custom-call | flops 4000000000 | bytes 1048576 | tf_op jit(solution)/shard_map/gate_back/pallas_call | solution.py:645
  275.7 51.8 %mixer_back.1 = (f32[1024,576]{1,0:T(8,128)S(1)}, f32[1024,128]{1,0:T(8,128)}, f32[128,576]{1,0:T(8,128)S(1)}, f32[1,576]{1,0:T(1,128)S(1)}, f32[1,576]{1,0:T(1,128)S(1)}, /*index=5*/f32[9,8,128]{2,1,0:T(8,128)S(1)}) custom-call(s32[1]{0:T(128)} %copy.54.length_ref, f32[1024,128]{1,0:T(8,128)S(1)} %copy-done.9, ...), custom_call_target="tpu_custom_call" | custom-call | flops 4000000000 | bytes 1048576 | tf_op jit(solution)/shard_map/mixer_back/pallas_call | solution.py:557
  327.4 1.5 copy-done.40
  329.4 1.4 slice.171
  332.9 1.5 collective-permute-start.43
  338.2 11.3 %collective-permute-done.39 = bf16[2,288,576]{2,1,0:T(8,128)(2,1)} collective-permute-done((bf16[2,288,576]{2,1,0:T(8,128)(2,1)}, bf16[2,288,576]{2,1,0:T(8,128)(2,1)}, u32[]{:S(2)}, u32[]{:S(2)}) %collective-permute-start.39) | collective-permute-done | bytes 663584 | tf_op jit(solution)/shard_map/ppermute | solution.py:30
  349.5 2.0 add_convert_fusion.1
  351.5 1.5 collective-permute-start.40
  354.2 12.2 %conv_back.1 = (bf16[1024,576]{1,0:T(8,128)(2,1)S(1)}, f32[2,288,576]{2,1,0:T(8,128)}, bf16[2,288,576]{2,1,0:T(8,128)(2,1)S(1)}, f32[128,576]{1,0:T(8,128)S(1)},...) custom-call(s32[1]{0:T(128)} %bitcast.me_ref, s32[6]{0:T(128)S(1)} %copy-done.39, s32[1]{0:T(128)} %copy.54.length_ref, ...), custom_call_target="tpu_custom_call" | custom-call | flops 4000000000 | bytes 1048576 | tf_op jit(solution)/shard_map/conv_back/pallas_call | solution.py:742
  366.9 8.6 %project_back.1 = (f32[2,256,1152]{2,1,0:T(8,128)S(1)}, bf16[2,256,1152]{2,1,0:T(8,128)(2,1)}, f32[1,1152]{1,0:T(1,128)S(1)}) custom-call(s32[1]{0:T(128)} %bitcast.me_ref, s32[6]{0:T(128)S(1)} %copy-done.39, bf16[256,1152]{1,0:T(8,128)(2,1)} %get-tuple-element.72.rest_0_, bf16[256,1152]{1,0:T(8,128)(2,1)} %collective-permute-done.3.rest_1_, ...), custom_call_target="tpu_custom_call" | custom-call | flops 4000000000 | bytes 1048576 | tf_op jit(solution)/shard_map/project_back/pallas_call | solution.py:818
  376.5 2.4 add_convert_fusion
  378.9 1.6 collective-permute-start.44
  383.2 2.3 collective-permute-done.31
  388.2 1.6 add_add_fusion
  389.9 1.4 copy-done.55
  393.3 1.4 collective-permute-start.38
  395.5 2.8 concatenate.29
  400.1 1.4 dynamic-slice_bitcast_fusion.1.out_near_ref
  401.5 3.1 collective-permute-start.45
  404.6 1.6 add_add_fusion.1
  408.1 1.6 collective-permute-start.35
  410.6 2.2 collective-permute-done.36
  412.8 1.4 fusion.6
  414.3 1.4 fusion.7
  417.0 18.9 %collective-permute-done.35 = bf16[201,576]{1,0:T(8,128)(2,1)S(1)} collective-permute-done((bf16[201,576]{1,0:T(8,128)(2,1)S(1)}, bf16[201,576]{1,0:T(8,128)(2,1)S(1)}, u32[]{:S(2)}, u32[]{:S(2)}) %collective-permute-start.35) | collective-permute-done | bytes 231584 | tf_op jit(solution)/shard_map/ppermute | solution.py:30
  435.9 1.9 collective-permute-start.41
  438.0 1.7 add_bitcast_fusion
  440.9 3.4 finish_rows.1
  446.2 2.4 collective-permute-done.47
  453.8 4.1 collective-permute-start.46
  458.6 2.0 add_add_fusion.3
  460.9 1.6 reshape.260
  462.5 14.8 %collective-permute-done.46 = bf16[1,576,384]{2,1,0:T(8,128)(2,1)S(1)} collective-permute-done((bf16[1,576,384]{2,1,0:T(8,128)(2,1)S(1)}, bf16[1,576,384]{2,1,0:T(8,128)(2,1)S(1)}, u32[]{:S(2)}, u32[]{:S(2)}) %collective-permute-start.46) | collective-permute-done | bytes 442400 | tf_op jit(solution)/shard_map/ppermute | solution.py:1278
  (327 shorter events, 61.8 us)
Async XLA Ops:
  7.2 445.4 %reduce-scatter.2.cloned.1.call-start = ((), (), s32[]{:S(2)}) async-start(), calls=%async_computation.1 | async-start | bytes 7962624 | tf_op jit(solution)/shard_map/reduce_scatter | solution.py:1235
  11.1 23.5 %copy-start = (f32[256,1152]{1,0:T(8,128)S(1)}, f32[256,1152]{1,0:T(8,128)}, u32[]{:S(2)}) copy-start(f32[256,1152]{1,0:T(8,128)} %tokens_ref.5) | copy-start | bytes 3538948
  16.1 37.1 %copy-start.1 = (f32[256,1152]{1,0:T(8,128)S(1)}, f32[256,1152]{1,0:T(8,128)}, u32[]{:S(2)}) copy-start(f32[256,1152]{1,0:T(8,128)} %cot_ref.1) | copy-start | bytes 3538948
  16.1 22.6 %collective-permute-start.7 = (bf16[288,1152]{1,0:T(8,128)(2,1)}, bf16[288,1152]{1,0:T(8,128)(2,1)}, u32[]{:S(2)}, u32[]{:S(2)}) collective-permute-start(bf16[288,1152]{1,0:T(8,128)(2,1)} %get-tuple-element.75), channel_id=1, source_target_pairs={{0,2},{1,3},{2,0},{3,1},{4,7},{5,6},{6,5},{7,4},{8,10},{9,11},{10,... | collective-permute-start | bytes 1990664 | tf_op jit(solution)/shard_map/ppermute | solution.py:76
  18.6 39.2 %copy-start.73 = (bf16[4,576]{1,0:T(4,128)(2,1)S(1)}, bf16[4,576]{1,0:T(4,128)(2,1)}, u32[]{:S(2)}) copy-start(bf16[4,576]{1,0:T(4,128)(2,1)} %param.29) | copy-start | bytes 13828
  18.6 39.2 %copy-start.76 = (bf16[576]{0:T(1024)(128)(2,1)S(1)}, bf16[576]{0:T(1024)(128)(2,1)}, u32[]{:S(2)}) copy-start(bf16[576]{0:T(1024)(128)(2,1)} %param.30) | copy-start | bytes 3460
  18.7 2.2 collective-permute-start
  19.4 14.8 %collective-permute-start.1 = (f32[16,288]{1,0:T(8,128)S(1)}, f32[16,288]{1,0:T(8,128)S(1)}, u32[]{:S(2)}, u32[]{:S(2)}) collective-permute-start(f32[16,288]{1,0:T(8,128)S(1)} %concatenate.23.rest_0_), channel_id=1, source_target_pairs={{0,2},{1,3},{2,0},{3,1},{4,6},{5,7},{6,4},{7,5},{8,10},{9,11},{10,... | collective-permute-start | bytes 55304 | tf_op jit(solution)/shard_map/ppermute | solution.py:25
  19.9 14.6 %collective-permute-start.2 = (f32[16,288]{1,0:T(8,128)S(1)}, f32[16,288]{1,0:T(8,128)S(1)}, u32[]{:S(2)}, u32[]{:S(2)}) collective-permute-start(f32[16,288]{1,0:T(8,128)S(1)} %concatenate.23.rest_0_), channel_id=1, source_target_pairs={{0,3},{1,2},{2,1},{3,0},{4,7},{5,6},{6,5},{7,4},{8,11},{9,10},{10,... | collective-permute-start | bytes 55304 | tf_op jit(solution)/shard_map/ppermute | solution.py:25
  36.3 15.7 %collective-permute-start.4 = (bf16[256,1152]{1,0:T(8,128)(2,1)}, bf16[256,1152]{1,0:T(8,128)(2,1)}, u32[]{:S(2)}, u32[]{:S(2)}) collective-permute-start(bf16[256,1152]{1,0:T(8,128)(2,1)} %get-tuple-element.72.rest_0_), channel_id=1, source_target_pairs={{0,2},{1,3},{2,0},{3,1},{4,6},{5,7},{6,4},{7,5},{8,10},{9,11},{10,... | collective-permute-start | bytes 1769480 | tf_op jit(solution)/shard_map/ppermute | solution.py:25
  37.9 21.0 %collective-permute-start.6 = (bf16[288,1152]{1,0:T(8,128)(2,1)}, bf16[288,1152]{1,0:T(8,128)(2,1)}, u32[]{:S(2)}, u32[]{:S(2)}) collective-permute-start(bf16[288,1152]{1,0:T(8,128)(2,1)} %copy-done.48), channel_id=1, source_target_pairs={{0,1},{1,0},{2,3},{3,2},{4,5},{5,4},{6,7},{7,6},{8,9},{9,8},{10,11... | collective-permute-start | bytes 1990664 | tf_op jit(solution)/shard_map/ppermute | solution.py:25
  38.8 20.2 %collective-permute-start.8 = (bf16[288,1152]{1,0:T(8,128)(2,1)}, bf16[288,1152]{1,0:T(8,128)(2,1)}, u32[]{:S(2)}, u32[]{:S(2)}) collective-permute-start(bf16[288,1152]{1,0:T(8,128)(2,1)} %collective-permute-done.7.rest_6_), channel_id=1, source_target_pairs={{0,4},{4,0},{8,12},{12,8},{16,20},{20,16},{24,28},{28,24},{1,5},{5... | collective-permute-start | bytes 1990664 | tf_op jit(solution)/shard_map/ppermute | solution.py:77
  39.6 19.3 %collective-permute-start.3 = (bf16[256,1152]{1,0:T(8,128)(2,1)}, bf16[256,1152]{1,0:T(8,128)(2,1)}, u32[]{:S(2)}, u32[]{:S(2)}) collective-permute-start(bf16[256,1152]{1,0:T(8,128)(2,1)} %get-tuple-element.72.rest_0_), channel_id=1, source_target_pairs={{0,1},{1,0},{2,3},{3,2},{4,5},{5,4},{6,7},{7,6},{8,9},{9,8},{10,11... | collective-permute-start | bytes 1769480 | tf_op jit(solution)/shard_map/ppermute | solution.py:25
  52.0 6.9 %collective-permute-start.5 = (bf16[256,1152]{1,0:T(8,128)(2,1)}, bf16[256,1152]{1,0:T(8,128)(2,1)}, u32[]{:S(2)}, u32[]{:S(2)}) collective-permute-start(bf16[256,1152]{1,0:T(8,128)(2,1)} %collective-permute-done.4.rest_2_), channel_id=1, source_target_pairs={{0,1},{1,0},{2,3},{3,2},{4,5},{5,4},{6,7},{7,6},{8,9},{9,8},{10,11... | collective-permute-start | bytes 1769480 | tf_op jit(solution)/shard_map/ppermute | solution.py:25
  54.5 18.4 %collective-permute-start.10 = (bf16[256,1152]{1,0:T(8,128)(2,1)}, bf16[256,1152]{1,0:T(8,128)(2,1)}, u32[]{:S(2)}, u32[]{:S(2)}) collective-permute-start(bf16[256,1152]{1,0:T(8,128)(2,1)} %convolution_convert_fusion.rest_4_), channel_id=1, source_target_pairs={{0,2},{1,3},{2,0},{3,1},{4,6},{5,7},{6,4},{7,5},{8,10},{9,11},{10,... | collective-permute-start | bytes 1769480 | tf_op jit(solution)/shard_map/ppermute | solution.py:25
  72.7 2.0 collective-permute-start.9
  74.8 14.2 %collective-permute-start.11 = (f32[1024,128]{1,0:T(8,128)S(1)}, f32[1024,128]{1,0:T(8,128)S(1)}, u32[]{:S(2)}, u32[]{:S(2)}) collective-permute-start(f32[1024,128]{1,0:T(8,128)S(1)} %add_add_fusion.8), channel_id=1, source_target_pairs={{0,2},{1,3},{2,0},{3,1},{4,6},{5,7},{6,4},{7,5},{8,10},{9,11},{10,... | collective-permute-start | bytes 1572872 | tf_op jit(solution)/shard_map/ppermute | solution.py:25
  89.1 34.1 %copy-start.8 = (f32[1024,128]{1,0:T(8,128)}, f32[1024,128]{1,0:T(8,128)S(1)}, u32[]{:S(2)}) copy-start(f32[1024,128]{1,0:T(8,128)S(1)} %add.330.selected_ref.rest_0_) | copy-start | bytes 1572868
  90.5 35.6 %collective-permute-start.12 = (bf16[2,288,768]{2,1,0:T(8,128)(2,1)S(1)}, bf16[2,288,768]{2,1,0:T(8,128)(2,1)}, u32[]{:S(2)}, u32[]{:S(2)}) collective-permute-start(bf16[2,288,768]{2,1,0:T(8,128)(2,1)S(1)} %broadcast_add_fusion.1), channel_id=1, source_target_pairs={{0,2},{1,3},{2,0},{3,1},{4,7},{5,6},{6,5},{7,4},{8,10},{9,11},{10,... | collective-permute-start | bytes 2654216 | tf_op jit(solution)/shard_map/ppermute | solution.py:76
  90.6 32.6 %copy-start.20 = (bf16[128,576]{1,0:T(8,128)(2,1)}, bf16[128,576]{1,0:T(8,128)(2,1)S(1)}, u32[]{:S(2)}) copy-start(bf16[128,576]{1,0:T(8,128)(2,1)S(1)} %pad.9.weight_ref.rest_5_) | copy-start | bytes 442372
  90.8 32.5 %copy-start.26 = (f32[9,8,128]{2,1,0:T(8,128)}, f32[9,8,128]{2,1,0:T(8,128)S(1)}, u32[]{:S(2)}) copy-start(f32[9,8,128]{2,1,0:T(8,128)S(1)} %pad_maximum_fusion.rate_ref.rest_8_) | copy-start | bytes 110596
  129.1 3.2 collective-permute-start.13
  135.9 15.7 %collective-permute-start.14 = (bf16[256,1152]{1,0:T(8,128)(2,1)S(1)}, bf16[256,1152]{1,0:T(8,128)(2,1)S(1)}, u32[]{:S(2)}, u32[]{:S(2)}) collective-permute-start(bf16[256,1152]{1,0:T(8,128)(2,1)S(1)} %fusion.1), channel_id=1, source_target_pairs={{0,2},{1,3},{2,0},{3,1},{4,6},{5,7},{6,4},{7,5},{8,10},{9,11},{10,... | collective-permute-start | bytes 1769480 | tf_op jit(solution)/shard_map/ppermute | solution.py:25
  157.7 16.5 %collective-permute-start.16 = (bf16[256,1280]{1,0:T(8,128)(2,1)}, bf16[256,1280]{1,0:T(8,128)(2,1)}, u32[]{:S(2)}, u32[]{:S(2)}) collective-permute-start(bf16[256,1280]{1,0:T(8,128)(2,1)} %get-tuple-element.83.rest_0_), channel_id=1, source_target_pairs={{0,2},{1,3},{2,0},{3,1},{4,6},{5,7},{6,4},{7,5},{8,10},{9,11},{10,... | collective-permute-start | bytes 1966088 | tf_op jit(solution)/shard_map/ppermute | solution.py:25
  159.3 15.0 %collective-permute-start.18 = (bf16[256,1152]{1,0:T(8,128)(2,1)}, bf16[256,1152]{1,0:T(8,128)(2,1)S(1)}, u32[]{:S(2)}, u32[]{:S(2)}) collective-permute-start(bf16[256,1152]{1,0:T(8,128)(2,1)} %convolution_convert_fusion.rest_4_), channel_id=1, source_target_pairs={{0,1},{1,0},{2,3},{3,2},{4,5},{5,4},{6,7},{7,6},{8,9},{9,8},{10,11... | collective-permute-start | bytes 1769480 | tf_op jit(solution)/shard_map/ppermute | solution.py:25
  159.3 18.3 %collective-permute-start.20 = (bf16[2,288,768]{2,1,0:T(8,128)(2,1)}, bf16[2,288,768]{2,1,0:T(8,128)(2,1)}, u32[]{:S(2)}, u32[]{:S(2)}) collective-permute-start(bf16[2,288,768]{2,1,0:T(8,128)(2,1)} %get-tuple-element.85), channel_id=1, source_target_pairs={{0,1},{1,0},{2,3},{3,2},{4,5},{5,4},{6,7},{7,6},{8,9},{9,8},{10,11... | collective-permute-start | bytes 2654216 | tf_op jit(solution)/shard_map/ppermute | solution.py:25
  159.8 21.9 %collective-permute-start.21 = (bf16[2,288,768]{2,1,0:T(8,128)(2,1)}, bf16[2,288,768]{2,1,0:T(8,128)(2,1)}, u32[]{:S(2)}, u32[]{:S(2)}) collective-permute-start(bf16[2,288,768]{2,1,0:T(8,128)(2,1)} %collective-permute-done.12.rest_10_), channel_id=1, source_target_pairs={{0,4},{4,0},{8,12},{12,8},{16,20},{20,16},{24,28},{28,24},{1,5},{5... | collective-permute-start | bytes 2654216 | tf_op jit(solution)/shard_map/ppermute | solution.py:77
  159.8 21.9 %collective-permute-start.15 = (bf16[256,1280]{1,0:T(8,128)(2,1)}, bf16[256,1280]{1,0:T(8,128)(2,1)}, u32[]{:S(2)}, u32[]{:S(2)}) collective-permute-start(bf16[256,1280]{1,0:T(8,128)(2,1)} %get-tuple-element.83.rest_0_), channel_id=1, source_target_pairs={{0,1},{1,0},{2,3},{3,2},{4,5},{5,4},{6,7},{7,6},{8,9},{9,8},{10,11... | collective-permute-start | bytes 1966088 | tf_op jit(solution)/shard_map/ppermute | solution.py:25
  174.2 7.4 %collective-permute-start.17 = (bf16[256,1280]{1,0:T(8,128)(2,1)}, bf16[256,1280]{1,0:T(8,128)(2,1)}, u32[]{:S(2)}, u32[]{:S(2)}) collective-permute-start(bf16[256,1280]{1,0:T(8,128)(2,1)} %collective-permute-done.16.rest_2_), channel_id=1, source_target_pairs={{0,1},{1,0},{2,3},{3,2},{4,5},{5,4},{6,7},{7,6},{8,9},{9,8},{10,11... | collective-permute-start | bytes 1966088 | tf_op jit(solution)/shard_map/ppermute | solution.py:25
  175.1 2.5 collective-permute-start.19
  220.0 3.3 collective-permute-start.22
  225.5 16.8 %collective-permute-start.23 = (bf16[256,1280]{1,0:T(8,128)(2,1)S(1)}, bf16[256,1280]{1,0:T(8,128)(2,1)S(1)}, u32[]{:S(2)}, u32[]{:S(2)}) collective-permute-start(bf16[256,1280]{1,0:T(8,128)(2,1)S(1)} %fusion), channel_id=1, source_target_pairs={{0,2},{1,3},{2,0},{3,1},{4,6},{5,7},{6,4},{7,5},{8,10},{9,11},{10,... | collective-permute-start | bytes 1966088 | tf_op jit(solution)/shard_map/ppermute | solution.py:25
  242.4 19.7 %copy-start.38 = (s32[6]{0:T(128)S(1)}, s32[6]{0:T(128)}, u32[]{:S(2)}) copy-start(s32[6]{0:T(128)} %copy-done.37) | copy-start | bytes 76
  245.4 14.6 %collective-permute-start.25 = (bf16[256,1152]{1,0:T(8,128)(2,1)S(1)}, bf16[256,1152]{1,0:T(8,128)(2,1)S(1)}, u32[]{:S(2)}, u32[]{:S(2)}) collective-permute-start(bf16[256,1152]{1,0:T(8,128)(2,1)S(1)} %get-tuple-element.91.rest_4_), channel_id=1, source_target_pairs={{0,2},{1,3},{2,0},{3,1},{4,6},{5,7},{6,4},{7,5},{8,10},{9,11},{10,... | collective-permute-start | bytes 1769480 | tf_op jit(solution)/shard_map/ppermute | solution.py:25
  245.9 14.2 %collective-permute-start.24 = (bf16[256,1152]{1,0:T(8,128)(2,1)S(1)}, bf16[256,1152]{1,0:T(8,128)(2,1)S(1)}, u32[]{:S(2)}, u32[]{:S(2)}) collective-permute-start(bf16[256,1152]{1,0:T(8,128)(2,1)S(1)} %get-tuple-element.91.rest_4_), channel_id=1, source_target_pairs={{0,1},{1,0},{2,3},{3,2},{4,5},{5,4},{6,7},{7,6},{8,9},{9,8},{10,11... | collective-permute-start | bytes 1769480 | tf_op jit(solution)/shard_map/ppermute | solution.py:25
  260.1 2.0 collective-permute-start.26
  275.6 51.9 %copy-start.43 = (bf16[2,288,576]{2,1,0:T(8,128)(2,1)}, bf16[2,288,576]{2,1,0:T(8,128)(2,1)S(1)}, u32[]{:S(2)}) copy-start(bf16[2,288,576]{2,1,0:T(8,128)(2,1)S(1)} %get-tuple-element.126) | copy-start | bytes 1990660
  275.6 51.8 %copy-start.44 = (bf16[2,288,576]{2,1,0:T(8,128)(2,1)}, bf16[2,288,576]{2,1,0:T(8,128)(2,1)S(1)}, u32[]{:S(2)}) copy-start(bf16[2,288,576]{2,1,0:T(8,128)(2,1)S(1)} %get-tuple-element.124) | copy-start | bytes 1990660
  328.9 5.5 %collective-permute-start.27 = (f32[1024,128]{1,0:T(8,128)}, f32[1024,128]{1,0:T(8,128)}, u32[]{:S(2)}, u32[]{:S(2)}) collective-permute-start(f32[1024,128]{1,0:T(8,128)} %get-tuple-element.97), channel_id=1, source_target_pairs={{0,1},{1,0},{2,3},{3,2},{4,5},{5,4},{6,7},{7,6},{8,9},{9,8},{10,11... | collective-permute-start | bytes 1572872 | tf_op jit(solution)/shard_map/ppermute | solution.py:25
  328.9 59.3 %collective-permute-start.34 = (bf16[2,256,1152]{2,1,0:T(8,128)(2,1)}, bf16[2,256,1152]{2,1,0:T(8,128)(2,1)}, u32[]{:S(2)}, u32[]{:S(2)}) collective-permute-start(bf16[2,256,1152]{2,1,0:T(8,128)(2,1)} %get-tuple-element.119), channel_id=1, source_target_pairs={{0,1},{1,0},{2,3},{3,2},{4,5},{5,4},{6,7},{7,6},{8,9},{9,8},{10,11... | collective-permute-start | bytes 3538952 | tf_op jit(solution)/shard_map/ppermute | solution.py:25
  330.8 18.7 %collective-permute-start.39 = (bf16[2,288,576]{2,1,0:T(8,128)(2,1)}, bf16[2,288,576]{2,1,0:T(8,128)(2,1)}, u32[]{:S(2)}, u32[]{:S(2)}) collective-permute-start(bf16[2,288,576]{2,1,0:T(8,128)(2,1)} %copy-done.44), channel_id=1, source_target_pairs={{0,4},{4,0},{8,12},{12,8},{16,20},{20,16},{24,28},{28,24},{1,5},{5... | collective-permute-start | bytes 1990664 | tf_op jit(solution)/shard_map/ppermute | solution.py:30
  332.9 43.6 %collective-permute-start.43 = (bf16[2,288,576]{2,1,0:T(8,128)(2,1)}, bf16[2,288,576]{2,1,0:T(8,128)(2,1)}, u32[]{:S(2)}, u32[]{:S(2)}) collective-permute-start(bf16[2,288,576]{2,1,0:T(8,128)(2,1)} %copy-done.43), channel_id=1, source_target_pairs={{0,8},{4,12},{8,0},{12,4},{16,24},{20,28},{24,16},{28,20},{1,9},{5... | collective-permute-start | bytes 1990664 | tf_op jit(solution)/shard_map/ppermute | solution.py:30
  335.7 18.5 %copy-start.29 = (bf16[576,128]{1,0:T(8,128)(2,1)S(1)}, bf16[576,128]{1,0:T(8,128)(2,1)}, u32[]{:S(2)}) copy-start(bf16[576,128]{1,0:T(8,128)(2,1)} %copy-done.28) | copy-start | bytes 442372
  335.7 17.3 %collective-permute-start.28 = (f32[1024,128]{1,0:T(8,128)S(1)}, f32[1024,128]{1,0:T(8,128)}, u32[]{:S(2)}, u32[]{:S(2)}) collective-permute-start(f32[1024,128]{1,0:T(8,128)S(1)} %add.340), channel_id=1, source_target_pairs={{0,2},{1,3},{2,0},{3,1},{4,6},{5,7},{6,4},{7,5},{8,10},{9,11},{10,... | collective-permute-start | bytes 1572872 | tf_op jit(solution)/shard_map/ppermute | solution.py:25
  351.5 58.8 %collective-permute-start.40 = (bf16[1,288,576]{2,1,0:T(8,128)(2,1)}, bf16[1,288,576]{2,1,0:T(8,128)(2,1)}, u32[]{:S(2)}, u32[]{:S(2)}) collective-permute-start(bf16[1,288,576]{2,1,0:T(8,128)(2,1)} %add_convert_fusion.1), channel_id=1, source_target_pairs={{0,8},{4,12},{8,0},{12,4},{16,24},{20,28},{24,16},{28,20},{1,9},{5... | collective-permute-start | bytes 995336 | tf_op jit(solution)/shard_map/ppermute | solution.py:30
  366.4 19.1 %collective-permute-start.31 = (bf16[2,288,576]{2,1,0:T(8,128)(2,1)S(1)}, bf16[2,288,576]{2,1,0:T(8,128)(2,1)S(1)}, u32[]{:S(2)}, u32[]{:S(2)}) collective-permute-start(bf16[2,288,576]{2,1,0:T(8,128)(2,1)S(1)} %get-tuple-element.115), channel_id=1, source_target_pairs={{0,4},{4,0},{8,12},{12,8},{16,20},{20,16},{24,28},{28,24},{1,5},{5... | collective-permute-start | bytes 1990664 | tf_op jit(solution)/shard_map/ppermute | solution.py:30
  376.4 6.6 %collective-permute-start.29 = (f32[4,1152]{1,0:T(4,128)S(1)}, f32[4,1152]{1,0:T(4,128)S(1)}, u32[]{:S(2)}, u32[]{:S(2)}) collective-permute-start(f32[4,1152]{1,0:T(4,128)S(1)} %pad_maximum_fusion.1), channel_id=1, source_target_pairs={{0,1},{1,0},{2,3},{3,2},{4,5},{5,4},{6,7},{7,6},{8,9},{9,8},{10,11... | collective-permute-start | bytes 55304 | tf_op jit(solution)/shard_map/ppermute | solution.py:25
  378.9 19.5 %collective-permute-start.44 = (bf16[2,1,144,576]{3,2,1,0:T(8,128)(2,1)}, bf16[2,1,144,576]{3,2,1,0:T(8,128)(2,1)}, u32[]{:S(2)}, u32[]{:S(2)}) collective-permute-start(bf16[2,1,144,576]{3,2,1,0:T(8,128)(2,1)} %get-tuple-element.139), channel_id=1, source_target_pairs={{0,4},{4,0},{8,12},{12,8},{16,20},{20,16},{24,28},{28,24},{1,5},{5... | collective-permute-start | bytes 995336 | tf_op jit(solution)/shard_map/ppermute | solution.py:30
  383.0 18.5 %collective-permute-start.33 = (bf16[2,256,1152]{2,1,0:T(8,128)(2,1)}, bf16[2,256,1152]{2,1,0:T(8,128)(2,1)}, u32[]{:S(2)}, u32[]{:S(2)}) collective-permute-start(bf16[2,256,1152]{2,1,0:T(8,128)(2,1)} %get-tuple-element.116), channel_id=1, source_target_pairs={{0,1},{1,0},{2,3},{3,2},{4,5},{5,4},{6,7},{7,6},{8,9},{9,8},{10,11... | collective-permute-start | bytes 3538952 | tf_op jit(solution)/shard_map/ppermute | solution.py:25
  385.5 9.9 %collective-permute-start.30 = (f32[4,1152]{1,0:T(4,128)S(1)}, f32[4,1152]{1,0:T(4,128)S(1)}, u32[]{:S(2)}, u32[]{:S(2)}) collective-permute-start(f32[4,1152]{1,0:T(4,128)S(1)} %fusion.20), channel_id=1, source_target_pairs={{0,2},{1,3},{2,0},{3,1},{4,6},{5,7},{6,4},{7,5},{8,10},{9,11},{10,... | collective-permute-start | bytes 55304 | tf_op jit(solution)/shard_map/ppermute | solution.py:25
  393.3 47.6 %collective-permute-start.38 = (bf16[256,1152]{1,0:T(8,128)(2,1)}, bf16[256,1152]{1,0:T(8,128)(2,1)}, u32[]{:S(2)}, u32[]{:S(2)}) collective-permute-start(bf16[256,1152]{1,0:T(8,128)(2,1)} %fusion.3), channel_id=1, source_target_pairs={{0,2},{1,3},{2,0},{3,1},{4,6},{5,7},{6,4},{7,5},{8,10},{9,11},{10,... | collective-permute-start | bytes 1769480 | tf_op jit(solution)/shard_map/ppermute | solution.py:25
  398.4 9.1 %collective-permute-start.32 = (bf16[201,576]{1,0:T(8,128)(2,1)S(1)}, bf16[201,576]{1,0:T(8,128)(2,1)S(1)}, u32[]{:S(2)}, u32[]{:S(2)}) collective-permute-start(bf16[201,576]{1,0:T(8,128)(2,1)S(1)} %concatenate.29), channel_id=1, source_target_pairs={{0,4},{4,0},{8,12},{12,8},{16,20},{20,16},{24,28},{28,24},{1,5},{5... | collective-permute-start | bytes 694664 | tf_op jit(solution)/shard_map/ppermute | solution.py:30
  398.5 14.4 %collective-permute-start.36 = (bf16[1,288,576]{2,1,0:T(8,128)(2,1)}, bf16[1,288,576]{2,1,0:T(8,128)(2,1)S(1)}, u32[]{:S(2)}, u32[]{:S(2)}) collective-permute-start(bf16[1,288,576]{2,1,0:T(8,128)(2,1)} %get-tuple-element.141), channel_id=1, source_target_pairs={{0,8},{4,12},{8,0},{12,4},{16,24},{20,28},{24,16},{28,20},{1,9},{5... | collective-permute-start | bytes 995336 | tf_op jit(solution)/shard_map/ppermute | solution.py:30
  401.5 36.4 %collective-permute-start.45 = (bf16[1,1,144,576]{3,2,1,0:T(8,128)(2,1)S(1)}, bf16[1,1,144,576]{3,2,1,0:T(8,128)(2,1)S(1)}, u32[]{:S(2)}, u32[]{:S(2)}) collective-permute-start(bf16[1,1,144,576]{3,2,1,0:T(8,128)(2,1)S(1)} %add_convert_fusion.6), channel_id=1, source_target_pairs={{0,16},{4,20},{8,24},{12,28},{16,0},{20,4},{24,8},{28,12},{1,17},{... | collective-permute-start | bytes 497672 | tf_op jit(solution)/shard_map/ppermute | solution.py:30
  408.1 27.8 %collective-permute-start.35 = (bf16[201,576]{1,0:T(8,128)(2,1)S(1)}, bf16[201,576]{1,0:T(8,128)(2,1)S(1)}, u32[]{:S(2)}, u32[]{:S(2)}) collective-permute-start(bf16[201,576]{1,0:T(8,128)(2,1)S(1)} %add_convert_fusion.4), channel_id=1, source_target_pairs={{0,8},{4,12},{8,0},{12,4},{16,24},{20,28},{24,16},{28,20},{1,9},{5... | collective-permute-start | bytes 694664 | tf_op jit(solution)/shard_map/ppermute | solution.py:30
  410.3 30.6 %collective-permute-start.37 = (bf16[256,1152]{1,0:T(8,128)(2,1)S(1)}, bf16[256,1152]{1,0:T(8,128)(2,1)S(1)}, u32[]{:S(2)}, u32[]{:S(2)}) collective-permute-start(bf16[256,1152]{1,0:T(8,128)(2,1)S(1)} %fusion.2), channel_id=1, source_target_pairs={{0,2},{1,3},{2,0},{3,1},{4,6},{5,7},{6,4},{7,5},{8,10},{9,11},{10,... | collective-permute-start | bytes 1769480 | tf_op jit(solution)/shard_map/ppermute | solution.py:25
  414.3 23.6 %copy-start.58 = (f32[2,1,144,576]{3,2,1,0:T(8,128)S(1)}, f32[2,1,144,576]{3,2,1,0:T(8,128)}, u32[]{:S(2)}) copy-start(f32[2,1,144,576]{3,2,1,0:T(8,128)} %get-tuple-element.140) | copy-start | bytes 1990660
  415.7 25.2 %copy-start.11 = (bf16[256,256]{1,0:T(8,128)(2,1)S(1)}, bf16[256,256]{1,0:T(8,128)(2,1)}, u32[]{:S(2)}) copy-start(bf16[256,256]{1,0:T(8,128)(2,1)} %copy-done.10) | copy-start | bytes 393220
  415.7 25.2 %copy-start.15 = (f32[256,1152]{1,0:T(8,128)S(1)}, f32[256,1152]{1,0:T(8,128)}, u32[]{:S(2)}) copy-start(f32[256,1152]{1,0:T(8,128)} %copy-done.14) | copy-start | bytes 3538948
  415.7 25.2 %copy-start.19 = (f32[16,1152]{1,0:T(8,128)S(1)}, f32[16,1152]{1,0:T(8,128)}, u32[]{:S(2)}) copy-start(f32[16,1152]{1,0:T(8,128)} %copy-done.16) | copy-start | bytes 221188
  416.9 41.6 %collective-permute-start.42 = (bf16[288,576]{1,0:T(8,128)(2,1)S(1)}, bf16[288,576]{1,0:T(8,128)(2,1)S(1)}, u32[]{:S(2)}, u32[]{:S(2)}) collective-permute-start(bf16[288,576]{1,0:T(8,128)(2,1)S(1)} %fusion.7), channel_id=1, source_target_pairs={{0,16},{1,20},{2,24},{3,28},{4,17},{5,21},{6,25},{7,29},{8,18},{9,... | collective-permute-start | bytes 995336 | tf_op jit(solution)/shard_map/ppermute | solution.py:1341
  435.9 22.7 %collective-permute-start.41 = (bf16[288,576]{1,0:T(8,128)(2,1)S(1)}, bf16[288,576]{1,0:T(8,128)(2,1)}, u32[]{:S(2)}, u32[]{:S(2)}) collective-permute-start(bf16[288,576]{1,0:T(8,128)(2,1)S(1)} %get-tuple-element.134), channel_id=1, source_target_pairs={{0,0},{1,4},{2,8},{3,12},{4,1},{5,5},{6,9},{7,13},{8,2},{9,6},{10,... | collective-permute-start | bytes 995336 | tf_op jit(solution)/shard_map/ppermute | solution.py:1340
  437.9 10.7 %collective-permute-start.47 = (bf16[201,576]{1,0:T(8,128)(2,1)S(1)}, bf16[201,576]{1,0:T(8,128)(2,1)S(1)}, u32[]{:S(2)}, u32[]{:S(2)}) collective-permute-start(bf16[201,576]{1,0:T(8,128)(2,1)S(1)} %add_convert_fusion.3), channel_id=1, source_target_pairs={{0,16},{4,20},{8,24},{12,28},{16,0},{20,4},{24,8},{28,12},{1,17},{... | collective-permute-start | bytes 694664 | tf_op jit(solution)/shard_map/ppermute | solution.py:30
  453.8 23.5 %collective-permute-start.46 = (bf16[1,576,384]{2,1,0:T(8,128)(2,1)S(1)}, bf16[1,576,384]{2,1,0:T(8,128)(2,1)S(1)}, u32[]{:S(2)}, u32[]{:S(2)}) collective-permute-start(bf16[1,576,384]{2,1,0:T(8,128)(2,1)S(1)} %get-tuple-element.144), channel_id=1, source_target_pairs={{0,0},{1,8},{2,16},{3,24},{4,1},{5,9},{6,17},{7,25},{8,2},{9,10},{... | collective-permute-start | bytes 1327112 | tf_op jit(solution)/shard_map/ppermute | solution.py:1278
  (68 other events, 455.3 us)
Sparse Core Ops, SparseCore 0:
  220.1 137.0 reduce-scatter.1

commit v4 on v3

--- a/solution.py
+++ b/solution.py
@@ -11,7 +11,7 @@
 E = 2
 CAP = 192
 EPSILON = 1e-05
-FTILE = 256
+FTILE = 768
 LOG2E = 1.4426950408889634
 
 NS = 16
@@ -585,7 +585,7 @@
     (
         gate_ref, mixed_ref, gated_ref, project_ref,
         mix_out, gate_out, gate_held, gate_given, out_held, out_given,
-        normed, grads, gate_sum, out_sum, sems,
+        normed, grads, lows, product, sems,
     ) = rest
     block = pl.program_id(0)
     rows, width = normed_refs[0].shape
@@ -601,8 +601,6 @@
             copies.append(pltpu.make_async_copy(grad_refs[k], grads.at[at], sems.at[parts + k]))
         for copy in copies:
             copy.start()
-        gate_sum[...] = jnp.zeros_like(gate_sum)
-        out_sum[...] = jnp.zeros_like(out_sum)
         for copy in copies:
             copy.wait()
 
@@ -614,21 +612,22 @@
     mix_out[...] = grad_gated * (gate * curve)
     low = (grad_gated * mixed_ref[...] * (curve * (1.0 + gate * (1.0 - curve)))).astype(jnp.bfloat16)
     gate_out[...] = low
-    gate_sum[...] += t_dot(normed[at], low)
-    out_sum[...] += t_dot(grad, gated_ref[...])
+    lows[at] = low
 
     @pl.when(block == parts - 1)
     def finish():
+        product[...] = t_dot(normed[...], lows[...])
         for h in range(parts // 2):
             at = pl.ds(pl.multiple_of((2 * h + odd) * slab, 8), slab)
-            gate_held[h] = gate_sum[at]
+            gate_held[h] = product[at]
             at = pl.ds(pl.multiple_of((2 * h + 1 - odd) * slab, 8), slab)
-            gate_given[h] = gate_sum[at].astype(jnp.bfloat16)
+            gate_given[h] = product[at].astype(jnp.bfloat16)
+        product[...] = t_dot(grads[...], gated_ref[...])
         for h in range(width // (2 * pair)):
             at = pl.ds(pl.multiple_of((2 * h + second) * pair, 8), pair)
-            out_held[h] = out_sum[at]
+            out_held[h] = product[at]
             at = pl.ds(pl.multiple_of((2 * h + 1 - second) * pair, 8), pair)
-            out_given[h] = out_sum[at].astype(jnp.bfloat16)
+            out_given[h] = product[at].astype(jnp.bfloat16)
 
 
 def gate_back(me, source, normed_pieces, grad_pieces, zgate, mixed, gated, out_weight, pair):
@@ -645,7 +644,7 @@
     return pl.pallas_call(
         functools.partial(gate_back_kernel, parts, pair),
         grid=(parts,),
-        in_specs=[smem] * 2 + [anywhere] * (2 * parts) + [row] * 3 + [vmem],
+        in_specs=[smem] * 2 + [anywhere] * (2 * parts) + [row] * 2 + [vmem] * 2,
         out_specs=[row] * 2 + [vmem] * 4,
         out_shape=[
             jax.ShapeDtypeStruct((total, inside), f32),
@@ -658,7 +657,7 @@
         scratch_shapes=[
             pltpu.VMEM((total, width), bf16),
             pltpu.VMEM((total, width), bf16),
-            pltpu.VMEM((width, inside), f32),
+            pltpu.VMEM((total, inside), bf16),
             pltpu.VMEM((width, inside), f32),
             pltpu.SemaphoreType.DMA((2 * parts,)),
         ],
@@ -673,7 +672,7 @@
     (
         selected_ref, conv_ref, summed_ref, inner_ref, low_ref, taps_ref, select_ref,
         inner_out, inner_held, inner_given, select_out, taps_out, bias_out,
-        normed, shifted, total, sems,
+        normed, shifted, lows, total, sems,
     ) = rest
     index = pl.program_id(0)
     block = parts - 1 - index
@@ -691,7 +690,6 @@
         for k in range(parts):
             fetched(k).start()
         shifted[rows:] = jnp.zeros((8, inside), jnp.float32)
-        total[...] = jnp.zeros_like(total)
         select_out[...] = jnp.zeros_like(select_out)
         taps_out[...] = jnp.zeros_like(taps_out)
         bias_out[...] = jnp.zeros_like(bias_out)
@@ -714,15 +712,13 @@
     low = jnp.where(live, grad_inner, 0.0).astype(jnp.bfloat16)
     inner_out[...] = low
 
-    @pl.when(index == 0)
-    def arrive():
+    lows[pl.ds(pl.multiple_of(block * rows, rows), rows)] = low
+
+    @pl.when(block == 0)
+    def finish():
         for k in range(parts):
             fetched(k).wait()
-
-    total[...] += t_dot(normed[pl.ds(pl.multiple_of(block * rows, rows), rows)], low)
-
-    @pl.when(block == 0)
-    def finish():
+        total[...] = t_dot(normed[...], lows[...])
         for h in range(parts // 2):
             at = pl.ds(pl.multiple_of((2 * h + odd) * slab, 8), slab)
             inner_held[h] = total[at]
@@ -759,6 +755,7 @@
         scratch_shapes=[
             pltpu.VMEM((total, width), bf16),
             pltpu.VMEM((rows + 8, inside), f32),
+            pltpu.VMEM((total, inside), bf16),
             pltpu.VMEM((width, inside), f32),
             pltpu.SemaphoreType.DMA((parts,)),
         ],
@@ -925,16 +922,25 @@
     count = parts * cap
     me = me_ref[0]
 
+    def weights(e):
+        base = 2 * parts + e * (parts + 1)
+        copies = [pltpu.make_async_copy(down_ref.at[e], down.at[e], sems.at[base])]
+        for k in range(parts):
+            at = pl.ds(pl.multiple_of(source_ref[k] * slab, 16), slab)
+            copies.append(pltpu.make_async_copy(up_refs[k].at[e], up.at[e, at], sems.at[base + 1 + k]))
+        return copies
+
     @pl.when(step == 0)
     def fetch():
-        copies = [pltpu.make_async_copy(down_ref, down, sems.at[0])]
+        copies = []
         for k in range(parts):
-            copies.append(pltpu.make_async_copy(sent_refs[k], rows.at[me ^ k], sems.at[1 + k]))
-            copies.append(pltpu.make_async_copy(cot_refs[k], cots.at[me ^ k], sems.at[1 + parts + k]))
-            at = pl.ds(pl.multiple_of(source_ref[k] * slab, 16), slab)
-            copies.append(pltpu.make_async_copy(up_refs[k], up.at[:, at], sems.at[1 + 2 * parts + k]))
+            copies.append(pltpu.make_async_copy(sent_refs[k], rows.at[me ^ k], sems.at[k]))
+            copies.append(pltpu.make_async_copy(cot_refs[k], cots.at[me ^ k], sems.at[parts + k]))
         for copy in copies:
             copy.start()
+        for e in range(2):
+            for copy in weights(e):
+                copy.start()
         grad_sum[...] = jnp.zeros_like(grad_sum)
         out_sum[...] = jnp.zeros_like(out_sum)
         dots[...] = jnp.zeros_like(dots)
@@ -957,6 +963,12 @@
             later = slot + offset >= counts_ref[b]
             live = jnp.where(expert == 0, first.astype(jnp.float32), later.astype(jnp.float32))
             scale[b * cap : (b + 1) * cap] = live * gate
+        for e in range(2):
+
+            @pl.when(expert == e)
+            def arrive():
+                for copy in weights(e):
+                    copy.wait()
 
     columns = pl.ds(pl.multiple_of(tile * FTILE, FTILE), FTILE)
     up_tile = up[expert, :, columns]
@@ -1047,7 +1059,7 @@
             pltpu.VMEM((parts, span, width), f32),
             pltpu.VMEM((parts, span, width), f32),
             pltpu.VMEM((width, FTILE), f32),
-            pltpu.SemaphoreType.DMA((1 + 3 * parts,)),
+            pltpu.SemaphoreType.DMA((2 * parts + 2 * (parts + 1),)),
         ],
         compiler_params=pltpu.CompilerParams(vmem_limit_bytes=60 * 2**20),
         cost_estimate=pl.CostEstimate(flops=4 * 10**9, bytes_accessed=2**20, transcendentals=0),

time: 487 us -> 487 us (level); the launches traced: 485 us -> 478 us
  Pallas kernels: 177 us -> 169 us
    pallas_call x1, Pallas kernels: 38.3 us -> 30.9 us  [experts(): pl.pallas_call(functools.partial(expert_kernel, parts, CAP, steps), grid=...]
where the time goes in v4:
time: 487 us; the launch traced here: 478 us
  Pallas kernels  169 us (35%)
  waiting for transfers between devices  160 us (33%)
  local copies, waits for them, and re-layouts  55.4 us (11%)
  starting transfers between devices  33.8 us (7%)
  other arithmetic  33.6 us (7%)
  between operations  25 us (5%)
    ppermute x31, waiting for transfers between devices, swap(): return lax.ppermute(value, 'shard', [(i, i ^ bit) for i in range(size)])  104 us
    pallas_call x1, Pallas kernels, mixer_back(): pl.pallas_call(functools.partial(mixer_back_kernel, tiles), grid=(steps,)...  51.8 us
    ppermute x10, waiting for transfers between devices, swap_groups(): return lax.ppermute(value, 'grp', [(g, g ^ bit) for g in range(size)])  37.3 us
    pallas_call x1, Pallas kernels, mixer(): pl.pallas_call(functools.partial(mixer_kernel, tiles, share), grid=(total...  32.2 us
    pallas_call x1, Pallas kernels, experts(): pl.pallas_call(functools.partial(expert_kernel, parts, CAP, steps), grid=...  30.9 us
    unnamed x169, local copies, waits for them, and re-layouts  28 us
    ppermute x31, starting transfers between devices, swap(): return lax.ppermute(value, 'shard', [(i, i ^ bit) for i in range(size)])  15.8 us
    ppermute x1, waiting for transfers between devices, body(): lax.ppermute(tie(up_sum, chip_selected), both_axes, [(g * parts + s, up_h...  14.7 us
  transfers between devices with their start and end apart: 49, of which 18 were waited for; matrix products, arithmetic and copies ran while one was open for 12% of the time, Pallas kernels for 28%

profile of v4, /device:TPU:2, one launch (start us, length us, event | category | flops | bytes accessed | tf_op | source)
XLA Modules:
  0.0 478.2 jit_solution(12104099805026573696)
XLA Ops:
  7.3 2.0 copy-done.2
  9.3 1.7 copy-done.3
  11.1 2.4 cut_weights.1
  20.8 13.3 %collective-permute-done.1.rest_2_ = f32[16,288]{1,0:T(8,128)S(1)} collective-permute-done((f32[16,288]{1,0:T(8,128)S(1)}, f32[16,288]{1,0:T(8,128)S(1)}, u32[]{:S(2)}, u32[]{:S(2)}) %collective-permute-start.1) | collective-permute-done | bytes 18464 | tf_op jit(solution)/shard_map/ppermute | solution.py:25
  36.3 1.6 collective-permute-start.4
  40.2 11.8 %collective-permute-done.4.rest_2_ = bf16[256,1152]{1,0:T(8,128)(2,1)} collective-permute-done((bf16[256,1152]{1,0:T(8,128)(2,1)}, bf16[256,1152]{1,0:T(8,128)(2,1)}, u32[]{:S(2)}, u32[]{:S(2)}) %collective-permute-start.4) | collective-permute-done | bytes 589856 | tf_op jit(solution)/shard_map/ppermute | solution.py:25
  54.5 1.6 collective-permute-start.10
  56.1 1.7 copy.41
  60.0 10.1 %project.1 = (f32[1024,576]{1,0:T(8,128)S(1)}, f32[1024,576]{1,0:T(8,128)S(1)}, f32[1024,576]{1,0:T(8,128)}, f32[1024,576]{1,0:T(8,128)}, bf16[1024,576]{1,0:T(8,128)(2,1)S(1)}, /*index=5*/f32[1024,128]{1,0:T(8,128)S(1)}) custom-call(s32[1]{0:T(128)} %bitcast.me_ref, s32[6]{0:T(128)S(1)} %stack.26.source_ref, s32[1]{0:T(128)} %copy.54.length_ref, ...), custom_call_target="tpu_custom_call" | custom-call | flops 4000000000 | bytes 1048576 | tf_op jit(solution)/shard_map/project/pallas_call | solution.py:365
  70.1 1.5 copy-done.51
  75.4 13.6 %collective-permute-done.11 = f32[1024,128]{1,0:T(8,128)S(1)} collective-permute-done((f32[1024,128]{1,0:T(8,128)S(1)}, f32[1024,128]{1,0:T(8,128)S(1)}, u32[]{:S(2)}, u32[]{:S(2)}) %collective-permute-start.11) | collective-permute-done | bytes 524320 | tf_op jit(solution)/shard_map/ppermute | solution.py:25
  91.0 32.2 %mixer.1 = (f32[1024,9,8,128]{3,2,1,0:T(8,128)}, f32[9,8,128]{2,1,0:T(8,128)S(1)}, f32[1024,576]{1,0:T(8,128)S(1)}, bf16[1024,576]{1,0:T(8,128)(2,1)S(1)}, f32[2...) custom-call(s32[1]{0:T(128)} %bitcast.me_ref, s32[1]{0:T(128)} %copy.54.length_ref, ...), custom_call_target="tpu_custom_call" | custom-call | flops 4000000000 | bytes 1048576 | tf_op jit(solution)/shard_map/mixer/pallas_call | solution.py:466
  123.2 1.4 copy-done.7
  124.6 1.5 copy-done.50
  129.5 2.8 collective-permute-done.13
  132.3 2.2 convert_add_fusion.1
  134.5 1.4 copy-done.56
  135.9 1.6 collective-permute-start.14
  138.4 1.4 dynamic-slice_bitcast_fusion.3.near_ref
  139.8 11.8 %collective-permute-done.14.got_ref = bf16[256,1152]{1,0:T(8,128)(2,1)S(1)} collective-permute-done((bf16[256,1152]{1,0:T(8,128)(2,1)S(1)}, bf16[256,1152]{1,0:T(8,128)(2,1)S(1)}, u32[]{:S(2)}, u32[]{:S(2)}) %collective-permute-start.14) | collective-permute-done | bytes 589856 | tf_op jit(solution)/shard_map/ppermute | solution.py:25
  154.4 1.9 route.1
  157.7 1.5 collective-permute-start.16
  159.8 14.4 %collective-permute-done.16.rest_2_ = bf16[256,1280]{1,0:T(8,128)(2,1)} collective-permute-done((bf16[256,1280]{1,0:T(8,128)(2,1)}, bf16[256,1280]{1,0:T(8,128)(2,1)}, u32[]{:S(2)}, u32[]{:S(2)}) %collective-permute-start.16) | collective-permute-done | bytes 655392 | tf_op jit(solution)/shard_map/ppermute | solution.py:25
  177.6 4.0 collective-permute-done.21.rest_11_
  181.7 30.9 %experts.1 = (f32[2,256,1280]{2,1,0:T(8,128)}, bf16[2,256,1280]{2,1,0:T(8,128)(2,1)}, f32[2,256,1152]{2,1,0:T(8,128)}, bf16[2,256,1152]{2,1,0:T(8,128)(2,1)}, bf16[2,4,1152,384]{3,2,1,0:T(8,128)(2,1)}) custom-call(s32[1]{0:T(128)} %bitcast.me_ref, s32[6]{0:T(128)} %copy-done.37, s32[4]{0:T(128)} %bitcast.101, bf16[256,1280]{1,0:T(8,128)(2,1)} %get-tuple-element.83.rest_0_, ...), custom_call_target="tpu_custom_call" | custom-call | flops 4000000000 | bytes 1048576 | tf_op jit(solution)/shard_map/experts/pallas_call | solution.py:1038
  212.7 3.2 collective-permute-done.22
  215.9 2.1 convert_add_fusion
  218.9 16.1 %collective-permute-done.23.got_ref = bf16[256,1280]{1,0:T(8,128)(2,1)S(1)} collective-permute-done((bf16[256,1280]{1,0:T(8,128)(2,1)S(1)}, bf16[256,1280]{1,0:T(8,128)(2,1)S(1)}, u32[]{:S(2)}, u32[]{:S(2)}) %collective-permute-start.23) | collective-permute-done | bytes 655392 | tf_op jit(solution)/shard_map/ppermute | solution.py:25
  235.0 1.4 return_rows.1
  238.6 14.2 %collective-permute-done.25.rest_6_ = bf16[256,1152]{1,0:T(8,128)(2,1)S(1)} collective-permute-done((bf16[256,1152]{1,0:T(8,128)(2,1)S(1)}, bf16[256,1152]{1,0:T(8,128)(2,1)S(1)}, u32[]{:S(2)}, u32[]{:S(2)}) %collective-permute-start.25) | collective-permute-done | bytes 589856 | tf_op jit(solution)/shard_map/ppermute | solution.py:25
  252.7 2.0 collective-permute-done.26.rest_7_
  254.7 14.1 %gate_back.1 = (f32[1024,576]{1,0:T(8,128)}, bf16[1024,576]{1,0:T(8,128)(2,1)}, f32[2,288,576]{2,1,0:T(8,128)}, bf16[2,288,576]{2,1,0:T(8,128)(2,1)S(1)}, f32[2,...) custom-call(s32[1]{0:T(128)} %bitcast.me_ref, s32[6]{0:T(128)S(1)} %copy-done.38, ...), custom_call_target="tpu_custom_call" | custom-call | flops 4000000000 | bytes 1048576 | tf_op jit(solution)/shard_map/gate_back/pallas_call | solution.py:644
  268.9 51.8 %mixer_back.1 = (f32[1024,576]{1,0:T(8,128)S(1)}, f32[1024,128]{1,0:T(8,128)}, f32[128,576]{1,0:T(8,128)S(1)}, f32[1,576]{1,0:T(1,128)S(1)}, f32[1,576]{1,0:T(1,128)S(1)}, /*index=5*/f32[9,8,128]{2,1,0:T(8,128)S(1)}) custom-call(s32[1]{0:T(128)} %copy.54.length_ref, f32[1024,128]{1,0:T(8,128)S(1)} %copy-done.9, ...), custom_call_target="tpu_custom_call" | custom-call | flops 4000000000 | bytes 1048576 | tf_op jit(solution)/shard_map/mixer_back/pallas_call | solution.py:557
  320.7 1.5 copy-done.40
  322.6 1.4 slice.171
  326.1 1.5 collective-permute-start.43
  331.4 11.4 %collective-permute-done.39 = bf16[2,288,576]{2,1,0:T(8,128)(2,1)} collective-permute-done((bf16[2,288,576]{2,1,0:T(8,128)(2,1)}, bf16[2,288,576]{2,1,0:T(8,128)(2,1)}, u32[]{:S(2)}, u32[]{:S(2)}) %collective-permute-start.39) | collective-permute-done | bytes 663584 | tf_op jit(solution)/shard_map/ppermute | solution.py:30
  342.8 2.0 add_convert_fusion.1
  344.8 1.5 collective-permute-start.40
  347.5 11.2 %conv_back.1 = (bf16[1024,576]{1,0:T(8,128)(2,1)S(1)}, f32[2,288,576]{2,1,0:T(8,128)}, bf16[2,288,576]{2,1,0:T(8,128)(2,1)S(1)}, f32[128,576]{1,0:T(8,128)S(1)},...) custom-call(s32[1]{0:T(128)} %bitcast.me_ref, s32[6]{0:T(128)S(1)} %copy-done.39, s32[1]{0:T(128)} %copy.54.length_ref, ...), custom_call_target="tpu_custom_call" | custom-call | flops 4000000000 | bytes 1048576 | tf_op jit(solution)/shard_map/conv_back/pallas_call | solution.py:738
  359.1 8.9 %project_back.1 = (f32[2,256,1152]{2,1,0:T(8,128)S(1)}, bf16[2,256,1152]{2,1,0:T(8,128)(2,1)}, f32[1,1152]{1,0:T(1,128)S(1)}) custom-call(s32[1]{0:T(128)} %bitcast.me_ref, s32[6]{0:T(128)S(1)} %copy-done.39, bf16[256,1152]{1,0:T(8,128)(2,1)} %get-tuple-element.72.rest_0_, bf16[256,1152]{1,0:T(8,128)(2,1)} %collective-permute-done.3.rest_1_, ...), custom_call_target="tpu_custom_call" | custom-call | flops 4000000000 | bytes 1048576 | tf_op jit(solution)/shard_map/project_back/pallas_call | solution.py:815
  369.0 2.4 add_convert_fusion
  371.4 1.6 collective-permute-start.44
  375.7 1.9 collective-permute-done.31
  380.2 1.6 add_add_fusion
  381.8 1.4 copy-done.55
  385.2 1.6 collective-permute-start.38
  387.7 2.8 concatenate.29
  392.4 1.4 dynamic-slice_bitcast_fusion.1.out_near_ref
  393.7 2.9 collective-permute-start.45
  396.6 1.6 add_add_fusion.1
  400.1 1.8 collective-permute-start.35
  402.6 2.7 collective-permute-done.36
  405.4 1.4 fusion.6
  406.9 1.4 fusion.7
  409.6 18.9 %collective-permute-done.35 = bf16[201,576]{1,0:T(8,128)(2,1)S(1)} collective-permute-done((bf16[201,576]{1,0:T(8,128)(2,1)S(1)}, bf16[201,576]{1,0:T(8,128)(2,1)S(1)}, u32[]{:S(2)}, u32[]{:S(2)}) %collective-permute-start.35) | collective-permute-done | bytes 231584 | tf_op jit(solution)/shard_map/ppermute | solution.py:30
  428.4 1.9 collective-permute-start.41
  430.6 1.7 add_bitcast_fusion
  433.5 3.4 finish_rows.1
  438.7 2.3 collective-permute-done.47
  446.3 4.3 collective-permute-start.46
  451.3 2.0 add_add_fusion.3
  453.6 1.6 reshape.260
  455.2 14.7 %collective-permute-done.46 = bf16[1,576,384]{2,1,0:T(8,128)(2,1)S(1)} collective-permute-done((bf16[1,576,384]{2,1,0:T(8,128)(2,1)S(1)}, bf16[1,576,384]{2,1,0:T(8,128)(2,1)S(1)}, u32[]{:S(2)}, u32[]{:S(2)}) %collective-permute-start.46) | collective-permute-done | bytes 442400 | tf_op jit(solution)/shard_map/ppermute | solution.py:1290
  (327 shorter events, 61.5 us)
Async XLA Ops:
  7.2 437.8 %reduce-scatter.2.cloned.1.call-start = ((), (), s32[]{:S(2)}) async-start(), calls=%async_computation.1 | async-start | bytes 7962624 | tf_op jit(solution)/shard_map/reduce_scatter | solution.py:1247
  11.1 23.5 %copy-start = (f32[256,1152]{1,0:T(8,128)S(1)}, f32[256,1152]{1,0:T(8,128)}, u32[]{:S(2)}) copy-start(f32[256,1152]{1,0:T(8,128)} %tokens_ref.5) | copy-start | bytes 3538948
  16.1 37.1 %copy-start.1 = (f32[256,1152]{1,0:T(8,128)S(1)}, f32[256,1152]{1,0:T(8,128)}, u32[]{:S(2)}) copy-start(f32[256,1152]{1,0:T(8,128)} %cot_ref.1) | copy-start | bytes 3538948
  16.1 22.6 %collective-permute-start.7 = (bf16[288,1152]{1,0:T(8,128)(2,1)}, bf16[288,1152]{1,0:T(8,128)(2,1)}, u32[]{:S(2)}, u32[]{:S(2)}) collective-permute-start(bf16[288,1152]{1,0:T(8,128)(2,1)} %get-tuple-element.75), channel_id=1, source_target_pairs={{0,2},{1,3},{2,0},{3,1},{4,7},{5,6},{6,5},{7,4},{8,10},{9,11},{10,... | collective-permute-start | bytes 1990664 | tf_op jit(solution)/shard_map/ppermute | solution.py:76
  18.6 39.2 %copy-start.73 = (bf16[4,576]{1,0:T(4,128)(2,1)S(1)}, bf16[4,576]{1,0:T(4,128)(2,1)}, u32[]{:S(2)}) copy-start(bf16[4,576]{1,0:T(4,128)(2,1)} %param.29) | copy-start | bytes 13828
  18.6 39.2 %copy-start.76 = (bf16[576]{0:T(1024)(128)(2,1)S(1)}, bf16[576]{0:T(1024)(128)(2,1)}, u32[]{:S(2)}) copy-start(bf16[576]{0:T(1024)(128)(2,1)} %param.30) | copy-start | bytes 3460
  18.7 2.2 collective-permute-start
  19.4 14.8 %collective-permute-start.1 = (f32[16,288]{1,0:T(8,128)S(1)}, f32[16,288]{1,0:T(8,128)S(1)}, u32[]{:S(2)}, u32[]{:S(2)}) collective-permute-start(f32[16,288]{1,0:T(8,128)S(1)} %concatenate.23.rest_0_), channel_id=1, source_target_pairs={{0,2},{1,3},{2,0},{3,1},{4,6},{5,7},{6,4},{7,5},{8,10},{9,11},{10,... | collective-permute-start | bytes 55304 | tf_op jit(solution)/shard_map/ppermute | solution.py:25
  19.9 14.6 %collective-permute-start.2 = (f32[16,288]{1,0:T(8,128)S(1)}, f32[16,288]{1,0:T(8,128)S(1)}, u32[]{:S(2)}, u32[]{:S(2)}) collective-permute-start(f32[16,288]{1,0:T(8,128)S(1)} %concatenate.23.rest_0_), channel_id=1, source_target_pairs={{0,3},{1,2},{2,1},{3,0},{4,7},{5,6},{6,5},{7,4},{8,11},{9,10},{10,... | collective-permute-start | bytes 55304 | tf_op jit(solution)/shard_map/ppermute | solution.py:25
  36.3 15.7 %collective-permute-start.4 = (bf16[256,1152]{1,0:T(8,128)(2,1)}, bf16[256,1152]{1,0:T(8,128)(2,1)}, u32[]{:S(2)}, u32[]{:S(2)}) collective-permute-start(bf16[256,1152]{1,0:T(8,128)(2,1)} %get-tuple-element.72.rest_0_), channel_id=1, source_target_pairs={{0,2},{1,3},{2,0},{3,1},{4,6},{5,7},{6,4},{7,5},{8,10},{9,11},{10,... | collective-permute-start | bytes 1769480 | tf_op jit(solution)/shard_map/ppermute | solution.py:25
  37.9 21.0 %collective-permute-start.6 = (bf16[288,1152]{1,0:T(8,128)(2,1)}, bf16[288,1152]{1,0:T(8,128)(2,1)}, u32[]{:S(2)}, u32[]{:S(2)}) collective-permute-start(bf16[288,1152]{1,0:T(8,128)(2,1)} %copy-done.48), channel_id=1, source_target_pairs={{0,1},{1,0},{2,3},{3,2},{4,5},{5,4},{6,7},{7,6},{8,9},{9,8},{10,11... | collective-permute-start | bytes 1990664 | tf_op jit(solution)/shard_map/ppermute | solution.py:25
  38.8 20.2 %collective-permute-start.8 = (bf16[288,1152]{1,0:T(8,128)(2,1)}, bf16[288,1152]{1,0:T(8,128)(2,1)}, u32[]{:S(2)}, u32[]{:S(2)}) collective-permute-start(bf16[288,1152]{1,0:T(8,128)(2,1)} %collective-permute-done.7.rest_6_), channel_id=1, source_target_pairs={{0,4},{4,0},{8,12},{12,8},{16,20},{20,16},{24,28},{28,24},{1,5},{5... | collective-permute-start | bytes 1990664 | tf_op jit(solution)/shard_map/ppermute | solution.py:77
  39.6 19.3 %collective-permute-start.3 = (bf16[256,1152]{1,0:T(8,128)(2,1)}, bf16[256,1152]{1,0:T(8,128)(2,1)}, u32[]{:S(2)}, u32[]{:S(2)}) collective-permute-start(bf16[256,1152]{1,0:T(8,128)(2,1)} %get-tuple-element.72.rest_0_), channel_id=1, source_target_pairs={{0,1},{1,0},{2,3},{3,2},{4,5},{5,4},{6,7},{7,6},{8,9},{9,8},{10,11... | collective-permute-start | bytes 1769480 | tf_op jit(solution)/shard_map/ppermute | solution.py:25
  52.0 6.9 %collective-permute-start.5 = (bf16[256,1152]{1,0:T(8,128)(2,1)}, bf16[256,1152]{1,0:T(8,128)(2,1)}, u32[]{:S(2)}, u32[]{:S(2)}) collective-permute-start(bf16[256,1152]{1,0:T(8,128)(2,1)} %collective-permute-done.4.rest_2_), channel_id=1, source_target_pairs={{0,1},{1,0},{2,3},{3,2},{4,5},{5,4},{6,7},{7,6},{8,9},{9,8},{10,11... | collective-permute-start | bytes 1769480 | tf_op jit(solution)/shard_map/ppermute | solution.py:25
  54.5 18.4 %collective-permute-start.10 = (bf16[256,1152]{1,0:T(8,128)(2,1)}, bf16[256,1152]{1,0:T(8,128)(2,1)}, u32[]{:S(2)}, u32[]{:S(2)}) collective-permute-start(bf16[256,1152]{1,0:T(8,128)(2,1)} %convolution_convert_fusion.rest_4_), channel_id=1, source_target_pairs={{0,2},{1,3},{2,0},{3,1},{4,6},{5,7},{6,4},{7,5},{8,10},{9,11},{10,... | collective-permute-start | bytes 1769480 | tf_op jit(solution)/shard_map/ppermute | solution.py:25
  72.7 2.0 collective-permute-start.9
  74.8 14.2 %collective-permute-start.11 = (f32[1024,128]{1,0:T(8,128)S(1)}, f32[1024,128]{1,0:T(8,128)S(1)}, u32[]{:S(2)}, u32[]{:S(2)}) collective-permute-start(f32[1024,128]{1,0:T(8,128)S(1)} %add_add_fusion.8), channel_id=1, source_target_pairs={{0,2},{1,3},{2,0},{3,1},{4,6},{5,7},{6,4},{7,5},{8,10},{9,11},{10,... | collective-permute-start | bytes 1572872 | tf_op jit(solution)/shard_map/ppermute | solution.py:25
  89.1 34.1 %copy-start.8 = (f32[1024,128]{1,0:T(8,128)}, f32[1024,128]{1,0:T(8,128)S(1)}, u32[]{:S(2)}) copy-start(f32[1024,128]{1,0:T(8,128)S(1)} %add.330.selected_ref.rest_0_) | copy-start | bytes 1572868
  90.5 35.6 %collective-permute-start.12 = (bf16[2,288,768]{2,1,0:T(8,128)(2,1)S(1)}, bf16[2,288,768]{2,1,0:T(8,128)(2,1)}, u32[]{:S(2)}, u32[]{:S(2)}) collective-permute-start(bf16[2,288,768]{2,1,0:T(8,128)(2,1)S(1)} %broadcast_add_fusion.1), channel_id=1, source_target_pairs={{0,2},{1,3},{2,0},{3,1},{4,7},{5,6},{6,5},{7,4},{8,10},{9,11},{10,... | collective-permute-start | bytes 2654216 | tf_op jit(solution)/shard_map/ppermute | solution.py:76
  90.6 32.6 %copy-start.20 = (bf16[128,576]{1,0:T(8,128)(2,1)}, bf16[128,576]{1,0:T(8,128)(2,1)S(1)}, u32[]{:S(2)}) copy-start(bf16[128,576]{1,0:T(8,128)(2,1)S(1)} %pad.9.weight_ref.rest_5_) | copy-start | bytes 442372
  90.8 32.5 %copy-start.26 = (f32[9,8,128]{2,1,0:T(8,128)}, f32[9,8,128]{2,1,0:T(8,128)S(1)}, u32[]{:S(2)}) copy-start(f32[9,8,128]{2,1,0:T(8,128)S(1)} %pad_maximum_fusion.rate_ref.rest_8_) | copy-start | bytes 110596
  129.1 3.2 collective-permute-start.13
  135.9 15.7 %collective-permute-start.14 = (bf16[256,1152]{1,0:T(8,128)(2,1)S(1)}, bf16[256,1152]{1,0:T(8,128)(2,1)S(1)}, u32[]{:S(2)}, u32[]{:S(2)}) collective-permute-start(bf16[256,1152]{1,0:T(8,128)(2,1)S(1)} %fusion.1), channel_id=1, source_target_pairs={{0,2},{1,3},{2,0},{3,1},{4,6},{5,7},{6,4},{7,5},{8,10},{9,11},{10,... | collective-permute-start | bytes 1769480 | tf_op jit(solution)/shard_map/ppermute | solution.py:25
  157.7 16.5 %collective-permute-start.16 = (bf16[256,1280]{1,0:T(8,128)(2,1)}, bf16[256,1280]{1,0:T(8,128)(2,1)}, u32[]{:S(2)}, u32[]{:S(2)}) collective-permute-start(bf16[256,1280]{1,0:T(8,128)(2,1)} %get-tuple-element.83.rest_0_), channel_id=1, source_target_pairs={{0,2},{1,3},{2,0},{3,1},{4,6},{5,7},{6,4},{7,5},{8,10},{9,11},{10,... | collective-permute-start | bytes 1966088 | tf_op jit(solution)/shard_map/ppermute | solution.py:25
  159.3 15.0 %collective-permute-start.18 = (bf16[256,1152]{1,0:T(8,128)(2,1)}, bf16[256,1152]{1,0:T(8,128)(2,1)S(1)}, u32[]{:S(2)}, u32[]{:S(2)}) collective-permute-start(bf16[256,1152]{1,0:T(8,128)(2,1)} %convolution_convert_fusion.rest_4_), channel_id=1, source_target_pairs={{0,1},{1,0},{2,3},{3,2},{4,5},{5,4},{6,7},{7,6},{8,9},{9,8},{10,11... | collective-permute-start | bytes 1769480 | tf_op jit(solution)/shard_map/ppermute | solution.py:25
  159.3 18.3 %collective-permute-start.20 = (bf16[2,288,768]{2,1,0:T(8,128)(2,1)}, bf16[2,288,768]{2,1,0:T(8,128)(2,1)}, u32[]{:S(2)}, u32[]{:S(2)}) collective-permute-start(bf16[2,288,768]{2,1,0:T(8,128)(2,1)} %get-tuple-element.85), channel_id=1, source_target_pairs={{0,1},{1,0},{2,3},{3,2},{4,5},{5,4},{6,7},{7,6},{8,9},{9,8},{10,11... | collective-permute-start | bytes 2654216 | tf_op jit(solution)/shard_map/ppermute | solution.py:25
  159.8 21.9 %collective-permute-start.21 = (bf16[2,288,768]{2,1,0:T(8,128)(2,1)}, bf16[2,288,768]{2,1,0:T(8,128)(2,1)}, u32[]{:S(2)}, u32[]{:S(2)}) collective-permute-start(bf16[2,288,768]{2,1,0:T(8,128)(2,1)} %collective-permute-done.12.rest_10_), channel_id=1, source_target_pairs={{0,4},{4,0},{8,12},{12,8},{16,20},{20,16},{24,28},{28,24},{1,5},{5... | collective-permute-start | bytes 2654216 | tf_op jit(solution)/shard_map/ppermute | solution.py:77
  159.8 21.9 %collective-permute-start.15 = (bf16[256,1280]{1,0:T(8,128)(2,1)}, bf16[256,1280]{1,0:T(8,128)(2,1)}, u32[]{:S(2)}, u32[]{:S(2)}) collective-permute-start(bf16[256,1280]{1,0:T(8,128)(2,1)} %get-tuple-element.83.rest_0_), channel_id=1, source_target_pairs={{0,1},{1,0},{2,3},{3,2},{4,5},{5,4},{6,7},{7,6},{8,9},{9,8},{10,11... | collective-permute-start | bytes 1966088 | tf_op jit(solution)/shard_map/ppermute | solution.py:25
  174.3 7.4 %collective-permute-start.17 = (bf16[256,1280]{1,0:T(8,128)(2,1)}, bf16[256,1280]{1,0:T(8,128)(2,1)}, u32[]{:S(2)}, u32[]{:S(2)}) collective-permute-start(bf16[256,1280]{1,0:T(8,128)(2,1)} %collective-permute-done.16.rest_2_), channel_id=1, source_target_pairs={{0,1},{1,0},{2,3},{3,2},{4,5},{5,4},{6,7},{7,6},{8,9},{9,8},{10,11... | collective-permute-start | bytes 1966088 | tf_op jit(solution)/shard_map/ppermute | solution.py:25
  175.1 2.5 collective-permute-start.19
  212.6 3.3 collective-permute-start.22
  218.2 16.8 %collective-permute-start.23 = (bf16[256,1280]{1,0:T(8,128)(2,1)S(1)}, bf16[256,1280]{1,0:T(8,128)(2,1)S(1)}, u32[]{:S(2)}, u32[]{:S(2)}) collective-permute-start(bf16[256,1280]{1,0:T(8,128)(2,1)S(1)} %fusion), channel_id=1, source_target_pairs={{0,2},{1,3},{2,0},{3,1},{4,6},{5,7},{6,4},{7,5},{8,10},{9,11},{10,... | collective-permute-start | bytes 1966088 | tf_op jit(solution)/shard_map/ppermute | solution.py:25
  235.0 19.7 %copy-start.38 = (s32[6]{0:T(128)S(1)}, s32[6]{0:T(128)}, u32[]{:S(2)}) copy-start(s32[6]{0:T(128)} %copy-done.37) | copy-start | bytes 76
  238.1 14.6 %collective-permute-start.25 = (bf16[256,1152]{1,0:T(8,128)(2,1)S(1)}, bf16[256,1152]{1,0:T(8,128)(2,1)S(1)}, u32[]{:S(2)}, u32[]{:S(2)}) collective-permute-start(bf16[256,1152]{1,0:T(8,128)(2,1)S(1)} %get-tuple-element.91.rest_4_), channel_id=1, source_target_pairs={{0,2},{1,3},{2,0},{3,1},{4,6},{5,7},{6,4},{7,5},{8,10},{9,11},{10,... | collective-permute-start | bytes 1769480 | tf_op jit(solution)/shard_map/ppermute | solution.py:25
  238.5 14.2 %collective-permute-start.24 = (bf16[256,1152]{1,0:T(8,128)(2,1)S(1)}, bf16[256,1152]{1,0:T(8,128)(2,1)S(1)}, u32[]{:S(2)}, u32[]{:S(2)}) collective-permute-start(bf16[256,1152]{1,0:T(8,128)(2,1)S(1)} %get-tuple-element.91.rest_4_), channel_id=1, source_target_pairs={{0,1},{1,0},{2,3},{3,2},{4,5},{5,4},{6,7},{7,6},{8,9},{9,8},{10,11... | collective-permute-start | bytes 1769480 | tf_op jit(solution)/shard_map/ppermute | solution.py:25
  252.7 2.0 collective-permute-start.26
  268.8 51.8 %copy-start.43 = (bf16[2,288,576]{2,1,0:T(8,128)(2,1)}, bf16[2,288,576]{2,1,0:T(8,128)(2,1)S(1)}, u32[]{:S(2)}) copy-start(bf16[2,288,576]{2,1,0:T(8,128)(2,1)S(1)} %get-tuple-element.126) | copy-start | bytes 1990660
  268.8 51.8 %copy-start.44 = (bf16[2,288,576]{2,1,0:T(8,128)(2,1)}, bf16[2,288,576]{2,1,0:T(8,128)(2,1)S(1)}, u32[]{:S(2)}) copy-start(bf16[2,288,576]{2,1,0:T(8,128)(2,1)S(1)} %get-tuple-element.124) | copy-start | bytes 1990660
  322.1 5.5 %collective-permute-start.27 = (f32[1024,128]{1,0:T(8,128)}, f32[1024,128]{1,0:T(8,128)}, u32[]{:S(2)}, u32[]{:S(2)}) collective-permute-start(f32[1024,128]{1,0:T(8,128)} %get-tuple-element.97), channel_id=1, source_target_pairs={{0,1},{1,0},{2,3},{3,2},{4,5},{5,4},{6,7},{7,6},{8,9},{9,8},{10,11... | collective-permute-start | bytes 1572872 | tf_op jit(solution)/shard_map/ppermute | solution.py:25
  322.2 57.9 %collective-permute-start.34 = (bf16[2,256,1152]{2,1,0:T(8,128)(2,1)}, bf16[2,256,1152]{2,1,0:T(8,128)(2,1)}, u32[]{:S(2)}, u32[]{:S(2)}) collective-permute-start(bf16[2,256,1152]{2,1,0:T(8,128)(2,1)} %get-tuple-element.119), channel_id=1, source_target_pairs={{0,1},{1,0},{2,3},{3,2},{4,5},{5,4},{6,7},{7,6},{8,9},{9,8},{10,11... | collective-permute-start | bytes 3538952 | tf_op jit(solution)/shard_map/ppermute | solution.py:25
  324.0 18.8 %collective-permute-start.39 = (bf16[2,288,576]{2,1,0:T(8,128)(2,1)}, bf16[2,288,576]{2,1,0:T(8,128)(2,1)}, u32[]{:S(2)}, u32[]{:S(2)}) collective-permute-start(bf16[2,288,576]{2,1,0:T(8,128)(2,1)} %copy-done.44), channel_id=1, source_target_pairs={{0,4},{4,0},{8,12},{12,8},{16,20},{20,16},{24,28},{28,24},{1,5},{5... | collective-permute-start | bytes 1990664 | tf_op jit(solution)/shard_map/ppermute | solution.py:30
  326.1 42.8 %collective-permute-start.43 = (bf16[2,288,576]{2,1,0:T(8,128)(2,1)}, bf16[2,288,576]{2,1,0:T(8,128)(2,1)}, u32[]{:S(2)}, u32[]{:S(2)}) collective-permute-start(bf16[2,288,576]{2,1,0:T(8,128)(2,1)} %copy-done.43), channel_id=1, source_target_pairs={{0,8},{4,12},{8,0},{12,4},{16,24},{20,28},{24,16},{28,20},{1,9},{5... | collective-permute-start | bytes 1990664 | tf_op jit(solution)/shard_map/ppermute | solution.py:30
  328.9 18.5 %copy-start.29 = (bf16[576,128]{1,0:T(8,128)(2,1)S(1)}, bf16[576,128]{1,0:T(8,128)(2,1)}, u32[]{:S(2)}) copy-start(bf16[576,128]{1,0:T(8,128)(2,1)} %copy-done.28) | copy-start | bytes 442372
  328.9 17.4 %collective-permute-start.28 = (f32[1024,128]{1,0:T(8,128)S(1)}, f32[1024,128]{1,0:T(8,128)}, u32[]{:S(2)}, u32[]{:S(2)}) collective-permute-start(f32[1024,128]{1,0:T(8,128)S(1)} %add.340), channel_id=1, source_target_pairs={{0,2},{1,3},{2,0},{3,1},{4,6},{5,7},{6,4},{7,5},{8,10},{9,11},{10,... | collective-permute-start | bytes 1572872 | tf_op jit(solution)/shard_map/ppermute | solution.py:25
  344.8 57.7 %collective-permute-start.40 = (bf16[1,288,576]{2,1,0:T(8,128)(2,1)}, bf16[1,288,576]{2,1,0:T(8,128)(2,1)}, u32[]{:S(2)}, u32[]{:S(2)}) collective-permute-start(bf16[1,288,576]{2,1,0:T(8,128)(2,1)} %add_convert_fusion.1), channel_id=1, source_target_pairs={{0,8},{4,12},{8,0},{12,4},{16,24},{20,28},{24,16},{28,20},{1,9},{5... | collective-permute-start | bytes 995336 | tf_op jit(solution)/shard_map/ppermute | solution.py:30
  358.6 19.0 %collective-permute-start.31 = (bf16[2,288,576]{2,1,0:T(8,128)(2,1)S(1)}, bf16[2,288,576]{2,1,0:T(8,128)(2,1)S(1)}, u32[]{:S(2)}, u32[]{:S(2)}) collective-permute-start(bf16[2,288,576]{2,1,0:T(8,128)(2,1)S(1)} %get-tuple-element.115), channel_id=1, source_target_pairs={{0,4},{4,0},{8,12},{12,8},{16,20},{20,16},{24,28},{28,24},{1,5},{5... | collective-permute-start | bytes 1990664 | tf_op jit(solution)/shard_map/ppermute | solution.py:30
  368.9 6.6 %collective-permute-start.29 = (f32[4,1152]{1,0:T(4,128)S(1)}, f32[4,1152]{1,0:T(4,128)S(1)}, u32[]{:S(2)}, u32[]{:S(2)}) collective-permute-start(f32[4,1152]{1,0:T(4,128)S(1)} %pad_maximum_fusion.1), channel_id=1, source_target_pairs={{0,1},{1,0},{2,3},{3,2},{4,5},{5,4},{6,7},{7,6},{8,9},{9,8},{10,11... | collective-permute-start | bytes 55304 | tf_op jit(solution)/shard_map/ppermute | solution.py:25
  371.4 19.2 %collective-permute-start.44 = (bf16[2,1,144,576]{3,2,1,0:T(8,128)(2,1)}, bf16[2,1,144,576]{3,2,1,0:T(8,128)(2,1)}, u32[]{:S(2)}, u32[]{:S(2)}) collective-permute-start(bf16[2,1,144,576]{3,2,1,0:T(8,128)(2,1)} %get-tuple-element.139), channel_id=1, source_target_pairs={{0,4},{4,0},{8,12},{12,8},{16,20},{20,16},{24,28},{28,24},{1,5},{5... | collective-permute-start | bytes 995336 | tf_op jit(solution)/shard_map/ppermute | solution.py:30
  375.5 18.3 %collective-permute-start.33 = (bf16[2,256,1152]{2,1,0:T(8,128)(2,1)}, bf16[2,256,1152]{2,1,0:T(8,128)(2,1)}, u32[]{:S(2)}, u32[]{:S(2)}) collective-permute-start(bf16[2,256,1152]{2,1,0:T(8,128)(2,1)} %get-tuple-element.116), channel_id=1, source_target_pairs={{0,1},{1,0},{2,3},{3,2},{4,5},{5,4},{6,7},{7,6},{8,9},{9,8},{10,11... | collective-permute-start | bytes 3538952 | tf_op jit(solution)/shard_map/ppermute | solution.py:25
  377.6 9.9 %collective-permute-start.30 = (f32[4,1152]{1,0:T(4,128)S(1)}, f32[4,1152]{1,0:T(4,128)S(1)}, u32[]{:S(2)}, u32[]{:S(2)}) collective-permute-start(f32[4,1152]{1,0:T(4,128)S(1)} %fusion.20), channel_id=1, source_target_pairs={{0,2},{1,3},{2,0},{3,1},{4,6},{5,7},{6,4},{7,5},{8,10},{9,11},{10,... | collective-permute-start | bytes 55304 | tf_op jit(solution)/shard_map/ppermute | solution.py:25
  385.2 48.2 %collective-permute-start.38 = (bf16[256,1152]{1,0:T(8,128)(2,1)}, bf16[256,1152]{1,0:T(8,128)(2,1)}, u32[]{:S(2)}, u32[]{:S(2)}) collective-permute-start(bf16[256,1152]{1,0:T(8,128)(2,1)} %fusion.3), channel_id=1, source_target_pairs={{0,2},{1,3},{2,0},{3,1},{4,6},{5,7},{6,4},{7,5},{8,10},{9,11},{10,... | collective-permute-start | bytes 1769480 | tf_op jit(solution)/shard_map/ppermute | solution.py:25
  390.5 9.0 %collective-permute-start.32 = (bf16[201,576]{1,0:T(8,128)(2,1)S(1)}, bf16[201,576]{1,0:T(8,128)(2,1)S(1)}, u32[]{:S(2)}, u32[]{:S(2)}) collective-permute-start(bf16[201,576]{1,0:T(8,128)(2,1)S(1)} %concatenate.29), channel_id=1, source_target_pairs={{0,4},{4,0},{8,12},{12,8},{16,20},{20,16},{24,28},{28,24},{1,5},{5... | collective-permute-start | bytes 694664 | tf_op jit(solution)/shard_map/ppermute | solution.py:30
  390.6 14.8 %collective-permute-start.36 = (bf16[1,288,576]{2,1,0:T(8,128)(2,1)}, bf16[1,288,576]{2,1,0:T(8,128)(2,1)S(1)}, u32[]{:S(2)}, u32[]{:S(2)}) collective-permute-start(bf16[1,288,576]{2,1,0:T(8,128)(2,1)} %get-tuple-element.141), channel_id=1, source_target_pairs={{0,8},{4,12},{8,0},{12,4},{16,24},{20,28},{24,16},{28,20},{1,9},{5... | collective-permute-start | bytes 995336 | tf_op jit(solution)/shard_map/ppermute | solution.py:30
  393.7 36.7 %collective-permute-start.45 = (bf16[1,1,144,576]{3,2,1,0:T(8,128)(2,1)S(1)}, bf16[1,1,144,576]{3,2,1,0:T(8,128)(2,1)S(1)}, u32[]{:S(2)}, u32[]{:S(2)}) collective-permute-start(bf16[1,1,144,576]{3,2,1,0:T(8,128)(2,1)S(1)} %add_convert_fusion.6), channel_id=1, source_target_pairs={{0,16},{4,20},{8,24},{12,28},{16,0},{20,4},{24,8},{28,12},{1,17},{... | collective-permute-start | bytes 497672 | tf_op jit(solution)/shard_map/ppermute | solution.py:30
  400.1 28.3 %collective-permute-start.35 = (bf16[201,576]{1,0:T(8,128)(2,1)S(1)}, bf16[201,576]{1,0:T(8,128)(2,1)S(1)}, u32[]{:S(2)}, u32[]{:S(2)}) collective-permute-start(bf16[201,576]{1,0:T(8,128)(2,1)S(1)} %add_convert_fusion.4), channel_id=1, source_target_pairs={{0,8},{4,12},{8,0},{12,4},{16,24},{20,28},{24,16},{28,20},{1,9},{5... | collective-permute-start | bytes 694664 | tf_op jit(solution)/shard_map/ppermute | solution.py:30
  402.6 30.9 %collective-permute-start.37 = (bf16[256,1152]{1,0:T(8,128)(2,1)S(1)}, bf16[256,1152]{1,0:T(8,128)(2,1)S(1)}, u32[]{:S(2)}, u32[]{:S(2)}) collective-permute-start(bf16[256,1152]{1,0:T(8,128)(2,1)S(1)} %fusion.2), channel_id=1, source_target_pairs={{0,2},{1,3},{2,0},{3,1},{4,6},{5,7},{6,4},{7,5},{8,10},{9,11},{10,... | collective-permute-start | bytes 1769480 | tf_op jit(solution)/shard_map/ppermute | solution.py:25
  406.9 23.7 %copy-start.58 = (f32[2,1,144,576]{3,2,1,0:T(8,128)S(1)}, f32[2,1,144,576]{3,2,1,0:T(8,128)}, u32[]{:S(2)}) copy-start(f32[2,1,144,576]{3,2,1,0:T(8,128)} %get-tuple-element.140) | copy-start | bytes 1990660
  408.3 25.2 %copy-start.11 = (bf16[256,256]{1,0:T(8,128)(2,1)S(1)}, bf16[256,256]{1,0:T(8,128)(2,1)}, u32[]{:S(2)}) copy-start(bf16[256,256]{1,0:T(8,128)(2,1)} %copy-done.10) | copy-start | bytes 393220
  408.3 25.2 %copy-start.15 = (f32[256,1152]{1,0:T(8,128)S(1)}, f32[256,1152]{1,0:T(8,128)}, u32[]{:S(2)}) copy-start(f32[256,1152]{1,0:T(8,128)} %copy-done.14) | copy-start | bytes 3538948
  408.3 25.2 %copy-start.19 = (f32[16,1152]{1,0:T(8,128)S(1)}, f32[16,1152]{1,0:T(8,128)}, u32[]{:S(2)}) copy-start(f32[16,1152]{1,0:T(8,128)} %copy-done.16) | copy-start | bytes 221188
  409.5 41.8 %collective-permute-start.42 = (bf16[288,576]{1,0:T(8,128)(2,1)S(1)}, bf16[288,576]{1,0:T(8,128)(2,1)S(1)}, u32[]{:S(2)}, u32[]{:S(2)}) collective-permute-start(bf16[288,576]{1,0:T(8,128)(2,1)S(1)} %fusion.7), channel_id=1, source_target_pairs={{0,16},{1,20},{2,24},{3,28},{4,17},{5,21},{6,25},{7,29},{8,18},{9,... | collective-permute-start | bytes 995336 | tf_op jit(solution)/shard_map/ppermute | solution.py:1353
  428.4 22.9 %collective-permute-start.41 = (bf16[288,576]{1,0:T(8,128)(2,1)S(1)}, bf16[288,576]{1,0:T(8,128)(2,1)}, u32[]{:S(2)}, u32[]{:S(2)}) collective-permute-start(bf16[288,576]{1,0:T(8,128)(2,1)S(1)} %get-tuple-element.134), channel_id=1, source_target_pairs={{0,0},{1,4},{2,8},{3,12},{4,1},{5,5},{6,9},{7,13},{8,2},{9,6},{10,... | collective-permute-start | bytes 995336 | tf_op jit(solution)/shard_map/ppermute | solution.py:1352
  430.5 10.6 %collective-permute-start.47 = (bf16[201,576]{1,0:T(8,128)(2,1)S(1)}, bf16[201,576]{1,0:T(8,128)(2,1)S(1)}, u32[]{:S(2)}, u32[]{:S(2)}) collective-permute-start(bf16[201,576]{1,0:T(8,128)(2,1)S(1)} %add_convert_fusion.3), channel_id=1, source_target_pairs={{0,16},{4,20},{8,24},{12,28},{16,0},{20,4},{24,8},{28,12},{1,17},{... | collective-permute-start | bytes 694664 | tf_op jit(solution)/shard_map/ppermute | solution.py:30
  446.3 23.7 %collective-permute-start.46 = (bf16[1,576,384]{2,1,0:T(8,128)(2,1)S(1)}, bf16[1,576,384]{2,1,0:T(8,128)(2,1)S(1)}, u32[]{:S(2)}, u32[]{:S(2)}) collective-permute-start(bf16[1,576,384]{2,1,0:T(8,128)(2,1)S(1)} %get-tuple-element.144), channel_id=1, source_target_pairs={{0,0},{1,8},{2,16},{3,24},{4,1},{5,9},{6,17},{7,25},{8,2},{9,10},{... | collective-permute-start | bytes 1327112 | tf_op jit(solution)/shard_map/ppermute | solution.py:1290
  (68 other events, 456.4 us)
Sparse Core Ops, SparseCore 0:
  212.7 136.4 reduce-scatter.1

commit v5 on v4

--- a/solution.py
+++ b/solution.py
@@ -17,7 +17,7 @@
 NS = 16
 LANES = 128
 STEP = 8
-CHUNK = 64
+CHUNK = 128
 
 
 def swap(value, bit):
@@ -1368,7 +1368,7 @@
         gains,
     )
     in_sum = join(own, other, result)
-    few = total_rest(join(few, few_got, result), bits[3:])
+    few = total_rest(join(few, few_got, result, up_sum), bits[3:])
     few = [few[a:b] for a, b in zip(starts[:-1], starts[1:])]
     select_grad, conv_grad, conv_bias_grad, step_grad, decay_grad, step_bias_grad, skip_grad, shared = few
     shared = shared.reshape(4, slab)

time: 487 us -> 478 us (0.982)
  Pallas kernels: 169 us -> 163 us
    ppermute x10, waiting for transfers between devices: 37.3 us -> 23.9 us  [swap_groups(): return lax.ppermute(value, 'grp', [(g, g ^ bit) for g in range(size)])]
    ppermute x1, waiting for transfers between devices: 14.7 us -> 24.4 us  [body(): lax.ppermute(tie(up_sum, chip_selected), both_axes, [(g * parts + s, up_h...]
    unnamed x169 -> x161, local copies, waits for them, and re-layouts: 28 us -> 23.7 us
    slice x12 -> x13, local copies, waits for them, and re-layouts: 9.49 us -> 10.7 us  [tie(): corner = other[(0,) * other.ndim].astype(jnp.float32)]
  transfers between devices with their start and end apart: 49 -> 49, of which waited for: 18 -> 17; matrix products, arithmetic and copies ran while one was open for 12% -> 12% of each run, Pallas kernels for 28% -> 27%
where the time goes in v5:
time: 478 us; the launch traced here: 469 us
  Pallas kernels  163 us (34%)
  waiting for transfers between devices  156 us (33%)
  local copies, waits for them, and re-layouts  51.7 us (11%)
  other arithmetic  38.4 us (8%)
  starting transfers between devices  33.4 us (7%)
  between operations  25.6 us (5%)
    ppermute x31, waiting for transfers between devices, swap(): return lax.ppermute(value, 'shard', [(i, i ^ bit) for i in range(size)])  104 us
    pallas_call x1, Pallas kernels, mixer_back(): pl.pallas_call(functools.partial(mixer_back_kernel, tiles), grid=(steps,)...  48.2 us
    pallas_call x1, Pallas kernels, experts(): pl.pallas_call(functools.partial(expert_kernel, parts, CAP, steps), grid=...  30.9 us
    pallas_call x1, Pallas kernels, mixer(): pl.pallas_call(functools.partial(mixer_kernel, tiles, share), grid=(total...  29.3 us
    ppermute x1, waiting for transfers between devices, body(): lax.ppermute(tie(up_sum, chip_selected), both_axes, [(g * parts + s, up_h...  24.4 us
    ppermute x10, waiting for transfers between devices, swap_groups(): return lax.ppermute(value, 'grp', [(g, g ^ bit) for g in range(size)])  23.9 us
    unnamed x161, local copies, waits for them, and re-layouts  23.7 us
    ppermute x31, starting transfers between devices, swap(): return lax.ppermute(value, 'shard', [(i, i ^ bit) for i in range(size)])  16 us
  transfers between devices with their start and end apart: 49, of which 17 were waited for; matrix products, arithmetic and copies ran while one was open for 12% of the time, Pallas kernels for 27%

profile of v5, /device:TPU:2, one launch (start us, length us, event | category | flops | bytes accessed | tf_op | source)
XLA Modules:
  0.0 469.0 jit_solution(16804834258558234351)
XLA Ops:
  7.3 2.0 copy-done.2
  9.3 1.7 copy-done.3
  11.1 2.4 cut_weights.1
  20.8 13.3 %collective-permute-done.1.rest_2_ = f32[16,288]{1,0:T(8,128)S(1)} collective-permute-done((f32[16,288]{1,0:T(8,128)S(1)}, f32[16,288]{1,0:T(8,128)S(1)}, u32[]{:S(2)}, u32[]{:S(2)}) %collective-permute-start.1) | collective-permute-done | bytes 18464 | tf_op jit(solution)/shard_map/ppermute | solution.py:25
  36.3 1.6 collective-permute-start.4
  40.2 11.8 %collective-permute-done.4.rest_2_ = bf16[256,1152]{1,0:T(8,128)(2,1)} collective-permute-done((bf16[256,1152]{1,0:T(8,128)(2,1)}, bf16[256,1152]{1,0:T(8,128)(2,1)}, u32[]{:S(2)}, u32[]{:S(2)}) %collective-permute-start.4) | collective-permute-done | bytes 589856 | tf_op jit(solution)/shard_map/ppermute | solution.py:25
  52.0 1.3 fusion.17
  53.3 1.2 convolution_convert_fusion.rest_4_
  54.5 1.6 collective-permute-start.10
  58.9 10.1 %project.1 = (f32[1024,576]{1,0:T(8,128)S(1)}, f32[1024,576]{1,0:T(8,128)S(1)}, f32[1024,576]{1,0:T(8,128)}, f32[1024,576]{1,0:T(8,128)}, bf16[1024,576]{1,0:T(8,128)(2,1)S(1)}, /*index=5*/f32[1024,128]{1,0:T(8,128)S(1)}) custom-call(s32[1]{0:T(128)} %bitcast.me_ref, s32[6]{0:T(128)S(1)} %stack.26.source_ref, s32[1]{0:T(128)} %copy.53.length_ref, ...), custom_call_target="tpu_custom_call" | custom-call | flops 4000000000 | bytes 1048576 | tf_op jit(solution)/shard_map/project/pallas_call | solution.py:365
  69.1 1.5 copy-done.51
  74.4 13.6 %collective-permute-done.11 = f32[1024,128]{1,0:T(8,128)S(1)} collective-permute-done((f32[1024,128]{1,0:T(8,128)S(1)}, f32[1024,128]{1,0:T(8,128)S(1)}, u32[]{:S(2)}, u32[]{:S(2)}) %collective-permute-start.11) | collective-permute-done | bytes 524320 | tf_op jit(solution)/shard_map/ppermute | solution.py:25
  90.0 29.3 %mixer.1 = (f32[1024,9,8,128]{3,2,1,0:T(8,128)}, f32[9,8,128]{2,1,0:T(8,128)S(1)}, f32[1024,576]{1,0:T(8,128)S(1)}, bf16[1024,576]{1,0:T(8,128)(2,1)S(1)}, f32[2...) custom-call(s32[1]{0:T(128)} %bitcast.me_ref, s32[1]{0:T(128)} %copy.53.length_ref, ...), custom_call_target="tpu_custom_call" | custom-call | flops 4000000000 | bytes 1048576 | tf_op jit(solution)/shard_map/mixer/pallas_call | solution.py:466
  119.2 1.4 copy-done.7
  120.6 1.5 copy-done.50
  124.6 2.6 collective-permute-done.13
  127.2 3.6 convert_add_fusion.1
  130.8 1.3 fusion.1
  132.2 1.6 collective-permute-start.14
  134.6 1.4 dynamic-slice_bitcast_fusion.3.near_ref
  136.0 11.8 %collective-permute-done.14.got_ref = bf16[256,1152]{1,0:T(8,128)(2,1)S(1)} collective-permute-done((bf16[256,1152]{1,0:T(8,128)(2,1)S(1)}, bf16[256,1152]{1,0:T(8,128)(2,1)S(1)}, u32[]{:S(2)}, u32[]{:S(2)}) %collective-permute-start.14) | collective-permute-done | bytes 589856 | tf_op jit(solution)/shard_map/ppermute | solution.py:25
  150.6 1.9 route.1
  154.0 1.6 collective-permute-start.16
  156.1 14.4 %collective-permute-done.16.rest_2_ = bf16[256,1280]{1,0:T(8,128)(2,1)} collective-permute-done((bf16[256,1280]{1,0:T(8,128)(2,1)}, bf16[256,1280]{1,0:T(8,128)(2,1)}, u32[]{:S(2)}, u32[]{:S(2)}) %collective-permute-start.16) | collective-permute-done | bytes 655392 | tf_op jit(solution)/shard_map/ppermute | solution.py:25
  173.9 4.1 collective-permute-done.21.rest_11_
  177.9 30.9 %experts.1 = (f32[2,256,1280]{2,1,0:T(8,128)}, bf16[2,256,1280]{2,1,0:T(8,128)(2,1)}, f32[2,256,1152]{2,1,0:T(8,128)}, bf16[2,256,1152]{2,1,0:T(8,128)(2,1)}, bf16[2,4,1152,384]{3,2,1,0:T(8,128)(2,1)}) custom-call(s32[1]{0:T(128)} %bitcast.me_ref, s32[6]{0:T(128)} %copy-done.37, s32[4]{0:T(128)} %bitcast.103, bf16[256,1280]{1,0:T(8,128)(2,1)} %get-tuple-element.83.rest_0_, ...), custom_call_target="tpu_custom_call" | custom-call | flops 4000000000 | bytes 1048576 | tf_op jit(solution)/shard_map/experts/pallas_call | solution.py:1038
  209.0 3.2 collective-permute-done.22
  212.2 2.1 convert_add_fusion
  215.2 16.1 %collective-permute-done.23.got_ref = bf16[256,1280]{1,0:T(8,128)(2,1)S(1)} collective-permute-done((bf16[256,1280]{1,0:T(8,128)(2,1)S(1)}, bf16[256,1280]{1,0:T(8,128)(2,1)S(1)}, u32[]{:S(2)}, u32[]{:S(2)}) %collective-permute-start.23) | collective-permute-done | bytes 655392 | tf_op jit(solution)/shard_map/ppermute | solution.py:25
  231.3 1.4 return_rows.1
  234.8 14.2 %collective-permute-done.25.rest_6_ = bf16[256,1152]{1,0:T(8,128)(2,1)S(1)} collective-permute-done((bf16[256,1152]{1,0:T(8,128)(2,1)S(1)}, bf16[256,1152]{1,0:T(8,128)(2,1)S(1)}, u32[]{:S(2)}, u32[]{:S(2)}) %collective-permute-start.25) | collective-permute-done | bytes 589856 | tf_op jit(solution)/shard_map/ppermute | solution.py:25
  249.0 2.0 collective-permute-done.26.rest_7_
  251.0 14.1 %gate_back.1 = (f32[1024,576]{1,0:T(8,128)}, bf16[1024,576]{1,0:T(8,128)(2,1)}, f32[2,288,576]{2,1,0:T(8,128)}, bf16[2,288,576]{2,1,0:T(8,128)(2,1)S(1)}, f32[2,...) custom-call(s32[1]{0:T(128)} %bitcast.me_ref, s32[6]{0:T(128)S(1)} %copy-done.38, ...), custom_call_target="tpu_custom_call" | custom-call | flops 4000000000 | bytes 1048576 | tf_op jit(solution)/shard_map/gate_back/pallas_call | solution.py:644
  265.2 48.2 %mixer_back.1 = (f32[1024,576]{1,0:T(8,128)S(1)}, f32[1024,128]{1,0:T(8,128)}, f32[128,576]{1,0:T(8,128)S(1)}, f32[1,576]{1,0:T(1,128)S(1)}, f32[1,576]{1,0:T(1,128)S(1)}, /*index=5*/f32[9,8,128]{2,1,0:T(8,128)S(1)}) custom-call(s32[1]{0:T(128)} %copy.53.length_ref, f32[1024,128]{1,0:T(8,128)S(1)} %copy-done.9, ...), custom_call_target="tpu_custom_call" | custom-call | flops 4000000000 | bytes 1048576 | tf_op jit(solution)/shard_map/mixer_back/pallas_call | solution.py:557
  313.3 1.5 copy-done.40
  317.0 1.6 collective-permute-start.43
  318.6 1.3 add.346
  322.4 12.5 %collective-permute-done.39 = bf16[2,288,576]{2,1,0:T(8,128)(2,1)} collective-permute-done((bf16[2,288,576]{2,1,0:T(8,128)(2,1)}, bf16[2,288,576]{2,1,0:T(8,128)(2,1)}, u32[]{:S(2)}, u32[]{:S(2)}) %collective-permute-start.39) | collective-permute-done | bytes 663584 | tf_op jit(solution)/shard_map/ppermute | solution.py:30
  334.9 2.0 add_convert_fusion.1
  336.9 1.4 collective-permute-start.40
  339.5 11.3 %conv_back.1 = (bf16[1024,576]{1,0:T(8,128)(2,1)S(1)}, f32[2,288,576]{2,1,0:T(8,128)}, bf16[2,288,576]{2,1,0:T(8,128)(2,1)S(1)}, f32[128,576]{1,0:T(8,128)S(1)},...) custom-call(s32[1]{0:T(128)} %bitcast.me_ref, s32[6]{0:T(128)S(1)} %copy-done.39, s32[1]{0:T(128)} %copy.53.length_ref, ...), custom_call_target="tpu_custom_call" | custom-call | flops 4000000000 | bytes 1048576 | tf_op jit(solution)/shard_map/conv_back/pallas_call | solution.py:738
  351.4 8.6 %project_back.1 = (f32[2,256,1152]{2,1,0:T(8,128)S(1)}, bf16[2,256,1152]{2,1,0:T(8,128)(2,1)}, f32[1,1152]{1,0:T(1,128)S(1)}) custom-call(s32[1]{0:T(128)} %bitcast.me_ref, s32[6]{0:T(128)S(1)} %copy-done.39, bf16[256,1152]{1,0:T(8,128)(2,1)} %get-tuple-element.72.rest_0_, bf16[256,1152]{1,0:T(8,128)(2,1)} %collective-permute-done.3.rest_1_, ...), custom_call_target="tpu_custom_call" | custom-call | flops 4000000000 | bytes 1048576 | tf_op jit(solution)/shard_map/project_back/pallas_call | solution.py:815
  361.0 2.4 add_convert_fusion
  363.4 1.6 collective-permute-start.44
  367.6 2.4 collective-permute-done.31
  372.8 3.0 add_add_fusion
  375.8 2.1 fusion.3
  379.1 1.4 collective-permute-start.38
  381.4 1.5 concatenate.29
  383.7 1.2 add_convert_fusion.6
  384.9 1.4 dynamic-slice_bitcast_fusion.1.out_near_ref
  386.3 2.8 collective-permute-start.45
  389.1 1.6 add_add_fusion.1
  392.5 1.6 collective-permute-start.35
  395.0 2.0 collective-permute-done.36
  397.0 2.1 fusion.6
  399.2 2.1 fusion.7
  402.6 3.8 collective-permute-start.41
  406.4 1.7 add_bitcast_fusion
  408.1 7.0 %collective-permute-done.35 = bf16[201,576]{1,0:T(8,128)(2,1)S(1)} collective-permute-done((bf16[201,576]{1,0:T(8,128)(2,1)S(1)}, bf16[201,576]{1,0:T(8,128)(2,1)S(1)}, u32[]{:S(2)}, u32[]{:S(2)}) %collective-permute-start.35) | collective-permute-done | bytes 231584 | tf_op jit(solution)/shard_map/ppermute | solution.py:30
  417.9 3.4 finish_rows.1
  424.4 1.9 collective-permute-start.46
  426.3 2.1 add_add_fusion.3
  429.4 24.4 %collective-permute-done.46 = bf16[1,576,384]{2,1,0:T(8,128)(2,1)S(1)} collective-permute-done((bf16[1,576,384]{2,1,0:T(8,128)(2,1)S(1)}, bf16[1,576,384]{2,1,0:T(8,128)(2,1)S(1)}, u32[]{:S(2)}, u32[]{:S(2)}) %collective-permute-start.46) | collective-permute-done | bytes 442400 | tf_op jit(solution)/shard_map/ppermute | solution.py:1290
  (320 shorter events, 58.9 us)
Async XLA Ops:
  7.2 416.0 %reduce-scatter.2.cloned.1.call-start = ((), (), s32[]{:S(2)}) async-start(), calls=%async_computation.1 | async-start | bytes 7962624 | tf_op jit(solution)/shard_map/reduce_scatter | solution.py:1247
  11.1 23.5 %copy-start = (f32[256,1152]{1,0:T(8,128)S(1)}, f32[256,1152]{1,0:T(8,128)}, u32[]{:S(2)}) copy-start(f32[256,1152]{1,0:T(8,128)} %tokens_ref.5) | copy-start | bytes 3538948
  16.1 37.1 %copy-start.1 = (f32[256,1152]{1,0:T(8,128)S(1)}, f32[256,1152]{1,0:T(8,128)}, u32[]{:S(2)}) copy-start(f32[256,1152]{1,0:T(8,128)} %cot_ref.1) | copy-start | bytes 3538948
  16.1 22.6 %collective-permute-start.7 = (bf16[288,1152]{1,0:T(8,128)(2,1)}, bf16[288,1152]{1,0:T(8,128)(2,1)}, u32[]{:S(2)}, u32[]{:S(2)}) collective-permute-start(bf16[288,1152]{1,0:T(8,128)(2,1)} %get-tuple-element.75), channel_id=1, source_target_pairs={{0,2},{1,3},{2,0},{3,1},{4,7},{5,6},{6,5},{7,4},{8,10},{9,11},{10,... | collective-permute-start | bytes 1990664 | tf_op jit(solution)/shard_map/ppermute | solution.py:76
  18.6 37.4 %copy-start.60 = (bf16[576,104]{0,1:T(8,128)(2,1)S(1)}, bf16[576,104]{0,1:T(8,128)(2,1)}, u32[]{:S(2)}) copy-start(bf16[576,104]{0,1:T(8,128)(2,1)} %param.23) | copy-start | bytes 359428
  18.6 2.2 collective-permute-start
  19.4 14.8 %collective-permute-start.1 = (f32[16,288]{1,0:T(8,128)S(1)}, f32[16,288]{1,0:T(8,128)S(1)}, u32[]{:S(2)}, u32[]{:S(2)}) collective-permute-start(f32[16,288]{1,0:T(8,128)S(1)} %concatenate.23.rest_0_), channel_id=1, source_target_pairs={{0,2},{1,3},{2,0},{3,1},{4,6},{5,7},{6,4},{7,5},{8,10},{9,11},{10,... | collective-permute-start | bytes 55304 | tf_op jit(solution)/shard_map/ppermute | solution.py:25
  19.9 14.6 %collective-permute-start.2 = (f32[16,288]{1,0:T(8,128)S(1)}, f32[16,288]{1,0:T(8,128)S(1)}, u32[]{:S(2)}, u32[]{:S(2)}) collective-permute-start(f32[16,288]{1,0:T(8,128)S(1)} %concatenate.23.rest_0_), channel_id=1, source_target_pairs={{0,3},{1,2},{2,1},{3,0},{4,7},{5,6},{6,5},{7,4},{8,11},{9,10},{10,... | collective-permute-start | bytes 55304 | tf_op jit(solution)/shard_map/ppermute | solution.py:25
  36.3 15.7 %collective-permute-start.4 = (bf16[256,1152]{1,0:T(8,128)(2,1)}, bf16[256,1152]{1,0:T(8,128)(2,1)}, u32[]{:S(2)}, u32[]{:S(2)}) collective-permute-start(bf16[256,1152]{1,0:T(8,128)(2,1)} %get-tuple-element.72.rest_0_), channel_id=1, source_target_pairs={{0,2},{1,3},{2,0},{3,1},{4,6},{5,7},{6,4},{7,5},{8,10},{9,11},{10,... | collective-permute-start | bytes 1769480 | tf_op jit(solution)/shard_map/ppermute | solution.py:25
  37.9 19.9 %collective-permute-start.6 = (bf16[288,1152]{1,0:T(8,128)(2,1)}, bf16[288,1152]{1,0:T(8,128)(2,1)}, u32[]{:S(2)}, u32[]{:S(2)}) collective-permute-start(bf16[288,1152]{1,0:T(8,128)(2,1)} %copy-done.48), channel_id=1, source_target_pairs={{0,1},{1,0},{2,3},{3,2},{4,5},{5,4},{6,7},{7,6},{8,9},{9,8},{10,11... | collective-permute-start | bytes 1990664 | tf_op jit(solution)/shard_map/ppermute | solution.py:25
  38.8 19.0 %collective-permute-start.8 = (bf16[288,1152]{1,0:T(8,128)(2,1)}, bf16[288,1152]{1,0:T(8,128)(2,1)}, u32[]{:S(2)}, u32[]{:S(2)}) collective-permute-start(bf16[288,1152]{1,0:T(8,128)(2,1)} %collective-permute-done.7.rest_6_), channel_id=1, source_target_pairs={{0,4},{4,0},{8,12},{12,8},{16,20},{20,16},{24,28},{28,24},{1,5},{5... | collective-permute-start | bytes 1990664 | tf_op jit(solution)/shard_map/ppermute | solution.py:77
  39.6 18.1 %collective-permute-start.3 = (bf16[256,1152]{1,0:T(8,128)(2,1)}, bf16[256,1152]{1,0:T(8,128)(2,1)}, u32[]{:S(2)}, u32[]{:S(2)}) collective-permute-start(bf16[256,1152]{1,0:T(8,128)(2,1)} %get-tuple-element.72.rest_0_), channel_id=1, source_target_pairs={{0,1},{1,0},{2,3},{3,2},{4,5},{5,4},{6,7},{7,6},{8,9},{9,8},{10,11... | collective-permute-start | bytes 1769480 | tf_op jit(solution)/shard_map/ppermute | solution.py:25
  52.0 5.8 %collective-permute-start.5 = (bf16[256,1152]{1,0:T(8,128)(2,1)}, bf16[256,1152]{1,0:T(8,128)(2,1)}, u32[]{:S(2)}, u32[]{:S(2)}) collective-permute-start(bf16[256,1152]{1,0:T(8,128)(2,1)} %collective-permute-done.4.rest_2_), channel_id=1, source_target_pairs={{0,1},{1,0},{2,3},{3,2},{4,5},{5,4},{6,7},{7,6},{8,9},{9,8},{10,11... | collective-permute-start | bytes 1769480 | tf_op jit(solution)/shard_map/ppermute | solution.py:25
  54.5 17.4 %collective-permute-start.10 = (bf16[256,1152]{1,0:T(8,128)(2,1)}, bf16[256,1152]{1,0:T(8,128)(2,1)}, u32[]{:S(2)}, u32[]{:S(2)}) collective-permute-start(bf16[256,1152]{1,0:T(8,128)(2,1)} %convolution_convert_fusion.rest_4_), channel_id=1, source_target_pairs={{0,2},{1,3},{2,0},{3,1},{4,6},{5,7},{6,4},{7,5},{8,10},{9,11},{10,... | collective-permute-start | bytes 1769480 | tf_op jit(solution)/shard_map/ppermute | solution.py:25
  71.6 2.1 collective-permute-start.9
  73.8 14.2 %collective-permute-start.11 = (f32[1024,128]{1,0:T(8,128)S(1)}, f32[1024,128]{1,0:T(8,128)S(1)}, u32[]{:S(2)}, u32[]{:S(2)}) collective-permute-start(f32[1024,128]{1,0:T(8,128)S(1)} %add_add_fusion.8), channel_id=1, source_target_pairs={{0,2},{1,3},{2,0},{3,1},{4,6},{5,7},{6,4},{7,5},{8,10},{9,11},{10,... | collective-permute-start | bytes 1572872 | tf_op jit(solution)/shard_map/ppermute | solution.py:25
  88.1 31.2 %copy-start.8 = (f32[1024,128]{1,0:T(8,128)}, f32[1024,128]{1,0:T(8,128)S(1)}, u32[]{:S(2)}) copy-start(f32[1024,128]{1,0:T(8,128)S(1)} %add.336.selected_ref.rest_0_) | copy-start | bytes 1572868
  89.5 32.7 %collective-permute-start.12 = (bf16[2,288,768]{2,1,0:T(8,128)(2,1)S(1)}, bf16[2,288,768]{2,1,0:T(8,128)(2,1)}, u32[]{:S(2)}, u32[]{:S(2)}) collective-permute-start(bf16[2,288,768]{2,1,0:T(8,128)(2,1)S(1)} %broadcast_add_fusion.1), channel_id=1, source_target_pairs={{0,2},{1,3},{2,0},{3,1},{4,7},{5,6},{6,5},{7,4},{8,10},{9,11},{10,... | collective-permute-start | bytes 2654216 | tf_op jit(solution)/shard_map/ppermute | solution.py:76
  89.6 29.6 %copy-start.20 = (bf16[128,576]{1,0:T(8,128)(2,1)}, bf16[128,576]{1,0:T(8,128)(2,1)S(1)}, u32[]{:S(2)}) copy-start(bf16[128,576]{1,0:T(8,128)(2,1)S(1)} %pad.9.weight_ref.rest_5_) | copy-start | bytes 442372
  89.8 29.5 %copy-start.26 = (f32[9,8,128]{2,1,0:T(8,128)}, f32[9,8,128]{2,1,0:T(8,128)S(1)}, u32[]{:S(2)}) copy-start(f32[9,8,128]{2,1,0:T(8,128)S(1)} %pad_maximum_fusion.rate_ref.rest_8_) | copy-start | bytes 110596
  124.1 3.0 collective-permute-start.13
  132.2 15.7 %collective-permute-start.14 = (bf16[256,1152]{1,0:T(8,128)(2,1)S(1)}, bf16[256,1152]{1,0:T(8,128)(2,1)S(1)}, u32[]{:S(2)}, u32[]{:S(2)}) collective-permute-start(bf16[256,1152]{1,0:T(8,128)(2,1)S(1)} %fusion.1), channel_id=1, source_target_pairs={{0,2},{1,3},{2,0},{3,1},{4,6},{5,7},{6,4},{7,5},{8,10},{9,11},{10,... | collective-permute-start | bytes 1769480 | tf_op jit(solution)/shard_map/ppermute | solution.py:25
  154.0 16.5 %collective-permute-start.16 = (bf16[256,1280]{1,0:T(8,128)(2,1)}, bf16[256,1280]{1,0:T(8,128)(2,1)}, u32[]{:S(2)}, u32[]{:S(2)}) collective-permute-start(bf16[256,1280]{1,0:T(8,128)(2,1)} %get-tuple-element.83.rest_0_), channel_id=1, source_target_pairs={{0,2},{1,3},{2,0},{3,1},{4,6},{5,7},{6,4},{7,5},{8,10},{9,11},{10,... | collective-permute-start | bytes 1966088 | tf_op jit(solution)/shard_map/ppermute | solution.py:25
  155.6 15.0 %collective-permute-start.18 = (bf16[256,1152]{1,0:T(8,128)(2,1)}, bf16[256,1152]{1,0:T(8,128)(2,1)S(1)}, u32[]{:S(2)}, u32[]{:S(2)}) collective-permute-start(bf16[256,1152]{1,0:T(8,128)(2,1)} %convolution_convert_fusion.rest_4_), channel_id=1, source_target_pairs={{0,1},{1,0},{2,3},{3,2},{4,5},{5,4},{6,7},{7,6},{8,9},{9,8},{10,11... | collective-permute-start | bytes 1769480 | tf_op jit(solution)/shard_map/ppermute | solution.py:25
  155.6 18.3 %collective-permute-start.20 = (bf16[2,288,768]{2,1,0:T(8,128)(2,1)}, bf16[2,288,768]{2,1,0:T(8,128)(2,1)}, u32[]{:S(2)}, u32[]{:S(2)}) collective-permute-start(bf16[2,288,768]{2,1,0:T(8,128)(2,1)} %get-tuple-element.85), channel_id=1, source_target_pairs={{0,1},{1,0},{2,3},{3,2},{4,5},{5,4},{6,7},{7,6},{8,9},{9,8},{10,11... | collective-permute-start | bytes 2654216 | tf_op jit(solution)/shard_map/ppermute | solution.py:25
  156.1 21.9 %collective-permute-start.21 = (bf16[2,288,768]{2,1,0:T(8,128)(2,1)}, bf16[2,288,768]{2,1,0:T(8,128)(2,1)}, u32[]{:S(2)}, u32[]{:S(2)}) collective-permute-start(bf16[2,288,768]{2,1,0:T(8,128)(2,1)} %collective-permute-done.12.rest_10_), channel_id=1, source_target_pairs={{0,4},{4,0},{8,12},{12,8},{16,20},{20,16},{24,28},{28,24},{1,5},{5... | collective-permute-start | bytes 2654216 | tf_op jit(solution)/shard_map/ppermute | solution.py:77
  156.1 21.9 %collective-permute-start.15 = (bf16[256,1280]{1,0:T(8,128)(2,1)}, bf16[256,1280]{1,0:T(8,128)(2,1)}, u32[]{:S(2)}, u32[]{:S(2)}) collective-permute-start(bf16[256,1280]{1,0:T(8,128)(2,1)} %get-tuple-element.83.rest_0_), channel_id=1, source_target_pairs={{0,1},{1,0},{2,3},{3,2},{4,5},{5,4},{6,7},{7,6},{8,9},{9,8},{10,11... | collective-permute-start | bytes 1966088 | tf_op jit(solution)/shard_map/ppermute | solution.py:25
  170.5 7.4 %collective-permute-start.17 = (bf16[256,1280]{1,0:T(8,128)(2,1)}, bf16[256,1280]{1,0:T(8,128)(2,1)}, u32[]{:S(2)}, u32[]{:S(2)}) collective-permute-start(bf16[256,1280]{1,0:T(8,128)(2,1)} %collective-permute-done.16.rest_2_), channel_id=1, source_target_pairs={{0,1},{1,0},{2,3},{3,2},{4,5},{5,4},{6,7},{7,6},{8,9},{9,8},{10,11... | collective-permute-start | bytes 1966088 | tf_op jit(solution)/shard_map/ppermute | solution.py:25
  171.4 2.5 collective-permute-start.19
  208.9 3.3 collective-permute-start.22
  214.4 16.9 %copy-start.13 = (s32[256,1]{1,0:T(8,128)S(1)}, s32[256,1]{1,0:T(8,128)}, u32[]{:S(2)}) copy-start(s32[256,1]{1,0:T(8,128)} %copy.44.routes_ref) | copy-start | bytes 3076
  214.4 16.9 %copy-start.18 = (f32[16,1152]{1,0:T(8,128)S(1)}, f32[16,1152]{1,0:T(8,128)}, u32[]{:S(2)}) copy-start(f32[16,1152]{1,0:T(8,128)} %copy-done.16) | copy-start | bytes 221188
  214.4 16.8 %collective-permute-start.23 = (bf16[256,1280]{1,0:T(8,128)(2,1)S(1)}, bf16[256,1280]{1,0:T(8,128)(2,1)S(1)}, u32[]{:S(2)}, u32[]{:S(2)}) collective-permute-start(bf16[256,1280]{1,0:T(8,128)(2,1)S(1)} %fusion), channel_id=1, source_target_pairs={{0,2},{1,3},{2,0},{3,1},{4,6},{5,7},{6,4},{7,5},{8,10},{9,11},{10,... | collective-permute-start | bytes 1966088 | tf_op jit(solution)/shard_map/ppermute | solution.py:25
  215.1 17.6 %copy-start.10 = (bf16[256,256]{1,0:T(8,128)(2,1)}, bf16[256,256]{1,0:T(8,128)(2,1)S(1)}, u32[]{:S(2)}) copy-start(bf16[256,256]{1,0:T(8,128)(2,1)S(1)} %fusion.9.order_ref) | copy-start | bytes 393220
  231.3 19.7 %copy-start.38 = (s32[6]{0:T(128)S(1)}, s32[6]{0:T(128)}, u32[]{:S(2)}) copy-start(s32[6]{0:T(128)} %copy-done.37) | copy-start | bytes 76
  234.3 14.6 %collective-permute-start.25 = (bf16[256,1152]{1,0:T(8,128)(2,1)S(1)}, bf16[256,1152]{1,0:T(8,128)(2,1)S(1)}, u32[]{:S(2)}, u32[]{:S(2)}) collective-permute-start(bf16[256,1152]{1,0:T(8,128)(2,1)S(1)} %get-tuple-element.91.rest_4_), channel_id=1, source_target_pairs={{0,2},{1,3},{2,0},{3,1},{4,6},{5,7},{6,4},{7,5},{8,10},{9,11},{10,... | collective-permute-start | bytes 1769480 | tf_op jit(solution)/shard_map/ppermute | solution.py:25
  234.8 14.2 %collective-permute-start.24 = (bf16[256,1152]{1,0:T(8,128)(2,1)S(1)}, bf16[256,1152]{1,0:T(8,128)(2,1)S(1)}, u32[]{:S(2)}, u32[]{:S(2)}) collective-permute-start(bf16[256,1152]{1,0:T(8,128)(2,1)S(1)} %get-tuple-element.91.rest_4_), channel_id=1, source_target_pairs={{0,1},{1,0},{2,3},{3,2},{4,5},{5,4},{6,7},{7,6},{8,9},{9,8},{10,11... | collective-permute-start | bytes 1769480 | tf_op jit(solution)/shard_map/ppermute | solution.py:25
  249.0 2.0 collective-permute-start.26
  265.1 48.2 %copy-start.43 = (bf16[2,288,576]{2,1,0:T(8,128)(2,1)}, bf16[2,288,576]{2,1,0:T(8,128)(2,1)S(1)}, u32[]{:S(2)}) copy-start(bf16[2,288,576]{2,1,0:T(8,128)(2,1)S(1)} %get-tuple-element.126) | copy-start | bytes 1990660
  265.1 48.2 %copy-start.44 = (bf16[2,288,576]{2,1,0:T(8,128)(2,1)}, bf16[2,288,576]{2,1,0:T(8,128)(2,1)S(1)}, u32[]{:S(2)}) copy-start(bf16[2,288,576]{2,1,0:T(8,128)(2,1)S(1)} %get-tuple-element.124) | copy-start | bytes 1990660
  314.8 3.8 collective-permute-start.27
  314.9 57.9 %collective-permute-start.34 = (bf16[2,256,1152]{2,1,0:T(8,128)(2,1)}, bf16[2,256,1152]{2,1,0:T(8,128)(2,1)}, u32[]{:S(2)}, u32[]{:S(2)}) collective-permute-start(bf16[2,256,1152]{2,1,0:T(8,128)(2,1)} %get-tuple-element.119), channel_id=1, source_target_pairs={{0,1},{1,0},{2,3},{3,2},{4,5},{5,4},{6,7},{7,6},{8,9},{9,8},{10,11... | collective-permute-start | bytes 3538952 | tf_op jit(solution)/shard_map/ppermute | solution.py:25
  316.1 18.8 %collective-permute-start.39 = (bf16[2,288,576]{2,1,0:T(8,128)(2,1)}, bf16[2,288,576]{2,1,0:T(8,128)(2,1)}, u32[]{:S(2)}, u32[]{:S(2)}) collective-permute-start(bf16[2,288,576]{2,1,0:T(8,128)(2,1)} %copy-done.44), channel_id=1, source_target_pairs={{0,4},{4,0},{8,12},{12,8},{16,20},{20,16},{24,28},{28,24},{1,5},{5... | collective-permute-start | bytes 1990664 | tf_op jit(solution)/shard_map/ppermute | solution.py:30
  317.0 43.9 %collective-permute-start.43 = (bf16[2,288,576]{2,1,0:T(8,128)(2,1)}, bf16[2,288,576]{2,1,0:T(8,128)(2,1)}, u32[]{:S(2)}, u32[]{:S(2)}) collective-permute-start(bf16[2,288,576]{2,1,0:T(8,128)(2,1)} %copy-done.43), channel_id=1, source_target_pairs={{0,8},{4,12},{8,0},{12,4},{16,24},{20,28},{24,16},{28,20},{1,9},{5... | collective-permute-start | bytes 1990664 | tf_op jit(solution)/shard_map/ppermute | solution.py:30
  319.9 19.6 %copy-start.29 = (bf16[576,128]{1,0:T(8,128)(2,1)S(1)}, bf16[576,128]{1,0:T(8,128)(2,1)}, u32[]{:S(2)}) copy-start(bf16[576,128]{1,0:T(8,128)(2,1)} %copy-done.28) | copy-start | bytes 442372
  319.9 19.6 %copy-start.35 = (f32[4,576]{1,0:T(4,128)S(1)}, f32[4,576]{1,0:T(4,128)}, u32[]{:S(2)}) copy-start(f32[4,576]{1,0:T(4,128)} %copy-done.34) | copy-start | bytes 27652
  319.9 19.6 %copy-start.39 = (s32[6]{0:T(128)S(1)}, s32[6]{0:T(128)}, u32[]{:S(2)}) copy-start(s32[6]{0:T(128)} %copy-done.37) | copy-start | bytes 76
  319.9 18.5 %collective-permute-start.28 = (f32[1024,128]{1,0:T(8,128)S(1)}, f32[1024,128]{1,0:T(8,128)}, u32[]{:S(2)}, u32[]{:S(2)}) collective-permute-start(f32[1024,128]{1,0:T(8,128)S(1)} %add.346), channel_id=1, source_target_pairs={{0,2},{1,3},{2,0},{3,1},{4,6},{5,7},{6,4},{7,5},{8,10},{9,11},{10,... | collective-permute-start | bytes 1572872 | tf_op jit(solution)/shard_map/ppermute | solution.py:25
  336.9 57.9 %collective-permute-start.40 = (bf16[1,288,576]{2,1,0:T(8,128)(2,1)}, bf16[1,288,576]{2,1,0:T(8,128)(2,1)}, u32[]{:S(2)}, u32[]{:S(2)}) collective-permute-start(bf16[1,288,576]{2,1,0:T(8,128)(2,1)} %add_convert_fusion.1), channel_id=1, source_target_pairs={{0,8},{4,12},{8,0},{12,4},{16,24},{20,28},{24,16},{28,20},{1,9},{5... | collective-permute-start | bytes 995336 | tf_op jit(solution)/shard_map/ppermute | solution.py:30
  350.9 19.2 %collective-permute-start.31 = (bf16[2,288,576]{2,1,0:T(8,128)(2,1)S(1)}, bf16[2,288,576]{2,1,0:T(8,128)(2,1)S(1)}, u32[]{:S(2)}, u32[]{:S(2)}) collective-permute-start(bf16[2,288,576]{2,1,0:T(8,128)(2,1)S(1)} %get-tuple-element.115), channel_id=1, source_target_pairs={{0,4},{4,0},{8,12},{12,8},{16,20},{20,16},{24,28},{28,24},{1,5},{5... | collective-permute-start | bytes 1990664 | tf_op jit(solution)/shard_map/ppermute | solution.py:30
  360.9 6.6 %collective-permute-start.29 = (f32[4,1152]{1,0:T(4,128)S(1)}, f32[4,1152]{1,0:T(4,128)S(1)}, u32[]{:S(2)}, u32[]{:S(2)}) collective-permute-start(f32[4,1152]{1,0:T(4,128)S(1)} %pad_maximum_fusion.1), channel_id=1, source_target_pairs={{0,1},{1,0},{2,3},{3,2},{4,5},{5,4},{6,7},{7,6},{8,9},{9,8},{10,11... | collective-permute-start | bytes 55304 | tf_op jit(solution)/shard_map/ppermute | solution.py:25
  363.4 19.6 %collective-permute-start.44 = (bf16[2,1,144,576]{3,2,1,0:T(8,128)(2,1)}, bf16[2,1,144,576]{3,2,1,0:T(8,128)(2,1)}, u32[]{:S(2)}, u32[]{:S(2)}) collective-permute-start(bf16[2,1,144,576]{3,2,1,0:T(8,128)(2,1)} %get-tuple-element.139), channel_id=1, source_target_pairs={{0,4},{4,0},{8,12},{12,8},{16,20},{20,16},{24,28},{28,24},{1,5},{5... | collective-permute-start | bytes 995336 | tf_op jit(solution)/shard_map/ppermute | solution.py:30
  367.4 18.8 %collective-permute-start.33 = (bf16[2,256,1152]{2,1,0:T(8,128)(2,1)}, bf16[2,256,1152]{2,1,0:T(8,128)(2,1)}, u32[]{:S(2)}, u32[]{:S(2)}) collective-permute-start(bf16[2,256,1152]{2,1,0:T(8,128)(2,1)} %get-tuple-element.116), channel_id=1, source_target_pairs={{0,1},{1,0},{2,3},{3,2},{4,5},{5,4},{6,7},{7,6},{8,9},{9,8},{10,11... | collective-permute-start | bytes 3538952 | tf_op jit(solution)/shard_map/ppermute | solution.py:25
  370.0 11.1 %collective-permute-start.30 = (f32[4,1152]{1,0:T(4,128)S(1)}, f32[4,1152]{1,0:T(4,128)S(1)}, u32[]{:S(2)}, u32[]{:S(2)}) collective-permute-start(f32[4,1152]{1,0:T(4,128)S(1)} %fusion.20), channel_id=1, source_target_pairs={{0,2},{1,3},{2,0},{3,1},{4,6},{5,7},{6,4},{7,5},{8,10},{9,11},{10,... | collective-permute-start | bytes 55304 | tf_op jit(solution)/shard_map/ppermute | solution.py:25
  379.1 38.7 %collective-permute-start.38 = (bf16[256,1152]{1,0:T(8,128)(2,1)}, bf16[256,1152]{1,0:T(8,128)(2,1)}, u32[]{:S(2)}, u32[]{:S(2)}) collective-permute-start(bf16[256,1152]{1,0:T(8,128)(2,1)} %fusion.3), channel_id=1, source_target_pairs={{0,2},{1,3},{2,0},{3,1},{4,6},{5,7},{6,4},{7,5},{8,10},{9,11},{10,... | collective-permute-start | bytes 1769480 | tf_op jit(solution)/shard_map/ppermute | solution.py:25
  382.9 9.1 %collective-permute-start.32 = (bf16[201,576]{1,0:T(8,128)(2,1)S(1)}, bf16[201,576]{1,0:T(8,128)(2,1)S(1)}, u32[]{:S(2)}, u32[]{:S(2)}) collective-permute-start(bf16[201,576]{1,0:T(8,128)(2,1)S(1)} %concatenate.29), channel_id=1, source_target_pairs={{0,4},{4,0},{8,12},{12,8},{16,20},{20,16},{24,28},{28,24},{1,5},{5... | collective-permute-start | bytes 694664 | tf_op jit(solution)/shard_map/ppermute | solution.py:30
  383.0 14.0 %collective-permute-start.36 = (bf16[1,288,576]{2,1,0:T(8,128)(2,1)}, bf16[1,288,576]{2,1,0:T(8,128)(2,1)S(1)}, u32[]{:S(2)}, u32[]{:S(2)}) collective-permute-start(bf16[1,288,576]{2,1,0:T(8,128)(2,1)} %get-tuple-element.141), channel_id=1, source_target_pairs={{0,8},{4,12},{8,0},{12,4},{16,24},{20,28},{24,16},{28,20},{1,9},{5... | collective-permute-start | bytes 995336 | tf_op jit(solution)/shard_map/ppermute | solution.py:30
  386.3 16.3 %collective-permute-start.45 = (bf16[1,1,144,576]{3,2,1,0:T(8,128)(2,1)S(1)}, bf16[1,1,144,576]{3,2,1,0:T(8,128)(2,1)S(1)}, u32[]{:S(2)}, u32[]{:S(2)}) collective-permute-start(bf16[1,1,144,576]{3,2,1,0:T(8,128)(2,1)S(1)} %add_convert_fusion.6), channel_id=1, source_target_pairs={{0,16},{4,20},{8,24},{12,28},{16,0},{20,4},{24,8},{28,12},{1,17},{... | collective-permute-start | bytes 497672 | tf_op jit(solution)/shard_map/ppermute | solution.py:30
  392.5 22.6 %collective-permute-start.35 = (bf16[201,576]{1,0:T(8,128)(2,1)S(1)}, bf16[201,576]{1,0:T(8,128)(2,1)S(1)}, u32[]{:S(2)}, u32[]{:S(2)}) collective-permute-start(bf16[201,576]{1,0:T(8,128)(2,1)S(1)} %add_convert_fusion.4), channel_id=1, source_target_pairs={{0,8},{4,12},{8,0},{12,4},{16,24},{20,28},{24,16},{28,20},{1,9},{5... | collective-permute-start | bytes 694664 | tf_op jit(solution)/shard_map/ppermute | solution.py:30
  394.8 23.1 %collective-permute-start.37 = (bf16[256,1152]{1,0:T(8,128)(2,1)S(1)}, bf16[256,1152]{1,0:T(8,128)(2,1)S(1)}, u32[]{:S(2)}, u32[]{:S(2)}) collective-permute-start(bf16[256,1152]{1,0:T(8,128)(2,1)S(1)} %fusion.2), channel_id=1, source_target_pairs={{0,2},{1,3},{2,0},{3,1},{4,6},{5,7},{6,4},{7,5},{8,10},{9,11},{10,... | collective-permute-start | bytes 1769480 | tf_op jit(solution)/shard_map/ppermute | solution.py:25
  402.5 23.8 %collective-permute-start.42 = (bf16[288,576]{1,0:T(8,128)(2,1)}, bf16[288,576]{1,0:T(8,128)(2,1)}, u32[]{:S(2)}, u32[]{:S(2)}) collective-permute-start(bf16[288,576]{1,0:T(8,128)(2,1)} %fusion.7), channel_id=1, source_target_pairs={{0,16},{1,20},{2,24},{3,28},{4,17},{5,21},{6,25},{7,29},{8,18},{9,... | collective-permute-start | bytes 995336 | tf_op jit(solution)/shard_map/ppermute | solution.py:1353
  402.6 23.7 %collective-permute-start.41 = (bf16[288,576]{1,0:T(8,128)(2,1)}, bf16[288,576]{1,0:T(8,128)(2,1)}, u32[]{:S(2)}, u32[]{:S(2)}) collective-permute-start(bf16[288,576]{1,0:T(8,128)(2,1)} %get-tuple-element.134), channel_id=1, source_target_pairs={{0,0},{1,4},{2,8},{3,12},{4,1},{5,5},{6,9},{7,13},{8,2},{9,6},{10,... | collective-permute-start | bytes 995336 | tf_op jit(solution)/shard_map/ppermute | solution.py:1352
  417.2 37.8 %collective-permute-start.47 = (bf16[201,576]{1,0:T(8,128)(2,1)}, bf16[201,576]{1,0:T(8,128)(2,1)}, u32[]{:S(2)}, u32[]{:S(2)}) collective-permute-start(bf16[201,576]{1,0:T(8,128)(2,1)} %add_convert_fusion.3), channel_id=1, source_target_pairs={{0,16},{4,20},{8,24},{12,28},{16,0},{20,4},{24,8},{28,12},{1,17},{... | collective-permute-start | bytes 694664 | tf_op jit(solution)/shard_map/ppermute | solution.py:30
  424.4 29.4 %collective-permute-start.46 = (bf16[1,576,384]{2,1,0:T(8,128)(2,1)S(1)}, bf16[1,576,384]{2,1,0:T(8,128)(2,1)S(1)}, u32[]{:S(2)}, u32[]{:S(2)}) collective-permute-start(bf16[1,576,384]{2,1,0:T(8,128)(2,1)S(1)} %get-tuple-element.144), channel_id=1, source_target_pairs={{0,0},{1,8},{2,16},{3,24},{4,1},{5,9},{6,17},{7,25},{8,2},{9,10},{... | collective-permute-start | bytes 1327112 | tf_op jit(solution)/shard_map/ppermute | solution.py:1290
  (64 other events, 414.8 us)
Sparse Core Ops, SparseCore 0:
  209.0 141.7 reduce-scatter.1

commit v6 on v5

--- a/solution.py
+++ b/solution.py
@@ -592,17 +592,18 @@
     slab = width // parts
     me, odd, second = (me_ref[0], source_ref[parts], source_ref[parts + 1])
 
+    def fetched(refs, target, base, k):
+        at = pl.ds(pl.multiple_of((me ^ k) * rows, 16), rows)
+        return pltpu.make_async_copy(refs[k], target.at[at], sems.at[base + k])
+
     @pl.when(block == 0)
     def fetch():
-        copies = []
         for k in range(parts):
-            at = pl.ds(pl.multiple_of((me ^ k) * rows, 16), rows)
-            copies.append(pltpu.make_async_copy(normed_refs[k], normed.at[at], sems.at[k]))
-            copies.append(pltpu.make_async_copy(grad_refs[k], grads.at[at], sems.at[parts + k]))
-        for copy in copies:
-            copy.start()
-        for copy in copies:
-            copy.wait()
+            fetched(grad_refs, grads, parts, k).start()
+        for k in range(parts):
+            fetched(normed_refs, normed, 0, k).start()
+        for k in range(parts):
+            fetched(grad_refs, grads, parts, k).wait()
 
     at = pl.ds(pl.multiple_of(block * rows, rows), rows)
     grad = grads[at]
@@ -616,6 +617,8 @@
 
     @pl.when(block == parts - 1)
     def finish():
+        for k in range(parts):
+            fetched(normed_refs, normed, 0, k).wait()
         product[...] = t_dot(normed[...], lows[...])
         for h in range(parts // 2):
             at = pl.ds(pl.multiple_of((2 * h + odd) * slab, 8), slab)

time: 478 us -> 477 us (level)
    ppermute x10, waiting for transfers between devices: 23.9 us -> 17 us  [swap_groups(): return lax.ppermute(value, 'grp', [(g, g ^ bit) for g in range(size)])]
where the time goes in v6:
time: 477 us; the launch traced here: 468 us
  Pallas kernels  162 us (34%)
  waiting for transfers between devices  154 us (32%)
  local copies, waits for them, and re-layouts  51.7 us (11%)
  other arithmetic  38.4 us (8%)
  starting transfers between devices  35.6 us (7%)
  between operations  25.6 us (5%)
    ppermute x31, waiting for transfers between devices, swap(): return lax.ppermute(value, 'shard', [(i, i ^ bit) for i in range(size)])  104 us
    pallas_call x1, Pallas kernels, mixer_back(): pl.pallas_call(functools.partial(mixer_back_kernel, tiles), grid=(steps,)...  48.2 us
    pallas_call x1, Pallas kernels, experts(): pl.pallas_call(functools.partial(expert_kernel, parts, CAP, steps), grid=...  30.9 us
    pallas_call x1, Pallas kernels, mixer(): pl.pallas_call(functools.partial(mixer_kernel, tiles, share), grid=(total...  29.3 us
    ppermute x1, waiting for transfers between devices, body(): lax.ppermute(tie(up_sum, chip_selected), both_axes, [(g * parts + s, up_h...  27.6 us
    unnamed x161, local copies, waits for them, and re-layouts  23.7 us
    ppermute x10, waiting for transfers between devices, swap_groups(): return lax.ppermute(value, 'grp', [(g, g ^ bit) for g in range(size)])  17 us
    ppermute x31, starting transfers between devices, swap(): return lax.ppermute(value, 'shard', [(i, i ^ bit) for i in range(size)])  16.1 us
  transfers between devices with their start and end apart: 49, of which 17 were waited for; matrix products, arithmetic and copies ran while one was open for 12% of the time, Pallas kernels for 27%

profile of v6, /device:TPU:2, one launch (start us, length us, event | category | flops | bytes accessed | tf_op | source)
XLA Modules:
  0.0 468.3 jit_solution(4911397473887473927)
XLA Ops:
  7.3 2.0 copy-done.2
  9.3 1.7 copy-done.3
  11.1 2.4 cut_weights.1
  20.8 13.3 %collective-permute-done.1.rest_2_ = f32[16,288]{1,0:T(8,128)S(1)} collective-permute-done((f32[16,288]{1,0:T(8,128)S(1)}, f32[16,288]{1,0:T(8,128)S(1)}, u32[]{:S(2)}, u32[]{:S(2)}) %collective-permute-start.1) | collective-permute-done | bytes 18464 | tf_op jit(solution)/shard_map/ppermute | solution.py:25
  36.3 1.6 collective-permute-start.4
  40.2 11.8 %collective-permute-done.4.rest_2_ = bf16[256,1152]{1,0:T(8,128)(2,1)} collective-permute-done((bf16[256,1152]{1,0:T(8,128)(2,1)}, bf16[256,1152]{1,0:T(8,128)(2,1)}, u32[]{:S(2)}, u32[]{:S(2)}) %collective-permute-start.4) | collective-permute-done | bytes 589856 | tf_op jit(solution)/shard_map/ppermute | solution.py:25
  52.0 1.3 fusion.17
  54.5 1.6 collective-permute-start.10
  58.9 10.1 %project.1 = (f32[1024,576]{1,0:T(8,128)S(1)}, f32[1024,576]{1,0:T(8,128)S(1)}, f32[1024,576]{1,0:T(8,128)}, f32[1024,576]{1,0:T(8,128)}, bf16[1024,576]{1,0:T(8,128)(2,1)S(1)}, /*index=5*/f32[1024,128]{1,0:T(8,128)S(1)}) custom-call(s32[1]{0:T(128)} %bitcast.me_ref, s32[6]{0:T(128)S(1)} %stack.26.source_ref, s32[1]{0:T(128)} %copy.53.length_ref, ...), custom_call_target="tpu_custom_call" | custom-call | flops 4000000000 | bytes 1048576 | tf_op jit(solution)/shard_map/project/pallas_call | solution.py:365
  69.1 1.5 copy-done.51
  74.4 13.6 %collective-permute-done.11 = f32[1024,128]{1,0:T(8,128)S(1)} collective-permute-done((f32[1024,128]{1,0:T(8,128)S(1)}, f32[1024,128]{1,0:T(8,128)S(1)}, u32[]{:S(2)}, u32[]{:S(2)}) %collective-permute-start.11) | collective-permute-done | bytes 524320 | tf_op jit(solution)/shard_map/ppermute | solution.py:25
  90.0 29.3 %mixer.1 = (f32[1024,9,8,128]{3,2,1,0:T(8,128)}, f32[9,8,128]{2,1,0:T(8,128)S(1)}, f32[1024,576]{1,0:T(8,128)S(1)}, bf16[1024,576]{1,0:T(8,128)(2,1)S(1)}, f32[2...) custom-call(s32[1]{0:T(128)} %bitcast.me_ref, s32[1]{0:T(128)} %copy.53.length_ref, ...), custom_call_target="tpu_custom_call" | custom-call | flops 4000000000 | bytes 1048576 | tf_op jit(solution)/shard_map/mixer/pallas_call | solution.py:466
  119.2 1.4 copy-done.7
  120.6 1.5 copy-done.50
  124.6 2.6 collective-permute-done.13
  127.2 3.6 convert_add_fusion.1
  130.8 1.3 fusion.1
  132.2 1.6 collective-permute-start.14
  134.6 1.4 dynamic-slice_bitcast_fusion.3.near_ref
  136.0 11.8 %collective-permute-done.14.got_ref = bf16[256,1152]{1,0:T(8,128)(2,1)S(1)} collective-permute-done((bf16[256,1152]{1,0:T(8,128)(2,1)S(1)}, bf16[256,1152]{1,0:T(8,128)(2,1)S(1)}, u32[]{:S(2)}, u32[]{:S(2)}) %collective-permute-start.14) | collective-permute-done | bytes 589856 | tf_op jit(solution)/shard_map/ppermute | solution.py:25
  150.6 1.9 route.1
  154.0 1.6 collective-permute-start.16
  156.1 14.4 %collective-permute-done.16.rest_2_ = bf16[256,1280]{1,0:T(8,128)(2,1)} collective-permute-done((bf16[256,1280]{1,0:T(8,128)(2,1)}, bf16[256,1280]{1,0:T(8,128)(2,1)}, u32[]{:S(2)}, u32[]{:S(2)}) %collective-permute-start.16) | collective-permute-done | bytes 655392 | tf_op jit(solution)/shard_map/ppermute | solution.py:25
  173.9 4.1 collective-permute-done.21.rest_11_
  177.9 30.9 %experts.1 = (f32[2,256,1280]{2,1,0:T(8,128)}, bf16[2,256,1280]{2,1,0:T(8,128)(2,1)}, f32[2,256,1152]{2,1,0:T(8,128)}, bf16[2,256,1152]{2,1,0:T(8,128)(2,1)}, bf16[2,4,1152,384]{3,2,1,0:T(8,128)(2,1)}) custom-call(s32[1]{0:T(128)} %bitcast.me_ref, s32[6]{0:T(128)} %copy-done.37, s32[4]{0:T(128)} %bitcast.103, bf16[256,1280]{1,0:T(8,128)(2,1)} %get-tuple-element.83.rest_0_, ...), custom_call_target="tpu_custom_call" | custom-call | flops 4000000000 | bytes 1048576 | tf_op jit(solution)/shard_map/experts/pallas_call | solution.py:1041
  209.0 3.2 collective-permute-done.22
  212.2 2.1 convert_add_fusion
  215.2 16.1 %collective-permute-done.23.got_ref = bf16[256,1280]{1,0:T(8,128)(2,1)S(1)} collective-permute-done((bf16[256,1280]{1,0:T(8,128)(2,1)S(1)}, bf16[256,1280]{1,0:T(8,128)(2,1)S(1)}, u32[]{:S(2)}, u32[]{:S(2)}) %collective-permute-start.23) | collective-permute-done | bytes 655392 | tf_op jit(solution)/shard_map/ppermute | solution.py:25
  231.3 1.4 return_rows.1
  234.8 14.2 %collective-permute-done.25.rest_6_ = bf16[256,1152]{1,0:T(8,128)(2,1)S(1)} collective-permute-done((bf16[256,1152]{1,0:T(8,128)(2,1)S(1)}, bf16[256,1152]{1,0:T(8,128)(2,1)S(1)}, u32[]{:S(2)}, u32[]{:S(2)}) %collective-permute-start.25) | collective-permute-done | bytes 589856 | tf_op jit(solution)/shard_map/ppermute | solution.py:25
  249.0 2.0 collective-permute-done.26.rest_7_
  251.0 13.0 %gate_back.1 = (f32[1024,576]{1,0:T(8,128)}, bf16[1024,576]{1,0:T(8,128)(2,1)}, f32[2,288,576]{2,1,0:T(8,128)}, bf16[2,288,576]{2,1,0:T(8,128)(2,1)S(1)}, f32[2,...) custom-call(s32[1]{0:T(128)} %bitcast.me_ref, s32[6]{0:T(128)S(1)} %copy-done.38, ...), custom_call_target="tpu_custom_call" | custom-call | flops 4000000000 | bytes 1048576 | tf_op jit(solution)/shard_map/gate_back/pallas_call | solution.py:647
  264.1 48.2 %mixer_back.1 = (f32[1024,576]{1,0:T(8,128)S(1)}, f32[1024,128]{1,0:T(8,128)}, f32[128,576]{1,0:T(8,128)S(1)}, f32[1,576]{1,0:T(1,128)S(1)}, f32[1,576]{1,0:T(1,128)S(1)}, /*index=5*/f32[9,8,128]{2,1,0:T(8,128)S(1)}) custom-call(s32[1]{0:T(128)} %copy.53.length_ref, f32[1024,128]{1,0:T(8,128)S(1)} %copy-done.9, ...), custom_call_target="tpu_custom_call" | custom-call | flops 4000000000 | bytes 1048576 | tf_op jit(solution)/shard_map/mixer_back/pallas_call | solution.py:557
  312.3 1.5 copy-done.40
  316.0 1.6 collective-permute-start.43
  317.6 1.3 add.346
  321.4 12.4 %collective-permute-done.39 = bf16[2,288,576]{2,1,0:T(8,128)(2,1)} collective-permute-done((bf16[2,288,576]{2,1,0:T(8,128)(2,1)}, bf16[2,288,576]{2,1,0:T(8,128)(2,1)}, u32[]{:S(2)}, u32[]{:S(2)}) %collective-permute-start.39) | collective-permute-done | bytes 663584 | tf_op jit(solution)/shard_map/ppermute | solution.py:30
  333.9 2.1 add_convert_fusion.1
  335.9 1.5 collective-permute-start.40
  338.6 11.3 %conv_back.1 = (bf16[1024,576]{1,0:T(8,128)(2,1)S(1)}, f32[2,288,576]{2,1,0:T(8,128)}, bf16[2,288,576]{2,1,0:T(8,128)(2,1)S(1)}, f32[128,576]{1,0:T(8,128)S(1)},...) custom-call(s32[1]{0:T(128)} %bitcast.me_ref, s32[6]{0:T(128)S(1)} %copy-done.39, s32[1]{0:T(128)} %copy.53.length_ref, ...), custom_call_target="tpu_custom_call" | custom-call | flops 4000000000 | bytes 1048576 | tf_op jit(solution)/shard_map/conv_back/pallas_call | solution.py:741
  350.4 8.7 %project_back.1 = (f32[2,256,1152]{2,1,0:T(8,128)S(1)}, bf16[2,256,1152]{2,1,0:T(8,128)(2,1)}, f32[1,1152]{1,0:T(1,128)S(1)}) custom-call(s32[1]{0:T(128)} %bitcast.me_ref, s32[6]{0:T(128)S(1)} %copy-done.39, bf16[256,1152]{1,0:T(8,128)(2,1)} %get-tuple-element.72.rest_0_, bf16[256,1152]{1,0:T(8,128)(2,1)} %collective-permute-done.3.rest_1_, ...), custom_call_target="tpu_custom_call" | custom-call | flops 4000000000 | bytes 1048576 | tf_op jit(solution)/shard_map/project_back/pallas_call | solution.py:818
  360.0 2.4 add_convert_fusion
  362.4 1.6 collective-permute-start.44
  366.7 2.4 collective-permute-done.31
  371.3 3.0 add_add_fusion
  374.3 2.1 fusion.3
  377.6 1.9 collective-permute-start.38
  380.4 1.5 concatenate.29
  382.4 1.2 add_convert_fusion.6
  383.6 1.4 dynamic-slice_bitcast_fusion.1.out_near_ref
  385.0 3.0 collective-permute-start.45
  388.0 1.6 add_add_fusion.1
  391.5 1.6 collective-permute-start.35
  394.0 2.2 collective-permute-done.36
  396.2 2.1 fusion.6
  398.5 2.1 fusion.7
  401.9 3.5 collective-permute-start.41
  405.4 1.7 add_bitcast_fusion
  409.1 2.5 collective-permute-start.47
  412.3 3.4 finish_rows.1
  418.8 1.9 collective-permute-start.46
  420.8 1.7 collective-permute-done.42
  422.4 2.1 add_add_fusion.3
  425.5 27.6 %collective-permute-done.46 = bf16[1,576,384]{2,1,0:T(8,128)(2,1)S(1)} collective-permute-done((bf16[1,576,384]{2,1,0:T(8,128)(2,1)S(1)}, bf16[1,576,384]{2,1,0:T(8,128)(2,1)S(1)}, u32[]{:S(2)}, u32[]{:S(2)}) %collective-permute-start.46) | collective-permute-done | bytes 442400 | tf_op jit(solution)/shard_map/ppermute | solution.py:1293
  (320 shorter events, 59.4 us)
Async XLA Ops:
  7.2 410.4 %reduce-scatter.2.cloned.1.call-start = ((), (), s32[]{:S(2)}) async-start(), calls=%async_computation.1 | async-start | bytes 7962624 | tf_op jit(solution)/shard_map/reduce_scatter | solution.py:1250
  11.1 23.5 %copy-start = (f32[256,1152]{1,0:T(8,128)S(1)}, f32[256,1152]{1,0:T(8,128)}, u32[]{:S(2)}) copy-start(f32[256,1152]{1,0:T(8,128)} %tokens_ref.5) | copy-start | bytes 3538948
  16.1 37.1 %copy-start.1 = (f32[256,1152]{1,0:T(8,128)S(1)}, f32[256,1152]{1,0:T(8,128)}, u32[]{:S(2)}) copy-start(f32[256,1152]{1,0:T(8,128)} %cot_ref.1) | copy-start | bytes 3538948
  16.1 22.6 %collective-permute-start.7 = (bf16[288,1152]{1,0:T(8,128)(2,1)}, bf16[288,1152]{1,0:T(8,128)(2,1)}, u32[]{:S(2)}, u32[]{:S(2)}) collective-permute-start(bf16[288,1152]{1,0:T(8,128)(2,1)} %get-tuple-element.75), channel_id=1, source_target_pairs={{0,2},{1,3},{2,0},{3,1},{4,7},{5,6},{6,5},{7,4},{8,10},{9,11},{10,... | collective-permute-start | bytes 1990664 | tf_op jit(solution)/shard_map/ppermute | solution.py:76
  18.6 37.4 %copy-start.60 = (bf16[576,104]{0,1:T(8,128)(2,1)S(1)}, bf16[576,104]{0,1:T(8,128)(2,1)}, u32[]{:S(2)}) copy-start(bf16[576,104]{0,1:T(8,128)(2,1)} %param.23) | copy-start | bytes 359428
  18.6 2.2 collective-permute-start
  19.4 14.8 %collective-permute-start.1 = (f32[16,288]{1,0:T(8,128)S(1)}, f32[16,288]{1,0:T(8,128)S(1)}, u32[]{:S(2)}, u32[]{:S(2)}) collective-permute-start(f32[16,288]{1,0:T(8,128)S(1)} %concatenate.23.rest_0_), channel_id=1, source_target_pairs={{0,2},{1,3},{2,0},{3,1},{4,6},{5,7},{6,4},{7,5},{8,10},{9,11},{10,... | collective-permute-start | bytes 55304 | tf_op jit(solution)/shard_map/ppermute | solution.py:25
  19.9 14.6 %collective-permute-start.2 = (f32[16,288]{1,0:T(8,128)S(1)}, f32[16,288]{1,0:T(8,128)S(1)}, u32[]{:S(2)}, u32[]{:S(2)}) collective-permute-start(f32[16,288]{1,0:T(8,128)S(1)} %concatenate.23.rest_0_), channel_id=1, source_target_pairs={{0,3},{1,2},{2,1},{3,0},{4,7},{5,6},{6,5},{7,4},{8,11},{9,10},{10,... | collective-permute-start | bytes 55304 | tf_op jit(solution)/shard_map/ppermute | solution.py:25
  36.3 15.7 %collective-permute-start.4 = (bf16[256,1152]{1,0:T(8,128)(2,1)}, bf16[256,1152]{1,0:T(8,128)(2,1)}, u32[]{:S(2)}, u32[]{:S(2)}) collective-permute-start(bf16[256,1152]{1,0:T(8,128)(2,1)} %get-tuple-element.72.rest_0_), channel_id=1, source_target_pairs={{0,2},{1,3},{2,0},{3,1},{4,6},{5,7},{6,4},{7,5},{8,10},{9,11},{10,... | collective-permute-start | bytes 1769480 | tf_op jit(solution)/shard_map/ppermute | solution.py:25
  37.9 19.9 %collective-permute-start.6 = (bf16[288,1152]{1,0:T(8,128)(2,1)}, bf16[288,1152]{1,0:T(8,128)(2,1)}, u32[]{:S(2)}, u32[]{:S(2)}) collective-permute-start(bf16[288,1152]{1,0:T(8,128)(2,1)} %copy-done.48), channel_id=1, source_target_pairs={{0,1},{1,0},{2,3},{3,2},{4,5},{5,4},{6,7},{7,6},{8,9},{9,8},{10,11... | collective-permute-start | bytes 1990664 | tf_op jit(solution)/shard_map/ppermute | solution.py:25
  38.8 19.0 %collective-permute-start.8 = (bf16[288,1152]{1,0:T(8,128)(2,1)}, bf16[288,1152]{1,0:T(8,128)(2,1)}, u32[]{:S(2)}, u32[]{:S(2)}) collective-permute-start(bf16[288,1152]{1,0:T(8,128)(2,1)} %collective-permute-done.7.rest_6_), channel_id=1, source_target_pairs={{0,4},{4,0},{8,12},{12,8},{16,20},{20,16},{24,28},{28,24},{1,5},{5... | collective-permute-start | bytes 1990664 | tf_op jit(solution)/shard_map/ppermute | solution.py:77
  39.6 18.1 %collective-permute-start.3 = (bf16[256,1152]{1,0:T(8,128)(2,1)}, bf16[256,1152]{1,0:T(8,128)(2,1)}, u32[]{:S(2)}, u32[]{:S(2)}) collective-permute-start(bf16[256,1152]{1,0:T(8,128)(2,1)} %get-tuple-element.72.rest_0_), channel_id=1, source_target_pairs={{0,1},{1,0},{2,3},{3,2},{4,5},{5,4},{6,7},{7,6},{8,9},{9,8},{10,11... | collective-permute-start | bytes 1769480 | tf_op jit(solution)/shard_map/ppermute | solution.py:25
  52.0 5.8 %collective-permute-start.5 = (bf16[256,1152]{1,0:T(8,128)(2,1)}, bf16[256,1152]{1,0:T(8,128)(2,1)}, u32[]{:S(2)}, u32[]{:S(2)}) collective-permute-start(bf16[256,1152]{1,0:T(8,128)(2,1)} %collective-permute-done.4.rest_2_), channel_id=1, source_target_pairs={{0,1},{1,0},{2,3},{3,2},{4,5},{5,4},{6,7},{7,6},{8,9},{9,8},{10,11... | collective-permute-start | bytes 1769480 | tf_op jit(solution)/shard_map/ppermute | solution.py:25
  54.5 17.4 %collective-permute-start.10 = (bf16[256,1152]{1,0:T(8,128)(2,1)}, bf16[256,1152]{1,0:T(8,128)(2,1)}, u32[]{:S(2)}, u32[]{:S(2)}) collective-permute-start(bf16[256,1152]{1,0:T(8,128)(2,1)} %convolution_convert_fusion.rest_4_), channel_id=1, source_target_pairs={{0,2},{1,3},{2,0},{3,1},{4,6},{5,7},{6,4},{7,5},{8,10},{9,11},{10,... | collective-permute-start | bytes 1769480 | tf_op jit(solution)/shard_map/ppermute | solution.py:25
  71.6 2.1 collective-permute-start.9
  73.8 14.2 %collective-permute-start.11 = (f32[1024,128]{1,0:T(8,128)S(1)}, f32[1024,128]{1,0:T(8,128)S(1)}, u32[]{:S(2)}, u32[]{:S(2)}) collective-permute-start(f32[1024,128]{1,0:T(8,128)S(1)} %add_add_fusion.8), channel_id=1, source_target_pairs={{0,2},{1,3},{2,0},{3,1},{4,6},{5,7},{6,4},{7,5},{8,10},{9,11},{10,... | collective-permute-start | bytes 1572872 | tf_op jit(solution)/shard_map/ppermute | solution.py:25
  88.1 31.2 %copy-start.8 = (f32[1024,128]{1,0:T(8,128)}, f32[1024,128]{1,0:T(8,128)S(1)}, u32[]{:S(2)}) copy-start(f32[1024,128]{1,0:T(8,128)S(1)} %add.336.selected_ref.rest_0_) | copy-start | bytes 1572868
  89.5 32.7 %collective-permute-start.12 = (bf16[2,288,768]{2,1,0:T(8,128)(2,1)S(1)}, bf16[2,288,768]{2,1,0:T(8,128)(2,1)}, u32[]{:S(2)}, u32[]{:S(2)}) collective-permute-start(bf16[2,288,768]{2,1,0:T(8,128)(2,1)S(1)} %broadcast_add_fusion.1), channel_id=1, source_target_pairs={{0,2},{1,3},{2,0},{3,1},{4,7},{5,6},{6,5},{7,4},{8,10},{9,11},{10,... | collective-permute-start | bytes 2654216 | tf_op jit(solution)/shard_map/ppermute | solution.py:76
  89.6 29.6 %copy-start.20 = (bf16[128,576]{1,0:T(8,128)(2,1)}, bf16[128,576]{1,0:T(8,128)(2,1)S(1)}, u32[]{:S(2)}) copy-start(bf16[128,576]{1,0:T(8,128)(2,1)S(1)} %pad.9.weight_ref.rest_5_) | copy-start | bytes 442372
  89.8 29.5 %copy-start.26 = (f32[9,8,128]{2,1,0:T(8,128)}, f32[9,8,128]{2,1,0:T(8,128)S(1)}, u32[]{:S(2)}) copy-start(f32[9,8,128]{2,1,0:T(8,128)S(1)} %pad_maximum_fusion.rate_ref.rest_8_) | copy-start | bytes 110596
  124.1 3.0 collective-permute-start.13
  132.2 15.7 %collective-permute-start.14 = (bf16[256,1152]{1,0:T(8,128)(2,1)S(1)}, bf16[256,1152]{1,0:T(8,128)(2,1)S(1)}, u32[]{:S(2)}, u32[]{:S(2)}) collective-permute-start(bf16[256,1152]{1,0:T(8,128)(2,1)S(1)} %fusion.1), channel_id=1, source_target_pairs={{0,2},{1,3},{2,0},{3,1},{4,6},{5,7},{6,4},{7,5},{8,10},{9,11},{10,... | collective-permute-start | bytes 1769480 | tf_op jit(solution)/shard_map/ppermute | solution.py:25
  154.0 16.5 %collective-permute-start.16 = (bf16[256,1280]{1,0:T(8,128)(2,1)}, bf16[256,1280]{1,0:T(8,128)(2,1)}, u32[]{:S(2)}, u32[]{:S(2)}) collective-permute-start(bf16[256,1280]{1,0:T(8,128)(2,1)} %get-tuple-element.83.rest_0_), channel_id=1, source_target_pairs={{0,2},{1,3},{2,0},{3,1},{4,6},{5,7},{6,4},{7,5},{8,10},{9,11},{10,... | collective-permute-start | bytes 1966088 | tf_op jit(solution)/shard_map/ppermute | solution.py:25
  155.6 15.0 %collective-permute-start.18 = (bf16[256,1152]{1,0:T(8,128)(2,1)}, bf16[256,1152]{1,0:T(8,128)(2,1)S(1)}, u32[]{:S(2)}, u32[]{:S(2)}) collective-permute-start(bf16[256,1152]{1,0:T(8,128)(2,1)} %convolution_convert_fusion.rest_4_), channel_id=1, source_target_pairs={{0,1},{1,0},{2,3},{3,2},{4,5},{5,4},{6,7},{7,6},{8,9},{9,8},{10,11... | collective-permute-start | bytes 1769480 | tf_op jit(solution)/shard_map/ppermute | solution.py:25
  155.6 18.3 %collective-permute-start.20 = (bf16[2,288,768]{2,1,0:T(8,128)(2,1)}, bf16[2,288,768]{2,1,0:T(8,128)(2,1)}, u32[]{:S(2)}, u32[]{:S(2)}) collective-permute-start(bf16[2,288,768]{2,1,0:T(8,128)(2,1)} %get-tuple-element.85), channel_id=1, source_target_pairs={{0,1},{1,0},{2,3},{3,2},{4,5},{5,4},{6,7},{7,6},{8,9},{9,8},{10,11... | collective-permute-start | bytes 2654216 | tf_op jit(solution)/shard_map/ppermute | solution.py:25
  156.1 21.9 %collective-permute-start.21 = (bf16[2,288,768]{2,1,0:T(8,128)(2,1)}, bf16[2,288,768]{2,1,0:T(8,128)(2,1)}, u32[]{:S(2)}, u32[]{:S(2)}) collective-permute-start(bf16[2,288,768]{2,1,0:T(8,128)(2,1)} %collective-permute-done.12.rest_10_), channel_id=1, source_target_pairs={{0,4},{4,0},{8,12},{12,8},{16,20},{20,16},{24,28},{28,24},{1,5},{5... | collective-permute-start | bytes 2654216 | tf_op jit(solution)/shard_map/ppermute | solution.py:77
  156.1 21.9 %collective-permute-start.15 = (bf16[256,1280]{1,0:T(8,128)(2,1)}, bf16[256,1280]{1,0:T(8,128)(2,1)}, u32[]{:S(2)}, u32[]{:S(2)}) collective-permute-start(bf16[256,1280]{1,0:T(8,128)(2,1)} %get-tuple-element.83.rest_0_), channel_id=1, source_target_pairs={{0,1},{1,0},{2,3},{3,2},{4,5},{5,4},{6,7},{7,6},{8,9},{9,8},{10,11... | collective-permute-start | bytes 1966088 | tf_op jit(solution)/shard_map/ppermute | solution.py:25
  170.5 7.4 %collective-permute-start.17 = (bf16[256,1280]{1,0:T(8,128)(2,1)}, bf16[256,1280]{1,0:T(8,128)(2,1)}, u32[]{:S(2)}, u32[]{:S(2)}) collective-permute-start(bf16[256,1280]{1,0:T(8,128)(2,1)} %collective-permute-done.16.rest_2_), channel_id=1, source_target_pairs={{0,1},{1,0},{2,3},{3,2},{4,5},{5,4},{6,7},{7,6},{8,9},{9,8},{10,11... | collective-permute-start | bytes 1966088 | tf_op jit(solution)/shard_map/ppermute | solution.py:25
  171.4 2.5 collective-permute-start.19
  208.9 3.3 collective-permute-start.22
  214.4 16.9 %copy-start.13 = (s32[256,1]{1,0:T(8,128)S(1)}, s32[256,1]{1,0:T(8,128)}, u32[]{:S(2)}) copy-start(s32[256,1]{1,0:T(8,128)} %copy.44.routes_ref) | copy-start | bytes 3076
  214.4 16.9 %copy-start.18 = (f32[16,1152]{1,0:T(8,128)S(1)}, f32[16,1152]{1,0:T(8,128)}, u32[]{:S(2)}) copy-start(f32[16,1152]{1,0:T(8,128)} %copy-done.16) | copy-start | bytes 221188
  214.4 16.8 %collective-permute-start.23 = (bf16[256,1280]{1,0:T(8,128)(2,1)S(1)}, bf16[256,1280]{1,0:T(8,128)(2,1)S(1)}, u32[]{:S(2)}, u32[]{:S(2)}) collective-permute-start(bf16[256,1280]{1,0:T(8,128)(2,1)S(1)} %fusion), channel_id=1, source_target_pairs={{0,2},{1,3},{2,0},{3,1},{4,6},{5,7},{6,4},{7,5},{8,10},{9,11},{10,... | collective-permute-start | bytes 1966088 | tf_op jit(solution)/shard_map/ppermute | solution.py:25
  215.1 17.6 %copy-start.10 = (bf16[256,256]{1,0:T(8,128)(2,1)}, bf16[256,256]{1,0:T(8,128)(2,1)S(1)}, u32[]{:S(2)}) copy-start(bf16[256,256]{1,0:T(8,128)(2,1)S(1)} %fusion.9.order_ref) | copy-start | bytes 393220
  231.3 19.7 %copy-start.38 = (s32[6]{0:T(128)S(1)}, s32[6]{0:T(128)}, u32[]{:S(2)}) copy-start(s32[6]{0:T(128)} %copy-done.37) | copy-start | bytes 76
  234.3 14.6 %collective-permute-start.25 = (bf16[256,1152]{1,0:T(8,128)(2,1)S(1)}, bf16[256,1152]{1,0:T(8,128)(2,1)S(1)}, u32[]{:S(2)}, u32[]{:S(2)}) collective-permute-start(bf16[256,1152]{1,0:T(8,128)(2,1)S(1)} %get-tuple-element.91.rest_4_), channel_id=1, source_target_pairs={{0,2},{1,3},{2,0},{3,1},{4,6},{5,7},{6,4},{7,5},{8,10},{9,11},{10,... | collective-permute-start | bytes 1769480 | tf_op jit(solution)/shard_map/ppermute | solution.py:25
  234.8 14.2 %collective-permute-start.24 = (bf16[256,1152]{1,0:T(8,128)(2,1)S(1)}, bf16[256,1152]{1,0:T(8,128)(2,1)S(1)}, u32[]{:S(2)}, u32[]{:S(2)}) collective-permute-start(bf16[256,1152]{1,0:T(8,128)(2,1)S(1)} %get-tuple-element.91.rest_4_), channel_id=1, source_target_pairs={{0,1},{1,0},{2,3},{3,2},{4,5},{5,4},{6,7},{7,6},{8,9},{9,8},{10,11... | collective-permute-start | bytes 1769480 | tf_op jit(solution)/shard_map/ppermute | solution.py:25
  249.0 2.0 collective-permute-start.26
  264.1 48.3 %copy-start.43 = (bf16[2,288,576]{2,1,0:T(8,128)(2,1)}, bf16[2,288,576]{2,1,0:T(8,128)(2,1)S(1)}, u32[]{:S(2)}) copy-start(bf16[2,288,576]{2,1,0:T(8,128)(2,1)S(1)} %get-tuple-element.126) | copy-start | bytes 1990660
  264.1 48.3 %copy-start.44 = (bf16[2,288,576]{2,1,0:T(8,128)(2,1)}, bf16[2,288,576]{2,1,0:T(8,128)(2,1)S(1)}, u32[]{:S(2)}) copy-start(bf16[2,288,576]{2,1,0:T(8,128)(2,1)S(1)} %get-tuple-element.124) | copy-start | bytes 1990660
  313.8 3.8 collective-permute-start.27
  313.9 57.4 %collective-permute-start.34 = (bf16[2,256,1152]{2,1,0:T(8,128)(2,1)}, bf16[2,256,1152]{2,1,0:T(8,128)(2,1)}, u32[]{:S(2)}, u32[]{:S(2)}) collective-permute-start(bf16[2,256,1152]{2,1,0:T(8,128)(2,1)} %get-tuple-element.119), channel_id=1, source_target_pairs={{0,1},{1,0},{2,3},{3,2},{4,5},{5,4},{6,7},{7,6},{8,9},{9,8},{10,11... | collective-permute-start | bytes 3538952 | tf_op jit(solution)/shard_map/ppermute | solution.py:25
  315.1 18.8 %collective-permute-start.39 = (bf16[2,288,576]{2,1,0:T(8,128)(2,1)}, bf16[2,288,576]{2,1,0:T(8,128)(2,1)}, u32[]{:S(2)}, u32[]{:S(2)}) collective-permute-start(bf16[2,288,576]{2,1,0:T(8,128)(2,1)} %copy-done.44), channel_id=1, source_target_pairs={{0,4},{4,0},{8,12},{12,8},{16,20},{20,16},{24,28},{28,24},{1,5},{5... | collective-permute-start | bytes 1990664 | tf_op jit(solution)/shard_map/ppermute | solution.py:30
  316.0 44.0 %collective-permute-start.43 = (bf16[2,288,576]{2,1,0:T(8,128)(2,1)}, bf16[2,288,576]{2,1,0:T(8,128)(2,1)}, u32[]{:S(2)}, u32[]{:S(2)}) collective-permute-start(bf16[2,288,576]{2,1,0:T(8,128)(2,1)} %copy-done.43), channel_id=1, source_target_pairs={{0,8},{4,12},{8,0},{12,4},{16,24},{20,28},{24,16},{28,20},{1,9},{5... | collective-permute-start | bytes 1990664 | tf_op jit(solution)/shard_map/ppermute | solution.py:30
  318.9 19.6 %copy-start.29 = (bf16[576,128]{1,0:T(8,128)(2,1)S(1)}, bf16[576,128]{1,0:T(8,128)(2,1)}, u32[]{:S(2)}) copy-start(bf16[576,128]{1,0:T(8,128)(2,1)} %copy-done.28) | copy-start | bytes 442372
  318.9 19.6 %copy-start.35 = (f32[4,576]{1,0:T(4,128)S(1)}, f32[4,576]{1,0:T(4,128)}, u32[]{:S(2)}) copy-start(f32[4,576]{1,0:T(4,128)} %copy-done.34) | copy-start | bytes 27652
  318.9 19.6 %copy-start.39 = (s32[6]{0:T(128)S(1)}, s32[6]{0:T(128)}, u32[]{:S(2)}) copy-start(s32[6]{0:T(128)} %copy-done.37) | copy-start | bytes 76
  318.9 18.5 %collective-permute-start.28 = (f32[1024,128]{1,0:T(8,128)S(1)}, f32[1024,128]{1,0:T(8,128)}, u32[]{:S(2)}, u32[]{:S(2)}) collective-permute-start(f32[1024,128]{1,0:T(8,128)S(1)} %add.346), channel_id=1, source_target_pairs={{0,2},{1,3},{2,0},{3,1},{4,6},{5,7},{6,4},{7,5},{8,10},{9,11},{10,... | collective-permute-start | bytes 1572872 | tf_op jit(solution)/shard_map/ppermute | solution.py:25
  335.9 57.8 %collective-permute-start.40 = (bf16[1,288,576]{2,1,0:T(8,128)(2,1)}, bf16[1,288,576]{2,1,0:T(8,128)(2,1)}, u32[]{:S(2)}, u32[]{:S(2)}) collective-permute-start(bf16[1,288,576]{2,1,0:T(8,128)(2,1)} %add_convert_fusion.1), channel_id=1, source_target_pairs={{0,8},{4,12},{8,0},{12,4},{16,24},{20,28},{24,16},{28,20},{1,9},{5... | collective-permute-start | bytes 995336 | tf_op jit(solution)/shard_map/ppermute | solution.py:30
  349.9 19.2 %collective-permute-start.31 = (bf16[2,288,576]{2,1,0:T(8,128)(2,1)S(1)}, bf16[2,288,576]{2,1,0:T(8,128)(2,1)S(1)}, u32[]{:S(2)}, u32[]{:S(2)}) collective-permute-start(bf16[2,288,576]{2,1,0:T(8,128)(2,1)S(1)} %get-tuple-element.115), channel_id=1, source_target_pairs={{0,4},{4,0},{8,12},{12,8},{16,20},{20,16},{24,28},{28,24},{1,5},{5... | collective-permute-start | bytes 1990664 | tf_op jit(solution)/shard_map/ppermute | solution.py:30
  359.9 6.6 %collective-permute-start.29 = (f32[4,1152]{1,0:T(4,128)S(1)}, f32[4,1152]{1,0:T(4,128)S(1)}, u32[]{:S(2)}, u32[]{:S(2)}) collective-permute-start(f32[4,1152]{1,0:T(4,128)S(1)} %pad_maximum_fusion.1), channel_id=1, source_target_pairs={{0,1},{1,0},{2,3},{3,2},{4,5},{5,4},{6,7},{7,6},{8,9},{9,8},{10,11... | collective-permute-start | bytes 55304 | tf_op jit(solution)/shard_map/ppermute | solution.py:25
  362.4 19.6 %collective-permute-start.44 = (bf16[2,1,144,576]{3,2,1,0:T(8,128)(2,1)}, bf16[2,1,144,576]{3,2,1,0:T(8,128)(2,1)}, u32[]{:S(2)}, u32[]{:S(2)}) collective-permute-start(bf16[2,1,144,576]{3,2,1,0:T(8,128)(2,1)} %get-tuple-element.139), channel_id=1, source_target_pairs={{0,4},{4,0},{8,12},{12,8},{16,20},{20,16},{24,28},{28,24},{1,5},{5... | collective-permute-start | bytes 995336 | tf_op jit(solution)/shard_map/ppermute | solution.py:30
  366.5 18.5 %collective-permute-start.33 = (bf16[2,256,1152]{2,1,0:T(8,128)(2,1)}, bf16[2,256,1152]{2,1,0:T(8,128)(2,1)}, u32[]{:S(2)}, u32[]{:S(2)}) collective-permute-start(bf16[2,256,1152]{2,1,0:T(8,128)(2,1)} %get-tuple-element.116), channel_id=1, source_target_pairs={{0,1},{1,0},{2,3},{3,2},{4,5},{5,4},{6,7},{7,6},{8,9},{9,8},{10,11... | collective-permute-start | bytes 3538952 | tf_op jit(solution)/shard_map/ppermute | solution.py:25
  369.1 11.1 %collective-permute-start.30 = (f32[4,1152]{1,0:T(4,128)S(1)}, f32[4,1152]{1,0:T(4,128)S(1)}, u32[]{:S(2)}, u32[]{:S(2)}) collective-permute-start(f32[4,1152]{1,0:T(4,128)S(1)} %fusion.20), channel_id=1, source_target_pairs={{0,2},{1,3},{2,0},{3,1},{4,6},{5,7},{6,4},{7,5},{8,10},{9,11},{10,... | collective-permute-start | bytes 55304 | tf_op jit(solution)/shard_map/ppermute | solution.py:25
  377.6 34.6 %collective-permute-start.38 = (bf16[256,1152]{1,0:T(8,128)(2,1)}, bf16[256,1152]{1,0:T(8,128)(2,1)}, u32[]{:S(2)}, u32[]{:S(2)}) collective-permute-start(bf16[256,1152]{1,0:T(8,128)(2,1)} %fusion.3), channel_id=1, source_target_pairs={{0,2},{1,3},{2,0},{3,1},{4,6},{5,7},{6,4},{7,5},{8,10},{9,11},{10,... | collective-permute-start | bytes 1769480 | tf_op jit(solution)/shard_map/ppermute | solution.py:25
  381.9 8.9 %collective-permute-start.32 = (bf16[201,576]{1,0:T(8,128)(2,1)S(1)}, bf16[201,576]{1,0:T(8,128)(2,1)S(1)}, u32[]{:S(2)}, u32[]{:S(2)}) collective-permute-start(bf16[201,576]{1,0:T(8,128)(2,1)S(1)} %concatenate.29), channel_id=1, source_target_pairs={{0,4},{4,0},{8,12},{12,8},{16,20},{20,16},{24,28},{28,24},{1,5},{5... | collective-permute-start | bytes 694664 | tf_op jit(solution)/shard_map/ppermute | solution.py:30
  382.0 14.2 %collective-permute-start.36 = (bf16[1,288,576]{2,1,0:T(8,128)(2,1)}, bf16[1,288,576]{2,1,0:T(8,128)(2,1)S(1)}, u32[]{:S(2)}, u32[]{:S(2)}) collective-permute-start(bf16[1,288,576]{2,1,0:T(8,128)(2,1)} %get-tuple-element.141), channel_id=1, source_target_pairs={{0,8},{4,12},{8,0},{12,4},{16,24},{20,28},{24,16},{28,20},{1,9},{5... | collective-permute-start | bytes 995336 | tf_op jit(solution)/shard_map/ppermute | solution.py:30
  385.0 16.8 %collective-permute-start.45 = (bf16[1,1,144,576]{3,2,1,0:T(8,128)(2,1)S(1)}, bf16[1,1,144,576]{3,2,1,0:T(8,128)(2,1)S(1)}, u32[]{:S(2)}, u32[]{:S(2)}) collective-permute-start(bf16[1,1,144,576]{3,2,1,0:T(8,128)(2,1)S(1)} %add_convert_fusion.6), channel_id=1, source_target_pairs={{0,16},{4,20},{8,24},{12,28},{16,0},{20,4},{24,8},{28,12},{1,17},{... | collective-permute-start | bytes 497672 | tf_op jit(solution)/shard_map/ppermute | solution.py:30
  391.5 15.7 %collective-permute-start.35 = (bf16[201,576]{1,0:T(8,128)(2,1)S(1)}, bf16[201,576]{1,0:T(8,128)(2,1)S(1)}, u32[]{:S(2)}, u32[]{:S(2)}) collective-permute-start(bf16[201,576]{1,0:T(8,128)(2,1)S(1)} %add_convert_fusion.4), channel_id=1, source_target_pairs={{0,8},{4,12},{8,0},{12,4},{16,24},{20,28},{24,16},{28,20},{1,9},{5... | collective-permute-start | bytes 694664 | tf_op jit(solution)/shard_map/ppermute | solution.py:30
  393.7 18.6 %collective-permute-start.37 = (bf16[256,1152]{1,0:T(8,128)(2,1)S(1)}, bf16[256,1152]{1,0:T(8,128)(2,1)S(1)}, u32[]{:S(2)}, u32[]{:S(2)}) collective-permute-start(bf16[256,1152]{1,0:T(8,128)(2,1)S(1)} %fusion.2), channel_id=1, source_target_pairs={{0,2},{1,3},{2,0},{3,1},{4,6},{5,7},{6,4},{7,5},{8,10},{9,11},{10,... | collective-permute-start | bytes 1769480 | tf_op jit(solution)/shard_map/ppermute | solution.py:25
  401.8 20.7 %collective-permute-start.42 = (bf16[288,576]{1,0:T(8,128)(2,1)}, bf16[288,576]{1,0:T(8,128)(2,1)}, u32[]{:S(2)}, u32[]{:S(2)}) collective-permute-start(bf16[288,576]{1,0:T(8,128)(2,1)} %fusion.7), channel_id=1, source_target_pairs={{0,16},{1,20},{2,24},{3,28},{4,17},{5,21},{6,25},{7,29},{8,18},{9,... | collective-permute-start | bytes 995336 | tf_op jit(solution)/shard_map/ppermute | solution.py:1356
  401.9 20.6 %collective-permute-start.41 = (bf16[288,576]{1,0:T(8,128)(2,1)}, bf16[288,576]{1,0:T(8,128)(2,1)}, u32[]{:S(2)}, u32[]{:S(2)}) collective-permute-start(bf16[288,576]{1,0:T(8,128)(2,1)} %get-tuple-element.134), channel_id=1, source_target_pairs={{0,0},{1,4},{2,8},{3,12},{4,1},{5,5},{6,9},{7,13},{8,2},{9,6},{10,... | collective-permute-start | bytes 995336 | tf_op jit(solution)/shard_map/ppermute | solution.py:1355
  409.1 45.1 %collective-permute-start.47 = (bf16[201,576]{1,0:T(8,128)(2,1)}, bf16[201,576]{1,0:T(8,128)(2,1)}, u32[]{:S(2)}, u32[]{:S(2)}) collective-permute-start(bf16[201,576]{1,0:T(8,128)(2,1)} %add_convert_fusion.3), channel_id=1, source_target_pairs={{0,16},{4,20},{8,24},{12,28},{16,0},{20,4},{24,8},{28,12},{1,17},{... | collective-permute-start | bytes 694664 | tf_op jit(solution)/shard_map/ppermute | solution.py:30
  418.8 34.3 %collective-permute-start.46 = (bf16[1,576,384]{2,1,0:T(8,128)(2,1)S(1)}, bf16[1,576,384]{2,1,0:T(8,128)(2,1)S(1)}, u32[]{:S(2)}, u32[]{:S(2)}) collective-permute-start(bf16[1,576,384]{2,1,0:T(8,128)(2,1)S(1)} %get-tuple-element.144), channel_id=1, source_target_pairs={{0,0},{1,8},{2,16},{3,24},{4,1},{5,9},{6,17},{7,25},{8,2},{9,10},{... | collective-permute-start | bytes 1327112 | tf_op jit(solution)/shard_map/ppermute | solution.py:1293
  (64 other events, 397.1 us)
Sparse Core Ops, SparseCore 0:
  209.0 142.6 reduce-scatter.1
